TPU v7x, 128 devices: a whole 4x4x4 slice. The times are simulated.
128 devices in a mesh: dp: 4 (over y), region: 32 (over z, x, core).
Axes of the slice: x: 4, y: 4, z: 4, core: 2. Of those that a mesh axis runs over, the one named last changes fastest.
Arguments:
- features: bfloat16 [4, 32, 16, 16, 16, 128], P('dp', 'region'), may hold values from -6 to 6
- conv_weight: bfloat16 [3, 3, 3, 128, 128], replicated, may hold values from -0.109375 to 0.109375
- down_weight: bfloat16 [2, 2, 2, 128, 128], replicated, may hold values from -0.1875 to 0.1875
- coarse_cotangent: bfloat16 [4, 32, 16, 16, 16, 128], P('dp', 'region'), may hold values from -6 to 6
- brick_coords: int32 [4, 32, 3], P('dp', 'region'), may hold values from 0 to 31, as said below
- neighbours: int32 [4, 32, 26], P('dp', 'region'), may hold values from -1 to 31, as said below
- parents: int32 [4, 32], P('dp', 'region'), may hold values from 0 to 31, as said below
Outputs:
- coarse_features: bfloat16 [4, 32, 16, 16, 16, 128], P('dp', 'region')
- input_grad: bfloat16 [4, 32, 16, 16, 16, 128], P('dp', 'region')
- conv_grad: float32 [3, 3, 3, 128, 128], replicated
- down_grad: float32 [2, 2, 2, 128, 128], replicated
Inputs may be any that keep to these rules, and one draw needn't show every extreme that they name: `brick_coords`: slot s lies on region index s; its first coordinate is s, the second below 4, the third below 2; the coordinates of one scene's slots are distinct. `neighbours`: entry d names the slot whose coordinates are the brick's own plus offset d, or -1 where no slot has them; named slots lie on the same or an adjacent region index, and the relation is symmetric. `parents`: the parent is 2 (x // 2) + (y // 2) of the brick's coordinates; coarse brick c lies on region index c.
All inputs are finite; a program needn't handle non-finite values.
Results may differ from a plain program's by a relative error of at most 0.005.
Values may be sent and summed in bfloat16 or wider, within the bound.
No kernel may reach another device: no remote copies, remote signals or barrier semaphores. Data moves between devices by JAX's collectives and lax.ppermute only.
A program may use at most 192 MiB of HBM per device.

v0:
```python
import functools
import jax
import jax.numpy as jnp
from jax import lax
from jax.experimental import pallas as pl
from jax.experimental.pallas import tpu as pltpu
from jax.sharding import PartitionSpec as P

BF, F32 = jnp.bfloat16, jnp.float32
SMEM = pl.BlockSpec(memory_space=pltpu.SMEM)
VMEM = pl.BlockSpec(memory_space=pltpu.VMEM)
NN = (((1,), (0,)), ((), ()))
NT = (((1,), (1,)), ((), ()))
TN = (((0,), (0,)), ((), ()))


def dot(lhs, rhs, dims):
    return lax.dot_general(lhs, rhs, dims, preferred_element_type=F32)


def z_index(rows):
    return lax.broadcasted_iota(jnp.int32, (rows, 128), 0) % 16


def lay_interior(field_ref, shifts_ref):
    z = z_index(256)

    @pl.loop(0, 16)
    def _(x):
        plain = field_ref[x].reshape(256, 128)
        wide = plain.astype(F32)
        lower = jnp.where(z == 0, 0.0, pltpu.roll(wide, 1, 0)).astype(BF)
        upper = jnp.where(z == 15, 0.0, pltpu.roll(wide, 255, 0)).astype(BF)
        for c, value in enumerate((lower, plain, upper)):
            rows = value.reshape(8, 2, 16, 128)
            shifts_ref[c, x + 1, 0:8, 1] = rows[:, 0]
            shifts_ref[c, x + 1, 1:9, 0] = rows[:, 1]
            shifts_ref[c, x + 1, 0, 0] = jnp.zeros((16, 128), BF)
            shifts_ref[c, x + 1, 8, 1] = jnp.zeros((16, 128), BF)


def lay_slab(layer, flag, shifts_ref, place):
    def three(value, b):
        rows = value.shape[0] * 16
        wide = value.astype(F32).reshape(rows, 128)
        z = z_index(rows)
        below, same, above = (flag(b, c) for c in (-1, 0, 1))
        lower = jnp.where(
            z == 0, pltpu.roll(wide, rows - 15, 0) * below, pltpu.roll(wide, 1, 0) * same
        )
        upper = jnp.where(
            z == 15, pltpu.roll(wide, 15, 0) * above, pltpu.roll(wide, rows - 1, 0) * same
        )
        return [v.astype(BF) for v in (lower, wide * same, upper)]

    for c, value in enumerate(three(layer, 0)):
        rows = value.reshape(8, 2, 16, 128)
        shifts_ref[c, place, 0:8, 1] = rows[:, 0]
        shifts_ref[c, place, 1:9, 0] = rows[:, 1]
    for c, value in enumerate(three(layer[15:16], -1)):
        shifts_ref[c, place, 0, 0] = value
    for c, value in enumerate(three(layer[0:1], 1)):
        shifts_ref[c, place, 8, 1] = value


def lay_field(field_ref, low_ref, high_ref, near_ref, shifts_ref):
    def flag(first):
        return lambda b, c: (near_ref[first + 3 * (b + 1) + c + 1] >= 0).astype(F32)

    lay_slab(low_ref[...], flag(0), shifts_ref, 0)
    lay_slab(high_ref[...], flag(17), shifts_ref, 17)
    lay_interior(field_ref, shifts_ref)


def window(shifts_ref, c, x, count):
    return jnp.concatenate(
        [
            shifts_ref[c, pl.ds(x, count), t // 2 : t // 2 + 8, t % 2].reshape(count * 128, 128)
            for t in range(4)
        ],
        axis=1,
    )


def grad_kernel(coords_ref, parent_ref, own_ref, other_ref, down_ref, grads_ref, spread_ref, wide_ref):
    x, y, z = coords_ref[0], coords_ref[1], coords_ref[2]
    oy, oz = y % 2, z % 2
    is_own = parent_ref[0] == x
    wide_ref[...] = jnp.zeros_like(wide_ref)
    for i in range(8):
        mine = own_ref[8 * (x % 2) + i, pl.ds(8 * oy, 8)].astype(F32)
        theirs = other_ref[i, pl.ds(8 * oy, 8)].astype(F32)
        both = jnp.where(is_own, mine, theirs)
        part = jnp.where(oz == 0, both[:, 0:8], both[:, 8:16]).reshape(64, 128)
        wide_ref[i, pl.ds(0, 64, stride=2), :] = part
    weights = jnp.concatenate(
        [
            jnp.concatenate([down_ref[p, q, r] for r in range(2)], axis=1)
            for p in range(2)
            for q in range(2)
        ],
        axis=0,
    )
    for i in range(8):
        even = wide_ref[i]
        spread = jnp.concatenate([even, pltpu.roll(even, 1, 0)], axis=1).astype(BF)
        spread_ref[i] = spread
        grads = dot(spread, weights, NT).astype(BF)
        for p in range(2):
            for q in range(2):
                at = (2 * p + q) * 128
                grads_ref[2 * i + p, :, q] = grads[:, at : at + 128].reshape(8, 16, 128)


def main_kernel(
    coords_ref, parent_ref, near_ref, field_ref, low_ref, high_ref, conv_ref, down_ref, grads_ref,
    spread_ref, keep_ref, send_ref, kept_rows_ref, sent_rows_ref,
    shifts_ref, weights_ref, outputs_ref, sums_ref, *, tile=4,
):
    x, y, z = coords_ref[0], coords_ref[1], coords_ref[2]
    first_core = x % 2 == 0

    def part_rows(tap, rows):
        kept_rows_ref[tap] = jnp.where(first_core, rows[0:64], rows[64:128])
        sent_rows_ref[tap] = jnp.where(first_core, rows[64:128], rows[0:64]).astype(BF)

    kept_rows_ref[35] = jnp.zeros((64, 128), F32)
    sent_rows_ref[35] = jnp.zeros((64, 128), BF)
    lay_field(field_ref, low_ref, high_ref, near_ref, shifts_ref)
    zero = jnp.zeros((128, 128), BF)
    for a in range(3):
        for c in range(3):
            for t in range(4):
                for s in range(2):
                    weights_ref[a, c, t * 128 : t * 128 + 128, s * 128 : s * 128 + 128] = (
                        conv_ref[a, t - s, c] if 0 <= t - s <= 2 else zero
                    )
    down = jnp.concatenate(
        [
            jnp.concatenate([down_ref[p, q, r] for r in range(2)], axis=1)
            for p in range(2)
            for q in range(2)
        ],
        axis=0,
    )
    if True:
        keep_ref[...] = jnp.zeros_like(keep_ref)
        send_ref[...] = jnp.zeros_like(send_ref)
        kept = (parent_ref[0] == x).astype(F32)
        oy, oz = y % 2, z % 2

        @pl.loop(0, 16 // tile)
        def _(step):
            first = step * tile
            acc = None
            for a in range(3):
                for c in range(3):
                    part = dot(window(shifts_ref, c, first + a, tile), weights_ref[a, c], NN)
                    acc = part if acc is None else acc + part
            for s in range(2):
                field = field_ref[pl.ds(first, tile), :, s].astype(F32)
                outputs_ref[pl.ds(first, tile), :, s] = (
                    acc[:, s * 128 : s * 128 + 128].reshape(tile, 8, 16, 128) + field
                ).astype(BF)
            half = tile // 2
            corners = jnp.concatenate(
                [
                    jnp.concatenate(
                        [outputs_ref[first + 2 * i + p, :, q].reshape(128, 128) for i in range(half)], axis=0
                    )
                    for p in range(2)
                    for q in range(2)
                ],
                axis=1,
            )
            sums = dot(corners, down, NN)
            sums_ref[0] = sums[:, 0:128]
            sums_ref[1] = sums[:, 128:256]
            rows = half * 64
            block = sums_ref[0, pl.ds(0, rows, stride=2), :] + sums_ref[1, pl.ds(1, rows, stride=2), :]
            block = block.reshape(half * 8, 8, 128)
            none = jnp.zeros_like(block)
            low = jnp.where(oz == 0, block, none)
            high = jnp.where(oz == 0, none, block)
            placed = jnp.concatenate([low, high], axis=1).reshape(half, 8, 16, 128)
            keep_ref[pl.ds(step * half, half), pl.ds(8 * oy, 8)] = (placed * kept).astype(BF)
            send_ref[pl.ds(step * half, half), pl.ds(8 * oy, 8)] = (placed * (1 - kept)).astype(BF)

    if True:
        spread = spread_ref[...].reshape(1024, 256)
        for p in range(2):
            for q in range(2):
                corner = jnp.concatenate(
                    [outputs_ref[2 * i + p, :, q].reshape(128, 128) for i in range(8)], axis=0
                )
                result = dot(corner, spread, TN) * (1.0 / 1024)
                part_rows(27 + 4 * p + 2 * q, result[:, 0:128])
                part_rows(28 + 4 * p + 2 * q, result[:, 128:256])

    if True:
        pair = jnp.concatenate([grads_ref[:, :, s].reshape(2048, 128) for s in range(2)], axis=1)
        for c in range(3):
            @pl.loop(0, 3)
            def _(a):
                result = dot(window(shifts_ref, c, a, 16), pair, TN) * (1.0 / 1024)
                for b in range(3):
                    part_rows(
                        9 * a + 3 * b + c,
                        result[b * 128 : b * 128 + 128, 0:128]
                        + result[b * 128 + 128 : b * 128 + 256, 128:256],
                    )


def input_kernel(near_ref, field_ref, low_ref, high_ref, conv_ref, result_ref, shifts_ref, weights_ref, *, tile=4):
    lay_field(field_ref, low_ref, high_ref, near_ref, shifts_ref)
    zero = jnp.zeros((128, 128), BF)
    for a in range(3):
        for c in range(3):
            for t in range(4):
                for s in range(2):
                    weights_ref[a, c, s * 128 : s * 128 + 128, t * 128 : t * 128 + 128] = (
                        conv_ref[2 - a, 2 - t + s, 2 - c] if 0 <= t - s <= 2 else zero
                    )

    @pl.loop(0, 16 // tile)
    def _(step):
        first = step * tile
        acc = None
        for a in range(3):
            for c in range(3):
                part = dot(window(shifts_ref, c, first + a, tile), weights_ref[a, c], NT)
                acc = part if acc is None else acc + part
        for s in range(2):
            field = field_ref[pl.ds(first, tile), :, s].astype(F32)
            result_ref[pl.ds(first, tile), :, s] = (
                acc[:, s * 128 : s * 128 + 128].reshape(tile, 8, 16, 128) + field
            ).astype(BF)


def coarse_kernel(coords_ref, keep_ref, got_ref, coarse_ref):
    upper = coords_ref[0] % 2
    coarse_ref[pl.ds(8 * upper, 8)] = keep_ref[...]
    coarse_ref[pl.ds(8 * (1 - upper), 8)] = got_ref[...]


PARAMS = dict(compiler_params=pltpu.CompilerParams(vmem_limit_bytes=60 * 2**20))
sds = jax.ShapeDtypeStruct


def call(kernel, ins, outs, scratch=(), flops=0, moved=4 << 20):
    return pl.pallas_call(
        kernel,
        in_specs=ins,
        out_specs=[VMEM] * len(outs),
        out_shape=outs,
        scratch_shapes=list(scratch),
        cost_estimate=pl.CostEstimate(flops=flops, bytes_accessed=moved, transcendentals=0),
        **PARAMS,
    )


def grad_call(coords, parent, own, other, down):
    return call(
        grad_kernel, [SMEM] * 2 + [VMEM] * 3,
        [sds((16, 8, 2, 16, 128), BF), sds((8, 128, 256), BF)],
        [pltpu.VMEM((8, 128, 128), F32)], flops=2 * 2**27,
    )(coords, parent, own, other, down)


def main_call(coords, parent, near, field, low, high, conv, down, grads, spread, **kw):
    tile = kw.get("tile", 4)
    return call(
        functools.partial(main_kernel, **kw), [SMEM] * 3 + [VMEM] * 7,
        [sds((8, 16, 16, 128), BF)] * 2 + [sds((36, 64, 128), F32), sds((36, 64, 128), BF)],
        [pltpu.VMEM((3, 18, 9, 2, 16, 128), BF), pltpu.VMEM((3, 3, 512, 256), BF),
         pltpu.VMEM((16, 8, 2, 16, 128), BF), pltpu.VMEM((2, 64 * tile, 128), F32)], flops=2 * 9 * 2048 * 512 * 256 * 2,
    )(coords, parent, near, field, low, high, conv, down, grads, spread)


def input_call(near, field, low, high, conv, **kw):
    return call(
        functools.partial(input_kernel, **kw), [SMEM] + [VMEM] * 4, [sds((16, 8, 2, 16, 128), BF)],
        [pltpu.VMEM((3, 18, 9, 2, 16, 128), BF), pltpu.VMEM((3, 3, 256, 512), BF)], flops=2 * 9 * 2048 * 512 * 256,
    )(near, field, low, high, conv)[0]


def coarse_call(coords, keep, got):
    return call(coarse_kernel, [SMEM] + [VMEM] * 2, [sds((16, 16, 16, 128), BF)])(coords, keep, got)[0]


def spread_rows(coords_ref, y_ref, kept_ref, got_ref, own_ref, *send_refs):
    for k, ref in enumerate((own_ref, *send_refs)):
        at = pl.multiple_of(16 * ((y_ref[0] + k) % 4), 16)
        rows = kept_ref[:, pl.ds(at, 16)] + got_ref[:, pl.ds(at, 16)].astype(F32)
        ref[...] = rows.astype(ref.dtype)


def spread_taps(coords_ref, y_ref, kept_ref, *refs):
    got_refs, out_refs = refs[:3], refs[3:]
    x = (coords_ref[0] // 2) % 4
    for k, ref in enumerate(out_refs):
        taps = pl.ds(9 * ((x + k) % 4), 9)
        total = kept_ref[taps]
        for got_ref in got_refs:
            total = total + got_ref[taps].astype(F32)
        ref[...] = total.astype(ref.dtype)


def add_up(coords_ref, y_ref, kept_ref, first_ref, second_ref, third_ref, total_ref):
    total_ref[...] = kept_ref[...] + first_ref[...] + second_ref[...] + third_ref[...]


def add_in_order(coords_ref, y_ref, own_ref, *refs):
    z = coords_ref[0] // 8
    slots_ref, total_ref = refs[4], refs[3]
    for k, ref in enumerate((own_ref, *refs[:3])):
        slots_ref[(z - k + 4) % 4] = ref[...]
    total_ref[...] = ((slots_ref[0] + slots_ref[1]) + (slots_ref[2] + slots_ref[3])).astype(BF)


def join_taps(coords_ref, y_ref, own_ref, *refs):
    x = (coords_ref[0] // 2) % 4
    for k, ref in enumerate((own_ref, *refs[:3])):
        refs[3][pl.ds(9 * ((x - k + 4) % 4), 9)] = ref[...]


def join_rows(coords_ref, y_ref, own_ref, *refs):
    for k, ref in enumerate((own_ref, *refs[:3])):
        at = pl.multiple_of(16 * ((y_ref[0] - k + 4) % 4), 16)
        refs[3][:, pl.ds(at, 16)] = ref[...]


def finish(coords_ref, y_ref, own_ref, got_ref, conv_ref, down_ref):
    core = coords_ref[0] % 2
    mine = pl.ds(pl.multiple_of(64 * core, 64), 64)
    theirs = pl.ds(pl.multiple_of(64 * (1 - core), 64), 64)
    conv_ref[:, mine] = own_ref[0:27].astype(F32)
    conv_ref[:, theirs] = got_ref[0:27].astype(F32)
    down_ref[:, mine] = own_ref[27:35].astype(F32)
    down_ref[:, theirs] = got_ref[27:35].astype(F32)


def ring(size, step, by):
    return [(i, i - i // step % size * step + (i // step + by) % size * step) for i in range(32)]


def over_core(value):
    return lax.ppermute(value, "region", [(i, i ^ 1) for i in range(32)])


def over_x(value, by):
    return lax.ppermute(value, "region", ring(4, 2, by))


def over_z(value, by):
    return lax.ppermute(value, "region", ring(4, 8, by))


def over_y(value, by):
    return lax.ppermute(value, "dp", [(i, (i + by) % 4) for i in range(4)])


def summed(kept, sent, coords, y):
    def run(kernel, values, outs, scratch=()):
        return call(kernel, [SMEM] * 2 + [VMEM] * len(values), outs, scratch)(coords, y, *values)

    got = over_core(sent)
    own, *sends = run(
        spread_rows, (kept, got), [sds((36, 16, 128), F32)] + [sds((36, 16, 128), BF)] * 3
    )
    gots = [over_y(v, k + 1) for k, v in enumerate(sends)]
    own, *sends = run(spread_taps, (own, *gots), [sds((9, 16, 128), F32)] * 4)
    gots = [over_x(v, k + 1) for k, v in enumerate(sends)]
    own = run(add_up, (own, *gots), [sds((9, 16, 128), F32)])[0]
    gots = [over_z(own, k) for k in (1, 2, 3)]
    own = run(
        add_in_order, (own, *gots), [sds((9, 16, 128), BF)], [pltpu.VMEM((4, 9, 16, 128), F32)]
    )[0]
    gots = [over_x(own, k) for k in (1, 2, 3)]
    own = run(join_taps, (own, *gots), [sds((36, 16, 128), BF)])[0]
    gots = [over_y(own, k) for k in (1, 2, 3)]
    own = run(join_rows, (own, *gots), [sds((36, 64, 128), BF)])[0]
    got = over_core(own)
    return run(finish, (own, got), [sds((27, 128, 128), F32), sds((8, 128, 128), F32)])


def halo(field):
    low = lax.ppermute(field[15], "region", [(i, i + 1) for i in range(31)])
    high = lax.ppermute(field[0], "region", [(i + 1, i) for i in range(31)])
    return low, high


def local(features, conv_weight, down_weight, coarse_cotangent, brick_coords, neighbours, parents):
    coords, near, parent = brick_coords.reshape(3), neighbours.reshape(26), parents.reshape(1)
    y = lax.axis_index("dp").reshape(1).astype(jnp.int32)
    core = lax.axis_index("region") % 2
    cotangent = coarse_cotangent.reshape(16, 16, 16, 128)
    theirs = over_core(lax.dynamic_slice_in_dim(cotangent, 8 * (1 - core), 8))
    field = features.reshape(16, 8, 2, 16, 128)
    low, high = halo(features.reshape(16, 16, 16, 128))
    grads, spread = grad_call(coords, parent, cotangent, theirs, down_weight)
    grads_low, grads_high = halo(grads.reshape(16, 16, 16, 128))
    keep, send, kept, sent = main_call(
        coords, parent, near, field, low, high, conv_weight, down_weight, grads, spread
    )
    conv_grad, down_grad = summed(kept, sent, coords, y)
    got = over_core(send)
    input_grad = input_call(near, grads, grads_low, grads_high, conv_weight)
    coarse = coarse_call(coords, keep, got)
    whole = (1, 1, 16, 16, 16, 128)
    return (
        coarse.reshape(whole),
        input_grad.reshape(whole),
        conv_grad.reshape(3, 3, 3, 128, 128),
        down_grad.reshape(2, 2, 2, 128, 128),
    )


def solution(mesh):
    bricks = P("dp", "region", None, None, None, None)
    return jax.shard_map(
        local,
        mesh=mesh,
        in_specs=(bricks, P(), P(), bricks, P("dp", "region", None), P("dp", "region", None), P("dp", "region")),
        out_specs=(bricks, bricks, P(), P()),
        check_vma=False,
    )
```

profile of v0, /device:TPU:1, one launch (start us, length us, event | category | flops | bytes accessed | tf_op | source)
XLA Modules:
  0.0 125.1 jit_solution(10646852325850922450)
XLA Ops:
  0.6 1.1 dynamic-slice_bitcast_fusion
  1.7 1.5 %collective-permute-start.2 = (bf16[8,16,16,128]{3,2,1,0:T(8,128)(2,1)S(1)}, bf16[8,16,16,128]{3,2,1,0:T(8,128)(2,1)S(1)}, u32[]{:S(2)}, u32[]{:S(2)}) collective-permute-start(bf16[8,16,16,128]{3,2,1,0:T(8,128)(2,1)S(1)} %dynamic-slice_bitcast_fusion), channel_id=1, source_target_pairs={{0,1},{1,0},{2,3},{3,2},{4,5},{5,4},{6,7},{7,6},{8,9},{9,8},{10,11... | collective-permute-start | bytes 1572872 | tf_op jit(solution)/shard_map/ppermute | solution.py:348
  3.2 0.9 slice_bitcast_fusion
  4.1 3.1 %collective-permute-start = (bf16[16,16,128]{2,1,0:T(8,128)(2,1)S(1)}, bf16[16,16,128]{2,1,0:T(8,128)(2,1)S(1)}, u32[]{:S(2)}, u32[]{:S(2)}) collective-permute-start(bf16[16,16,128]{2,1,0:T(8,128)(2,1)S(1)} %get-tuple-element.39), channel_id=1, source_target_pairs={{0,1},{1,2},{2,3},{3,4},{4,5},{5,6},{6,7},{7,8},{8,9},{9,10},{10,1... | collective-permute-start | bytes 196616 | tf_op jit(solution)/shard_map/ppermute | solution.py:388
  7.2 1.9 %collective-permute-start.1 = (bf16[16,16,128]{2,1,0:T(8,128)(2,1)S(1)}, bf16[16,16,128]{2,1,0:T(8,128)(2,1)S(1)}, u32[]{:S(2)}, u32[]{:S(2)}) collective-permute-start(bf16[16,16,128]{2,1,0:T(8,128)(2,1)S(1)} %get-tuple-element.38), channel_id=1, source_target_pairs={{1,0},{2,1},{3,2},{4,3},{5,4},{6,5},{7,6},{8,7},{9,8},{10,9},{11,1... | collective-permute-start | bytes 196616 | tf_op jit(solution)/shard_map/ppermute | solution.py:389
  9.8 0.8 copy-done.3
  10.6 3.3 %shard_map.102 = (bf16[16,8,2,16,128]{4,3,2,1,0:T(8,128)(2,1)}, bf16[8,128,256]{2,1,0:T(8,128)(2,1)}) custom-call(s32[3]{0:T(128)} %bitcast.24, s32[1]{0:T(128)} %bitcast.18.parent_ref, bf16[16,16,16,128]{3,2,1,0:T(8,128)(2,1)} %bitcast.20, bf16[8,16,16,128]{3,2,1,0:T(8,128)(2,1)} %copy-done.3, bf16[2,2,2,128,128]{4,3,2,1,0:T(8,128)(2,1)} %down_ref.3), custom_call_target="tpu_custom_call" | custom-call | flops 268435456 | bytes 4194304 | tf_op jit(solution)/shard_map/pallas_call | solution.py:263
  14.5 18.6 %shard_map.103 = (bf16[8,16,16,128]{3,2,1,0:T(8,128)(2,1)}, bf16[8,16,16,128]{3,2,1,0:T(8,128)(2,1)}, f32[36,64,128]{2,1,0:T(8,128)}, bf16[36,64,128]{2,1,0:T(8,128)(2,1)}) custom-call(s32[3]{0:T(128)} %bitcast.25, s32[1]{0:T(128)} %bitcast.19.parent_ref, s32[26]{0:T(128)} %bitcast.37, bf16[16,8,2,16,128]{4,3,2,1,0:T(8,128)(2,1)} %bitcast.34, ...), custom_call_target="tpu_custom_call" | custom-call | flops 9663676416 | bytes 4194304 | tf_op jit(solution)/shard_map/pallas_call | solution.py:272
  33.2 2.2 %collective-permute-done.6.got_ref = bf16[36,64,128]{2,1,0:T(8,128)(2,1)S(1)} collective-permute-done((bf16[36,64,128]{2,1,0:T(8,128)(2,1)}, bf16[36,64,128]{2,1,0:T(8,128)(2,1)S(1)}, u32[]{:S(2)}, u32[]{:S(2)}) %collective-permute-start.6) | collective-permute-done | bytes 589856 | tf_op jit(solution)/shard_map/ppermute | solution.py:348
  35.4 0.8 copy-done
  36.2 2.5 %shard_map.106 = (f32[36,16,128]{2,1,0:T(8,128)}, bf16[36,16,128]{2,1,0:T(8,128)(2,1)}, bf16[36,16,128]{2,1,0:T(8,128)(2,1)}, bf16[36,16,128]{2,1,0:T(8,128)(2,1)}) custom-call(s32[3]{0:T(128)} %bitcast.26, s32[1]{0:T(128)} %bitcast.12.y_ref, f32[36,64,128]{2,1,0:T(8,128)} %get-tuple-element.24.kept_ref, bf16[36,64,128]{2,1,0:T(8,128)(2,1)} %copy-done), custom_call_target="tpu_custom_call" | custom-call | bytes 4194304 | tf_op jit(solution)/shard_map/pallas_call | solution.py:365
  38.7 1.3 %collective-permute-start.7 = (bf16[36,16,128]{2,1,0:T(8,128)(2,1)}, bf16[36,16,128]{2,1,0:T(8,128)(2,1)S(1)}, u32[]{:S(2)}, u32[]{:S(2)}) collective-permute-start(bf16[36,16,128]{2,1,0:T(8,128)(2,1)} %get-tuple-element.27), channel_id=1, source_target_pairs={{0,32},{32,64},{64,96},{96,0},{1,33},{33,65},{65,97},{97,1},{2,34}... | collective-permute-start | bytes 442376 | tf_op jit(solution)/shard_map/ppermute | solution.py:360
  40.0 2.6 %collective-permute-start.8 = (bf16[36,16,128]{2,1,0:T(8,128)(2,1)}, bf16[36,16,128]{2,1,0:T(8,128)(2,1)S(1)}, u32[]{:S(2)}, u32[]{:S(2)}) collective-permute-start(bf16[36,16,128]{2,1,0:T(8,128)(2,1)} %get-tuple-element.28), channel_id=1, source_target_pairs={{0,64},{32,96},{64,0},{96,32},{1,65},{33,97},{65,1},{97,33},{2,66}... | collective-permute-start | bytes 442376 | tf_op jit(solution)/shard_map/ppermute | solution.py:360
  42.6 1.1 collective-permute-start.9
  43.7 1.9 %collective-permute-done.7.refs_0_ = bf16[36,16,128]{2,1,0:T(8,128)(2,1)S(1)} collective-permute-done((bf16[36,16,128]{2,1,0:T(8,128)(2,1)}, bf16[36,16,128]{2,1,0:T(8,128)(2,1)S(1)}, u32[]{:S(2)}, u32[]{:S(2)}) %collective-permute-start.7) | collective-permute-done | bytes 147488 | tf_op jit(solution)/shard_map/ppermute | solution.py:360
  45.6 4.2 %collective-permute-done.8.refs_1_ = bf16[36,16,128]{2,1,0:T(8,128)(2,1)S(1)} collective-permute-done((bf16[36,16,128]{2,1,0:T(8,128)(2,1)}, bf16[36,16,128]{2,1,0:T(8,128)(2,1)S(1)}, u32[]{:S(2)}, u32[]{:S(2)}) %collective-permute-start.8) | collective-permute-done | bytes 147488 | tf_op jit(solution)/shard_map/ppermute | solution.py:360
  50.6 1.9 %shard_map.107 = (f32[9,16,128]{2,1,0:T(8,128)}, f32[9,16,128]{2,1,0:T(8,128)}, f32[9,16,128]{2,1,0:T(8,128)}, f32[9,16,128]{2,1,0:T(8,128)}) custom-call(s32[3]{0:T(128)} %bitcast.27, s32[1]{0:T(128)} %bitcast.12.y_ref, f32[36,16,128]{2,1,0:T(8,128)} %get-tuple-element.26.kept_ref, bf16[36,16,128]{2,1,0:T(8,128)(2,1)} %copy-done.4, ...), custom_call_target="tpu_custom_call" | custom-call | bytes 4194304 | tf_op jit(solution)/shard_map/pallas_call | solution.py:365
  52.5 1.2 collective-permute-start.10
  53.7 3.8 %collective-permute-start.11 = (f32[9,16,128]{2,1,0:T(8,128)}, f32[9,16,128]{2,1,0:T(8,128)S(1)}, u32[]{:S(2)}, u32[]{:S(2)}) collective-permute-start(f32[9,16,128]{2,1,0:T(8,128)} %get-tuple-element.32), channel_id=1, source_target_pairs={{0,4},{1,5},{2,6},{3,7},{4,0},{5,1},{6,2},{7,3},{8,12},{9,13},{10,... | collective-permute-start | bytes 221192 | tf_op jit(solution)/shard_map/ppermute | solution.py:352
  57.5 0.8 collective-permute-done.10.first_ref
  58.2 2.1 %collective-permute-done.11.second_ref = f32[9,16,128]{2,1,0:T(8,128)S(1)} collective-permute-done((f32[9,16,128]{2,1,0:T(8,128)}, f32[9,16,128]{2,1,0:T(8,128)S(1)}, u32[]{:S(2)}, u32[]{:S(2)}) %collective-permute-start.11) | collective-permute-done | bytes 73760 | tf_op jit(solution)/shard_map/ppermute | solution.py:352
  60.3 1.1 collective-permute-done.12.third_ref
  62.0 1.7 %shard_map.108.own_ref = f32[9,16,128]{2,1,0:T(8,128)} custom-call(s32[3]{0:T(128)} %bitcast.28, s32[1]{0:T(128)} %bitcast.12.y_ref, f32[9,16,128]{2,1,0:T(8,128)} %get-tuple-element.30.kept_ref, f32[9,16,128]{2,1,0:T(8,128)} %copy-done.10, f32[9,16,128]{2,1,0:T(8,128)} %copy-done.11, f32[9,16,128]{2,1,0:T(8,128)} %copy-done.13), custom_call_target="tpu_custom_call" | custom-call | bytes 4194304 | tf_op jit(solution)/shard_map/pallas_call | solution.py:365
  63.6 1.4 %collective-permute-start.13 = (f32[9,16,128]{2,1,0:T(8,128)}, f32[9,16,128]{2,1,0:T(8,128)S(1)}, u32[]{:S(2)}, u32[]{:S(2)}) collective-permute-start(f32[9,16,128]{2,1,0:T(8,128)} %shard_map.108.own_ref), channel_id=1, source_target_pairs={{0,8},{1,9},{2,10},{3,11},{4,12},{5,13},{6,14},{7,15},{8,16},{9,17... | collective-permute-start | bytes 221192 | tf_op jit(solution)/shard_map/ppermute | solution.py:356
  65.1 3.0 %collective-permute-start.14 = (f32[9,16,128]{2,1,0:T(8,128)}, f32[9,16,128]{2,1,0:T(8,128)S(1)}, u32[]{:S(2)}, u32[]{:S(2)}) collective-permute-start(f32[9,16,128]{2,1,0:T(8,128)} %shard_map.108.own_ref), channel_id=1, source_target_pairs={{0,16},{1,17},{2,18},{3,19},{4,20},{5,21},{6,22},{7,23},{8,24},{9,... | collective-permute-start | bytes 221192 | tf_op jit(solution)/shard_map/ppermute | solution.py:356
  68.1 0.7 collective-permute-start.15
  68.9 2.0 %collective-permute-done.14.refs_1_ = f32[9,16,128]{2,1,0:T(8,128)S(1)} collective-permute-done((f32[9,16,128]{2,1,0:T(8,128)}, f32[9,16,128]{2,1,0:T(8,128)S(1)}, u32[]{:S(2)}, u32[]{:S(2)}) %collective-permute-start.14) | collective-permute-done | bytes 73760 | tf_op jit(solution)/shard_map/ppermute | solution.py:356
  70.9 1.0 collective-permute-done.15.refs_2_
  72.5 1.7 %shard_map.109.own_ref = bf16[9,16,128]{2,1,0:T(8,128)(2,1)} custom-call(s32[3]{0:T(128)} %bitcast.29, s32[1]{0:T(128)} %bitcast.12.y_ref, f32[9,16,128]{2,1,0:T(8,128)} %shard_map.108.own_ref, f32[9,16,128]{2,1,0:T(8,128)} %copy-done.12, f32[9,16,128]{2,1,0:T(8,128)} %copy-done.14, f32[9,16,128]{2,1,0:T(8,128)} %copy-done.15), custom_call_target="tpu_custom_call" | custom-call | bytes 4194304 | tf_op jit(solution)/shard_map/pallas_call | solution.py:365
  74.2 1.2 collective-permute-start.16
  75.4 1.7 %collective-permute-start.17 = (bf16[9,16,128]{2,1,0:T(8,128)(2,1)}, bf16[9,16,128]{2,1,0:T(8,128)(2,1)S(1)}, u32[]{:S(2)}, u32[]{:S(2)}) collective-permute-start(bf16[9,16,128]{2,1,0:T(8,128)(2,1)} %shard_map.109.own_ref), channel_id=1, source_target_pairs={{0,4},{1,5},{2,6},{3,7},{4,0},{5,1},{6,2},{7,3},{8,12},{9,13},{10,... | collective-permute-start | bytes 110600 | tf_op jit(solution)/shard_map/ppermute | solution.py:352
  77.1 0.7 collective-permute-start.18
  78.4 1.5 %collective-permute-done.17.refs_1_ = bf16[9,16,128]{2,1,0:T(8,128)(2,1)S(1)} collective-permute-done((bf16[9,16,128]{2,1,0:T(8,128)(2,1)}, bf16[9,16,128]{2,1,0:T(8,128)(2,1)S(1)}, u32[]{:S(2)}, u32[]{:S(2)}) %collective-permute-start.17) | collective-permute-done | bytes 36896 | tf_op jit(solution)/shard_map/ppermute | solution.py:352
  81.1 1.5 %shard_map.110.own_ref = bf16[36,16,128]{2,1,0:T(8,128)(2,1)} custom-call(s32[3]{0:T(128)} %bitcast.30, s32[1]{0:T(128)} %bitcast.12.y_ref, bf16[9,16,128]{2,1,0:T(8,128)(2,1)} %shard_map.109.own_ref, bf16[9,16,128]{2,1,0:T(8,128)(2,1)} %copy-done.16, bf16[9,16,128]{2,1,0:T(8,128)(2,1)} %copy-done.17, bf16[9,16,128]{2,1,0:T(8,128)(2,1)} %copy-done.18), custom_call_target="tpu_custom_call" | custom-call | bytes 4194304 | tf_op jit(solution)/shard_map/pallas_call | solution.py:365
  82.7 0.8 collective-permute-start.19
  83.5 2.3 %collective-permute-start.20 = (bf16[36,16,128]{2,1,0:T(8,128)(2,1)}, bf16[36,16,128]{2,1,0:T(8,128)(2,1)S(1)}, u32[]{:S(2)}, u32[]{:S(2)}) collective-permute-start(bf16[36,16,128]{2,1,0:T(8,128)(2,1)} %shard_map.110.own_ref), channel_id=1, source_target_pairs={{0,64},{32,96},{64,0},{96,32},{1,65},{33,97},{65,1},{97,33},{2,66}... | collective-permute-start | bytes 442376 | tf_op jit(solution)/shard_map/ppermute | solution.py:360
  86.3 7.1 %collective-permute-start.3 = (bf16[8,16,16,128]{3,2,1,0:T(8,128)(2,1)S(1)}, bf16[8,16,16,128]{3,2,1,0:T(8,128)(2,1)S(1)}, u32[]{:S(2)}, u32[]{:S(2)}) collective-permute-start(bf16[8,16,16,128]{3,2,1,0:T(8,128)(2,1)S(1)} %copy-done.19), channel_id=1, source_target_pairs={{0,1},{1,0},{2,3},{3,2},{4,5},{5,4},{6,7},{7,6},{8,9},{9,8},{10,11... | collective-permute-start | bytes 1572872 | tf_op jit(solution)/shard_map/ppermute | solution.py:348
  94.8 2.0 %shard_map.111.own_ref = bf16[36,64,128]{2,1,0:T(8,128)(2,1)} custom-call(s32[3]{0:T(128)} %bitcast.31, s32[1]{0:T(128)} %bitcast.12.y_ref, bf16[36,16,128]{2,1,0:T(8,128)(2,1)} %shard_map.110.own_ref, bf16[36,16,128]{2,1,0:T(8,128)(2,1)} %copy-done.6, bf16[36,16,128]{2,1,0:T(8,128)(2,1)} %copy-done.8, bf16[36,16,128]{2,1,0:T(8,128)(2,1)} %copy-done.9), custom_call_target="tpu_custom_call" | custom-call | bytes 4194304 | tf_op jit(solution)/shard_map/pallas_call | solution.py:365
  96.9 3.2 %collective-permute-start.22 = (bf16[36,64,128]{2,1,0:T(8,128)(2,1)}, bf16[36,64,128]{2,1,0:T(8,128)(2,1)S(1)}, u32[]{:S(2)}, u32[]{:S(2)}) collective-permute-start(bf16[36,64,128]{2,1,0:T(8,128)(2,1)} %shard_map.111.own_ref), channel_id=1, source_target_pairs={{0,1},{1,0},{2,3},{3,2},{4,5},{5,4},{6,7},{7,6},{8,9},{9,8},{10,11... | collective-permute-start | bytes 1769480 | tf_op jit(solution)/shard_map/ppermute | solution.py:348
  100.0 0.9 fusion
  100.9 1.9 %collective-permute-start.4 = (bf16[16,16,128]{2,1,0:T(8,128)(2,1)S(1)}, bf16[16,16,128]{2,1,0:T(8,128)(2,1)S(1)}, u32[]{:S(2)}, u32[]{:S(2)}) collective-permute-start(bf16[16,16,128]{2,1,0:T(8,128)(2,1)S(1)} %bitcast.23), channel_id=1, source_target_pairs={{0,1},{1,2},{2,3},{3,4},{4,5},{5,6},{6,7},{7,8},{8,9},{9,10},{10,1... | collective-permute-start | bytes 196616 | tf_op jit(solution)/shard_map/ppermute | solution.py:388
  102.9 2.4 %collective-permute-start.5 = (bf16[16,16,128]{2,1,0:T(8,128)(2,1)S(1)}, bf16[16,16,128]{2,1,0:T(8,128)(2,1)S(1)}, u32[]{:S(2)}, u32[]{:S(2)}) collective-permute-start(bf16[16,16,128]{2,1,0:T(8,128)(2,1)S(1)} %bitcast.22), channel_id=1, source_target_pairs={{1,0},{2,1},{3,2},{4,3},{5,4},{6,5},{7,6},{8,7},{9,8},{10,9},{11,1... | collective-permute-start | bytes 196616 | tf_op jit(solution)/shard_map/ppermute | solution.py:389
  105.3 3.1 %collective-permute-done.5.high_ref = bf16[16,16,128]{2,1,0:T(8,128)(2,1)S(1)} collective-permute-done((bf16[16,16,128]{2,1,0:T(8,128)(2,1)S(1)}, bf16[16,16,128]{2,1,0:T(8,128)(2,1)S(1)}, u32[]{:S(2)}, u32[]{:S(2)}) %collective-permute-start.5) | collective-permute-done | bytes 65568 | tf_op jit(solution)/shard_map/ppermute | solution.py:389
  109.1 9.3 %shard_map.105 = bf16[16,8,2,16,128]{4,3,2,1,0:T(8,128)(2,1)} custom-call(s32[26]{0:T(128)} %bitcast.38, bf16[16,8,2,16,128]{4,3,2,1,0:T(8,128)(2,1)} %get-tuple-element.20.grads_ref.field_ref, bf16[16,16,128]{2,1,0:T(8,128)(2,1)} %copy-done.22, bf16[16,16,128]{2,1,0:T(8,128)(2,1)} %copy-done.23, bf16[3,3,3,128,128]{4,3,2,1,0:T(8,128)(2,1)} %conv_ref.3), custom_call_target="tpu_custom_call" | custom-call | flops 4831838208 | bytes 4194304 | tf_op jit(solution)/shard_map/pallas_call | solution.py:281
  118.4 0.8 copy-done.2
  119.2 2.3 %shard_map.104 = bf16[16,16,16,128]{3,2,1,0:T(8,128)(2,1)} custom-call(s32[3]{0:T(128)} %bitcast.32, bf16[8,16,16,128]{3,2,1,0:T(8,128)(2,1)} %get-tuple-element.22.keep_ref, bf16[8,16,16,128]{3,2,1,0:T(8,128)(2,1)} %copy-done.2), custom_call_target="tpu_custom_call" | custom-call | bytes 4194304 | tf_op jit(solution)/shard_map/pallas_call | solution.py:288
  121.5 0.8 copy-done.1
  122.3 2.8 %shard_map.112 = (f32[27,128,128]{2,1,0:T(8,128)}, f32[8,128,128]{2,1,0:T(8,128)}) custom-call(s32[3]{0:T(128)} %bitcast.33, s32[1]{0:T(128)} %bitcast.12.y_ref, bf16[36,64,128]{2,1,0:T(8,128)(2,1)} %shard_map.111.own_ref, bf16[36,64,128]{2,1,0:T(8,128)(2,1)} %copy-done.1), custom_call_target="tpu_custom_call" | custom-call | bytes 4194304 | tf_op jit(solution)/shard_map/pallas_call | solution.py:365
  (60 shorter events, 7.0 us)
Async XLA Ops:
  1.7 8.1 %collective-permute-start.2 = (bf16[8,16,16,128]{3,2,1,0:T(8,128)(2,1)S(1)}, bf16[8,16,16,128]{3,2,1,0:T(8,128)(2,1)S(1)}, u32[]{:S(2)}, u32[]{:S(2)}) collective-permute-start(bf16[8,16,16,128]{3,2,1,0:T(8,128)(2,1)S(1)} %dynamic-slice_bitcast_fusion), channel_id=1, source_target_pairs={{0,1},{1,0},{2,3},{3,2},{4,5},{5,4},{6,7},{7,6},{8,9},{9,8},{10,11... | collective-permute-start | bytes 1572872 | tf_op jit(solution)/shard_map/ppermute | solution.py:348
  4.1 9.8 %collective-permute-start = (bf16[16,16,128]{2,1,0:T(8,128)(2,1)S(1)}, bf16[16,16,128]{2,1,0:T(8,128)(2,1)S(1)}, u32[]{:S(2)}, u32[]{:S(2)}) collective-permute-start(bf16[16,16,128]{2,1,0:T(8,128)(2,1)S(1)} %get-tuple-element.39), channel_id=1, source_target_pairs={{0,1},{1,2},{2,3},{3,4},{4,5},{5,6},{6,7},{7,8},{8,9},{9,10},{10,1... | collective-permute-start | bytes 196616 | tf_op jit(solution)/shard_map/ppermute | solution.py:388
  7.2 6.7 %collective-permute-start.1 = (bf16[16,16,128]{2,1,0:T(8,128)(2,1)S(1)}, bf16[16,16,128]{2,1,0:T(8,128)(2,1)S(1)}, u32[]{:S(2)}, u32[]{:S(2)}) collective-permute-start(bf16[16,16,128]{2,1,0:T(8,128)(2,1)S(1)} %get-tuple-element.38), channel_id=1, source_target_pairs={{1,0},{2,1},{3,2},{4,3},{5,4},{6,5},{7,6},{8,7},{9,8},{10,9},{11,1... | collective-permute-start | bytes 196616 | tf_op jit(solution)/shard_map/ppermute | solution.py:389
  9.8 0.8 copy-start.3
  13.9 0.6 copy-start.20
  13.9 0.6 copy-start.21
  33.2 53.1 %copy-start.19 = (bf16[8,16,16,128]{3,2,1,0:T(8,128)(2,1)S(1)}, bf16[8,16,16,128]{3,2,1,0:T(8,128)(2,1)}, u32[]{:S(2)}) copy-start(bf16[8,16,16,128]{3,2,1,0:T(8,128)(2,1)} %get-tuple-element.23) | copy-start | bytes 1572868
  33.2 2.2 %collective-permute-start.6 = (bf16[36,64,128]{2,1,0:T(8,128)(2,1)}, bf16[36,64,128]{2,1,0:T(8,128)(2,1)S(1)}, u32[]{:S(2)}, u32[]{:S(2)}) collective-permute-start(bf16[36,64,128]{2,1,0:T(8,128)(2,1)} %get-tuple-element.25), channel_id=1, source_target_pairs={{0,1},{1,0},{2,3},{3,2},{4,5},{5,4},{6,7},{7,6},{8,9},{9,8},{10,11... | collective-permute-start | bytes 1769480 | tf_op jit(solution)/shard_map/ppermute | solution.py:348
  35.4 0.8 copy-start
  38.7 6.9 %collective-permute-start.7 = (bf16[36,16,128]{2,1,0:T(8,128)(2,1)}, bf16[36,16,128]{2,1,0:T(8,128)(2,1)S(1)}, u32[]{:S(2)}, u32[]{:S(2)}) collective-permute-start(bf16[36,16,128]{2,1,0:T(8,128)(2,1)} %get-tuple-element.27), channel_id=1, source_target_pairs={{0,32},{32,64},{64,96},{96,0},{1,33},{33,65},{65,97},{97,1},{2,34}... | collective-permute-start | bytes 442376 | tf_op jit(solution)/shard_map/ppermute | solution.py:360
  40.0 9.8 %collective-permute-start.8 = (bf16[36,16,128]{2,1,0:T(8,128)(2,1)}, bf16[36,16,128]{2,1,0:T(8,128)(2,1)S(1)}, u32[]{:S(2)}, u32[]{:S(2)}) collective-permute-start(bf16[36,16,128]{2,1,0:T(8,128)(2,1)} %get-tuple-element.28), channel_id=1, source_target_pairs={{0,64},{32,96},{64,0},{96,32},{1,65},{33,97},{65,1},{97,33},{2,66}... | collective-permute-start | bytes 442376 | tf_op jit(solution)/shard_map/ppermute | solution.py:360
  42.6 7.2 %collective-permute-start.9 = (bf16[36,16,128]{2,1,0:T(8,128)(2,1)}, bf16[36,16,128]{2,1,0:T(8,128)(2,1)S(1)}, u32[]{:S(2)}, u32[]{:S(2)}) collective-permute-start(bf16[36,16,128]{2,1,0:T(8,128)(2,1)} %get-tuple-element.29), channel_id=1, source_target_pairs={{0,96},{32,0},{64,32},{96,64},{1,97},{33,1},{65,33},{97,65},{2,98}... | collective-permute-start | bytes 442376 | tf_op jit(solution)/shard_map/ppermute | solution.py:360
  45.6 4.3 %copy-start.4 = (bf16[36,16,128]{2,1,0:T(8,128)(2,1)}, bf16[36,16,128]{2,1,0:T(8,128)(2,1)S(1)}, u32[]{:S(2)}) copy-start(bf16[36,16,128]{2,1,0:T(8,128)(2,1)S(1)} %collective-permute-done.7.refs_0_) | copy-start | bytes 442372
  49.8 0.7 copy-start.5
  49.8 0.7 copy-start.7
  52.5 5.8 %collective-permute-start.10 = (f32[9,16,128]{2,1,0:T(8,128)}, f32[9,16,128]{2,1,0:T(8,128)S(1)}, u32[]{:S(2)}, u32[]{:S(2)}) collective-permute-start(f32[9,16,128]{2,1,0:T(8,128)} %get-tuple-element.31), channel_id=1, source_target_pairs={{0,2},{1,3},{2,4},{3,5},{4,6},{5,7},{6,0},{7,1},{8,10},{9,11},{10,... | collective-permute-start | bytes 221192 | tf_op jit(solution)/shard_map/ppermute | solution.py:352
  53.7 6.6 %collective-permute-start.11 = (f32[9,16,128]{2,1,0:T(8,128)}, f32[9,16,128]{2,1,0:T(8,128)S(1)}, u32[]{:S(2)}, u32[]{:S(2)}) collective-permute-start(f32[9,16,128]{2,1,0:T(8,128)} %get-tuple-element.32), channel_id=1, source_target_pairs={{0,4},{1,5},{2,6},{3,7},{4,0},{5,1},{6,2},{7,3},{8,12},{9,13},{10,... | collective-permute-start | bytes 221192 | tf_op jit(solution)/shard_map/ppermute | solution.py:352
  57.5 3.9 %collective-permute-start.12 = (f32[9,16,128]{2,1,0:T(8,128)}, f32[9,16,128]{2,1,0:T(8,128)S(1)}, u32[]{:S(2)}, u32[]{:S(2)}) collective-permute-start(f32[9,16,128]{2,1,0:T(8,128)} %get-tuple-element.33), channel_id=1, source_target_pairs={{0,6},{1,7},{2,0},{3,1},{4,2},{5,3},{6,4},{7,5},{8,14},{9,15},{10,... | collective-permute-start | bytes 221192 | tf_op jit(solution)/shard_map/ppermute | solution.py:352
  58.2 3.1 %copy-start.10 = (f32[9,16,128]{2,1,0:T(8,128)}, f32[9,16,128]{2,1,0:T(8,128)S(1)}, u32[]{:S(2)}) copy-start(f32[9,16,128]{2,1,0:T(8,128)S(1)} %collective-permute-done.10.first_ref) | copy-start | bytes 221188
  60.3 1.1 copy-start.11
  61.4 0.6 copy-start.13
  63.6 5.2 %collective-permute-start.13 = (f32[9,16,128]{2,1,0:T(8,128)}, f32[9,16,128]{2,1,0:T(8,128)S(1)}, u32[]{:S(2)}, u32[]{:S(2)}) collective-permute-start(f32[9,16,128]{2,1,0:T(8,128)} %shard_map.108.own_ref), channel_id=1, source_target_pairs={{0,8},{1,9},{2,10},{3,11},{4,12},{5,13},{6,14},{7,15},{8,16},{9,17... | collective-permute-start | bytes 221192 | tf_op jit(solution)/shard_map/ppermute | solution.py:356
  65.1 5.8 %collective-permute-start.14 = (f32[9,16,128]{2,1,0:T(8,128)}, f32[9,16,128]{2,1,0:T(8,128)S(1)}, u32[]{:S(2)}, u32[]{:S(2)}) collective-permute-start(f32[9,16,128]{2,1,0:T(8,128)} %shard_map.108.own_ref), channel_id=1, source_target_pairs={{0,16},{1,17},{2,18},{3,19},{4,20},{5,21},{6,22},{7,23},{8,24},{9,... | collective-permute-start | bytes 221192 | tf_op jit(solution)/shard_map/ppermute | solution.py:356
  68.1 3.8 %collective-permute-start.15 = (f32[9,16,128]{2,1,0:T(8,128)}, f32[9,16,128]{2,1,0:T(8,128)S(1)}, u32[]{:S(2)}, u32[]{:S(2)}) collective-permute-start(f32[9,16,128]{2,1,0:T(8,128)} %shard_map.108.own_ref), channel_id=1, source_target_pairs={{0,24},{1,25},{2,26},{3,27},{4,28},{5,29},{6,30},{7,31},{8,0},{9,1... | collective-permute-start | bytes 221192 | tf_op jit(solution)/shard_map/ppermute | solution.py:356
  68.9 3.0 %copy-start.12 = (f32[9,16,128]{2,1,0:T(8,128)}, f32[9,16,128]{2,1,0:T(8,128)S(1)}, u32[]{:S(2)}) copy-start(f32[9,16,128]{2,1,0:T(8,128)S(1)} %collective-permute-done.13.refs_0_) | copy-start | bytes 221188
  70.9 1.1 copy-start.14
  71.9 0.6 copy-start.15
  74.2 4.2 %collective-permute-start.16 = (bf16[9,16,128]{2,1,0:T(8,128)(2,1)}, bf16[9,16,128]{2,1,0:T(8,128)(2,1)S(1)}, u32[]{:S(2)}, u32[]{:S(2)}) collective-permute-start(bf16[9,16,128]{2,1,0:T(8,128)(2,1)} %shard_map.109.own_ref), channel_id=1, source_target_pairs={{0,2},{1,3},{2,4},{3,5},{4,6},{5,7},{6,0},{7,1},{8,10},{9,11},{10,... | collective-permute-start | bytes 110600 | tf_op jit(solution)/shard_map/ppermute | solution.py:352
  75.4 4.5 %collective-permute-start.17 = (bf16[9,16,128]{2,1,0:T(8,128)(2,1)}, bf16[9,16,128]{2,1,0:T(8,128)(2,1)S(1)}, u32[]{:S(2)}, u32[]{:S(2)}) collective-permute-start(bf16[9,16,128]{2,1,0:T(8,128)(2,1)} %shard_map.109.own_ref), channel_id=1, source_target_pairs={{0,4},{1,5},{2,6},{3,7},{4,0},{5,1},{6,2},{7,3},{8,12},{9,13},{10,... | collective-permute-start | bytes 110600 | tf_op jit(solution)/shard_map/ppermute | solution.py:352
  77.1 3.0 %collective-permute-start.18 = (bf16[9,16,128]{2,1,0:T(8,128)(2,1)}, bf16[9,16,128]{2,1,0:T(8,128)(2,1)S(1)}, u32[]{:S(2)}, u32[]{:S(2)}) collective-permute-start(bf16[9,16,128]{2,1,0:T(8,128)(2,1)} %shard_map.109.own_ref), channel_id=1, source_target_pairs={{0,6},{1,7},{2,0},{3,1},{4,2},{5,3},{6,4},{7,5},{8,14},{9,15},{10,... | collective-permute-start | bytes 110600 | tf_op jit(solution)/shard_map/ppermute | solution.py:352
  78.4 1.7 %copy-start.16 = (bf16[9,16,128]{2,1,0:T(8,128)(2,1)}, bf16[9,16,128]{2,1,0:T(8,128)(2,1)S(1)}, u32[]{:S(2)}) copy-start(bf16[9,16,128]{2,1,0:T(8,128)(2,1)S(1)} %collective-permute-done.16.refs_0_) | copy-start | bytes 110596
  79.9 0.6 copy-start.17
  80.5 0.6 copy-start.18
  82.7 10.8 %collective-permute-start.19 = (bf16[36,16,128]{2,1,0:T(8,128)(2,1)}, bf16[36,16,128]{2,1,0:T(8,128)(2,1)S(1)}, u32[]{:S(2)}, u32[]{:S(2)}) collective-permute-start(bf16[36,16,128]{2,1,0:T(8,128)(2,1)} %shard_map.110.own_ref), channel_id=1, source_target_pairs={{0,32},{32,64},{64,96},{96,0},{1,33},{33,65},{65,97},{97,1},{2,34}... | collective-permute-start | bytes 442376 | tf_op jit(solution)/shard_map/ppermute | solution.py:360
  83.5 10.0 %collective-permute-start.20 = (bf16[36,16,128]{2,1,0:T(8,128)(2,1)}, bf16[36,16,128]{2,1,0:T(8,128)(2,1)S(1)}, u32[]{:S(2)}, u32[]{:S(2)}) collective-permute-start(bf16[36,16,128]{2,1,0:T(8,128)(2,1)} %shard_map.110.own_ref), channel_id=1, source_target_pairs={{0,64},{32,96},{64,0},{96,32},{1,65},{33,97},{65,1},{97,33},{2,66}... | collective-permute-start | bytes 442376 | tf_op jit(solution)/shard_map/ppermute | solution.py:360
  85.8 7.7 %collective-permute-start.21 = (bf16[36,16,128]{2,1,0:T(8,128)(2,1)}, bf16[36,16,128]{2,1,0:T(8,128)(2,1)S(1)}, u32[]{:S(2)}, u32[]{:S(2)}) collective-permute-start(bf16[36,16,128]{2,1,0:T(8,128)(2,1)} %shard_map.110.own_ref), channel_id=1, source_target_pairs={{0,96},{32,0},{64,32},{96,64},{1,97},{33,1},{65,33},{97,65},{2,98}... | collective-permute-start | bytes 442376 | tf_op jit(solution)/shard_map/ppermute | solution.py:360
  86.3 32.1 %collective-permute-start.3 = (bf16[8,16,16,128]{3,2,1,0:T(8,128)(2,1)S(1)}, bf16[8,16,16,128]{3,2,1,0:T(8,128)(2,1)S(1)}, u32[]{:S(2)}, u32[]{:S(2)}) collective-permute-start(bf16[8,16,16,128]{3,2,1,0:T(8,128)(2,1)S(1)} %copy-done.19), channel_id=1, source_target_pairs={{0,1},{1,0},{2,3},{3,2},{4,5},{5,4},{6,7},{7,6},{8,9},{9,8},{10,11... | collective-permute-start | bytes 1572872 | tf_op jit(solution)/shard_map/ppermute | solution.py:348
  93.5 0.7 copy-start.6
  93.5 0.7 copy-start.8
  94.2 0.7 copy-start.9
  96.9 24.6 %collective-permute-start.22 = (bf16[36,64,128]{2,1,0:T(8,128)(2,1)}, bf16[36,64,128]{2,1,0:T(8,128)(2,1)S(1)}, u32[]{:S(2)}, u32[]{:S(2)}) collective-permute-start(bf16[36,64,128]{2,1,0:T(8,128)(2,1)} %shard_map.111.own_ref), channel_id=1, source_target_pairs={{0,1},{1,0},{2,3},{3,2},{4,5},{5,4},{6,7},{7,6},{8,9},{9,8},{10,11... | collective-permute-start | bytes 1769480 | tf_op jit(solution)/shard_map/ppermute | solution.py:348
  100.9 4.3 %collective-permute-start.4 = (bf16[16,16,128]{2,1,0:T(8,128)(2,1)S(1)}, bf16[16,16,128]{2,1,0:T(8,128)(2,1)S(1)}, u32[]{:S(2)}, u32[]{:S(2)}) collective-permute-start(bf16[16,16,128]{2,1,0:T(8,128)(2,1)S(1)} %bitcast.23), channel_id=1, source_target_pairs={{0,1},{1,2},{2,3},{3,4},{4,5},{5,6},{6,7},{7,8},{8,9},{9,10},{10,1... | collective-permute-start | bytes 196616 | tf_op jit(solution)/shard_map/ppermute | solution.py:388
  102.9 5.6 %collective-permute-start.5 = (bf16[16,16,128]{2,1,0:T(8,128)(2,1)S(1)}, bf16[16,16,128]{2,1,0:T(8,128)(2,1)S(1)}, u32[]{:S(2)}, u32[]{:S(2)}) collective-permute-start(bf16[16,16,128]{2,1,0:T(8,128)(2,1)S(1)} %bitcast.22), channel_id=1, source_target_pairs={{1,0},{2,1},{3,2},{4,3},{5,4},{6,5},{7,6},{8,7},{9,8},{10,9},{11,1... | collective-permute-start | bytes 196616 | tf_op jit(solution)/shard_map/ppermute | solution.py:389
  105.3 3.2 %copy-start.22 = (bf16[16,16,128]{2,1,0:T(8,128)(2,1)}, bf16[16,16,128]{2,1,0:T(8,128)(2,1)S(1)}, u32[]{:S(2)}) copy-start(bf16[16,16,128]{2,1,0:T(8,128)(2,1)S(1)} %collective-permute-done.4.low_ref) | copy-start | bytes 196612
  108.4 0.6 copy-start.23
  118.4 0.8 copy-start.2
  121.5 0.8 copy-start.1
where the time goes:
time: 127 us; the launch traced here: 125 us
  Pallas kernels  47.5 us (37%)
  starting transfers between devices  43.6 us (34%)
  waiting for transfers between devices  20.8 us (16%)
  local copies, waits for them, and re-layouts  11.6 us (9%)
  between operations  1.47 us (1%)
    pallas_call x1, Pallas kernels, main_call(): call(functools.partial(main_kernel, **kw), [SMEM] * 3 + [VMEM] * 7, [sds(...  18.6 us
    pallas_call x7, Pallas kernels, run(): call(kernel, [SMEM] * 2 + [VMEM] * len(values), outs, scratch)  14 us
    ppermute x4, starting transfers between devices, over_core(): return lax.ppermute(value, 'region', [(i, i ^ 1) for i in range(32)])  11.8 us
    pallas_call x1, Pallas kernels, input_call(): call(functools.partial(input_kernel, **kw), [SMEM] + [VMEM] * 4, [sds((16...  9.34 us
    unnamed x48, local copies, waits for them, and re-layouts  8.81 us
    ppermute x6, starting transfers between devices, over_y(): return lax.ppermute(value, 'dp', [(i, (i + by) % 4) for i in range(4)])  8.64 us
    ppermute x6, starting transfers between devices, over_x(): return lax.ppermute(value, 'region', ring(4, 2, by))  8.58 us
    ppermute x6, waiting for transfers between devices, over_x(): return lax.ppermute(value, 'region', ring(4, 2, by))  6.24 us
  transfers between devices with their start and end apart: 23, of which 12 were waited for; matrix products, arithmetic and copies ran while one was open for 1% of the time, Pallas kernels for 14%

commit v1 on v0

v1 whole, which is shorter than its diff:
```python
import functools
import jax
import jax.numpy as jnp
from jax import lax
from jax.experimental import pallas as pl
from jax.experimental.pallas import tpu as pltpu
from jax.sharding import PartitionSpec as P

BF, F32 = jnp.bfloat16, jnp.float32
SMEM = pl.BlockSpec(memory_space=pltpu.SMEM)
VMEM = pl.BlockSpec(memory_space=pltpu.VMEM)
NN = (((1,), (0,)), ((), ()))
NT = (((1,), (1,)), ((), ()))
TN = (((0,), (0,)), ((), ()))


def dot(lhs, rhs, dims):
    return lax.dot_general(lhs, rhs, dims, preferred_element_type=F32)


def z_index(rows):
    return lax.broadcasted_iota(jnp.int32, (rows, 128), 0) % 16


def lay_interior(field_ref, shifts_ref, start=0, stop=16, base=1):
    z = z_index(256)

    @pl.loop(start, stop)
    def _(x):
        plain = field_ref[x].reshape(256, 128)
        wide = plain.astype(F32)
        lower = jnp.where(z == 0, 0.0, pltpu.roll(wide, 1, 0)).astype(BF)
        upper = jnp.where(z == 15, 0.0, pltpu.roll(wide, 255, 0)).astype(BF)
        for c, value in enumerate((lower, plain, upper)):
            rows = value.reshape(8, 2, 16, 128)
            shifts_ref[c, x + base, 0:8, 1] = rows[:, 0]
            shifts_ref[c, x + base, 1:9, 0] = rows[:, 1]
            shifts_ref[c, x + base, 0, 0] = jnp.zeros((16, 128), BF)
            shifts_ref[c, x + base, 8, 1] = jnp.zeros((16, 128), BF)


def lay_slab(layer, flag, slab_ref):
    def three(value, b):
        rows = value.shape[0] * 16
        wide = value.astype(F32).reshape(rows, 128)
        z = z_index(rows)
        below, same, above = (flag(b, c) for c in (-1, 0, 1))
        lower = jnp.where(
            z == 0, pltpu.roll(wide, rows - 15, 0) * below, pltpu.roll(wide, 1, 0) * same
        )
        upper = jnp.where(
            z == 15, pltpu.roll(wide, 15, 0) * above, pltpu.roll(wide, rows - 1, 0) * same
        )
        return [v.astype(BF) for v in (lower, wide * same, upper)]

    for c, value in enumerate(three(layer, 0)):
        rows = value.reshape(8, 2, 16, 128)
        slab_ref[c, 0:8, 1] = rows[:, 0]
        slab_ref[c, 1:9, 0] = rows[:, 1]
    for c, value in enumerate(three(layer[15:16], -1)):
        slab_ref[c, 0, 0] = value.reshape(16, 128)
    for c, value in enumerate(three(layer[0:1], 1)):
        slab_ref[c, 8, 1] = value.reshape(16, 128)


def near_flag(near_ref, first):
    return lambda b, c: (near_ref[first + 3 * (b + 1) + c + 1] >= 0).astype(F32)


def window(shifts_ref, c, x, count):
    return jnp.concatenate(
        [
            shifts_ref[c, pl.ds(x, count), t // 2 : t // 2 + 8, t % 2].reshape(count * 128, 128)
            for t in range(4)
        ],
        axis=1,
    )


def joined_down(down_ref):
    return jnp.concatenate(
        [
            jnp.concatenate([down_ref[p, q, r] for r in range(2)], axis=1)
            for p in range(2)
            for q in range(2)
        ],
        axis=0,
    )


def grad_kernel(
    coords_ref, parent_ref, own_ref, other_ref, down_ref, field_ref,
    grads_ref, spread_ref, up_ref, back_ref, wide_ref, sems,
):
    last = pltpu.make_async_copy(field_ref.at[15], up_ref.at[0], sems.at[0])
    first = pltpu.make_async_copy(field_ref.at[0], back_ref.at[0], sems.at[1])
    last.start()
    first.start()
    x, oy, oz = coords_ref[0], coords_ref[1] % 2, coords_ref[2] % 2
    is_own = parent_ref[0] == x
    down = joined_down(down_ref)
    wide_ref[...] = jnp.zeros_like(wide_ref)
    for i in range(8):
        mine = own_ref[8 * (x % 2) + i, pl.ds(8 * oy, 8)].astype(F32)
        theirs = other_ref[i, pl.ds(8 * oy, 8)].astype(F32)
        both = jnp.where(is_own, mine, theirs)
        part = jnp.where(oz == 0, both[:, 0:8], both[:, 8:16]).reshape(64, 128)
        wide_ref[i, pl.ds(0, 64, stride=2), :] = part
    for i in range(8):
        even = wide_ref[i]
        spread = jnp.concatenate([even, pltpu.roll(even, 1, 0)], axis=1).astype(BF)
        spread_ref[i] = spread
        grads = dot(spread, down, NT).astype(BF)
        for p in range(2):
            for q in range(2):
                at = (2 * p + q) * 128
                part = grads[:, at : at + 128].reshape(8, 16, 128)
                grads_ref[2 * i + p, :, q] = part
                if 2 * i + p == 15:
                    up_ref[1, :, q] = part
                if 2 * i + p == 0:
                    back_ref[1, :, q] = part
    last.wait()
    first.wait()


def lay_weights(conv_ref, weights_ref):
    zero = jnp.zeros((128, 128), BF)
    for a in range(3):
        for c in range(3):
            for t in range(4):
                for s in range(2):
                    weights_ref[a, c, t * 128 : t * 128 + 128, s * 128 : s * 128 + 128] = (
                        conv_ref[a, t - s, c] if 0 <= t - s <= 2 else zero
                    )


def inner_kernel(field_ref, conv_ref, shifts_ref, weights_ref, outputs_ref):
    lay_interior(field_ref, shifts_ref, 0, 16, 0)
    lay_weights(conv_ref, weights_ref)
    for first, count in ((1, 7), (8, 7)):
        acc = None
        for a in range(3):
            for c in range(3):
                part = dot(window(shifts_ref, c, first + a - 1, count), weights_ref[a, c], NN)
                acc = part if acc is None else acc + part
        for s in range(2):
            field = field_ref[first : first + count, :, s].astype(F32)
            outputs_ref[first : first + count, :, s] = (
                acc[:, s * 128 : s * 128 + 128].reshape(count, 8, 16, 128) + field
            ).astype(BF)


def taps(rows):
    return jnp.concatenate(
        [rows[t // 2 : t // 2 + 8, t % 2].reshape(128, 128) for t in range(4)], axis=1
    )


def main_kernel(
    coords_ref, parent_ref, near_ref, field_ref, low_ref, high_ref, shifts_ref, weights_ref,
    inner_ref, down_ref, grads_ref, spread_ref,
    kept_rows_ref, sent_ref, keep_ref, low_shifts_ref, high_shifts_ref, edges_ref, sums_ref,
):
    x, oy, oz = coords_ref[0], coords_ref[1] % 2, coords_ref[2] % 2
    first_core = x % 2 == 0
    kept = (parent_ref[0] == x).astype(F32)

    def part_rows(tap, rows):
        kept_rows_ref[tap] = jnp.where(first_core, rows[0:64], rows[64:128])
        sent_ref[tap] = jnp.where(first_core, rows[64:128], rows[0:64]).astype(BF)

    kept_rows_ref[35] = jnp.zeros((64, 128), F32)
    sent_ref[35] = jnp.zeros((64, 128), BF)
    sent_ref[52] = jnp.full((64, 128), oy, jnp.int32).astype(F32).astype(BF)
    lay_slab(low_ref[0].reshape(16, 16, 128), near_flag(near_ref, 0), low_shifts_ref)
    lay_slab(high_ref[0].reshape(16, 16, 128), near_flag(near_ref, 17), high_shifts_ref)

    acc = None
    for a in range(3):
        for c in range(3):
            below = taps(low_shifts_ref[c] if a == 0 else shifts_ref[c, a - 1])
            above = taps(high_shifts_ref[c] if a == 2 else shifts_ref[c, 14 + a])
            part = dot(jnp.concatenate([below, above], axis=0), weights_ref[a, c], NN)
            acc = part if acc is None else acc + part
    for s in range(2):
        for k in range(2):
            value = acc[128 * k : 128 * k + 128, s * 128 : s * 128 + 128].reshape(8, 16, 128)
            edges_ref[k, :, s] = (value + field_ref[15 * k, :, s].astype(F32)).astype(BF)

    down = joined_down(down_ref)

    def corner(i, p, q):
        at = 2 * i + p
        rows = edges_ref[at // 15, :, q] if at in (0, 15) else inner_ref[at, :, q]
        return rows.reshape(128, 128)

    for i in range(8):
        corners = jnp.concatenate([corner(i, p, q) for p in range(2) for q in range(2)], axis=1)
        sums = dot(corners, down, NN)
        sums_ref[i, 0] = sums[:, 0:128]
        sums_ref[i, 1] = sums[:, 128:256]
        block = sums_ref[i, 0, pl.ds(0, 64, stride=2), :] + sums_ref[i, 1, pl.ds(1, 64, stride=2), :]
        block = block.reshape(8, 8, 128)
        none = jnp.zeros_like(block)
        low = jnp.where(oz == 0, block, none)
        high = jnp.where(oz == 0, none, block)
        placed = jnp.concatenate([low, high], axis=1).reshape(128, 128)
        keep_ref[i] = (placed * kept).astype(BF).reshape(8, 16, 128)
        away = (placed * (1 - kept)).astype(BF)
        sent_ref[36 + 2 * i] = away[0:64]
        sent_ref[37 + 2 * i] = away[64:128]

    spread = spread_ref[...].reshape(1024, 256)
    for p in range(2):
        for q in range(2):
            rows = jnp.concatenate([corner(i, p, q) for i in range(8)], axis=0)
            result = dot(rows, spread, TN) * (1.0 / 1024)
            part_rows(27 + 4 * p + 2 * q, result[:, 0:128])
            part_rows(28 + 4 * p + 2 * q, result[:, 128:256])

    pair = jnp.concatenate([grads_ref[:, :, s].reshape(2048, 128) for s in range(2)], axis=1)
    for a in range(3):
        for c in range(3):
            if a == 0:
                rows = jnp.concatenate(
                    [taps(low_shifts_ref[c]), window(shifts_ref, c, 0, 15)], axis=0
                )
            elif a == 1:
                rows = window(shifts_ref, c, 0, 16)
            else:
                rows = jnp.concatenate(
                    [window(shifts_ref, c, 1, 15), taps(high_shifts_ref[c])], axis=0
                )
            result = dot(rows, pair, TN) * (1.0 / 1024)
            for b in range(3):
                part_rows(
                    9 * a + 3 * b + c,
                    result[b * 128 : b * 128 + 128, 0:128]
                    + result[b * 128 + 128 : b * 128 + 256, 128:256],
                )


def input_kernel(near_ref, field_ref, layer_ref, conv_ref, *refs, half, tile=4):
    result_ref, token_ref, shifts_ref, weights_ref, held_ref, sems = refs[-6:]
    token_ref[...] = jnp.zeros_like(token_ref)
    if half == 0:
        lay_slab(layer_ref[1].reshape(16, 16, 128), near_flag(near_ref, 0), shifts_ref.at[:, 0])
        lay_interior(field_ref, shifts_ref, 0, 9, 1)
    else:
        lay_interior(field_ref, shifts_ref, 7, 16, -7)
        lay_slab(layer_ref[1].reshape(16, 16, 128), near_flag(near_ref, 17), shifts_ref.at[:, 9])
    zero = jnp.zeros((128, 128), BF)
    for a in range(3):
        for c in range(3):
            for t in range(4):
                for s in range(2):
                    weights_ref[a, c, s * 128 : s * 128 + 128, t * 128 : t * 128 + 128] = (
                        conv_ref[2 - a, 2 - t + s, 2 - c] if 0 <= t - s <= 2 else zero
                    )
    copies = []
    for step in range(8 // tile):
        first = step * tile
        acc = None
        for a in range(3):
            for c in range(3):
                part = dot(window(shifts_ref, c, first + a, tile), weights_ref[a, c], NT)
                acc = part if acc is None else acc + part
        here = 8 * half + first
        for s in range(2):
            field = field_ref[here : here + tile, :, s].astype(F32)
            held_ref[first : first + tile, :, s] = (
                acc[:, s * 128 : s * 128 + 128].reshape(tile, 8, 16, 128) + field
            ).astype(BF)
        copy = pltpu.make_async_copy(
            held_ref.at[pl.ds(first, tile)], result_ref.at[pl.ds(here, tile)], sems.at[step]
        )
        copy.start()
        copies.append(copy)
    for copy in copies:
        copy.wait()


def coarse_kernel(coords_ref, keep_ref, got_ref, coarse_ref, token_ref, held_ref, sems):
    token_ref[...] = jnp.zeros_like(token_ref)
    upper, oy = coords_ref[0] % 2, coords_ref[1] % 2
    there = got_ref[52, 0:16].astype(F32)
    none = jnp.zeros((8, 16, 128), BF)
    for i in range(8):
        rows = jnp.concatenate([got_ref[36 + 2 * i], got_ref[37 + 2 * i]], axis=0)
        rows = rows.reshape(8, 16, 128).astype(F32)
        held_ref[0, i, pl.ds(8 * oy, 8)] = keep_ref[i]
        held_ref[0, i, pl.ds(8 - 8 * oy, 8)] = none
        held_ref[1, i, 0:8] = jnp.where(there == 0, rows, 0.0).astype(BF)
        held_ref[1, i, 8:16] = jnp.where(there == 1, rows, 0.0).astype(BF)
    keep = pltpu.make_async_copy(held_ref.at[0], coarse_ref.at[pl.ds(8 * upper, 8)], sems.at[0])
    got = pltpu.make_async_copy(held_ref.at[1], coarse_ref.at[pl.ds(8 - 8 * upper, 8)], sems.at[1])
    keep.start()
    got.start()
    keep.wait()
    got.wait()


ANY = pl.BlockSpec(memory_space=pl.ANY)
TOKEN = jax.ShapeDtypeStruct((8, 128), F32)
sds = jax.ShapeDtypeStruct


def call(kernel, ins, outs, scratch=(), flops=0, moved=1 << 20, limit=8, out=VMEM, **kw):
    return pl.pallas_call(
        kernel,
        in_specs=ins,
        out_specs=[VMEM if shape is TOKEN else out for shape in outs],
        out_shape=outs,
        scratch_shapes=list(scratch),
        cost_estimate=pl.CostEstimate(flops=flops, bytes_accessed=moved, transcendentals=0),
        compiler_params=pltpu.CompilerParams(vmem_limit_bytes=limit << 20),
        **kw,
    )


def grad_call(coords, parent, own, other, down, field):
    layers = sds((2, 8, 2, 16, 128), BF)
    return call(
        grad_kernel, [SMEM] * 2 + [VMEM] * 3 + [ANY],
        [sds((16, 8, 2, 16, 128), BF), sds((8, 128, 256), BF), layers, layers],
        [pltpu.VMEM((8, 128, 128), F32), pltpu.SemaphoreType.DMA((2,))],
        flops=2 * 2**27, moved=4 << 20,
    )(coords, parent, own, other, down, field)


def inner_call(field, conv):
    return call(
        inner_kernel, [VMEM] * 2,
        [sds((3, 16, 9, 2, 16, 128), BF), sds((3, 3, 512, 256), BF), sds((16, 8, 2, 16, 128), BF)],
        flops=2 * 9 * 2048 * 512 * 256, moved=2 << 20, limit=16,
    )(field, conv)


def main_call(coords, parent, near, field, low, high, inner, down, grads, spread):
    slab = pltpu.VMEM((3, 9, 2, 16, 128), BF)
    return call(
        main_kernel, [SMEM] * 3 + [VMEM] * 9,
        [sds((36, 64, 128), F32), sds((53, 64, 128), BF), sds((8, 8, 16, 128), BF)],
        [slab, slab, pltpu.VMEM((2, 8, 2, 16, 128), BF), pltpu.VMEM((8, 2, 128, 128), F32)],
        flops=2 * 9 * 2048 * 512 * 256, limit=24,
    )(coords, parent, near, field, low, high, *inner, down, grads, spread)


def input_call(near, field, layer, conv, after, half, base=None):
    ins, values = [SMEM] + [VMEM] * 3 + [ANY], [near, field, layer, conv, after]
    aliases = {}
    if base is not None:
        ins, values, aliases = ins + [ANY], values + [base], {5: 0}
    return call(
        functools.partial(input_kernel, half=half), ins, [sds((16, 8, 2, 16, 128), BF), TOKEN],
        [pltpu.VMEM((3, 10, 9, 2, 16, 128), BF), pltpu.VMEM((3, 3, 256, 512), BF),
         pltpu.VMEM((8, 8, 2, 16, 128), BF), pltpu.SemaphoreType.DMA((2,))],
        flops=9 * 2048 * 512 * 256, limit=24, out=ANY, input_output_aliases=aliases,
    )(*values)


def coarse_call(coords, keep, got, after):
    def kernel(coords_ref, keep_ref, got_ref, after_ref, *refs):
        coarse_kernel(coords_ref, keep_ref, got_ref, *refs)

    return call(
        kernel, [SMEM] + [VMEM] * 2 + [ANY], [sds((16, 16, 16, 128), BF), TOKEN],
        [pltpu.VMEM((2, 8, 16, 16, 128), BF), pltpu.SemaphoreType.DMA((2,))], out=ANY,
    )(coords, keep, got, after)


def places(coords_ref, y_ref):
    core, x = coords_ref[0] % 2, (coords_ref[0] // 2) % 4
    return jnp.where(core == 0, y_ref[0], x), jnp.where(core == 0, x, y_ref[0])


def spread_rows(coords_ref, y_ref, kept_ref, got_ref, own_ref, *send_refs):
    place = places(coords_ref, y_ref)[0]
    for k, ref in enumerate((own_ref, *send_refs)):
        at = pl.multiple_of(16 * ((place + k) % 4), 16)
        rows = kept_ref[:, pl.ds(at, 16)] + got_ref[0:36, pl.ds(at, 16)].astype(F32)
        ref[...] = rows.astype(ref.dtype)


def spread_taps(coords_ref, y_ref, kept_ref, *refs):
    got_refs, out_refs = refs[:3], refs[-4:]
    x = places(coords_ref, y_ref)[1]
    for k, ref in enumerate(out_refs):
        taps = pl.ds(9 * ((x + k) % 4), 9)
        total = kept_ref[taps]
        for got_ref in got_refs:
            total = total + got_ref[taps].astype(F32)
        ref[...] = total.astype(ref.dtype)


def add_up(coords_ref, y_ref, kept_ref, first_ref, second_ref, third_ref, *refs):
    refs[-1][...] = kept_ref[...] + first_ref[...] + second_ref[...] + third_ref[...]


def add_pair(coords_ref, y_ref, own_ref, got_ref, *refs):
    refs[-1][...] = (own_ref[...] + got_ref[...]).astype(refs[-1].dtype)


def join_taps(coords_ref, y_ref, own_ref, *refs):
    x = places(coords_ref, y_ref)[1]
    for k, ref in enumerate((own_ref, *refs[:3])):
        refs[-1][pl.ds(9 * ((x - k + 4) % 4), 9)] = ref[...]


def join_rows(coords_ref, y_ref, own_ref, *refs):
    place = places(coords_ref, y_ref)[0]
    for k, ref in enumerate((own_ref, *refs[:3])):
        at = pl.multiple_of(16 * ((place - k + 4) % 4), 16)
        refs[-1][:, pl.ds(at, 16)] = ref[...]


def finish(coords_ref, y_ref, own_ref, got_ref, conv_ref, down_ref):
    core = coords_ref[0] % 2
    mine = pl.ds(pl.multiple_of(64 * core, 64), 64)
    theirs = pl.ds(pl.multiple_of(64 * (1 - core), 64), 64)
    conv_ref[:, mine] = own_ref[0:27].astype(F32)
    conv_ref[:, theirs] = got_ref[0:27].astype(F32)
    down_ref[:, mine] = own_ref[27:35].astype(F32)
    down_ref[:, theirs] = got_ref[27:35].astype(F32)


def ring(size, step, by):
    return [(i, i - i // step % size * step + (i // step + by) % size * step) for i in range(32)]


def over_core(value):
    return lax.ppermute(value, "region", [(i, i ^ 1) for i in range(32)])


def over_z(value, mask):
    return lax.ppermute(value, "region", [(i, i ^ (8 * mask)) for i in range(32)])


def over_plane(value, by, second):
    along_x, route = ring(4, 2, by), []
    for y in range(4):
        for region, target in along_x:
            if region % 2 == second:
                route.append((32 * y + region, 32 * ((y + by) % 4) + region))
            else:
                route.append((32 * y + region, 32 * y + target))
    return lax.ppermute(value, ("dp", "region"), route)


def stage(kernel, coords, y, values, outs, after=(), scratch=()):
    ins = [SMEM] * 2 + [VMEM] * len(values) + [ANY] * len(after)
    return call(kernel, ins, outs, scratch)(coords, y, *values, *after)


def next_region(value):
    return lax.ppermute(value, "region", [(i, i + 1) for i in range(31)])


def previous_region(value):
    return lax.ppermute(value, "region", [(i + 1, i) for i in range(31)])


def local(features, conv_weight, down_weight, coarse_cotangent, brick_coords, neighbours, parents):
    coords, near, parent = brick_coords.reshape(3), neighbours.reshape(26), parents.reshape(1)
    y = lax.axis_index("dp").reshape(1).astype(jnp.int32)
    core = lax.axis_index("region") % 2
    cotangent = coarse_cotangent.reshape(16, 16, 16, 128)
    theirs = over_core(lax.dynamic_slice_in_dim(cotangent, 8 * (1 - core), 8))
    field = features.reshape(16, 8, 2, 16, 128)
    grads, spread, up, back = grad_call(coords, parent, cotangent, theirs, down_weight, field)
    low, high = next_region(up), previous_region(back)
    inner = inner_call(field, conv_weight)
    kept, sent, keep = main_call(
        coords, parent, near, field, low, high, inner, down_weight, grads, spread
    )
    run = functools.partial(stage, coords=coords, y=y)

    got = over_core(sent)
    own, *sends = run(
        spread_rows, values=(kept, got), outs=[sds((36, 16, 128), F32)] + [sds((36, 16, 128), BF)] * 3
    )
    gots = [over_plane(v, k + 1, 0) for k, v in enumerate(sends)]
    partial_grad, token = input_call(near, grads, low, conv_weight, own, 0)
    own, *sends = run(
        spread_taps, values=(own, *gots), outs=[sds((9, 16, 128), F32)] * 4, after=(token,)
    )
    gots = [over_plane(v, k + 1, 1) for k, v in enumerate(sends)]
    coarse, token = coarse_call(coords, keep, got, own)
    own = run(add_up, values=(own, *gots), outs=[sds((9, 16, 128), F32)], after=(token,))[0]
    own = run(add_pair, values=(own, over_z(own, 1)), outs=[sds((9, 16, 128), F32)])[0]
    own = run(add_pair, values=(own, over_z(own, 3)), outs=[sds((9, 16, 128), BF)])[0]

    gots = [over_plane(own, k, 1) for k in (1, 2, 3)]
    own = run(join_taps, values=(own, *gots), outs=[sds((36, 16, 128), BF)])[0]
    gots = [over_plane(own, k, 0) for k in (1, 2, 3)]
    input_grad, token = input_call(near, grads, high, conv_weight, own, 1, partial_grad)
    own = run(join_rows, values=(own, *gots), outs=[sds((36, 64, 128), BF)], after=(token,))[0]
    got = over_core(own)
    conv_grad, down_grad = run(
        finish, values=(own, got), outs=[sds((27, 128, 128), F32), sds((8, 128, 128), F32)]
    )
    whole = (1, 1, 16, 16, 16, 128)
    return (
        coarse.reshape(whole),
        input_grad.reshape(whole),
        conv_grad.reshape(3, 3, 3, 128, 128),
        down_grad.reshape(2, 2, 2, 128, 128),
    )


def solution(mesh):
    bricks = P("dp", "region", None, None, None, None)
    return jax.shard_map(
        local,
        mesh=mesh,
        in_specs=(bricks, P(), P(), bricks, P("dp", "region", None), P("dp", "region", None), P("dp", "region")),
        out_specs=(bricks, bricks, P(), P()),
        check_vma=False,
    )
```

time: 127 us -> 94.5 us (0.74); the launches traced: 125 us -> 94.1 us
  Pallas kernels: 47.5 us -> 33.1 us
  waiting for transfers between devices: 20.8 us -> 12.8 us
  starting transfers between devices: 43.6 us -> 38 us
  local copies, waits for them, and re-layouts: 11.6 us -> 8.55 us
    pallas_call x11 -> x14, Pallas kernels: 47.5 us -> 33.1 us  [the longest x1 9.15 us: main_call(): call(main_kernel, [SMEM] * 3 + [VMEM] * 9, [sds((36, 64, 128), F32), sds(...]
    ppermute x19 -> x16, waiting for transfers between devices: 18.6 us -> 7.71 us  [the longest x12 4.22 us: over_plane(): return lax.ppermute(value, ('dp', 'region'), route)]
    ppermute x19 -> x16, starting transfers between devices: 31.8 us -> 28.7 us  [the longest x12 17.8 us: over_plane(): return lax.ppermute(value, ('dp', 'region'), route)]
    ppermute x4 -> x3, waiting for transfers between devices: 2.21 us -> 5.13 us  [over_core(): return lax.ppermute(value, 'region', [(i, i ^ 1) for i in range(32)])]
    ppermute x4 -> x3, starting transfers between devices: 11.8 us -> 9.34 us  [over_core(): return lax.ppermute(value, 'region', [(i, i ^ 1) for i in range(32)])]
    unnamed x48 -> x28, local copies, waits for them, and re-layouts: 8.81 us -> 7.39 us
  transfers between devices with their start and end apart: 23 -> 19, of which waited for: 12 -> 8; matrix products, arithmetic and copies ran while one was open for 1% -> 0% of each run, Pallas kernels for 14% -> 17%
where the time goes in v1:
time: 94.5 us; the launch traced here: 94.1 us
  starting transfers between devices  38 us (40%)
  Pallas kernels  33.1 us (35%)
  waiting for transfers between devices  12.8 us (14%)
  local copies, waits for them, and re-layouts  8.55 us (9%)
  between operations  1.59 us (2%)
    ppermute x12, starting transfers between devices, over_plane(): return lax.ppermute(value, ('dp', 'region'), route)  17.8 us
    ppermute x3, starting transfers between devices, over_core(): return lax.ppermute(value, 'region', [(i, i ^ 1) for i in range(32)])  9.34 us
    pallas_call x1, Pallas kernels, main_call(): call(main_kernel, [SMEM] * 3 + [VMEM] * 9, [sds((36, 64, 128), F32), sds(...  9.15 us
    pallas_call x2, Pallas kernels, input_call(): call(functools.partial(input_kernel, half=half), ins, [sds((16, 8, 2, 16,...  9.06 us
    unnamed x28, local copies, waits for them, and re-layouts  7.39 us
    pallas_call x8, Pallas kernels, stage(): return call(kernel, ins, outs, scratch)(coords, y, *values, *after)  6.29 us
    ppermute x2, starting transfers between devices, over_z(): return lax.ppermute(value, 'region', [(i, i ^ 8 * mask) for i in range(32)])  5.37 us
    pallas_call x1, Pallas kernels, inner_call(): call(inner_kernel, [VMEM] * 2, [sds((3, 16, 9, 2, 16, 128), BF), sds((3,...  5.34 us
  transfers between devices with their start and end apart: 19, of which 8 were waited for; matrix products, arithmetic and copies ran while one was open for 0% of the time, Pallas kernels for 17%

profile of v1, /device:TPU:1, one launch (start us, length us, event | category | flops | bytes accessed | tf_op | source)
XLA Modules:
  0.0 94.1 jit_solution(878251046970860209)
XLA Ops:
  0.6 0.0 copy-start.2
  0.7 1.2 %dynamic-slice_bitcast_fusion = bf16[8,16,16,128]{3,2,1,0:T(8,128)(2,1)S(1)} fusion(bf16[1,1,16,16,16,128]{5,4,3,2,1,0:T(8,128)(2,1)} %param.10, s32[]{:T(128)S(6)} %select_n.11), kind=kLoop, calls=%fused_computation | loop fusion | bytes 1048580 | tf_op jit(solution)/shard_map/dynamic_slice | solution.py:469
  1.8 1.5 %collective-permute-start = (bf16[8,16,16,128]{3,2,1,0:T(8,128)(2,1)S(1)}, bf16[8,16,16,128]{3,2,1,0:T(8,128)(2,1)S(1)}, u32[]{:S(2)}, u32[]{:S(2)}) collective-permute-start(bf16[8,16,16,128]{3,2,1,0:T(8,128)(2,1)S(1)} %dynamic-slice_bitcast_fusion), channel_id=1, source_target_pairs={{0,1},{1,0},{2,3},{3,2},{4,5},{5,4},{6,7},{7,6},{8,9},{9,8},{10,11... | collective-permute-start | bytes 1572872 | tf_op jit(solution)/shard_map/ppermute | solution.py:433
  4.0 0.9 collective-permute-done.other_ref
  4.9 1.2 %copy-done = bf16[1,1,16,16,16,128]{5,4,3,2,1,0:T(8,128)(2,1)S(1)} copy-done((bf16[1,1,16,16,16,128]{5,4,3,2,1,0:T(8,128)(2,1)S(1)}, bf16[1,1,16,16,16,128]{5,4,3,2,1,0:T(8,128)(2,1)}, u32[]{:S(2)}) %copy-start) | copy-done | bytes 1048600
  6.1 1.2 %copy-done.1 = bf16[1,1,16,16,16,128]{5,4,3,2,1,0:T(8,128)(2,1)S(1)} copy-done((bf16[1,1,16,16,16,128]{5,4,3,2,1,0:T(8,128)(2,1)S(1)}, bf16[1,1,16,16,16,128]{5,4,3,2,1,0:T(8,128)(2,1)}, u32[]{:S(2)}) %copy-start.1) | copy-done | bytes 1048600
  7.3 0.9 %copy-done.3 = bf16[2,2,2,128,128]{4,3,2,1,0:T(8,128)(2,1)S(1)} copy-done((bf16[2,2,2,128,128]{4,3,2,1,0:T(8,128)(2,1)S(1)}, bf16[2,2,2,128,128]{4,3,2,1,0:T(8,128)(2,1)}, u32[]{:S(2)}) %copy-start.3) | copy-done | bytes 262168
  8.3 0.7 copy-done.5
  8.9 1.6 %shard_map.102 = (bf16[16,8,2,16,128]{4,3,2,1,0:T(8,128)(2,1)S(1)}, bf16[8,128,256]{2,1,0:T(8,128)(2,1)S(1)}, bf16[2,8,2,16,128]{4,3,2,1,0:T(8,128)(2,1)S(1)}, bf16[2,8,2,16,128]{4,3,2,1,0:T(8,128)(2,1)S(1)}) custom-call(s32[3]{0:T(128)S(1)} %bitcast.18, s32[1]{0:T(128)} %bitcast.12.parent_ref, bf16[16,16,16,128]{3,2,1,0:T(8,128)(2,1)S(1)} %bitcast.14, ...), custom_call_target="tpu_custom_call" | custom-call | flops 268435456 | bytes 4194304 | tf_op jit(solution)/shard_map/pallas_call | solution.py:324
  10.6 3.5 %collective-permute-start.1 = (bf16[2,8,2,16,128]{4,3,2,1,0:T(8,128)(2,1)S(1)}, bf16[2,8,2,16,128]{4,3,2,1,0:T(8,128)(2,1)S(1)}, u32[]{:S(2)}, u32[]{:S(2)}) collective-permute-start(bf16[2,8,2,16,128]{4,3,2,1,0:T(8,128)(2,1)S(1)} %get-tuple-element.30), channel_id=1, source_target_pairs={{0,1},{1,2},{2,3},{3,4},{4,5},{5,6},{6,7},{7,8},{8,9},{9,10},{10,1... | collective-permute-start | bytes 393224 | tf_op jit(solution)/shard_map/ppermute | solution.py:457
  14.1 2.1 %collective-permute-start.2 = (bf16[2,8,2,16,128]{4,3,2,1,0:T(8,128)(2,1)S(1)}, bf16[2,8,2,16,128]{4,3,2,1,0:T(8,128)(2,1)S(1)}, u32[]{:S(2)}, u32[]{:S(2)}) collective-permute-start(bf16[2,8,2,16,128]{4,3,2,1,0:T(8,128)(2,1)S(1)} %get-tuple-element.31), channel_id=1, source_target_pairs={{1,0},{2,1},{3,2},{4,3},{5,4},{6,5},{7,6},{8,7},{9,8},{10,9},{11,1... | collective-permute-start | bytes 393224 | tf_op jit(solution)/shard_map/ppermute | solution.py:461
  16.1 5.3 %shard_map.103 = (bf16[3,16,9,2,16,128]{5,4,3,2,1,0:T(8,128)(2,1)S(1)}, bf16[3,3,512,256]{3,2,1,0:T(8,128)(2,1)S(1)}, bf16[16,8,2,16,128]{4,3,2,1,0:T(8,128)(2,1)S(1)}) custom-call(bf16[16,8,2,16,128]{4,3,2,1,0:T(8,128)(2,1)S(1)} %bitcast.16, bf16[3,3,3,128,128]{4,3,2,1,0:T(8,128)(2,1)S(1)} %copy-done.9), custom_call_target="tpu_custom_call" | custom-call | flops 4831838208 | bytes 2097152 | tf_op jit(solution)/shard_map/pallas_call | solution.py:333
  21.6 9.1 %shard_map.104 = (f32[36,64,128]{2,1,0:T(8,128)S(1)}, bf16[53,64,128]{2,1,0:T(8,128)(2,1)}, bf16[8,8,16,128]{3,2,1,0:T(8,128)(2,1)S(1)}) custom-call(s32[3]{0:T(128)S(1)} %bitcast.19, s32[1]{0:T(128)} %bitcast.13.parent_ref, s32[26]{0:T(128)S(1)} %bitcast.29, bf16[16,8,2,16,128]{4,3,2,1,0:T(8,128)(2,1)S(1)} %bitcast.17, ...), custom_call_target="tpu_custom_call" | custom-call | flops 4831838208 | bytes 1048576 | tf_op jit(solution)/shard_map/pallas_call | solution.py:342
  30.7 2.6 %collective-permute-done.3.got_ref = bf16[53,64,128]{2,1,0:T(8,128)(2,1)S(1)} collective-permute-done((bf16[53,64,128]{2,1,0:T(8,128)(2,1)}, bf16[53,64,128]{2,1,0:T(8,128)(2,1)S(1)}, u32[]{:S(2)}, u32[]{:S(2)}) %collective-permute-start.3) | collective-permute-done | bytes 868384 | tf_op jit(solution)/shard_map/ppermute | solution.py:433
  33.3 0.7 shard_map.105
  34.0 1.5 %collective-permute-start.4 = (bf16[36,16,128]{2,1,0:T(8,128)(2,1)S(1)}, bf16[36,16,128]{2,1,0:T(8,128)(2,1)S(1)}, u32[]{:S(2)}, u32[]{:S(2)}) collective-permute-start(bf16[36,16,128]{2,1,0:T(8,128)(2,1)S(1)} %get-tuple-element.41), channel_id=1, source_target_pairs={{0,32},{1,3},{2,34},{3,5},{4,36},{5,7},{6,38},{7,1},{8,40},{9,11},... | collective-permute-start | bytes 442376 | tf_op jit(solution)/shard_map/ppermute | solution.py:448
  35.6 3.6 %collective-permute-start.5 = (bf16[36,16,128]{2,1,0:T(8,128)(2,1)S(1)}, bf16[36,16,128]{2,1,0:T(8,128)(2,1)S(1)}, u32[]{:S(2)}, u32[]{:S(2)}) collective-permute-start(bf16[36,16,128]{2,1,0:T(8,128)(2,1)S(1)} %get-tuple-element.42), channel_id=1, source_target_pairs={{0,64},{1,5},{2,66},{3,7},{4,68},{5,1},{6,70},{7,3},{8,72},{9,13},... | collective-permute-start | bytes 442376 | tf_op jit(solution)/shard_map/ppermute | solution.py:448
  39.2 0.0 collective-permute-start.6
  39.2 1.2 %copy-done.8 = bf16[16,8,2,16,128]{4,3,2,1,0:T(8,128)(2,1)S(1)} copy-done((bf16[16,8,2,16,128]{4,3,2,1,0:T(8,128)(2,1)S(1)}, bf16[16,8,2,16,128]{4,3,2,1,0:T(8,128)(2,1)}, u32[]{:S(2)}) %copy-start.8) | copy-done | bytes 1048600
  40.4 1.2 %copy-done.10 = bf16[3,3,3,128,128]{4,3,2,1,0:T(8,128)(2,1)S(1)} copy-done((bf16[3,3,3,128,128]{4,3,2,1,0:T(8,128)(2,1)S(1)}, bf16[3,3,3,128,128]{4,3,2,1,0:T(8,128)(2,1)}, u32[]{:S(2)}) %copy-start.10) | copy-done | bytes 884760
  41.6 0.9 copy-done.12
  42.5 4.6 %shard_map.106 = (bf16[16,8,2,16,128]{4,3,2,1,0:T(8,128)(2,1)}, f32[8,128]{1,0:T(8,128)S(1)}) custom-call(s32[26]{0:T(128)S(1)} %bitcast.30, bf16[16,8,2,16,128]{4,3,2,1,0:T(8,128)(2,1)S(1)} %copy-done.8, bf16[2,8,2,16,128]{4,3,2,1,0:T(8,128)(2,1)S(1)} %copy-done.12, bf16[3,3,3,128,128]{4,3,2,1,0:T(8,128)(2,1)S(1)} %copy-done.10, ...), custom_call_target="tpu_custom_call" | custom-call | flops 2415919104 | bytes 1048576 | tf_op jit(solution)/shard_map/pallas_call | solution.py:355
  47.1 0.6 shard_map.107
  47.7 1.4 %collective-permute-start.7 = (f32[9,16,128]{2,1,0:T(8,128)S(1)}, f32[9,16,128]{2,1,0:T(8,128)S(1)}, u32[]{:S(2)}, u32[]{:S(2)}) collective-permute-start(f32[9,16,128]{2,1,0:T(8,128)S(1)} %get-tuple-element.47), channel_id=1, source_target_pairs={{0,2},{1,33},{2,4},{3,35},{4,6},{5,37},{6,0},{7,39},{8,10},{9,41},... | collective-permute-start | bytes 221192 | tf_op jit(solution)/shard_map/ppermute | solution.py:448
  49.1 2.6 %collective-permute-start.8 = (f32[9,16,128]{2,1,0:T(8,128)S(1)}, f32[9,16,128]{2,1,0:T(8,128)S(1)}, u32[]{:S(2)}, u32[]{:S(2)}) collective-permute-start(f32[9,16,128]{2,1,0:T(8,128)S(1)} %get-tuple-element.48), channel_id=1, source_target_pairs={{0,4},{1,65},{2,6},{3,67},{4,0},{5,69},{6,2},{7,71},{8,12},{9,73},... | collective-permute-start | bytes 221192 | tf_op jit(solution)/shard_map/ppermute | solution.py:448
  51.7 1.1 %collective-permute-start.9 = (f32[9,16,128]{2,1,0:T(8,128)S(1)}, f32[9,16,128]{2,1,0:T(8,128)S(1)}, u32[]{:S(2)}, u32[]{:S(2)}) collective-permute-start(f32[9,16,128]{2,1,0:T(8,128)S(1)} %get-tuple-element.49), channel_id=1, source_target_pairs={{0,6},{1,97},{2,0},{3,99},{4,2},{5,101},{6,4},{7,103},{8,14},{9,10... | collective-permute-start | bytes 221192 | tf_op jit(solution)/shard_map/ppermute | solution.py:448
  52.8 1.7 %shard_map.108 = (bf16[16,16,16,128]{3,2,1,0:T(8,128)(2,1)}, f32[8,128]{1,0:T(8,128)S(1)}) custom-call(s32[3]{0:T(128)S(1)} %bitcast.22, bf16[8,8,16,128]{3,2,1,0:T(8,128)(2,1)S(1)} %get-tuple-element.37.keep_ref, bf16[53,64,128]{2,1,0:T(8,128)(2,1)S(1)} %collective-permute-done.3.got_ref, f32[9,16,128]{2,1,0:T(8,128)S(1)} %get-tuple-element.45.after_ref.kept_ref), custom_call_target="tpu_custom_call" | custom-call | bytes 1048576 | tf_op jit(solution)/shard_map/pallas_call | solution.py:367
  54.5 0.5 collective-permute-done.9.third_ref
  54.9 0.6 shard_map.109.own_ref
  55.5 1.7 %collective-permute-start.10 = (f32[9,16,128]{2,1,0:T(8,128)S(1)}, f32[9,16,128]{2,1,0:T(8,128)S(1)}, u32[]{:S(2)}, u32[]{:S(2)}) collective-permute-start(f32[9,16,128]{2,1,0:T(8,128)S(1)} %shard_map.109.own_ref), channel_id=1, source_target_pairs={{0,8},{1,9},{2,10},{3,11},{4,12},{5,13},{6,14},{7,15},{8,0},{9,1},... | collective-permute-start | bytes 221192 | tf_op jit(solution)/shard_map/ppermute | solution.py:437
  57.2 1.7 %collective-permute-done.10.got_ref = f32[9,16,128]{2,1,0:T(8,128)S(1)} collective-permute-done((f32[9,16,128]{2,1,0:T(8,128)S(1)}, f32[9,16,128]{2,1,0:T(8,128)S(1)}, u32[]{:S(2)}, u32[]{:S(2)}) %collective-permute-start.10) | collective-permute-done | bytes 73760 | tf_op jit(solution)/shard_map/ppermute | solution.py:437
  58.9 0.5 shard_map.110.own_ref
  59.5 3.7 %collective-permute-start.11 = (f32[9,16,128]{2,1,0:T(8,128)S(1)}, f32[9,16,128]{2,1,0:T(8,128)S(1)}, u32[]{:S(2)}, u32[]{:S(2)}) collective-permute-start(f32[9,16,128]{2,1,0:T(8,128)S(1)} %shard_map.110.own_ref), channel_id=1, source_target_pairs={{0,24},{1,25},{2,26},{3,27},{4,28},{5,29},{6,30},{7,31},{8,16},{9,... | collective-permute-start | bytes 221192 | tf_op jit(solution)/shard_map/ppermute | solution.py:437
  63.1 1.7 %collective-permute-done.11.got_ref = f32[9,16,128]{2,1,0:T(8,128)S(1)} collective-permute-done((f32[9,16,128]{2,1,0:T(8,128)S(1)}, f32[9,16,128]{2,1,0:T(8,128)S(1)}, u32[]{:S(2)}, u32[]{:S(2)}) %collective-permute-start.11) | collective-permute-done | bytes 73760 | tf_op jit(solution)/shard_map/ppermute | solution.py:437
  64.9 0.6 shard_map.111.own_ref
  65.4 2.3 %collective-permute-start.14 = (bf16[9,16,128]{2,1,0:T(8,128)(2,1)S(1)}, bf16[9,16,128]{2,1,0:T(8,128)(2,1)S(1)}, u32[]{:S(2)}, u32[]{:S(2)}) collective-permute-start(bf16[9,16,128]{2,1,0:T(8,128)(2,1)S(1)} %shard_map.111.own_ref), channel_id=1, source_target_pairs={{0,6},{1,97},{2,0},{3,99},{4,2},{5,101},{6,4},{7,103},{8,14},{9,10... | collective-permute-start | bytes 110600 | tf_op jit(solution)/shard_map/ppermute | solution.py:448
  67.8 0.7 collective-permute-start.12
  68.5 0.4 collective-permute-done.14.refs_2_
  68.9 3.4 %collective-permute-done.13.refs_1_ = bf16[9,16,128]{2,1,0:T(8,128)(2,1)S(1)} collective-permute-done((bf16[9,16,128]{2,1,0:T(8,128)(2,1)S(1)}, bf16[9,16,128]{2,1,0:T(8,128)(2,1)S(1)}, u32[]{:S(2)}, u32[]{:S(2)}) %collective-permute-start.13) | collective-permute-done | bytes 36896 | tf_op jit(solution)/shard_map/ppermute | solution.py:448
  72.2 0.6 shard_map.112.refs_0_.own_ref
  72.8 0.8 collective-permute-start.17
  73.6 3.0 %collective-permute-start.16 = (bf16[36,16,128]{2,1,0:T(8,128)(2,1)S(1)}, bf16[36,16,128]{2,1,0:T(8,128)(2,1)S(1)}, u32[]{:S(2)}, u32[]{:S(2)}) collective-permute-start(bf16[36,16,128]{2,1,0:T(8,128)(2,1)S(1)} %shard_map.112.refs_0_.own_ref), channel_id=1, source_target_pairs={{0,64},{1,5},{2,66},{3,7},{4,68},{5,1},{6,70},{7,3},{8,72},{9,13},... | collective-permute-start | bytes 442376 | tf_op jit(solution)/shard_map/ppermute | solution.py:448
  76.6 0.8 collective-permute-start.15
  77.4 4.5 %shard_map.113 = (bf16[16,8,2,16,128]{4,3,2,1,0:T(8,128)(2,1)}, f32[8,128]{1,0:T(8,128)S(1)}) custom-call(s32[26]{0:T(128)S(1)} %bitcast.31, bf16[16,8,2,16,128]{4,3,2,1,0:T(8,128)(2,1)S(1)} %copy-done.8, bf16[2,8,2,16,128]{4,3,2,1,0:T(8,128)(2,1)S(1)} %collective-permute-done.2.high_ref.layer_ref, ...), custom_call_target="tpu_custom_call", output_to_operand_aliasing={{0}: (5, {})} | custom-call | flops 2415919104 | bytes 1048576 | tf_op jit(solution)/shard_map/pallas_call | solution.py:355
  81.9 0.6 shard_map.114.own_ref
  82.5 7.8 %collective-permute-start.18 = (bf16[36,64,128]{2,1,0:T(8,128)(2,1)S(1)}, bf16[36,64,128]{2,1,0:T(8,128)(2,1)S(1)}, u32[]{:S(2)}, u32[]{:S(2)}) collective-permute-start(bf16[36,64,128]{2,1,0:T(8,128)(2,1)S(1)} %shard_map.114.own_ref), channel_id=1, source_target_pairs={{0,1},{1,0},{2,3},{3,2},{4,5},{5,4},{6,7},{7,6},{8,9},{9,8},{10,11... | collective-permute-start | bytes 1769480 | tf_op jit(solution)/shard_map/ppermute | solution.py:433
  90.4 1.6 %collective-permute-done.18.got_ref = bf16[36,64,128]{2,1,0:T(8,128)(2,1)S(1)} collective-permute-done((bf16[36,64,128]{2,1,0:T(8,128)(2,1)S(1)}, bf16[36,64,128]{2,1,0:T(8,128)(2,1)S(1)}, u32[]{:S(2)}, u32[]{:S(2)}) %collective-permute-start.18) | collective-permute-done | bytes 589856 | tf_op jit(solution)/shard_map/ppermute | solution.py:433
  92.0 2.1 %shard_map.115 = (f32[27,128,128]{2,1,0:T(8,128)}, f32[8,128,128]{2,1,0:T(8,128)}) custom-call(s32[3]{0:T(128)S(1)} %bitcast.28, s32[1]{0:T(128)} %bitcast.6.y_ref, bf16[36,64,128]{2,1,0:T(8,128)(2,1)S(1)} %shard_map.114.own_ref, bf16[36,64,128]{2,1,0:T(8,128)(2,1)S(1)} %collective-permute-done.18.got_ref), custom_call_target="tpu_custom_call" | custom-call | bytes 1048576 | tf_op jit(solution)/shard_map/pallas_call | solution.py:453
  (33 shorter events, 0.1 us)
Async XLA Ops:
  0.6 15.5 %copy-start.2 = (bf16[1,1,16,16,16,128]{5,4,3,2,1,0:T(8,128)(2,1)S(1)}, bf16[1,1,16,16,16,128]{5,4,3,2,1,0:T(8,128)(2,1)}, u32[]{:S(2)}) copy-start(bf16[1,1,16,16,16,128]{5,4,3,2,1,0:T(8,128)(2,1)} %param.7) | copy-start | bytes 3145732
  1.8 3.0 %collective-permute-start = (bf16[8,16,16,128]{3,2,1,0:T(8,128)(2,1)S(1)}, bf16[8,16,16,128]{3,2,1,0:T(8,128)(2,1)S(1)}, u32[]{:S(2)}, u32[]{:S(2)}) collective-permute-start(bf16[8,16,16,128]{3,2,1,0:T(8,128)(2,1)S(1)} %dynamic-slice_bitcast_fusion), channel_id=1, source_target_pairs={{0,1},{1,0},{2,3},{3,2},{4,5},{5,4},{6,7},{7,6},{8,9},{9,8},{10,11... | collective-permute-start | bytes 1572872 | tf_op jit(solution)/shard_map/ppermute | solution.py:433
  4.9 1.2 %copy-start = (bf16[1,1,16,16,16,128]{5,4,3,2,1,0:T(8,128)(2,1)S(1)}, bf16[1,1,16,16,16,128]{5,4,3,2,1,0:T(8,128)(2,1)}, u32[]{:S(2)}) copy-start(bf16[1,1,16,16,16,128]{5,4,3,2,1,0:T(8,128)(2,1)} %param.10) | copy-start | bytes 3145732
  6.1 1.2 %copy-start.1 = (bf16[1,1,16,16,16,128]{5,4,3,2,1,0:T(8,128)(2,1)S(1)}, bf16[1,1,16,16,16,128]{5,4,3,2,1,0:T(8,128)(2,1)}, u32[]{:S(2)}) copy-start(bf16[1,1,16,16,16,128]{5,4,3,2,1,0:T(8,128)(2,1)} %param.7) | copy-start | bytes 3145732
  7.3 0.9 %copy-start.3 = (bf16[2,2,2,128,128]{4,3,2,1,0:T(8,128)(2,1)S(1)}, bf16[2,2,2,128,128]{4,3,2,1,0:T(8,128)(2,1)}, u32[]{:S(2)}) copy-start(bf16[2,2,2,128,128]{4,3,2,1,0:T(8,128)(2,1)} %down_ref.3) | copy-start | bytes 786436
  8.3 0.7 copy-start.5
  8.9 7.2 %copy-start.9 = (bf16[3,3,3,128,128]{4,3,2,1,0:T(8,128)(2,1)S(1)}, bf16[3,3,3,128,128]{4,3,2,1,0:T(8,128)(2,1)}, u32[]{:S(2)}) copy-start(bf16[3,3,3,128,128]{4,3,2,1,0:T(8,128)(2,1)} %conv_ref.5) | copy-start | bytes 2654212
  10.5 11.0 %copy-start.7 = (bf16[16,8,2,16,128]{4,3,2,1,0:T(8,128)(2,1)}, bf16[16,8,2,16,128]{4,3,2,1,0:T(8,128)(2,1)S(1)}, u32[]{:S(2)}) copy-start(bf16[16,8,2,16,128]{4,3,2,1,0:T(8,128)(2,1)S(1)} %get-tuple-element.35.grads_ref.field_ref) | copy-start | bytes 3145732
  10.6 10.9 %collective-permute-start.1 = (bf16[2,8,2,16,128]{4,3,2,1,0:T(8,128)(2,1)S(1)}, bf16[2,8,2,16,128]{4,3,2,1,0:T(8,128)(2,1)S(1)}, u32[]{:S(2)}, u32[]{:S(2)}) collective-permute-start(bf16[2,8,2,16,128]{4,3,2,1,0:T(8,128)(2,1)S(1)} %get-tuple-element.30), channel_id=1, source_target_pairs={{0,1},{1,2},{2,3},{3,4},{4,5},{5,6},{6,7},{7,8},{8,9},{9,10},{10,1... | collective-permute-start | bytes 393224 | tf_op jit(solution)/shard_map/ppermute | solution.py:457
  14.0 7.5 %copy-start.4 = (bf16[2,2,2,128,128]{4,3,2,1,0:T(8,128)(2,1)S(1)}, bf16[2,2,2,128,128]{4,3,2,1,0:T(8,128)(2,1)}, u32[]{:S(2)}) copy-start(bf16[2,2,2,128,128]{4,3,2,1,0:T(8,128)(2,1)} %down_ref.3) | copy-start | bytes 786436
  14.0 7.5 %copy-start.6 = (s32[1,1,3]{2,1,0:T(1,128)S(1)}, s32[1,1,3]{2,1,0:T(1,128)}, u32[]{:S(2)}) copy-start(s32[1,1,3]{2,1,0:T(1,128)} %param.11) | copy-start | bytes 40
  14.0 7.5 %copy-start.13 = (s32[1,1,26]{2,1,0:T(1,128)S(1)}, s32[1,1,26]{2,1,0:T(1,128)}, u32[]{:S(2)}) copy-start(s32[1,1,26]{2,1,0:T(1,128)} %param.12) | copy-start | bytes 316
  14.1 7.4 %collective-permute-start.2 = (bf16[2,8,2,16,128]{4,3,2,1,0:T(8,128)(2,1)S(1)}, bf16[2,8,2,16,128]{4,3,2,1,0:T(8,128)(2,1)S(1)}, u32[]{:S(2)}, u32[]{:S(2)}) collective-permute-start(bf16[2,8,2,16,128]{4,3,2,1,0:T(8,128)(2,1)S(1)} %get-tuple-element.31), channel_id=1, source_target_pairs={{1,0},{2,1},{3,2},{4,3},{5,4},{6,5},{7,6},{8,7},{9,8},{10,9},{11,1... | collective-permute-start | bytes 393224 | tf_op jit(solution)/shard_map/ppermute | solution.py:461
  21.5 9.2 %copy-start.11 = (bf16[2,8,2,16,128]{4,3,2,1,0:T(8,128)(2,1)}, bf16[2,8,2,16,128]{4,3,2,1,0:T(8,128)(2,1)S(1)}, u32[]{:S(2)}) copy-start(bf16[2,8,2,16,128]{4,3,2,1,0:T(8,128)(2,1)S(1)} %collective-permute-done.1.low_ref.layer_ref) | copy-start | bytes 393220
  30.7 2.6 %collective-permute-start.3 = (bf16[53,64,128]{2,1,0:T(8,128)(2,1)}, bf16[53,64,128]{2,1,0:T(8,128)(2,1)S(1)}, u32[]{:S(2)}, u32[]{:S(2)}) collective-permute-start(bf16[53,64,128]{2,1,0:T(8,128)(2,1)} %get-tuple-element.38), channel_id=1, source_target_pairs={{0,1},{1,0},{2,3},{3,2},{4,5},{5,4},{6,7},{7,6},{8,9},{9,8},{10,11... | collective-permute-start | bytes 2605064 | tf_op jit(solution)/shard_map/ppermute | solution.py:433
  34.0 13.0 %collective-permute-start.4 = (bf16[36,16,128]{2,1,0:T(8,128)(2,1)S(1)}, bf16[36,16,128]{2,1,0:T(8,128)(2,1)S(1)}, u32[]{:S(2)}, u32[]{:S(2)}) collective-permute-start(bf16[36,16,128]{2,1,0:T(8,128)(2,1)S(1)} %get-tuple-element.41), channel_id=1, source_target_pairs={{0,32},{1,3},{2,34},{3,5},{4,36},{5,7},{6,38},{7,1},{8,40},{9,11},... | collective-permute-start | bytes 442376 | tf_op jit(solution)/shard_map/ppermute | solution.py:448
  35.6 11.5 %collective-permute-start.5 = (bf16[36,16,128]{2,1,0:T(8,128)(2,1)S(1)}, bf16[36,16,128]{2,1,0:T(8,128)(2,1)S(1)}, u32[]{:S(2)}, u32[]{:S(2)}) collective-permute-start(bf16[36,16,128]{2,1,0:T(8,128)(2,1)S(1)} %get-tuple-element.42), channel_id=1, source_target_pairs={{0,64},{1,5},{2,66},{3,7},{4,68},{5,1},{6,70},{7,3},{8,72},{9,13},... | collective-permute-start | bytes 442376 | tf_op jit(solution)/shard_map/ppermute | solution.py:448
  39.2 7.9 %collective-permute-start.6 = (bf16[36,16,128]{2,1,0:T(8,128)(2,1)S(1)}, bf16[36,16,128]{2,1,0:T(8,128)(2,1)S(1)}, u32[]{:S(2)}, u32[]{:S(2)}) collective-permute-start(bf16[36,16,128]{2,1,0:T(8,128)(2,1)S(1)} %get-tuple-element.43), channel_id=1, source_target_pairs={{0,96},{1,7},{2,98},{3,1},{4,100},{5,3},{6,102},{7,5},{8,104},{9,1... | collective-permute-start | bytes 442376 | tf_op jit(solution)/shard_map/ppermute | solution.py:448
  39.2 1.2 %copy-start.8 = (bf16[16,8,2,16,128]{4,3,2,1,0:T(8,128)(2,1)S(1)}, bf16[16,8,2,16,128]{4,3,2,1,0:T(8,128)(2,1)}, u32[]{:S(2)}) copy-start(bf16[16,8,2,16,128]{4,3,2,1,0:T(8,128)(2,1)} %copy-done.7) | copy-start | bytes 3145732
  40.4 1.2 %copy-start.10 = (bf16[3,3,3,128,128]{4,3,2,1,0:T(8,128)(2,1)S(1)}, bf16[3,3,3,128,128]{4,3,2,1,0:T(8,128)(2,1)}, u32[]{:S(2)}) copy-start(bf16[3,3,3,128,128]{4,3,2,1,0:T(8,128)(2,1)} %conv_ref.5) | copy-start | bytes 2654212
  41.6 0.9 copy-start.12
  47.7 6.7 %collective-permute-start.7 = (f32[9,16,128]{2,1,0:T(8,128)S(1)}, f32[9,16,128]{2,1,0:T(8,128)S(1)}, u32[]{:S(2)}, u32[]{:S(2)}) collective-permute-start(f32[9,16,128]{2,1,0:T(8,128)S(1)} %get-tuple-element.47), channel_id=1, source_target_pairs={{0,2},{1,33},{2,4},{3,35},{4,6},{5,37},{6,0},{7,39},{8,10},{9,41},... | collective-permute-start | bytes 221192 | tf_op jit(solution)/shard_map/ppermute | solution.py:448
  49.1 5.4 %collective-permute-start.8 = (f32[9,16,128]{2,1,0:T(8,128)S(1)}, f32[9,16,128]{2,1,0:T(8,128)S(1)}, u32[]{:S(2)}, u32[]{:S(2)}) collective-permute-start(f32[9,16,128]{2,1,0:T(8,128)S(1)} %get-tuple-element.48), channel_id=1, source_target_pairs={{0,4},{1,65},{2,6},{3,67},{4,0},{5,69},{6,2},{7,71},{8,12},{9,73},... | collective-permute-start | bytes 221192 | tf_op jit(solution)/shard_map/ppermute | solution.py:448
  51.7 3.2 %collective-permute-start.9 = (f32[9,16,128]{2,1,0:T(8,128)S(1)}, f32[9,16,128]{2,1,0:T(8,128)S(1)}, u32[]{:S(2)}, u32[]{:S(2)}) collective-permute-start(f32[9,16,128]{2,1,0:T(8,128)S(1)} %get-tuple-element.49), channel_id=1, source_target_pairs={{0,6},{1,97},{2,0},{3,99},{4,2},{5,101},{6,4},{7,103},{8,14},{9,10... | collective-permute-start | bytes 221192 | tf_op jit(solution)/shard_map/ppermute | solution.py:448
  55.5 3.5 %collective-permute-start.10 = (f32[9,16,128]{2,1,0:T(8,128)S(1)}, f32[9,16,128]{2,1,0:T(8,128)S(1)}, u32[]{:S(2)}, u32[]{:S(2)}) collective-permute-start(f32[9,16,128]{2,1,0:T(8,128)S(1)} %shard_map.109.own_ref), channel_id=1, source_target_pairs={{0,8},{1,9},{2,10},{3,11},{4,12},{5,13},{6,14},{7,15},{8,0},{9,1},... | collective-permute-start | bytes 221192 | tf_op jit(solution)/shard_map/ppermute | solution.py:437
  59.5 5.4 %collective-permute-start.11 = (f32[9,16,128]{2,1,0:T(8,128)S(1)}, f32[9,16,128]{2,1,0:T(8,128)S(1)}, u32[]{:S(2)}, u32[]{:S(2)}) collective-permute-start(f32[9,16,128]{2,1,0:T(8,128)S(1)} %shard_map.110.own_ref), channel_id=1, source_target_pairs={{0,24},{1,25},{2,26},{3,27},{4,28},{5,29},{6,30},{7,31},{8,16},{9,... | collective-permute-start | bytes 221192 | tf_op jit(solution)/shard_map/ppermute | solution.py:437
  65.4 3.4 %collective-permute-start.14 = (bf16[9,16,128]{2,1,0:T(8,128)(2,1)S(1)}, bf16[9,16,128]{2,1,0:T(8,128)(2,1)S(1)}, u32[]{:S(2)}, u32[]{:S(2)}) collective-permute-start(bf16[9,16,128]{2,1,0:T(8,128)(2,1)S(1)} %shard_map.111.own_ref), channel_id=1, source_target_pairs={{0,6},{1,97},{2,0},{3,99},{4,2},{5,101},{6,4},{7,103},{8,14},{9,10... | collective-permute-start | bytes 110600 | tf_op jit(solution)/shard_map/ppermute | solution.py:448
  67.8 4.4 %collective-permute-start.13 = (bf16[9,16,128]{2,1,0:T(8,128)(2,1)S(1)}, bf16[9,16,128]{2,1,0:T(8,128)(2,1)S(1)}, u32[]{:S(2)}, u32[]{:S(2)}) collective-permute-start(bf16[9,16,128]{2,1,0:T(8,128)(2,1)S(1)} %shard_map.111.own_ref), channel_id=1, source_target_pairs={{0,4},{1,65},{2,6},{3,67},{4,0},{5,69},{6,2},{7,71},{8,12},{9,73},... | collective-permute-start | bytes 110600 | tf_op jit(solution)/shard_map/ppermute | solution.py:448
  67.8 4.4 %collective-permute-start.12 = (bf16[9,16,128]{2,1,0:T(8,128)(2,1)S(1)}, bf16[9,16,128]{2,1,0:T(8,128)(2,1)S(1)}, u32[]{:S(2)}, u32[]{:S(2)}) collective-permute-start(bf16[9,16,128]{2,1,0:T(8,128)(2,1)S(1)} %shard_map.111.own_ref), channel_id=1, source_target_pairs={{0,2},{1,33},{2,4},{3,35},{4,6},{5,37},{6,0},{7,39},{8,10},{9,41},... | collective-permute-start | bytes 110600 | tf_op jit(solution)/shard_map/ppermute | solution.py:448
  72.8 9.1 %collective-permute-start.17 = (bf16[36,16,128]{2,1,0:T(8,128)(2,1)S(1)}, bf16[36,16,128]{2,1,0:T(8,128)(2,1)S(1)}, u32[]{:S(2)}, u32[]{:S(2)}) collective-permute-start(bf16[36,16,128]{2,1,0:T(8,128)(2,1)S(1)} %shard_map.112.refs_0_.own_ref), channel_id=1, source_target_pairs={{0,96},{1,7},{2,98},{3,1},{4,100},{5,3},{6,102},{7,5},{8,104},{9,1... | collective-permute-start | bytes 442376 | tf_op jit(solution)/shard_map/ppermute | solution.py:448
  73.6 8.3 %collective-permute-start.16 = (bf16[36,16,128]{2,1,0:T(8,128)(2,1)S(1)}, bf16[36,16,128]{2,1,0:T(8,128)(2,1)S(1)}, u32[]{:S(2)}, u32[]{:S(2)}) collective-permute-start(bf16[36,16,128]{2,1,0:T(8,128)(2,1)S(1)} %shard_map.112.refs_0_.own_ref), channel_id=1, source_target_pairs={{0,64},{1,5},{2,66},{3,7},{4,68},{5,1},{6,70},{7,3},{8,72},{9,13},... | collective-permute-start | bytes 442376 | tf_op jit(solution)/shard_map/ppermute | solution.py:448
  76.6 5.3 %collective-permute-start.15 = (bf16[36,16,128]{2,1,0:T(8,128)(2,1)S(1)}, bf16[36,16,128]{2,1,0:T(8,128)(2,1)S(1)}, u32[]{:S(2)}, u32[]{:S(2)}) collective-permute-start(bf16[36,16,128]{2,1,0:T(8,128)(2,1)S(1)} %shard_map.112.refs_0_.own_ref), channel_id=1, source_target_pairs={{0,32},{1,3},{2,34},{3,5},{4,36},{5,7},{6,38},{7,1},{8,40},{9,11},... | collective-permute-start | bytes 442376 | tf_op jit(solution)/shard_map/ppermute | solution.py:448
  82.5 9.5 %collective-permute-start.18 = (bf16[36,64,128]{2,1,0:T(8,128)(2,1)S(1)}, bf16[36,64,128]{2,1,0:T(8,128)(2,1)S(1)}, u32[]{:S(2)}, u32[]{:S(2)}) collective-permute-start(bf16[36,64,128]{2,1,0:T(8,128)(2,1)S(1)} %shard_map.114.own_ref), channel_id=1, source_target_pairs={{0,1},{1,0},{2,3},{3,2},{4,5},{5,4},{6,7},{7,6},{8,9},{9,8},{10,11... | collective-permute-start | bytes 1769480 | tf_op jit(solution)/shard_map/ppermute | solution.py:433

commit v2 on v1

--- a/solution.py
+++ b/solution.py
@@ -89,19 +89,27 @@
 
 
 def grad_kernel(
-    coords_ref, parent_ref, own_ref, other_ref, down_ref, field_ref,
-    grads_ref, spread_ref, up_ref, back_ref, wide_ref, sems,
+    coords_ref, parent_ref, own_hbm, other_ref, down_hbm, field_hbm,
+    grads_ref, spread_ref, up_ref, back_ref, wide_ref, own_ref, down_ref, sems,
 ):
-    last = pltpu.make_async_copy(field_ref.at[15], up_ref.at[0], sems.at[0])
-    first = pltpu.make_async_copy(field_ref.at[0], back_ref.at[0], sems.at[1])
-    last.start()
-    first.start()
     x, oy, oz = coords_ref[0], coords_ref[1] % 2, coords_ref[2] % 2
+    copies = [
+        pltpu.make_async_copy(
+            own_hbm.at[pl.ds(8 * (x % 2), 8), pl.ds(8 * oy, 8)], own_ref, sems.at[0]
+        ),
+        pltpu.make_async_copy(down_hbm, down_ref, sems.at[1]),
+        pltpu.make_async_copy(field_hbm.at[15], up_ref.at[0], sems.at[2]),
+        pltpu.make_async_copy(field_hbm.at[0], back_ref.at[0], sems.at[3]),
+    ]
+    for copy in copies:
+        copy.start()
     is_own = parent_ref[0] == x
+    copies[0].wait()
+    copies[1].wait()
     down = joined_down(down_ref)
     wide_ref[...] = jnp.zeros_like(wide_ref)
     for i in range(8):
-        mine = own_ref[8 * (x % 2) + i, pl.ds(8 * oy, 8)].astype(F32)
+        mine = own_ref[i].astype(F32)
         theirs = other_ref[i, pl.ds(8 * oy, 8)].astype(F32)
         both = jnp.where(is_own, mine, theirs)
         part = jnp.where(oz == 0, both[:, 0:8], both[:, 8:16]).reshape(64, 128)
@@ -120,8 +128,8 @@
                     up_ref[1, :, q] = part
                 if 2 * i + p == 0:
                     back_ref[1, :, q] = part
-    last.wait()
-    first.wait()
+    copies[2].wait()
+    copies[3].wait()
 
 
 def lay_weights(conv_ref, weights_ref):
@@ -241,17 +249,33 @@
                 )
 
 
-def input_kernel(near_ref, field_ref, layer_ref, conv_ref, *refs, half, tile=4):
-    result_ref, token_ref, shifts_ref, weights_ref, held_ref, sems = refs[-6:]
+def input_kernel(near_ref, field_hbm, layer_hbm, conv_hbm, *refs, half, tile=4):
+    (result_ref, token_ref, shifts_ref, weights_ref, held_ref, field_ref, layer_ref, conv_ref,
+     sems) = refs[-9:]
     token_ref[...] = jnp.zeros_like(token_ref)
-    if half == 0:
-        lay_slab(layer_ref[1].reshape(16, 16, 128), near_flag(near_ref, 0), shifts_ref.at[:, 0])
-        lay_interior(field_ref, shifts_ref, 0, 9, 1)
-    else:
-        lay_interior(field_ref, shifts_ref, 7, 16, -7)
-        lay_slab(layer_ref[1].reshape(16, 16, 128), near_flag(near_ref, 17), shifts_ref.at[:, 9])
+    first_layer = 7 * half
+    fetches = [
+        pltpu.make_async_copy(
+            field_hbm.at[pl.ds(first_layer + 3 * k, 3)], field_ref.at[pl.ds(3 * k, 3)], sems.at[2 + k]
+        )
+        for k in range(3)
+    ]
+    layer_copy = pltpu.make_async_copy(layer_hbm.at[1], layer_ref, sems.at[5])
+    conv_copies = [
+        pltpu.make_async_copy(conv_hbm.at[a], conv_ref.at[a], sems.at[6 + a]) for a in range(3)
+    ]
+    for copy in (*fetches, layer_copy, *conv_copies):
+        copy.start()
+    for k in range(3):
+        fetches[k].wait()
+        lay_interior(field_ref, shifts_ref, 3 * k, 3 * k + 3, 1 - half)
+    layer_copy.wait()
+    lay_slab(
+        layer_ref[...].reshape(16, 16, 128), near_flag(near_ref, 17 * half), shifts_ref.at[:, 9 * half]
+    )
     zero = jnp.zeros((128, 128), BF)
-    for a in range(3):
+    for a in (2, 1, 0):
+        conv_copies[2 - a].wait()
         for c in range(3):
             for t in range(4):
                 for s in range(2):
@@ -268,7 +292,7 @@
                 acc = part if acc is None else acc + part
         here = 8 * half + first
         for s in range(2):
-            field = field_ref[here : here + tile, :, s].astype(F32)
+            field = field_ref[first + half : first + half + tile, :, s].astype(F32)
             held_ref[first : first + tile, :, s] = (
                 acc[:, s * 128 : s * 128 + 128].reshape(tile, 8, 16, 128) + field
             ).astype(BF)
@@ -302,6 +326,7 @@
 
 
 ANY = pl.BlockSpec(memory_space=pl.ANY)
+HBM = pl.BlockSpec(memory_space=pltpu.HBM)
 TOKEN = jax.ShapeDtypeStruct((8, 128), F32)
 sds = jax.ShapeDtypeStruct
 
@@ -322,9 +347,10 @@
 def grad_call(coords, parent, own, other, down, field):
     layers = sds((2, 8, 2, 16, 128), BF)
     return call(
-        grad_kernel, [SMEM] * 2 + [VMEM] * 3 + [ANY],
+        grad_kernel, [SMEM] * 2 + [HBM, VMEM, HBM, HBM],
         [sds((16, 8, 2, 16, 128), BF), sds((8, 128, 256), BF), layers, layers],
-        [pltpu.VMEM((8, 128, 128), F32), pltpu.SemaphoreType.DMA((2,))],
+        [pltpu.VMEM((8, 128, 128), F32), pltpu.VMEM((8, 8, 16, 128), BF),
+         pltpu.VMEM((2, 2, 2, 128, 128), BF), pltpu.SemaphoreType.DMA((4,))],
         flops=2 * 2**27, moved=4 << 20,
     )(coords, parent, own, other, down, field)
 
@@ -348,14 +374,16 @@
 
 
 def input_call(near, field, layer, conv, after, half, base=None):
-    ins, values = [SMEM] + [VMEM] * 3 + [ANY], [near, field, layer, conv, after]
+    ins, values = [SMEM] + [HBM] * 3 + [ANY], [near, field, layer, conv, after]
     aliases = {}
     if base is not None:
         ins, values, aliases = ins + [ANY], values + [base], {5: 0}
     return call(
         functools.partial(input_kernel, half=half), ins, [sds((16, 8, 2, 16, 128), BF), TOKEN],
         [pltpu.VMEM((3, 10, 9, 2, 16, 128), BF), pltpu.VMEM((3, 3, 256, 512), BF),
-         pltpu.VMEM((8, 8, 2, 16, 128), BF), pltpu.SemaphoreType.DMA((2,))],
+         pltpu.VMEM((8, 8, 2, 16, 128), BF), pltpu.VMEM((9, 8, 2, 16, 128), BF),
+         pltpu.VMEM((8, 2, 16, 128), BF), pltpu.VMEM((3, 3, 3, 128, 128), BF),
+         pltpu.SemaphoreType.DMA((9,))],
         flops=9 * 2048 * 512 * 256, limit=24, out=ANY, input_output_aliases=aliases,
     )(*values)
 
@@ -370,53 +398,30 @@
     )(coords, keep, got, after)
 
 
-def places(coords_ref, y_ref):
-    core, x = coords_ref[0] % 2, (coords_ref[0] // 2) % 4
-    return jnp.where(core == 0, y_ref[0], x), jnp.where(core == 0, x, y_ref[0])
-
-
-def spread_rows(coords_ref, y_ref, kept_ref, got_ref, own_ref, *send_refs):
-    place = places(coords_ref, y_ref)[0]
-    for k, ref in enumerate((own_ref, *send_refs)):
-        at = pl.multiple_of(16 * ((place + k) % 4), 16)
-        rows = kept_ref[:, pl.ds(at, 16)] + got_ref[0:36, pl.ds(at, 16)].astype(F32)
-        ref[...] = rows.astype(ref.dtype)
-
-
-def spread_taps(coords_ref, y_ref, kept_ref, *refs):
-    got_refs, out_refs = refs[:3], refs[-4:]
-    x = places(coords_ref, y_ref)[1]
-    for k, ref in enumerate(out_refs):
-        taps = pl.ds(9 * ((x + k) % 4), 9)
-        total = kept_ref[taps]
-        for got_ref in got_refs:
-            total = total + got_ref[taps].astype(F32)
-        ref[...] = total.astype(ref.dtype)
-
-
-def add_up(coords_ref, y_ref, kept_ref, first_ref, second_ref, third_ref, *refs):
-    refs[-1][...] = kept_ref[...] + first_ref[...] + second_ref[...] + third_ref[...]
-
-
-def add_pair(coords_ref, y_ref, own_ref, got_ref, *refs):
-    refs[-1][...] = (own_ref[...] + got_ref[...]).astype(refs[-1].dtype)
-
-
-def join_taps(coords_ref, y_ref, own_ref, *refs):
-    x = places(coords_ref, y_ref)[1]
+def add_halves(kept_ref, got_ref, total_ref):
+    total_ref[...] = (kept_ref[...] + got_ref[0:36].astype(F32)).astype(BF)
+
+
+def add_sixteen(got_ref, *refs):
+    total = got_ref[0].astype(F32)
+    for k in range(1, 16):
+        total = total + got_ref[k].astype(F32)
+    refs[-1][...] = total
+
+
+def add_in_order(own_ref, *refs):
+    y = lax.axis_index("dp")
+    total_ref, slots_ref = refs[-2:]
     for k, ref in enumerate((own_ref, *refs[:3])):
-        refs[-1][pl.ds(9 * ((x - k + 4) % 4), 9)] = ref[...]
-
-
-def join_rows(coords_ref, y_ref, own_ref, *refs):
-    place = places(coords_ref, y_ref)[0]
-    for k, ref in enumerate((own_ref, *refs[:3])):
-        at = pl.multiple_of(16 * ((place - k + 4) % 4), 16)
-        refs[-1][:, pl.ds(at, 16)] = ref[...]
-
-
-def finish(coords_ref, y_ref, own_ref, got_ref, conv_ref, down_ref):
-    core = coords_ref[0] % 2
+        slots_ref[(y - k + 4) % 4] = ref[...]
+    total = ((slots_ref[0] + slots_ref[1]) + (slots_ref[2] + slots_ref[3])).astype(BF)
+    for k in range(16):
+        total_ref[k] = total
+
+
+def finish(own_ref, got_ref, *refs):
+    conv_ref, down_ref = refs[-2:]
+    core = lax.axis_index("core")
     mine = pl.ds(pl.multiple_of(64 * core, 64), 64)
     theirs = pl.ds(pl.multiple_of(64 * (1 - core), 64), 64)
     conv_ref[:, mine] = own_ref[0:27].astype(F32)
@@ -425,80 +430,64 @@
     down_ref[:, theirs] = got_ref[27:35].astype(F32)
 
 
-def ring(size, step, by):
-    return [(i, i - i // step % size * step + (i // step + by) % size * step) for i in range(32)]
-
-
 def over_core(value):
-    return lax.ppermute(value, "region", [(i, i ^ 1) for i in range(32)])
-
-
-def over_z(value, mask):
-    return lax.ppermute(value, "region", [(i, i ^ (8 * mask)) for i in range(32)])
-
-
-def over_plane(value, by, second):
-    along_x, route = ring(4, 2, by), []
-    for y in range(4):
-        for region, target in along_x:
-            if region % 2 == second:
-                route.append((32 * y + region, 32 * ((y + by) % 4) + region))
-            else:
-                route.append((32 * y + region, 32 * y + target))
-    return lax.ppermute(value, ("dp", "region"), route)
-
-
-def stage(kernel, coords, y, values, outs, after=(), scratch=()):
-    ins = [SMEM] * 2 + [VMEM] * len(values) + [ANY] * len(after)
-    return call(kernel, ins, outs, scratch)(coords, y, *values, *after)
+    return lax.ppermute(value, "core", [(0, 1), (1, 0)])
+
+
+def over_y(value, by):
+    return lax.ppermute(value, "dp", [(i, (i + by) % 4) for i in range(4)])
+
+
+def over_plane(value):
+    return lax.all_to_all(value, ("z", "x"), 0, 0, tiled=True)
+
+
+def stage(kernel, values, outs, after=(), scratch=()):
+    return call(kernel, [VMEM] * len(values) + [ANY] * len(after), outs, scratch)(*values, *after)
 
 
 def next_region(value):
-    return lax.ppermute(value, "region", [(i, i + 1) for i in range(31)])
+    return lax.ppermute(value, ("z", "x", "core"), [(i, i + 1) for i in range(31)])
 
 
 def previous_region(value):
-    return lax.ppermute(value, "region", [(i + 1, i) for i in range(31)])
+    return lax.ppermute(value, ("z", "x", "core"), [(i + 1, i) for i in range(31)])
 
 
 def local(features, conv_weight, down_weight, coarse_cotangent, brick_coords, neighbours, parents):
     coords, near, parent = brick_coords.reshape(3), neighbours.reshape(26), parents.reshape(1)
-    y = lax.axis_index("dp").reshape(1).astype(jnp.int32)
-    core = lax.axis_index("region") % 2
+    core = lax.axis_index("core")
     cotangent = coarse_cotangent.reshape(16, 16, 16, 128)
     theirs = over_core(lax.dynamic_slice_in_dim(cotangent, 8 * (1 - core), 8))
     field = features.reshape(16, 8, 2, 16, 128)
-    grads, spread, up, back = grad_call(coords, parent, cotangent, theirs, down_weight, field)
+    far = functools.partial(pltpu.with_memory_space_constraint, memory_space=pltpu.HBM)
+    grads, spread, up, back = grad_call(
+        coords, parent, far(cotangent), theirs, far(down_weight), far(field)
+    )
     low, high = next_region(up), previous_region(back)
     inner = inner_call(field, conv_weight)
     kept, sent, keep = main_call(
         coords, parent, near, field, low, high, inner, down_weight, grads, spread
     )
-    run = functools.partial(stage, coords=coords, y=y)
 
     got = over_core(sent)
-    own, *sends = run(
-        spread_rows, values=(kept, got), outs=[sds((36, 16, 128), F32)] + [sds((36, 16, 128), BF)] * 3
-    )
-    gots = [over_plane(v, k + 1, 0) for k, v in enumerate(sends)]
-    partial_grad, token = input_call(near, grads, low, conv_weight, own, 0)
-    own, *sends = run(
-        spread_taps, values=(own, *gots), outs=[sds((9, 16, 128), F32)] * 4, after=(token,)
-    )
-    gots = [over_plane(v, k + 1, 1) for k, v in enumerate(sends)]
-    coarse, token = coarse_call(coords, keep, got, own)
-    own = run(add_up, values=(own, *gots), outs=[sds((9, 16, 128), F32)], after=(token,))[0]
-    own = run(add_pair, values=(own, over_z(own, 1)), outs=[sds((9, 16, 128), F32)])[0]
-    own = run(add_pair, values=(own, over_z(own, 3)), outs=[sds((9, 16, 128), BF)])[0]
-
-    gots = [over_plane(own, k, 1) for k in (1, 2, 3)]
-    own = run(join_taps, values=(own, *gots), outs=[sds((36, 16, 128), BF)])[0]
-    gots = [over_plane(own, k, 0) for k in (1, 2, 3)]
-    input_grad, token = input_call(near, grads, high, conv_weight, own, 1, partial_grad)
-    own = run(join_rows, values=(own, *gots), outs=[sds((36, 64, 128), BF)], after=(token,))[0]
+    own = stage(add_halves, (kept, got), [sds((36, 64, 128), BF)])[0]
+    gots = over_plane(own.reshape(16, 144, 128))
+    partial_grad, token = input_call(near, grads, low, far(conv_weight), own, 0)
+    coarse, token = coarse_call(coords, keep, got, token)
+    own = stage(add_sixteen, (gots,), [sds((144, 128), F32)], (token,))[0]
+    gots = [over_y(own, k) for k in (1, 2, 3)]
+    shares = stage(
+        add_in_order, (own, *gots), [sds((16, 144, 128), BF)],
+        scratch=[pltpu.VMEM((4, 144, 128), F32)],
+    )[0]
+
+    own = over_plane(shares).reshape(36, 64, 128)
+    input_grad, token = input_call(near, grads, high, far(conv_weight), shares, 1, partial_grad)
+    own, token = lax.optimization_barrier((own, token))
     got = over_core(own)
-    conv_grad, down_grad = run(
-        finish, values=(own, got), outs=[sds((27, 128, 128), F32), sds((8, 128, 128), F32)]
+    conv_grad, down_grad = stage(
+        finish, (own, got), [sds((27, 128, 128), F32), sds((8, 128, 128), F32)], (token,)
     )
     whole = (1, 1, 16, 16, 16, 128)
     return (
@@ -510,11 +499,15 @@
 
 
 def solution(mesh):
-    bricks = P("dp", "region", None, None, None, None)
+    sizes = (mesh.devices.shape[0], 4, 4, 2)
+    mesh = jax.sharding.Mesh(mesh.devices.reshape(sizes), ("dp", "z", "x", "core"))
+    region = ("z", "x", "core")
+    bricks = P("dp", region, None, None, None, None)
+    rows = P("dp", region, None)
     return jax.shard_map(
         local,
         mesh=mesh,
-        in_specs=(bricks, P(), P(), bricks, P("dp", "region", None), P("dp", "region", None), P("dp", "region")),
+        in_specs=(bricks, P(), P(), bricks, rows, rows, P("dp", region)),
         out_specs=(bricks, bricks, P(), P()),
         check_vma=False,
     )

time: 94.5 us -> 80.9 us (0.86)
  starting transfers between devices: 38 us -> 26.5 us
  local copies, waits for them, and re-layouts: 8.55 us -> 1.85 us
  waiting for transfers between devices: 12.8 us -> 17.3 us
    ppermute x19 -> x8, starting transfers between devices: 38 us -> 14 us  [the longest x3 4.68 us: over_core(): return lax.ppermute(value, 'core', [(0, 1), (1, 0)])]
    all_to_all x0 -> x2, starting transfers between devices: none -> 12.5 us  [over_plane(): return lax.all_to_all(value, ('z', 'x'), 0, 0, tiled=True)]
    all_to_all x0 -> x2, waiting for transfers between devices: none -> 7.9 us  [over_plane(): return lax.all_to_all(value, ('z', 'x'), 0, 0, tiled=True)]
    unnamed x28 -> x12, local copies, waits for them, and re-layouts: 7.39 us -> 0.68 us
    ppermute x19 -> x8, waiting for transfers between devices: 12.8 us -> 9.37 us  [the longest x3 4.9 us: over_core(): return lax.ppermute(value, 'core', [(0, 1), (1, 0)])]
    pallas_call x2, Pallas kernels: 9.06 us -> 12.2 us  [input_call(): call(functools.partial(input_kernel, half=half), ins, [sds((16, 8, 2, 16,...]
    pallas_call x9 -> x5, Pallas kernels: 7.89 us -> 5.96 us  [the longest x4 3.46 us: stage(): call(kernel, [VMEM] * len(values) + [ANY] * len(after), outs, scratch)]
  transfers between devices with their start and end apart: 19 -> 10, of which waited for: 8 -> 8; matrix products, arithmetic and copies ran while one was open for 0% -> 0% of each run, Pallas kernels for 17% -> 24%
where the time goes in v2:
time: 80.9 us; the launch traced here: 80.5 us
  Pallas kernels  33.4 us (41%)
  starting transfers between devices  26.5 us (33%)
  waiting for transfers between devices  17.3 us (21%)
  local copies, waits for them, and re-layouts  1.85 us (2%)
  between operations  1.47 us (2%)
    all_to_all x2, starting transfers between devices, over_plane(): return lax.all_to_all(value, ('z', 'x'), 0, 0, tiled=True)  12.5 us
    pallas_call x2, Pallas kernels, input_call(): call(functools.partial(input_kernel, half=half), ins, [sds((16, 8, 2, 16,...  12.2 us
    pallas_call x1, Pallas kernels, main_call(): call(main_kernel, [SMEM] * 3 + [VMEM] * 9, [sds((36, 64, 128), F32), sds(...  8.24 us
    all_to_all x2, waiting for transfers between devices, over_plane(): return lax.all_to_all(value, ('z', 'x'), 0, 0, tiled=True)  7.9 us
    pallas_call x1, Pallas kernels, inner_call(): call(inner_kernel, [VMEM] * 2, [sds((3, 16, 9, 2, 16, 128), BF), sds((3,...  5.33 us
    ppermute x3, waiting for transfers between devices, over_core(): return lax.ppermute(value, 'core', [(0, 1), (1, 0)])  4.9 us
    ppermute x3, starting transfers between devices, over_core(): return lax.ppermute(value, 'core', [(0, 1), (1, 0)])  4.68 us
    ppermute x3, waiting for transfers between devices, over_y(): return lax.ppermute(value, 'dp', [(i, (i + by) % 4) for i in range(4)])  4.46 us
  transfers between devices with their start and end apart: 10, of which 8 were waited for; matrix products, arithmetic and copies ran while one was open for 0% of the time, Pallas kernels for 24%

profile of v2, /device:TPU:1, one launch (start us, length us, event | category | flops | bytes accessed | tf_op | source)
XLA Modules:
  0.0 80.5 jit_solution(2341244407443667867)
XLA Ops:
  0.6 0.0 copy-start
  0.6 1.2 %dynamic-slice_bitcast_fusion = bf16[8,16,16,128]{3,2,1,0:T(8,128)(2,1)S(1)} fusion(bf16[1,1,16,16,16,128]{5,4,3,2,1,0:T(8,128)(2,1)} %param.10, s32[]{:T(128)S(6)} %select_n.3), kind=kLoop, calls=%fused_computation | loop fusion | bytes 1048580 | tf_op jit(solution)/shard_map/dynamic_slice | solution.py:461
  1.8 1.5 %collective-permute-start = (bf16[8,16,16,128]{3,2,1,0:T(8,128)(2,1)S(1)}, bf16[8,16,16,128]{3,2,1,0:T(8,128)(2,1)S(1)}, u32[]{:S(2)}, u32[]{:S(2)}) collective-permute-start(bf16[8,16,16,128]{3,2,1,0:T(8,128)(2,1)S(1)} %dynamic-slice_bitcast_fusion), channel_id=1, source_target_pairs={{0,1},{1,0},{2,3},{3,2},{4,5},{5,4},{6,7},{7,6},{8,9},{9,8},{10,11... | collective-permute-start | bytes 1572872 | tf_op jit(solution)/shard_map/ppermute | solution.py:434
  4.0 0.9 %collective-permute-done.other_ref = bf16[8,16,16,128]{3,2,1,0:T(8,128)(2,1)S(1)} collective-permute-done((bf16[8,16,16,128]{3,2,1,0:T(8,128)(2,1)S(1)}, bf16[8,16,16,128]{3,2,1,0:T(8,128)(2,1)S(1)}, u32[]{:S(2)}, u32[]{:S(2)}) %collective-permute-start) | collective-permute-done | bytes 524320 | tf_op jit(solution)/shard_map/ppermute | solution.py:434
  4.9 0.0 copy-start.2
  4.9 0.7 copy-done.2
  5.5 0.0 copy-start.4
  5.5 2.5 %shard_map.102 = (bf16[16,8,2,16,128]{4,3,2,1,0:T(8,128)(2,1)S(1)}, bf16[8,128,256]{2,1,0:T(8,128)(2,1)S(1)}, bf16[2,8,2,16,128]{4,3,2,1,0:T(8,128)(2,1)S(1)}, bf16[2,8,2,16,128]{4,3,2,1,0:T(8,128)(2,1)S(1)}) custom-call(s32[3]{0:T(128)S(1)} %bitcast.20, s32[1]{0:T(128)} %bitcast.13.parent_ref, bf16[16,16,16,128]{3,2,1,0:T(8,128)(2,1)} %bitcast.26, ...), custom_call_target="tpu_custom_call" | custom-call | flops 268435456 | bytes 4194304 | tf_op jit(solution)/shard_map/pallas_call | solution.py:349
  8.0 3.5 %collective-permute-start.1 = (bf16[2,8,2,16,128]{4,3,2,1,0:T(8,128)(2,1)S(1)}, bf16[2,8,2,16,128]{4,3,2,1,0:T(8,128)(2,1)S(1)}, u32[]{:S(2)}, u32[]{:S(2)}) collective-permute-start(bf16[2,8,2,16,128]{4,3,2,1,0:T(8,128)(2,1)S(1)} %get-tuple-element.24), channel_id=1, source_target_pairs={{0,1},{1,2},{2,3},{3,4},{4,5},{5,6},{6,7},{7,8},{8,9},{9,10},{10,1... | collective-permute-start | bytes 393224 | tf_op jit(solution)/shard_map/ppermute | solution.py:450
  11.5 0.0 copy-start.1
  11.5 0.0 copy-start.3
  11.5 0.0 copy-start.5
  11.5 2.1 %collective-permute-start.2 = (bf16[2,8,2,16,128]{4,3,2,1,0:T(8,128)(2,1)S(1)}, bf16[2,8,2,16,128]{4,3,2,1,0:T(8,128)(2,1)S(1)}, u32[]{:S(2)}, u32[]{:S(2)}) collective-permute-start(bf16[2,8,2,16,128]{4,3,2,1,0:T(8,128)(2,1)S(1)} %get-tuple-element.25), channel_id=1, source_target_pairs={{1,0},{2,1},{3,2},{4,3},{5,4},{6,5},{7,6},{8,7},{9,8},{10,9},{11,1... | collective-permute-start | bytes 393224 | tf_op jit(solution)/shard_map/ppermute | solution.py:454
  13.6 0.0 copy-done
  13.6 0.0 copy-done.4
  13.6 5.3 %shard_map.103 = (bf16[3,16,9,2,16,128]{5,4,3,2,1,0:T(8,128)(2,1)S(1)}, bf16[3,3,512,256]{3,2,1,0:T(8,128)(2,1)S(1)}, bf16[16,8,2,16,128]{4,3,2,1,0:T(8,128)(2,1)S(1)}) custom-call(bf16[16,8,2,16,128]{4,3,2,1,0:T(8,128)(2,1)S(1)} %bitcast.18, bf16[3,3,3,128,128]{4,3,2,1,0:T(8,128)(2,1)S(1)} %copy-done.4), custom_call_target="tpu_custom_call" | custom-call | flops 4831838208 | bytes 2097152 | tf_op jit(solution)/shard_map/pallas_call | solution.py:359
  19.0 0.0 collective-permute-done.1.low_ref.layer_hbm
  19.0 0.0 collective-permute-done.2.high_ref.layer_hbm
  19.0 0.0 copy-done.1
  19.0 0.0 copy-done.3
  19.0 0.0 copy-done.5
  19.0 8.2 %shard_map.104 = (f32[36,64,128]{2,1,0:T(8,128)S(1)}, bf16[53,64,128]{2,1,0:T(8,128)(2,1)S(1)}, bf16[8,8,16,128]{3,2,1,0:T(8,128)(2,1)S(1)}) custom-call(s32[3]{0:T(128)S(1)} %bitcast.21, s32[1]{0:T(128)} %bitcast.14.parent_ref, s32[26]{0:T(128)S(1)} %bitcast.23, bf16[16,8,2,16,128]{4,3,2,1,0:T(8,128)(2,1)S(1)} %bitcast.19, ...), custom_call_target="tpu_custom_call" | custom-call | flops 4831838208 | bytes 1048576 | tf_op jit(solution)/shard_map/pallas_call | solution.py:368
  27.3 0.1 collective-permute-start.3
  27.3 2.4 %collective-permute-done.3.got_ref = bf16[53,64,128]{2,1,0:T(8,128)(2,1)S(1)} collective-permute-done((bf16[53,64,128]{2,1,0:T(8,128)(2,1)S(1)}, bf16[53,64,128]{2,1,0:T(8,128)(2,1)S(1)}, u32[]{:S(2)}, u32[]{:S(2)}) %collective-permute-start.3) | collective-permute-done | bytes 868384 | tf_op jit(solution)/shard_map/ppermute | solution.py:434
  29.7 0.9 %shard_map.105.refs_0_ = bf16[36,64,128]{2,1,0:T(8,128)(2,1)} custom-call(f32[36,64,128]{2,1,0:T(8,128)S(1)} %get-tuple-element.33.kept_ref, bf16[53,64,128]{2,1,0:T(8,128)(2,1)S(1)} %collective-permute-done.3.got_ref), custom_call_target="tpu_custom_call" | custom-call | bytes 1048576 | tf_op jit(solution)/shard_map/pallas_call | solution.py:446
  30.7 8.3 %all-to-all-start = ((bf16[16,144,128]{2,1,0:T(8,128)(2,1)}), bf16[16,144,128]{2,1,0:T(8,128)(2,1)S(1)}, u32[]{:S(2)}, u32[]{:S(2)}) async-start(bf16[16,144,128]{2,1,0:T(8,128)(2,1)} %bitcast.7), calls=%async_computation | async-start | bytes 1179648 | tf_op jit(solution)/shard_map/all_to_all | solution.py:442
  39.0 6.1 %shard_map.106 = (bf16[16,8,2,16,128]{4,3,2,1,0:T(8,128)(2,1)}, f32[8,128]{1,0:T(8,128)S(1)}) custom-call(s32[26]{0:T(128)S(1)} %bitcast.24, bf16[16,8,2,16,128]{4,3,2,1,0:T(8,128)(2,1)S(1)} %get-tuple-element.29.grads_ref.field_hbm, bf16[2,8,2,16,128]{4,3,2,1,0:T(8,128)(2,1)S(1)} %collective-permute-done.1.low_ref.layer_hbm, ...), custom_call_target="tpu_custom_call" | custom-call | flops 2415919104 | bytes 1048576 | tf_op jit(solution)/shard_map/pallas_call | solution.py:381
  45.1 1.7 %shard_map.107 = (bf16[16,16,16,128]{3,2,1,0:T(8,128)(2,1)}, f32[8,128]{1,0:T(8,128)S(1)}) custom-call(s32[3]{0:T(128)S(1)} %bitcast.22, bf16[8,8,16,128]{3,2,1,0:T(8,128)(2,1)S(1)} %get-tuple-element.31.keep_ref, bf16[53,64,128]{2,1,0:T(8,128)(2,1)S(1)} %collective-permute-done.3.got_ref, f32[8,128]{1,0:T(8,128)S(1)} %get-tuple-element.34.after_ref), custom_call_target="tpu_custom_call" | custom-call | bytes 1048576 | tf_op jit(solution)/shard_map/pallas_call | solution.py:395
  46.7 3.9 %all-to-all-done.got_ref = bf16[16,144,128]{2,1,0:T(8,128)(2,1)S(1)} async-done(((bf16[16,144,128]{2,1,0:T(8,128)(2,1)}), bf16[16,144,128]{2,1,0:T(8,128)(2,1)S(1)}, u32[]{:S(2)}, u32[]{:S(2)}) %all-to-all-start) | async-done | bytes 589856 | tf_op jit(solution)/shard_map/all_to_all | solution.py:442
  50.6 0.1 shard_map.108.own_ref
  50.7 2.8 %collective-permute-start.6 = (f32[144,128]{1,0:T(8,128)S(1)}, f32[144,128]{1,0:T(8,128)S(1)}, u32[]{:S(2)}, u32[]{:S(2)}) collective-permute-start(f32[144,128]{1,0:T(8,128)S(1)} %shard_map.108.own_ref), channel_id=1, source_target_pairs={{0,96},{32,0},{64,32},{96,64},{1,97},{33,1},{65,33},{97,65},{2,98}... | collective-permute-start | bytes 221192 | tf_op jit(solution)/shard_map/ppermute | solution.py:438
  53.5 0.3 collective-permute-start.5
  53.8 0.7 collective-permute-start.4
  54.5 0.4 collective-permute-done.6.refs_2_
  54.9 3.4 %collective-permute-done.5.refs_1_ = f32[144,128]{1,0:T(8,128)S(1)} collective-permute-done((f32[144,128]{1,0:T(8,128)S(1)}, f32[144,128]{1,0:T(8,128)S(1)}, u32[]{:S(2)}, u32[]{:S(2)}) %collective-permute-start.5) | collective-permute-done | bytes 73760 | tf_op jit(solution)/shard_map/ppermute | solution.py:438
  58.3 0.7 collective-permute-done.4.refs_0_
  59.0 0.9 %shard_map.109.refs_0_ = bf16[16,144,128]{2,1,0:T(8,128)(2,1)} custom-call(f32[144,128]{1,0:T(8,128)S(1)} %shard_map.108.own_ref, f32[144,128]{1,0:T(8,128)S(1)} %collective-permute-done.4.refs_0_, f32[144,128]{1,0:T(8,128)S(1)} %collective-permute-done.5.refs_1_, f32[144,128]{1,0:T(8,128)S(1)} %collective-permute-done.6.refs_2_), custom_call_target="tpu_custom_call" | custom-call | bytes 1048576 | tf_op jit(solution)/shard_map/pallas_call | solution.py:446
  59.9 4.2 %all-to-all-start.1 = ((bf16[16,144,128]{2,1,0:T(8,128)(2,1)}), bf16[16,144,128]{2,1,0:T(8,128)(2,1)S(1)}, u32[]{:S(2)}, u32[]{:S(2)}) async-start(bf16[16,144,128]{2,1,0:T(8,128)(2,1)} %shard_map.109.refs_0_), calls=%async_computation.1 | async-start | bytes 1179648 | tf_op jit(solution)/shard_map/all_to_all | solution.py:442
  64.1 6.1 %shard_map.110 = (bf16[16,8,2,16,128]{4,3,2,1,0:T(8,128)(2,1)}, f32[8,128]{1,0:T(8,128)S(1)}) custom-call(s32[26]{0:T(128)S(1)} %bitcast.25, bf16[16,8,2,16,128]{4,3,2,1,0:T(8,128)(2,1)S(1)} %get-tuple-element.29.grads_ref.field_hbm, bf16[2,8,2,16,128]{4,3,2,1,0:T(8,128)(2,1)S(1)} %collective-permute-done.2.high_ref.layer_hbm, ...), custom_call_target="tpu_custom_call", output_to_operand_aliasing={{0}: (5, {})} | custom-call | flops 2415919104 | bytes 1048576 | tf_op jit(solution)/shard_map/pallas_call | solution.py:381
  70.2 4.0 %all-to-all-done.1 = bf16[16,144,128]{2,1,0:T(8,128)(2,1)S(1)} async-done(((bf16[16,144,128]{2,1,0:T(8,128)(2,1)}), bf16[16,144,128]{2,1,0:T(8,128)(2,1)S(1)}, u32[]{:S(2)}, u32[]{:S(2)}) %all-to-all-start.1) | async-done | bytes 589856 | tf_op jit(solution)/shard_map/all_to_all | solution.py:442
  74.2 3.1 %collective-permute-start.7 = (bf16[36,64,128]{2,1,0:T(8,128)(2,1)S(1)}, bf16[36,64,128]{2,1,0:T(8,128)(2,1)S(1)}, u32[]{:S(2)}, u32[]{:S(2)}) collective-permute-start(bf16[36,64,128]{2,1,0:T(8,128)(2,1)S(1)} %bitcast.15), channel_id=1, source_target_pairs={{0,1},{1,0},{2,3},{3,2},{4,5},{5,4},{6,7},{7,6},{8,9},{9,8},{10,11... | collective-permute-start | bytes 1769480 | tf_op jit(solution)/shard_map/ppermute | solution.py:434
  77.3 1.6 %collective-permute-done.7.got_ref = bf16[36,64,128]{2,1,0:T(8,128)(2,1)S(1)} collective-permute-done((bf16[36,64,128]{2,1,0:T(8,128)(2,1)S(1)}, bf16[36,64,128]{2,1,0:T(8,128)(2,1)S(1)}, u32[]{:S(2)}, u32[]{:S(2)}) %collective-permute-start.7) | collective-permute-done | bytes 589856 | tf_op jit(solution)/shard_map/ppermute | solution.py:434
  78.9 1.5 %shard_map.111 = (f32[27,128,128]{2,1,0:T(8,128)}, f32[8,128,128]{2,1,0:T(8,128)}) custom-call(bf16[36,64,128]{2,1,0:T(8,128)(2,1)S(1)} %bitcast.16, bf16[36,64,128]{2,1,0:T(8,128)(2,1)S(1)} %collective-permute-done.7.got_ref, f32[8,128]{1,0:T(8,128)S(1)} %get-tuple-element.41.refs_0_), custom_call_target="tpu_custom_call" | custom-call | bytes 1048576 | tf_op jit(solution)/shard_map/pallas_call | solution.py:446
Async XLA Ops:
  0.6 13.0 %copy-start = (bf16[1,1,16,16,16,128]{5,4,3,2,1,0:T(8,128)(2,1)S(1)}, bf16[1,1,16,16,16,128]{5,4,3,2,1,0:T(8,128)(2,1)}, u32[]{:S(2)}) copy-start(bf16[1,1,16,16,16,128]{5,4,3,2,1,0:T(8,128)(2,1)} %param.7) | copy-start | bytes 3145732
  1.8 3.0 %collective-permute-start = (bf16[8,16,16,128]{3,2,1,0:T(8,128)(2,1)S(1)}, bf16[8,16,16,128]{3,2,1,0:T(8,128)(2,1)S(1)}, u32[]{:S(2)}, u32[]{:S(2)}) collective-permute-start(bf16[8,16,16,128]{3,2,1,0:T(8,128)(2,1)S(1)} %dynamic-slice_bitcast_fusion), channel_id=1, source_target_pairs={{0,1},{1,0},{2,3},{3,2},{4,5},{5,4},{6,7},{7,6},{8,9},{9,8},{10,11... | collective-permute-start | bytes 1572872 | tf_op jit(solution)/shard_map/ppermute | solution.py:434
  4.9 0.7 copy-start.2
  5.5 8.1 %copy-start.4 = (bf16[3,3,3,128,128]{4,3,2,1,0:T(8,128)(2,1)S(1)}, bf16[3,3,3,128,128]{4,3,2,1,0:T(8,128)(2,1)}, u32[]{:S(2)}) copy-start(bf16[3,3,3,128,128]{4,3,2,1,0:T(8,128)(2,1)} %conv_hbm.3) | copy-start | bytes 2654212
  8.0 10.9 %collective-permute-start.1 = (bf16[2,8,2,16,128]{4,3,2,1,0:T(8,128)(2,1)S(1)}, bf16[2,8,2,16,128]{4,3,2,1,0:T(8,128)(2,1)S(1)}, u32[]{:S(2)}, u32[]{:S(2)}) collective-permute-start(bf16[2,8,2,16,128]{4,3,2,1,0:T(8,128)(2,1)S(1)} %get-tuple-element.24), channel_id=1, source_target_pairs={{0,1},{1,2},{2,3},{3,4},{4,5},{5,6},{6,7},{7,8},{8,9},{9,10},{10,1... | collective-permute-start | bytes 393224 | tf_op jit(solution)/shard_map/ppermute | solution.py:450
  11.5 7.5 %copy-start.1 = (bf16[2,2,2,128,128]{4,3,2,1,0:T(8,128)(2,1)S(1)}, bf16[2,2,2,128,128]{4,3,2,1,0:T(8,128)(2,1)}, u32[]{:S(2)}) copy-start(bf16[2,2,2,128,128]{4,3,2,1,0:T(8,128)(2,1)} %down_ref.1) | copy-start | bytes 786436
  11.5 7.5 %copy-start.3 = (s32[1,1,3]{2,1,0:T(1,128)S(1)}, s32[1,1,3]{2,1,0:T(1,128)}, u32[]{:S(2)}) copy-start(s32[1,1,3]{2,1,0:T(1,128)} %param.11) | copy-start | bytes 40
  11.5 7.5 %copy-start.5 = (s32[1,1,26]{2,1,0:T(1,128)S(1)}, s32[1,1,26]{2,1,0:T(1,128)}, u32[]{:S(2)}) copy-start(s32[1,1,26]{2,1,0:T(1,128)} %param.12) | copy-start | bytes 316
  11.5 7.4 %collective-permute-start.2 = (bf16[2,8,2,16,128]{4,3,2,1,0:T(8,128)(2,1)S(1)}, bf16[2,8,2,16,128]{4,3,2,1,0:T(8,128)(2,1)S(1)}, u32[]{:S(2)}, u32[]{:S(2)}) collective-permute-start(bf16[2,8,2,16,128]{4,3,2,1,0:T(8,128)(2,1)S(1)} %get-tuple-element.25), channel_id=1, source_target_pairs={{1,0},{2,1},{3,2},{4,3},{5,4},{6,5},{7,6},{8,7},{9,8},{10,9},{11,1... | collective-permute-start | bytes 393224 | tf_op jit(solution)/shard_map/ppermute | solution.py:454
  27.3 2.5 %collective-permute-start.3 = (bf16[53,64,128]{2,1,0:T(8,128)(2,1)S(1)}, bf16[53,64,128]{2,1,0:T(8,128)(2,1)S(1)}, u32[]{:S(2)}, u32[]{:S(2)}) collective-permute-start(bf16[53,64,128]{2,1,0:T(8,128)(2,1)S(1)} %get-tuple-element.32), channel_id=1, source_target_pairs={{0,1},{1,0},{2,3},{3,2},{4,5},{5,4},{6,7},{7,6},{8,9},{9,8},{10,11... | collective-permute-start | bytes 2605064 | tf_op jit(solution)/shard_map/ppermute | solution.py:434
  30.7 19.9 %all-to-all-start = ((bf16[16,144,128]{2,1,0:T(8,128)(2,1)}), bf16[16,144,128]{2,1,0:T(8,128)(2,1)S(1)}, u32[]{:S(2)}, u32[]{:S(2)}) async-start(bf16[16,144,128]{2,1,0:T(8,128)(2,1)} %bitcast.7), calls=%async_computation | async-start | bytes 1179648 | tf_op jit(solution)/shard_map/all_to_all | solution.py:442
  50.7 4.2 %collective-permute-start.6 = (f32[144,128]{1,0:T(8,128)S(1)}, f32[144,128]{1,0:T(8,128)S(1)}, u32[]{:S(2)}, u32[]{:S(2)}) collective-permute-start(f32[144,128]{1,0:T(8,128)S(1)} %shard_map.108.own_ref), channel_id=1, source_target_pairs={{0,96},{32,0},{64,32},{96,64},{1,97},{33,1},{65,33},{97,65},{2,98}... | collective-permute-start | bytes 221192 | tf_op jit(solution)/shard_map/ppermute | solution.py:438
  53.5 4.8 %collective-permute-start.5 = (f32[144,128]{1,0:T(8,128)S(1)}, f32[144,128]{1,0:T(8,128)S(1)}, u32[]{:S(2)}, u32[]{:S(2)}) collective-permute-start(f32[144,128]{1,0:T(8,128)S(1)} %shard_map.108.own_ref), channel_id=1, source_target_pairs={{0,64},{32,96},{64,0},{96,32},{1,65},{33,97},{65,1},{97,33},{2,66}... | collective-permute-start | bytes 221192 | tf_op jit(solution)/shard_map/ppermute | solution.py:438
  53.8 5.2 %collective-permute-start.4 = (f32[144,128]{1,0:T(8,128)S(1)}, f32[144,128]{1,0:T(8,128)S(1)}, u32[]{:S(2)}, u32[]{:S(2)}) collective-permute-start(f32[144,128]{1,0:T(8,128)S(1)} %shard_map.108.own_ref), channel_id=1, source_target_pairs={{0,32},{32,64},{64,96},{96,0},{1,33},{33,65},{65,97},{97,1},{2,34}... | collective-permute-start | bytes 221192 | tf_op jit(solution)/shard_map/ppermute | solution.py:438
  59.9 14.3 %all-to-all-start.1 = ((bf16[16,144,128]{2,1,0:T(8,128)(2,1)}), bf16[16,144,128]{2,1,0:T(8,128)(2,1)S(1)}, u32[]{:S(2)}, u32[]{:S(2)}) async-start(bf16[16,144,128]{2,1,0:T(8,128)(2,1)} %shard_map.109.refs_0_), calls=%async_computation.1 | async-start | bytes 1179648 | tf_op jit(solution)/shard_map/all_to_all | solution.py:442
  74.2 4.7 %collective-permute-start.7 = (bf16[36,64,128]{2,1,0:T(8,128)(2,1)S(1)}, bf16[36,64,128]{2,1,0:T(8,128)(2,1)S(1)}, u32[]{:S(2)}, u32[]{:S(2)}) collective-permute-start(bf16[36,64,128]{2,1,0:T(8,128)(2,1)S(1)} %bitcast.15), channel_id=1, source_target_pairs={{0,1},{1,0},{2,3},{3,2},{4,5},{5,4},{6,7},{7,6},{8,9},{9,8},{10,11... | collective-permute-start | bytes 1769480 | tf_op jit(solution)/shard_map/ppermute | solution.py:434

commit v3 on v2

--- a/solution.py
+++ b/solution.py
@@ -88,29 +88,41 @@
     )
 
 
-def grad_kernel(
-    coords_ref, parent_ref, own_hbm, other_ref, down_hbm, field_hbm,
-    grads_ref, spread_ref, up_ref, back_ref, wide_ref, own_ref, down_ref, sems,
+def prepare_kernel(
+    coords_ref, cotangent_hbm, down_hbm, field_hbm, after_ref,
+    mine_ref, down_ref, partner_ref, other_ref, held_ref, sems,
 ):
-    x, oy, oz = coords_ref[0], coords_ref[1] % 2, coords_ref[2] % 2
+    x, oy = coords_ref[0], coords_ref[1] % 2
+    upper = x % 2
     copies = [
         pltpu.make_async_copy(
-            own_hbm.at[pl.ds(8 * (x % 2), 8), pl.ds(8 * oy, 8)], own_ref, sems.at[0]
+            cotangent_hbm.at[pl.ds(8 * upper, 8), pl.ds(8 * oy, 8)], mine_ref, sems.at[0]
         ),
-        pltpu.make_async_copy(down_hbm, down_ref, sems.at[1]),
-        pltpu.make_async_copy(field_hbm.at[15], up_ref.at[0], sems.at[2]),
-        pltpu.make_async_copy(field_hbm.at[0], back_ref.at[0], sems.at[3]),
+        pltpu.make_async_copy(down_hbm, held_ref, sems.at[1]),
+        pltpu.make_async_copy(field_hbm.at[15 - 15 * upper], partner_ref, sems.at[2]),
+        pltpu.make_async_copy(field_hbm.at[15 * upper], other_ref, sems.at[3]),
     ]
     for copy in copies:
         copy.start()
+    copies[1].wait()
+    down_ref[...] = joined_down(held_ref)
+    for k in (0, 2, 3):
+        copies[k].wait()
+
+
+def grad_kernel(
+    coords_ref, parent_ref, mine_ref, theirs_ref, down_ref, partner_ref, other_ref,
+    grads_ref, spread_ref, to_partner_ref, to_other_ref, wide_ref,
+):
+    x, oy, oz = coords_ref[0], coords_ref[1] % 2, coords_ref[2] % 2
     is_own = parent_ref[0] == x
-    copies[0].wait()
-    copies[1].wait()
-    down = joined_down(down_ref)
+    down = down_ref[...]
+    to_partner_ref[0] = partner_ref[...]
+    to_other_ref[0] = other_ref[...]
     wide_ref[...] = jnp.zeros_like(wide_ref)
     for i in range(8):
-        mine = own_ref[i].astype(F32)
-        theirs = other_ref[i, pl.ds(8 * oy, 8)].astype(F32)
+        mine = mine_ref[i].astype(F32)
+        theirs = theirs_ref[i, pl.ds(8 * oy, 8)].astype(F32)
         both = jnp.where(is_own, mine, theirs)
         part = jnp.where(oz == 0, both[:, 0:8], both[:, 8:16]).reshape(64, 128)
         wide_ref[i, pl.ds(0, 64, stride=2), :] = part
@@ -124,12 +136,9 @@
                 at = (2 * p + q) * 128
                 part = grads[:, at : at + 128].reshape(8, 16, 128)
                 grads_ref[2 * i + p, :, q] = part
-                if 2 * i + p == 15:
-                    up_ref[1, :, q] = part
-                if 2 * i + p == 0:
-                    back_ref[1, :, q] = part
-    copies[2].wait()
-    copies[3].wait()
+    upper = x % 2
+    to_partner_ref[1] = grads_ref[15 - 15 * upper]
+    to_other_ref[1] = grads_ref[15 * upper]
 
 
 def lay_weights(conv_ref, weights_ref):
@@ -166,7 +175,7 @@
 
 
 def main_kernel(
-    coords_ref, parent_ref, near_ref, field_ref, low_ref, high_ref, shifts_ref, weights_ref,
+    coords_ref, parent_ref, near_ref, field_ref, partner_ref, other_ref, shifts_ref, weights_ref,
     inner_ref, down_ref, grads_ref, spread_ref,
     kept_rows_ref, sent_ref, keep_ref, low_shifts_ref, high_shifts_ref, edges_ref, sums_ref,
 ):
@@ -181,8 +190,11 @@
     kept_rows_ref[35] = jnp.zeros((64, 128), F32)
     sent_ref[35] = jnp.zeros((64, 128), BF)
     sent_ref[52] = jnp.full((64, 128), oy, jnp.int32).astype(F32).astype(BF)
-    lay_slab(low_ref[0].reshape(16, 16, 128), near_flag(near_ref, 0), low_shifts_ref)
-    lay_slab(high_ref[0].reshape(16, 16, 128), near_flag(near_ref, 17), high_shifts_ref)
+    partner, other = partner_ref[0].astype(F32), other_ref[0].astype(F32)
+    low = jnp.where(first_core, other, partner).reshape(16, 16, 128)
+    high = jnp.where(first_core, partner, other).reshape(16, 16, 128)
+    lay_slab(low, near_flag(near_ref, 0), low_shifts_ref)
+    lay_slab(high, near_flag(near_ref, 17), high_shifts_ref)
 
     acc = None
     for a in range(3):
@@ -196,7 +208,7 @@
             value = acc[128 * k : 128 * k + 128, s * 128 : s * 128 + 128].reshape(8, 16, 128)
             edges_ref[k, :, s] = (value + field_ref[15 * k, :, s].astype(F32)).astype(BF)
 
-    down = joined_down(down_ref)
+    down = down_ref[...]
 
     def corner(i, p, q):
         at = 2 * i + p
@@ -249,7 +261,7 @@
                 )
 
 
-def input_kernel(near_ref, field_hbm, layer_hbm, conv_hbm, *refs, half, tile=4):
+def input_kernel(near_ref, field_hbm, partner_hbm, other_hbm, conv_hbm, *refs, half, tile=4):
     (result_ref, token_ref, shifts_ref, weights_ref, held_ref, field_ref, layer_ref, conv_ref,
      sems) = refs[-9:]
     token_ref[...] = jnp.zeros_like(token_ref)
@@ -260,18 +272,25 @@
         )
         for k in range(3)
     ]
-    layer_copy = pltpu.make_async_copy(layer_hbm.at[1], layer_ref, sems.at[5])
+    layer_copies = [
+        pltpu.make_async_copy(partner_hbm.at[1], layer_ref.at[0], sems.at[5]),
+        pltpu.make_async_copy(other_hbm.at[1], layer_ref.at[1], sems.at[9]),
+    ]
     conv_copies = [
         pltpu.make_async_copy(conv_hbm.at[a], conv_ref.at[a], sems.at[6 + a]) for a in range(3)
     ]
-    for copy in (*fetches, layer_copy, *conv_copies):
+    for copy in (*fetches, *layer_copies, *conv_copies):
         copy.start()
     for k in range(3):
         fetches[k].wait()
         lay_interior(field_ref, shifts_ref, 3 * k, 3 * k + 3, 1 - half)
-    layer_copy.wait()
+    for copy in layer_copies:
+        copy.wait()
+    layer = jnp.where(
+        lax.axis_index("core") == half, layer_ref[1].astype(F32), layer_ref[0].astype(F32)
+    )
     lay_slab(
-        layer_ref[...].reshape(16, 16, 128), near_flag(near_ref, 17 * half), shifts_ref.at[:, 9 * half]
+        layer.reshape(16, 16, 128), near_flag(near_ref, 17 * half), shifts_ref.at[:, 9 * half]
     )
     zero = jnp.zeros((128, 128), BF)
     for a in (2, 1, 0):
@@ -344,15 +363,22 @@
     )
 
 
-def grad_call(coords, parent, own, other, down, field):
+def prepare_call(coords, cotangent, down, field, after):
+    layer = sds((8, 2, 16, 128), BF)
+    return call(
+        prepare_kernel, [SMEM] + [HBM] * 3 + [ANY],
+        [sds((8, 8, 16, 128), BF), sds((512, 256), BF), layer, layer],
+        [pltpu.VMEM((2, 2, 2, 128, 128), BF), pltpu.SemaphoreType.DMA((4,))], moved=1 << 20,
+    )(coords, cotangent, down, field, after)
+
+
+def grad_call(coords, parent, mine, theirs, down, partner, other):
     layers = sds((2, 8, 2, 16, 128), BF)
     return call(
-        grad_kernel, [SMEM] * 2 + [HBM, VMEM, HBM, HBM],
+        grad_kernel, [SMEM] * 2 + [VMEM] * 5,
         [sds((16, 8, 2, 16, 128), BF), sds((8, 128, 256), BF), layers, layers],
-        [pltpu.VMEM((8, 128, 128), F32), pltpu.VMEM((8, 8, 16, 128), BF),
-         pltpu.VMEM((2, 2, 2, 128, 128), BF), pltpu.SemaphoreType.DMA((4,))],
-        flops=2 * 2**27, moved=4 << 20,
-    )(coords, parent, own, other, down, field)
+        [pltpu.VMEM((8, 128, 128), F32)], flops=2 * 2**27, moved=4 << 20,
+    )(coords, parent, mine, theirs, down, partner, other)
 
 
 def inner_call(field, conv):
@@ -363,27 +389,27 @@
     )(field, conv)
 
 
-def main_call(coords, parent, near, field, low, high, inner, down, grads, spread):
+def main_call(coords, parent, near, field, partner, other, inner, down, grads, spread):
     slab = pltpu.VMEM((3, 9, 2, 16, 128), BF)
     return call(
         main_kernel, [SMEM] * 3 + [VMEM] * 9,
         [sds((36, 64, 128), F32), sds((53, 64, 128), BF), sds((8, 8, 16, 128), BF)],
         [slab, slab, pltpu.VMEM((2, 8, 2, 16, 128), BF), pltpu.VMEM((8, 2, 128, 128), F32)],
         flops=2 * 9 * 2048 * 512 * 256, limit=24,
-    )(coords, parent, near, field, low, high, *inner, down, grads, spread)
-
-
-def input_call(near, field, layer, conv, after, half, base=None):
-    ins, values = [SMEM] + [HBM] * 3 + [ANY], [near, field, layer, conv, after]
+    )(coords, parent, near, field, partner, other, *inner, down, grads, spread)
+
+
+def input_call(near, field, partner, other, conv, after, half, base=None):
+    ins, values = [SMEM] + [HBM] * 4 + [ANY], [near, field, partner, other, conv, after]
     aliases = {}
     if base is not None:
-        ins, values, aliases = ins + [ANY], values + [base], {5: 0}
+        ins, values, aliases = ins + [ANY], values + [base], {6: 0}
     return call(
         functools.partial(input_kernel, half=half), ins, [sds((16, 8, 2, 16, 128), BF), TOKEN],
         [pltpu.VMEM((3, 10, 9, 2, 16, 128), BF), pltpu.VMEM((3, 3, 256, 512), BF),
          pltpu.VMEM((8, 8, 2, 16, 128), BF), pltpu.VMEM((9, 8, 2, 16, 128), BF),
-         pltpu.VMEM((8, 2, 16, 128), BF), pltpu.VMEM((3, 3, 3, 128, 128), BF),
-         pltpu.SemaphoreType.DMA((9,))],
+         pltpu.VMEM((2, 8, 2, 16, 128), BF), pltpu.VMEM((3, 3, 3, 128, 128), BF),
+         pltpu.SemaphoreType.DMA((10,))],
         flops=9 * 2048 * 512 * 256, limit=24, out=ANY, input_output_aliases=aliases,
     )(*values)
 
@@ -406,28 +432,44 @@
     total = got_ref[0].astype(F32)
     for k in range(1, 16):
         total = total + got_ref[k].astype(F32)
-    refs[-1][...] = total
+    refs[-1][...] = total.astype(BF)
 
 
 def add_in_order(own_ref, *refs):
     y = lax.axis_index("dp")
     total_ref, slots_ref = refs[-2:]
     for k, ref in enumerate((own_ref, *refs[:3])):
-        slots_ref[(y - k + 4) % 4] = ref[...]
+        slots_ref[(y - k + 4) % 4] = ref[...].astype(F32)
     total = ((slots_ref[0] + slots_ref[1]) + (slots_ref[2] + slots_ref[3])).astype(BF)
     for k in range(16):
         total_ref[k] = total
 
 
-def finish(own_ref, got_ref, *refs):
-    conv_ref, down_ref = refs[-2:]
+def write_half(rows_ref, *refs, own):
+    conv_ref, down_ref, token_ref, wide_ref, sems = refs[-5:]
+    token_ref[...] = jnp.zeros_like(token_ref)
     core = lax.axis_index("core")
-    mine = pl.ds(pl.multiple_of(64 * core, 64), 64)
-    theirs = pl.ds(pl.multiple_of(64 * (1 - core), 64), 64)
-    conv_ref[:, mine] = own_ref[0:27].astype(F32)
-    conv_ref[:, theirs] = got_ref[0:27].astype(F32)
-    down_ref[:, mine] = own_ref[27:35].astype(F32)
-    down_ref[:, theirs] = got_ref[27:35].astype(F32)
+    here = pl.ds(pl.multiple_of(64 * (core if own else 1 - core), 64), 64)
+    copies = []
+    for k, (start, stop) in enumerate(((0, 9), (9, 18), (18, 27), (27, 35))):
+        wide_ref[start:stop] = rows_ref[start:stop].astype(F32)
+        if start < 27:
+            target = conv_ref.at[start:stop, here]
+        else:
+            target = down_ref.at[:, here]
+        copies.append(pltpu.make_async_copy(wide_ref.at[start:stop], target, sems.at[k]))
+        copies[-1].start()
+    for copy in copies:
+        copy.wait()
+
+
+def write_call(rows, bases=(), own=True):
+    return call(
+        functools.partial(write_half, own=own), [VMEM] + [ANY] * len(bases),
+        [sds((27, 128, 128), F32), sds((8, 128, 128), F32), TOKEN],
+        [pltpu.VMEM((36, 64, 128), F32), pltpu.SemaphoreType.DMA((4,))], out=ANY,
+        input_output_aliases={1: 0, 2: 1} if bases else {},
+    )(rows, *bases)[:2]
 
 
 def over_core(value):
@@ -446,36 +488,33 @@
     return call(kernel, [VMEM] * len(values) + [ANY] * len(after), outs, scratch)(*values, *after)
 
 
-def next_region(value):
-    return lax.ppermute(value, ("z", "x", "core"), [(i, i + 1) for i in range(31)])
-
-
-def previous_region(value):
-    return lax.ppermute(value, ("z", "x", "core"), [(i + 1, i) for i in range(31)])
+def over_other(value):
+    pairs = [(i, i + 1) for i in range(1, 31, 2)] + [(i + 1, i) for i in range(1, 31, 2)]
+    return lax.ppermute(value, ("z", "x", "core"), pairs)
 
 
 def local(features, conv_weight, down_weight, coarse_cotangent, brick_coords, neighbours, parents):
     coords, near, parent = brick_coords.reshape(3), neighbours.reshape(26), parents.reshape(1)
     core = lax.axis_index("core")
     cotangent = coarse_cotangent.reshape(16, 16, 16, 128)
-    theirs = over_core(lax.dynamic_slice_in_dim(cotangent, 8 * (1 - core), 8))
+    half = lax.dynamic_slice_in_dim(cotangent, 8 * (1 - core), 8)
+    theirs = over_core(half)
     field = features.reshape(16, 8, 2, 16, 128)
     far = functools.partial(pltpu.with_memory_space_constraint, memory_space=pltpu.HBM)
-    grads, spread, up, back = grad_call(
-        coords, parent, far(cotangent), theirs, far(down_weight), far(field)
-    )
-    low, high = next_region(up), previous_region(back)
+    mine, down, *layers = prepare_call(far(coords), far(cotangent), far(down_weight), far(field), half)
+    grads, spread, to_partner, to_other = grad_call(far(coords), parent, mine, theirs, down, *layers)
+    partner, other = over_core(to_partner), over_other(to_other)
     inner = inner_call(field, conv_weight)
     kept, sent, keep = main_call(
-        coords, parent, near, field, low, high, inner, down_weight, grads, spread
+        coords, parent, near, field, partner, other, inner, down, grads, spread
     )
 
     got = over_core(sent)
     own = stage(add_halves, (kept, got), [sds((36, 64, 128), BF)])[0]
     gots = over_plane(own.reshape(16, 144, 128))
-    partial_grad, token = input_call(near, grads, low, far(conv_weight), own, 0)
+    partial_grad, token = input_call(near, grads, partner, other, far(conv_weight), own, 0)
     coarse, token = coarse_call(coords, keep, got, token)
-    own = stage(add_sixteen, (gots,), [sds((144, 128), F32)], (token,))[0]
+    own = stage(add_sixteen, (gots,), [sds((144, 128), BF)], (token,))[0]
     gots = [over_y(own, k) for k in (1, 2, 3)]
     shares = stage(
         add_in_order, (own, *gots), [sds((16, 144, 128), BF)],
@@ -483,12 +522,11 @@
     )[0]
 
     own = over_plane(shares).reshape(36, 64, 128)
-    input_grad, token = input_call(near, grads, high, far(conv_weight), shares, 1, partial_grad)
+    input_grad, token = input_call(near, grads, partner, other, far(conv_weight), shares, 1, partial_grad)
     own, token = lax.optimization_barrier((own, token))
     got = over_core(own)
-    conv_grad, down_grad = stage(
-        finish, (own, got), [sds((27, 128, 128), F32), sds((8, 128, 128), F32)], (token,)
-    )
+    halves = write_call(own)
+    conv_grad, down_grad = write_call(got, halves, own=False)
     whole = (1, 1, 16, 16, 16, 128)
     return (
         coarse.reshape(whole),

time: 80.9 us -> 81.9 us (1.012)
  blocking collectives: 0 us -> 12.8 us
  waiting for transfers between devices: 17.3 us -> 9.82 us
  starting transfers between devices: 26.5 us -> 20 us
  Pallas kernels: 33.4 us -> 36.1 us
    all_to_all x0 -> x1, blocking collectives: none -> 12.8 us  [over_plane(): return lax.all_to_all(value, ('z', 'x'), 0, 0, tiled=True)]
    all_to_all x2 -> x1, starting transfers between devices: 12.5 us -> 7.31 us  [over_plane(): return lax.all_to_all(value, ('z', 'x'), 0, 0, tiled=True)]
    pallas_call x1 -> x4, Pallas kernels: 2.51 us -> 6.77 us  [the longest x2 3.28 us: write_call(): call(functools.partial(write_half, own=own), [VMEM] + [ANY] * len(bases),...]
    all_to_all x2 -> x1, waiting for transfers between devices: 7.9 us -> 3.76 us  [over_plane(): return lax.all_to_all(value, ('z', 'x'), 0, 0, tiled=True)]
    ppermute x3 -> x4, waiting for transfers between devices: 4.9 us -> 2.4 us  [over_core(): return lax.ppermute(value, 'core', [(0, 1), (1, 0)])]
    pallas_call x4 -> x3, Pallas kernels: 3.46 us -> 1.11 us  [stage(): call(kernel, [VMEM] * len(values) + [ANY] * len(after), outs, scratch)]
    ppermute x2 -> x1, starting transfers between devices: 5.52 us -> 3.68 us  [over_other(): return lax.ppermute(value, ('z', 'x', 'core'), pairs)]
    ppermute x3 -> x4, starting transfers between devices: 4.68 us -> 5.2 us  [over_core(): return lax.ppermute(value, 'core', [(0, 1), (1, 0)])]
  transfers between devices with their start and end apart: 10 -> 9, of which waited for: 8 -> 4; matrix products, arithmetic and copies ran while one was open for 0% -> 0% of each run, Pallas kernels for 24% -> 29%
where the time goes in v3:
time: 81.9 us; the launch traced here: 81.5 us
  Pallas kernels  36.1 us (44%)
  starting transfers between devices  20 us (24%)
  blocking collectives  12.8 us (16%)
  waiting for transfers between devices  9.82 us (12%)
  between operations  1.64 us (2%)
  local copies, waits for them, and re-layouts  1.11 us (1%)
    pallas_call x2, Pallas kernels, input_call(): call(functools.partial(input_kernel, half=half), ins, [sds((16, 8, 2, 16,...  13 us
    all_to_all x1, blocking collectives, over_plane(): return lax.all_to_all(value, ('z', 'x'), 0, 0, tiled=True)  12.8 us
    pallas_call x1, Pallas kernels, main_call(): call(main_kernel, [SMEM] * 3 + [VMEM] * 9, [sds((36, 64, 128), F32), sds(...  8.25 us
    all_to_all x1, starting transfers between devices, over_plane(): return lax.all_to_all(value, ('z', 'x'), 0, 0, tiled=True)  7.31 us
    pallas_call x1, Pallas kernels, inner_call(): call(inner_kernel, [VMEM] * 2, [sds((3, 16, 9, 2, 16, 128), BF), sds((3,...  5.34 us
    ppermute x4, starting transfers between devices, over_core(): return lax.ppermute(value, 'core', [(0, 1), (1, 0)])  5.2 us
    ppermute x3, starting transfers between devices, over_y(): return lax.ppermute(value, 'dp', [(i, (i + by) % 4) for i in range(4)])  3.84 us
    all_to_all x1, waiting for transfers between devices, over_plane(): return lax.all_to_all(value, ('z', 'x'), 0, 0, tiled=True)  3.76 us
  transfers between devices with their start and end apart: 9, of which 4 were waited for; matrix products, arithmetic and copies ran while one was open for 0% of the time, Pallas kernels for 29%

profile of v3, /device:TPU:1, one launch (start us, length us, event | category | flops | bytes accessed | tf_op | source)
XLA Modules:
  0.0 81.5 jit_solution(9464119210089591273)
XLA Ops:
  0.6 1.1 %dynamic-slice_bitcast_fusion.after_ref = bf16[8,16,16,128]{3,2,1,0:T(8,128)(2,1)S(1)} fusion(bf16[1,1,16,16,16,128]{5,4,3,2,1,0:T(8,128)(2,1)} %param.10, s32[]{:T(128)S(6)} %select_n.3), kind=kLoop, calls=%fused_computation | loop fusion | bytes 1048580 | tf_op jit(solution)/shard_map/dynamic_slice | solution.py:500
  1.7 1.5 %collective-permute-start = (bf16[8,16,16,128]{3,2,1,0:T(8,128)(2,1)S(1)}, bf16[8,16,16,128]{3,2,1,0:T(8,128)(2,1)S(1)}, u32[]{:S(2)}, u32[]{:S(2)}) collective-permute-start(bf16[8,16,16,128]{3,2,1,0:T(8,128)(2,1)S(1)} %dynamic-slice_bitcast_fusion.after_ref), channel_id=1, source_target_pairs={{0,1},{1,0},{2,3},{3,2},{4,5},{5,4},{6,7},{7,6},{8,9},{9,8},{10,11... | collective-permute-start | bytes 1572872 | tf_op jit(solution)/shard_map/ppermute | solution.py:476
  3.9 0.0 copy-start
  3.9 0.0 copy-start.2
  3.9 1.9 %shard_map.102 = (bf16[8,8,16,128]{3,2,1,0:T(8,128)(2,1)S(1)}, bf16[512,256]{1,0:T(8,128)(2,1)S(1)}, bf16[8,2,16,128]{3,2,1,0:T(8,128)(2,1)S(1)}, bf16[8,2,16,128]{3,2,1,0:T(8,128)(2,1)S(1)}) custom-call(s32[3]{0:T(128)} %bitcast.20, bf16[16,16,16,128]{3,2,1,0:T(8,128)(2,1)} %bitcast.27, bf16[2,2,2,128,128]{4,3,2,1,0:T(8,128)(2,1)} %down_hbm.1, ...), custom_call_target="tpu_custom_call" | custom-call | bytes 1048576 | tf_op jit(solution)/shard_map/pallas_call | solution.py:368
  5.8 0.0 collective-permute-done.theirs_ref
  5.8 1.6 %shard_map.103 = (bf16[16,8,2,16,128]{4,3,2,1,0:T(8,128)(2,1)S(1)}, bf16[8,128,256]{2,1,0:T(8,128)(2,1)S(1)}, bf16[2,8,2,16,128]{4,3,2,1,0:T(8,128)(2,1)S(1)}, bf16[2,8,2,16,128]{4,3,2,1,0:T(8,128)(2,1)S(1)}) custom-call(s32[3]{0:T(128)} %bitcast.21, s32[1]{0:T(128)} %bitcast.13.parent_ref, bf16[8,8,16,128]{3,2,1,0:T(8,128)(2,1)S(1)} %get-tuple-element.27.mine_ref, ...), custom_call_target="tpu_custom_call" | custom-call | flops 268435456 | bytes 4194304 | tf_op jit(solution)/shard_map/pallas_call | solution.py:377
  7.4 0.1 collective-permute-start.1
  7.5 0.0 copy-start.1
  7.5 0.0 copy-start.3
  7.5 3.7 %collective-permute-start.2 = (bf16[2,8,2,16,128]{4,3,2,1,0:T(8,128)(2,1)S(1)}, bf16[2,8,2,16,128]{4,3,2,1,0:T(8,128)(2,1)S(1)}, u32[]{:S(2)}, u32[]{:S(2)}) collective-permute-start(bf16[2,8,2,16,128]{4,3,2,1,0:T(8,128)(2,1)S(1)} %get-tuple-element.32), channel_id=1, source_target_pairs={{1,2},{3,4},{5,6},{7,8},{9,10},{11,12},{13,14},{15,16},{17,18},{19... | collective-permute-start | bytes 393224 | tf_op jit(solution)/shard_map/ppermute | solution.py:493
  11.2 0.0 copy-done
  11.2 0.0 copy-done.2
  11.2 5.3 %shard_map.104 = (bf16[3,16,9,2,16,128]{5,4,3,2,1,0:T(8,128)(2,1)S(1)}, bf16[3,3,512,256]{3,2,1,0:T(8,128)(2,1)S(1)}, bf16[16,8,2,16,128]{4,3,2,1,0:T(8,128)(2,1)S(1)}) custom-call(bf16[16,8,2,16,128]{4,3,2,1,0:T(8,128)(2,1)S(1)} %bitcast.18, bf16[3,3,3,128,128]{4,3,2,1,0:T(8,128)(2,1)S(1)} %copy-done.2), custom_call_target="tpu_custom_call" | custom-call | flops 4831838208 | bytes 2097152 | tf_op jit(solution)/shard_map/pallas_call | solution.py:385
  16.6 0.0 collective-permute-done.1.partner_ref.partner_hbm
  16.6 0.0 collective-permute-done.2.other_ref.other_hbm
  16.6 0.0 copy-done.1
  16.6 0.0 copy-done.3
  16.6 8.3 %shard_map.105 = (f32[36,64,128]{2,1,0:T(8,128)S(1)}, bf16[53,64,128]{2,1,0:T(8,128)(2,1)S(1)}, bf16[8,8,16,128]{3,2,1,0:T(8,128)(2,1)S(1)}) custom-call(s32[3]{0:T(128)S(1)} %bitcast.22, s32[1]{0:T(128)} %bitcast.14.parent_ref, s32[26]{0:T(128)S(1)} %bitcast.24, bf16[16,8,2,16,128]{4,3,2,1,0:T(8,128)(2,1)S(1)} %bitcast.19, ...), custom_call_target="tpu_custom_call" | custom-call | flops 4831838208 | bytes 1048576 | tf_op jit(solution)/shard_map/pallas_call | solution.py:394
  24.9 0.1 collective-permute-start.3
  25.0 2.4 %collective-permute-done.3.got_ref = bf16[53,64,128]{2,1,0:T(8,128)(2,1)S(1)} collective-permute-done((bf16[53,64,128]{2,1,0:T(8,128)(2,1)S(1)}, bf16[53,64,128]{2,1,0:T(8,128)(2,1)S(1)}, u32[]{:S(2)}, u32[]{:S(2)}) %collective-permute-start.3) | collective-permute-done | bytes 868384 | tf_op jit(solution)/shard_map/ppermute | solution.py:476
  27.4 0.9 %shard_map.106.refs_0_ = bf16[36,64,128]{2,1,0:T(8,128)(2,1)} custom-call(f32[36,64,128]{2,1,0:T(8,128)S(1)} %get-tuple-element.40.kept_ref, bf16[53,64,128]{2,1,0:T(8,128)(2,1)S(1)} %collective-permute-done.3.got_ref), custom_call_target="tpu_custom_call" | custom-call | bytes 1048576 | tf_op jit(solution)/shard_map/pallas_call | solution.py:488
  28.3 7.3 %all-to-all-start = ((bf16[16,144,128]{2,1,0:T(8,128)(2,1)}), bf16[16,144,128]{2,1,0:T(8,128)(2,1)S(1)}, u32[]{:S(2)}, u32[]{:S(2)}) async-start(bf16[16,144,128]{2,1,0:T(8,128)(2,1)} %bitcast.7), calls=%async_computation | async-start | bytes 1179648 | tf_op jit(solution)/shard_map/all_to_all | solution.py:484
  35.6 6.2 %shard_map.107 = (bf16[16,8,2,16,128]{4,3,2,1,0:T(8,128)(2,1)}, f32[8,128]{1,0:T(8,128)S(1)}) custom-call(s32[26]{0:T(128)S(1)} %bitcast.25, bf16[16,8,2,16,128]{4,3,2,1,0:T(8,128)(2,1)S(1)} %get-tuple-element.36.grads_ref.field_hbm, bf16[2,8,2,16,128]{4,3,2,1,0:T(8,128)(2,1)S(1)} %collective-permute-done.1.partner_ref.partner_hbm, ...), custom_call_target="tpu_custom_call" | custom-call | flops 2415919104 | bytes 1048576 | tf_op jit(solution)/shard_map/pallas_call | solution.py:407
  41.8 1.7 %shard_map.108 = (bf16[16,16,16,128]{3,2,1,0:T(8,128)(2,1)}, f32[8,128]{1,0:T(8,128)S(1)}) custom-call(s32[3]{0:T(128)S(1)} %bitcast.23, bf16[8,8,16,128]{3,2,1,0:T(8,128)(2,1)S(1)} %get-tuple-element.38.keep_ref, bf16[53,64,128]{2,1,0:T(8,128)(2,1)S(1)} %collective-permute-done.3.got_ref, f32[8,128]{1,0:T(8,128)S(1)} %get-tuple-element.41.after_ref), custom_call_target="tpu_custom_call" | custom-call | bytes 1048576 | tf_op jit(solution)/shard_map/pallas_call | solution.py:421
  43.5 3.8 %all-to-all-done.got_ref = bf16[16,144,128]{2,1,0:T(8,128)(2,1)S(1)} async-done(((bf16[16,144,128]{2,1,0:T(8,128)(2,1)}), bf16[16,144,128]{2,1,0:T(8,128)(2,1)S(1)}, u32[]{:S(2)}, u32[]{:S(2)}) %all-to-all-start) | async-done | bytes 589856 | tf_op jit(solution)/shard_map/all_to_all | solution.py:484
  47.2 0.1 shard_map.109.own_ref
  47.3 2.8 %collective-permute-start.6 = (bf16[144,128]{1,0:T(8,128)(2,1)S(1)}, bf16[144,128]{1,0:T(8,128)(2,1)S(1)}, u32[]{:S(2)}, u32[]{:S(2)}) collective-permute-start(bf16[144,128]{1,0:T(8,128)(2,1)S(1)} %shard_map.109.own_ref), channel_id=1, source_target_pairs={{0,96},{32,0},{64,32},{96,64},{1,97},{33,1},{65,33},{97,65},{2,98}... | collective-permute-start | bytes 110600 | tf_op jit(solution)/shard_map/ppermute | solution.py:480
  50.1 0.3 collective-permute-start.5
  50.5 0.7 collective-permute-start.4
  51.2 0.0 collective-permute-done.6.refs_2_
  51.2 3.3 %collective-permute-done.5.refs_1_ = bf16[144,128]{1,0:T(8,128)(2,1)S(1)} collective-permute-done((bf16[144,128]{1,0:T(8,128)(2,1)S(1)}, bf16[144,128]{1,0:T(8,128)(2,1)S(1)}, u32[]{:S(2)}, u32[]{:S(2)}) %collective-permute-start.5) | collective-permute-done | bytes 36896 | tf_op jit(solution)/shard_map/ppermute | solution.py:480
  54.5 0.4 collective-permute-done.4.refs_0_
  54.8 0.1 shard_map.110.refs_0_
  54.9 12.8 %all_to_all.10 = bf16[16,144,128]{2,1,0:T(8,128)(2,1)S(1)} all-to-all(bf16[16,144,128]{2,1,0:T(8,128)(2,1)S(1)} %shard_map.110.refs_0_), channel_id=1, replica_groups=mesh['dp'=4,'z'=4,'x'=4,'core'=2] {'z','x'}, dimensions={0} | all-to-all | bytes 1179648 | tf_op jit(solution)/shard_map/all_to_all | solution.py:484
  67.8 3.5 %collective-permute-start.7 = (bf16[36,64,128]{2,1,0:T(8,128)(2,1)S(1)}, bf16[36,64,128]{2,1,0:T(8,128)(2,1)S(1)}, u32[]{:S(2)}, u32[]{:S(2)}) collective-permute-start(bf16[36,64,128]{2,1,0:T(8,128)(2,1)S(1)} %bitcast.15), channel_id=1, source_target_pairs={{0,1},{1,0},{2,3},{3,2},{4,5},{5,4},{6,7},{7,6},{8,9},{9,8},{10,11... | collective-permute-start | bytes 1769480 | tf_op jit(solution)/shard_map/ppermute | solution.py:476
  71.3 6.8 %shard_map.111 = (bf16[16,8,2,16,128]{4,3,2,1,0:T(8,128)(2,1)}, f32[8,128]{1,0:T(8,128)}) custom-call(s32[26]{0:T(128)S(1)} %bitcast.26, bf16[16,8,2,16,128]{4,3,2,1,0:T(8,128)(2,1)S(1)} %get-tuple-element.36.grads_ref.field_hbm, bf16[2,8,2,16,128]{4,3,2,1,0:T(8,128)(2,1)S(1)} %collective-permute-done.1.partner_ref.partner_hbm, ...), custom_call_target="tpu_custom_call", output_to_operand_aliasing={{0}: (6, {})} | custom-call | flops 2415919104 | bytes 1048576 | tf_op jit(solution)/shard_map/pallas_call | solution.py:407
  78.1 1.6 %shard_map.112 = (f32[27,128,128]{2,1,0:T(8,128)}, f32[8,128,128]{2,1,0:T(8,128)}, f32[8,128]{1,0:T(8,128)}) custom-call(bf16[36,64,128]{2,1,0:T(8,128)(2,1)S(1)} %bitcast.16), custom_call_target="tpu_custom_call" | custom-call | bytes 1048576 | tf_op jit(solution)/shard_map/pallas_call | solution.py:467
  79.7 0.0 collective-permute-done.7.rows_ref
  79.7 1.6 %shard_map.113 = (f32[27,128,128]{2,1,0:T(8,128)}, f32[8,128,128]{2,1,0:T(8,128)}, f32[8,128]{1,0:T(8,128)}) custom-call(bf16[36,64,128]{2,1,0:T(8,128)(2,1)S(1)} %collective-permute-done.7.rows_ref, f32[27,128,128]{2,1,0:T(8,128)} %get-tuple-element.46.refs_0_, f32[8,128,128]{2,1,0:T(8,128)} %get-tuple-element.47.refs_1_), custom_call_target="tpu_custom_call", output_to_operand_aliasing={{0}: (1, {}), {1}: (2, {})} | custom-call | bytes 1048576 | tf_op jit(solution)/shard_map/pallas_call | solution.py:467
Async XLA Ops:
  1.7 4.1 %collective-permute-start = (bf16[8,16,16,128]{3,2,1,0:T(8,128)(2,1)S(1)}, bf16[8,16,16,128]{3,2,1,0:T(8,128)(2,1)S(1)}, u32[]{:S(2)}, u32[]{:S(2)}) collective-permute-start(bf16[8,16,16,128]{3,2,1,0:T(8,128)(2,1)S(1)} %dynamic-slice_bitcast_fusion.after_ref), channel_id=1, source_target_pairs={{0,1},{1,0},{2,3},{3,2},{4,5},{5,4},{6,7},{7,6},{8,9},{9,8},{10,11... | collective-permute-start | bytes 1572872 | tf_op jit(solution)/shard_map/ppermute | solution.py:476
  3.9 7.3 %copy-start = (bf16[1,1,16,16,16,128]{5,4,3,2,1,0:T(8,128)(2,1)S(1)}, bf16[1,1,16,16,16,128]{5,4,3,2,1,0:T(8,128)(2,1)}, u32[]{:S(2)}) copy-start(bf16[1,1,16,16,16,128]{5,4,3,2,1,0:T(8,128)(2,1)} %param.7) | copy-start | bytes 3145732
  3.9 7.3 %copy-start.2 = (bf16[3,3,3,128,128]{4,3,2,1,0:T(8,128)(2,1)S(1)}, bf16[3,3,3,128,128]{4,3,2,1,0:T(8,128)(2,1)}, u32[]{:S(2)}) copy-start(bf16[3,3,3,128,128]{4,3,2,1,0:T(8,128)(2,1)} %conv_hbm.3) | copy-start | bytes 2654212
  7.4 9.2 %collective-permute-start.1 = (bf16[2,8,2,16,128]{4,3,2,1,0:T(8,128)(2,1)S(1)}, bf16[2,8,2,16,128]{4,3,2,1,0:T(8,128)(2,1)S(1)}, u32[]{:S(2)}, u32[]{:S(2)}) collective-permute-start(bf16[2,8,2,16,128]{4,3,2,1,0:T(8,128)(2,1)S(1)} %get-tuple-element.31), channel_id=1, source_target_pairs={{0,1},{1,0},{2,3},{3,2},{4,5},{5,4},{6,7},{7,6},{8,9},{9,8},{10,11... | collective-permute-start | bytes 393224 | tf_op jit(solution)/shard_map/ppermute | solution.py:476
  7.5 9.1 %copy-start.1 = (s32[1,1,3]{2,1,0:T(1,128)S(1)}, s32[1,1,3]{2,1,0:T(1,128)}, u32[]{:S(2)}) copy-start(s32[1,1,3]{2,1,0:T(1,128)} %param.11) | copy-start | bytes 40
  7.5 9.1 %copy-start.3 = (s32[1,1,26]{2,1,0:T(1,128)S(1)}, s32[1,1,26]{2,1,0:T(1,128)}, u32[]{:S(2)}) copy-start(s32[1,1,26]{2,1,0:T(1,128)} %param.12) | copy-start | bytes 316
  7.5 9.1 %collective-permute-start.2 = (bf16[2,8,2,16,128]{4,3,2,1,0:T(8,128)(2,1)S(1)}, bf16[2,8,2,16,128]{4,3,2,1,0:T(8,128)(2,1)S(1)}, u32[]{:S(2)}, u32[]{:S(2)}) collective-permute-start(bf16[2,8,2,16,128]{4,3,2,1,0:T(8,128)(2,1)S(1)} %get-tuple-element.32), channel_id=1, source_target_pairs={{1,2},{3,4},{5,6},{7,8},{9,10},{11,12},{13,14},{15,16},{17,18},{19... | collective-permute-start | bytes 393224 | tf_op jit(solution)/shard_map/ppermute | solution.py:493
  24.9 2.5 %collective-permute-start.3 = (bf16[53,64,128]{2,1,0:T(8,128)(2,1)S(1)}, bf16[53,64,128]{2,1,0:T(8,128)(2,1)S(1)}, u32[]{:S(2)}, u32[]{:S(2)}) collective-permute-start(bf16[53,64,128]{2,1,0:T(8,128)(2,1)S(1)} %get-tuple-element.39), channel_id=1, source_target_pairs={{0,1},{1,0},{2,3},{3,2},{4,5},{5,4},{6,7},{7,6},{8,9},{9,8},{10,11... | collective-permute-start | bytes 2605064 | tf_op jit(solution)/shard_map/ppermute | solution.py:476
  28.3 18.9 %all-to-all-start = ((bf16[16,144,128]{2,1,0:T(8,128)(2,1)}), bf16[16,144,128]{2,1,0:T(8,128)(2,1)S(1)}, u32[]{:S(2)}, u32[]{:S(2)}) async-start(bf16[16,144,128]{2,1,0:T(8,128)(2,1)} %bitcast.7), calls=%async_computation | async-start | bytes 1179648 | tf_op jit(solution)/shard_map/all_to_all | solution.py:484
  47.3 3.9 %collective-permute-start.6 = (bf16[144,128]{1,0:T(8,128)(2,1)S(1)}, bf16[144,128]{1,0:T(8,128)(2,1)S(1)}, u32[]{:S(2)}, u32[]{:S(2)}) collective-permute-start(bf16[144,128]{1,0:T(8,128)(2,1)S(1)} %shard_map.109.own_ref), channel_id=1, source_target_pairs={{0,96},{32,0},{64,32},{96,64},{1,97},{33,1},{65,33},{97,65},{2,98}... | collective-permute-start | bytes 110600 | tf_op jit(solution)/shard_map/ppermute | solution.py:480
  50.1 4.3 %collective-permute-start.5 = (bf16[144,128]{1,0:T(8,128)(2,1)S(1)}, bf16[144,128]{1,0:T(8,128)(2,1)S(1)}, u32[]{:S(2)}, u32[]{:S(2)}) collective-permute-start(bf16[144,128]{1,0:T(8,128)(2,1)S(1)} %shard_map.109.own_ref), channel_id=1, source_target_pairs={{0,64},{32,96},{64,0},{96,32},{1,65},{33,97},{65,1},{97,33},{2,66}... | collective-permute-start | bytes 110600 | tf_op jit(solution)/shard_map/ppermute | solution.py:480
  50.5 4.4 %collective-permute-start.4 = (bf16[144,128]{1,0:T(8,128)(2,1)S(1)}, bf16[144,128]{1,0:T(8,128)(2,1)S(1)}, u32[]{:S(2)}, u32[]{:S(2)}) collective-permute-start(bf16[144,128]{1,0:T(8,128)(2,1)S(1)} %shard_map.109.own_ref), channel_id=1, source_target_pairs={{0,32},{32,64},{64,96},{96,0},{1,33},{33,65},{65,97},{97,1},{2,34}... | collective-permute-start | bytes 110600 | tf_op jit(solution)/shard_map/ppermute | solution.py:480
  67.8 12.0 %collective-permute-start.7 = (bf16[36,64,128]{2,1,0:T(8,128)(2,1)S(1)}, bf16[36,64,128]{2,1,0:T(8,128)(2,1)S(1)}, u32[]{:S(2)}, u32[]{:S(2)}) collective-permute-start(bf16[36,64,128]{2,1,0:T(8,128)(2,1)S(1)} %bitcast.15), channel_id=1, source_target_pairs={{0,1},{1,0},{2,3},{3,2},{4,5},{5,4},{6,7},{7,6},{8,9},{9,8},{10,11... | collective-permute-start | bytes 1769480 | tf_op jit(solution)/shard_map/ppermute | solution.py:476

commit v4 on v3

--- a/solution.py
+++ b/solution.py
@@ -432,17 +432,27 @@
     total = got_ref[0].astype(F32)
     for k in range(1, 16):
         total = total + got_ref[k].astype(F32)
-    refs[-1][...] = total.astype(BF)
+    refs[-1][...] = total
 
 
 def add_in_order(own_ref, *refs):
     y = lax.axis_index("dp")
     total_ref, slots_ref = refs[-2:]
     for k, ref in enumerate((own_ref, *refs[:3])):
-        slots_ref[(y - k + 4) % 4] = ref[...].astype(F32)
+        slots_ref[(y - k + 4) % 4] = ref[...]
     total = ((slots_ref[0] + slots_ref[1]) + (slots_ref[2] + slots_ref[3])).astype(BF)
     for k in range(16):
         total_ref[k] = total
+
+
+def after_call(value, token):
+    def kernel(value_ref, token_ref, same_ref):
+        pass
+
+    return call(
+        kernel, [ANY] * 2, [sds(value.shape, value.dtype)], out=ANY, input_output_aliases={0: 0},
+        moved=1024,
+    )(value, token)[0]
 
 
 def write_half(rows_ref, *refs, own):
@@ -514,7 +524,7 @@
     gots = over_plane(own.reshape(16, 144, 128))
     partial_grad, token = input_call(near, grads, partner, other, far(conv_weight), own, 0)
     coarse, token = coarse_call(coords, keep, got, token)
-    own = stage(add_sixteen, (gots,), [sds((144, 128), BF)], (token,))[0]
+    own = stage(add_sixteen, (gots,), [sds((144, 128), F32)], (token,))[0]
     gots = [over_y(own, k) for k in (1, 2, 3)]
     shares = stage(
         add_in_order, (own, *gots), [sds((16, 144, 128), BF)],
@@ -523,7 +533,7 @@
 
     own = over_plane(shares).reshape(36, 64, 128)
     input_grad, token = input_call(near, grads, partner, other, far(conv_weight), shares, 1, partial_grad)
-    own, token = lax.optimization_barrier((own, token))
+    own = after_call(own, token)
     got = over_core(own)
     halves = write_call(own)
     conv_grad, down_grad = write_call(got, halves, own=False)

time: 81.9 us -> 77.8 us (0.950)
  blocking collectives: 12.8 us -> 0 us
  waiting for transfers between devices: 9.82 us -> 14.6 us
  starting transfers between devices: 20 us -> 23.8 us
    all_to_all x1 -> x0, blocking collectives: 12.8 us -> none  [over_plane(): return lax.all_to_all(value, ('z', 'x'), 0, 0, tiled=True)]
    all_to_all x1 -> x2, starting transfers between devices: 7.31 us -> 11.5 us  [over_plane(): return lax.all_to_all(value, ('z', 'x'), 0, 0, tiled=True)]
    all_to_all x1 -> x2, waiting for transfers between devices: 3.76 us -> 7.71 us  [over_plane(): return lax.all_to_all(value, ('z', 'x'), 0, 0, tiled=True)]
  transfers between devices with their start and end apart: 9 -> 10, of which waited for: 4 -> 6; matrix products, arithmetic and copies ran while one was open for 0% -> 0% of each run, Pallas kernels for 29% -> 30%
where the time goes in v4:
time: 77.8 us; the launch traced here: 77.4 us
  Pallas kernels  36.3 us (47%)
  starting transfers between devices  23.8 us (31%)
  waiting for transfers between devices  14.6 us (19%)
  between operations  1.64 us (2%)
  local copies, waits for them, and re-layouts  1.11 us (1%)
    pallas_call x2, Pallas kernels, input_call(): call(functools.partial(input_kernel, half=half), ins, [sds((16, 8, 2, 16,...  12.4 us
    all_to_all x2, starting transfers between devices, over_plane(): return lax.all_to_all(value, ('z', 'x'), 0, 0, tiled=True)  11.5 us
    pallas_call x1, Pallas kernels, main_call(): call(main_kernel, [SMEM] * 3 + [VMEM] * 9, [sds((36, 64, 128), F32), sds(...  8.25 us
    all_to_all x2, waiting for transfers between devices, over_plane(): return lax.all_to_all(value, ('z', 'x'), 0, 0, tiled=True)  7.71 us
    pallas_call x1, Pallas kernels, inner_call(): call(inner_kernel, [VMEM] * 2, [sds((3, 16, 9, 2, 16, 128), BF), sds((3,...  5.34 us
    ppermute x4, starting transfers between devices, over_core(): return lax.ppermute(value, 'core', [(0, 1), (1, 0)])  4.76 us
    ppermute x3, waiting for transfers between devices, over_y(): return lax.ppermute(value, 'dp', [(i, (i + by) % 4) for i in range(4)])  4.46 us
    ppermute x3, starting transfers between devices, over_y(): return lax.ppermute(value, 'dp', [(i, (i + by) % 4) for i in range(4)])  3.84 us
  transfers between devices with their start and end apart: 10, of which 6 were waited for; matrix products, arithmetic and copies ran while one was open for 0% of the time, Pallas kernels for 30%

profile of v4, /device:TPU:1, one launch (start us, length us, event | category | flops | bytes accessed | tf_op | source)
XLA Modules:
  0.0 77.4 jit_solution(4985751976942160937)
XLA Ops:
  0.6 1.1 %dynamic-slice_bitcast_fusion.after_ref = bf16[8,16,16,128]{3,2,1,0:T(8,128)(2,1)S(1)} fusion(bf16[1,1,16,16,16,128]{5,4,3,2,1,0:T(8,128)(2,1)} %param.10, s32[]{:T(128)S(6)} %select_n.3), kind=kLoop, calls=%fused_computation | loop fusion | bytes 1048580 | tf_op jit(solution)/shard_map/dynamic_slice | solution.py:510
  1.7 1.5 %collective-permute-start = (bf16[8,16,16,128]{3,2,1,0:T(8,128)(2,1)S(1)}, bf16[8,16,16,128]{3,2,1,0:T(8,128)(2,1)S(1)}, u32[]{:S(2)}, u32[]{:S(2)}) collective-permute-start(bf16[8,16,16,128]{3,2,1,0:T(8,128)(2,1)S(1)} %dynamic-slice_bitcast_fusion.after_ref), channel_id=1, source_target_pairs={{0,1},{1,0},{2,3},{3,2},{4,5},{5,4},{6,7},{7,6},{8,9},{9,8},{10,11... | collective-permute-start | bytes 1572872 | tf_op jit(solution)/shard_map/ppermute | solution.py:486
  3.9 0.0 copy-start
  3.9 0.0 copy-start.2
  3.9 1.9 %shard_map.102 = (bf16[8,8,16,128]{3,2,1,0:T(8,128)(2,1)S(1)}, bf16[512,256]{1,0:T(8,128)(2,1)S(1)}, bf16[8,2,16,128]{3,2,1,0:T(8,128)(2,1)S(1)}, bf16[8,2,16,128]{3,2,1,0:T(8,128)(2,1)S(1)}) custom-call(s32[3]{0:T(128)} %bitcast.19, bf16[16,16,16,128]{3,2,1,0:T(8,128)(2,1)} %bitcast.26, bf16[2,2,2,128,128]{4,3,2,1,0:T(8,128)(2,1)} %down_hbm.1, ...), custom_call_target="tpu_custom_call" | custom-call | bytes 1048576 | tf_op jit(solution)/shard_map/pallas_call | solution.py:368
  5.8 0.0 collective-permute-done.theirs_ref
  5.8 1.6 %shard_map.103 = (bf16[16,8,2,16,128]{4,3,2,1,0:T(8,128)(2,1)S(1)}, bf16[8,128,256]{2,1,0:T(8,128)(2,1)S(1)}, bf16[2,8,2,16,128]{4,3,2,1,0:T(8,128)(2,1)S(1)}, bf16[2,8,2,16,128]{4,3,2,1,0:T(8,128)(2,1)S(1)}) custom-call(s32[3]{0:T(128)} %bitcast.20, s32[1]{0:T(128)} %bitcast.13.parent_ref, bf16[8,8,16,128]{3,2,1,0:T(8,128)(2,1)S(1)} %get-tuple-element.28.mine_ref, ...), custom_call_target="tpu_custom_call" | custom-call | flops 268435456 | bytes 4194304 | tf_op jit(solution)/shard_map/pallas_call | solution.py:377
  7.4 0.1 collective-permute-start.1
  7.5 0.0 copy-start.1
  7.5 0.0 copy-start.3
  7.5 3.7 %collective-permute-start.2 = (bf16[2,8,2,16,128]{4,3,2,1,0:T(8,128)(2,1)S(1)}, bf16[2,8,2,16,128]{4,3,2,1,0:T(8,128)(2,1)S(1)}, u32[]{:S(2)}, u32[]{:S(2)}) collective-permute-start(bf16[2,8,2,16,128]{4,3,2,1,0:T(8,128)(2,1)S(1)} %get-tuple-element.33), channel_id=1, source_target_pairs={{1,2},{3,4},{5,6},{7,8},{9,10},{11,12},{13,14},{15,16},{17,18},{19... | collective-permute-start | bytes 393224 | tf_op jit(solution)/shard_map/ppermute | solution.py:503
  11.2 0.0 copy-done
  11.2 0.0 copy-done.2
  11.2 5.3 %shard_map.104 = (bf16[3,16,9,2,16,128]{5,4,3,2,1,0:T(8,128)(2,1)S(1)}, bf16[3,3,512,256]{3,2,1,0:T(8,128)(2,1)S(1)}, bf16[16,8,2,16,128]{4,3,2,1,0:T(8,128)(2,1)S(1)}) custom-call(bf16[16,8,2,16,128]{4,3,2,1,0:T(8,128)(2,1)S(1)} %bitcast.17, bf16[3,3,3,128,128]{4,3,2,1,0:T(8,128)(2,1)S(1)} %copy-done.2), custom_call_target="tpu_custom_call" | custom-call | flops 4831838208 | bytes 2097152 | tf_op jit(solution)/shard_map/pallas_call | solution.py:385
  16.6 0.0 collective-permute-done.1.partner_ref.partner_hbm
  16.6 0.0 collective-permute-done.2.other_ref.other_hbm
  16.6 0.0 copy-done.1
  16.6 0.0 copy-done.3
  16.6 8.3 %shard_map.105 = (f32[36,64,128]{2,1,0:T(8,128)S(1)}, bf16[53,64,128]{2,1,0:T(8,128)(2,1)S(1)}, bf16[8,8,16,128]{3,2,1,0:T(8,128)(2,1)S(1)}) custom-call(s32[3]{0:T(128)S(1)} %bitcast.21, s32[1]{0:T(128)} %bitcast.14.parent_ref, s32[26]{0:T(128)S(1)} %bitcast.23, bf16[16,8,2,16,128]{4,3,2,1,0:T(8,128)(2,1)S(1)} %bitcast.18, ...), custom_call_target="tpu_custom_call" | custom-call | flops 4831838208 | bytes 1048576 | tf_op jit(solution)/shard_map/pallas_call | solution.py:394
  24.9 0.1 collective-permute-start.3
  25.0 2.4 %collective-permute-done.3.got_ref = bf16[53,64,128]{2,1,0:T(8,128)(2,1)S(1)} collective-permute-done((bf16[53,64,128]{2,1,0:T(8,128)(2,1)S(1)}, bf16[53,64,128]{2,1,0:T(8,128)(2,1)S(1)}, u32[]{:S(2)}, u32[]{:S(2)}) %collective-permute-start.3) | collective-permute-done | bytes 868384 | tf_op jit(solution)/shard_map/ppermute | solution.py:486
  27.4 0.9 %shard_map.106.refs_0_ = bf16[36,64,128]{2,1,0:T(8,128)(2,1)} custom-call(f32[36,64,128]{2,1,0:T(8,128)S(1)} %get-tuple-element.41.kept_ref, bf16[53,64,128]{2,1,0:T(8,128)(2,1)S(1)} %collective-permute-done.3.got_ref), custom_call_target="tpu_custom_call" | custom-call | bytes 1048576 | tf_op jit(solution)/shard_map/pallas_call | solution.py:498
  28.3 7.3 %all-to-all-start = ((bf16[16,144,128]{2,1,0:T(8,128)(2,1)}), bf16[16,144,128]{2,1,0:T(8,128)(2,1)S(1)}, u32[]{:S(2)}, u32[]{:S(2)}) async-start(bf16[16,144,128]{2,1,0:T(8,128)(2,1)} %bitcast.7), calls=%async_computation | async-start | bytes 1179648 | tf_op jit(solution)/shard_map/all_to_all | solution.py:494
  35.6 6.2 %shard_map.107 = (bf16[16,8,2,16,128]{4,3,2,1,0:T(8,128)(2,1)}, f32[8,128]{1,0:T(8,128)S(1)}) custom-call(s32[26]{0:T(128)S(1)} %bitcast.24, bf16[16,8,2,16,128]{4,3,2,1,0:T(8,128)(2,1)S(1)} %get-tuple-element.37.grads_ref.field_hbm, bf16[2,8,2,16,128]{4,3,2,1,0:T(8,128)(2,1)S(1)} %collective-permute-done.1.partner_ref.partner_hbm, ...), custom_call_target="tpu_custom_call" | custom-call | flops 2415919104 | bytes 1048576 | tf_op jit(solution)/shard_map/pallas_call | solution.py:407
  41.8 1.7 %shard_map.108 = (bf16[16,16,16,128]{3,2,1,0:T(8,128)(2,1)}, f32[8,128]{1,0:T(8,128)S(1)}) custom-call(s32[3]{0:T(128)S(1)} %bitcast.22, bf16[8,8,16,128]{3,2,1,0:T(8,128)(2,1)S(1)} %get-tuple-element.39.keep_ref, bf16[53,64,128]{2,1,0:T(8,128)(2,1)S(1)} %collective-permute-done.3.got_ref, f32[8,128]{1,0:T(8,128)S(1)} %get-tuple-element.42.after_ref), custom_call_target="tpu_custom_call" | custom-call | bytes 1048576 | tf_op jit(solution)/shard_map/pallas_call | solution.py:421
  43.5 3.8 %all-to-all-done.got_ref = bf16[16,144,128]{2,1,0:T(8,128)(2,1)S(1)} async-done(((bf16[16,144,128]{2,1,0:T(8,128)(2,1)}), bf16[16,144,128]{2,1,0:T(8,128)(2,1)S(1)}, u32[]{:S(2)}, u32[]{:S(2)}) %all-to-all-start) | async-done | bytes 589856 | tf_op jit(solution)/shard_map/all_to_all | solution.py:494
  47.2 0.1 shard_map.109.own_ref
  47.3 2.8 %collective-permute-start.6 = (f32[144,128]{1,0:T(8,128)S(1)}, f32[144,128]{1,0:T(8,128)S(1)}, u32[]{:S(2)}, u32[]{:S(2)}) collective-permute-start(f32[144,128]{1,0:T(8,128)S(1)} %shard_map.109.own_ref), channel_id=1, source_target_pairs={{0,96},{32,0},{64,32},{96,64},{1,97},{33,1},{65,33},{97,65},{2,98}... | collective-permute-start | bytes 221192 | tf_op jit(solution)/shard_map/ppermute | solution.py:490
  50.1 0.3 collective-permute-start.5
  50.5 0.7 collective-permute-start.4
  51.2 0.4 collective-permute-done.6.refs_2_
  51.5 3.4 %collective-permute-done.5.refs_1_ = f32[144,128]{1,0:T(8,128)S(1)} collective-permute-done((f32[144,128]{1,0:T(8,128)S(1)}, f32[144,128]{1,0:T(8,128)S(1)}, u32[]{:S(2)}, u32[]{:S(2)}) %collective-permute-start.5) | collective-permute-done | bytes 73760 | tf_op jit(solution)/shard_map/ppermute | solution.py:490
  54.9 0.7 collective-permute-done.4.refs_0_
  55.6 0.9 %shard_map.110.refs_0_ = bf16[16,144,128]{2,1,0:T(8,128)(2,1)} custom-call(f32[144,128]{1,0:T(8,128)S(1)} %shard_map.109.own_ref, f32[144,128]{1,0:T(8,128)S(1)} %collective-permute-done.4.refs_0_, f32[144,128]{1,0:T(8,128)S(1)} %collective-permute-done.5.refs_1_, f32[144,128]{1,0:T(8,128)S(1)} %collective-permute-done.6.refs_2_), custom_call_target="tpu_custom_call" | custom-call | bytes 1048576 | tf_op jit(solution)/shard_map/pallas_call | solution.py:498
  56.5 4.2 %all-to-all-start.1 = ((bf16[16,144,128]{2,1,0:T(8,128)(2,1)}), bf16[16,144,128]{2,1,0:T(8,128)(2,1)S(1)}, u32[]{:S(2)}, u32[]{:S(2)}) async-start(bf16[16,144,128]{2,1,0:T(8,128)(2,1)} %shard_map.110.refs_0_), calls=%async_computation.1 | async-start | bytes 1179648 | tf_op jit(solution)/shard_map/all_to_all | solution.py:494
  60.7 6.2 %shard_map.111 = (bf16[16,8,2,16,128]{4,3,2,1,0:T(8,128)(2,1)}, f32[8,128]{1,0:T(8,128)S(1)}) custom-call(s32[26]{0:T(128)S(1)} %bitcast.25, bf16[16,8,2,16,128]{4,3,2,1,0:T(8,128)(2,1)S(1)} %get-tuple-element.37.grads_ref.field_hbm, bf16[2,8,2,16,128]{4,3,2,1,0:T(8,128)(2,1)S(1)} %collective-permute-done.1.partner_ref.partner_hbm, ...), custom_call_target="tpu_custom_call", output_to_operand_aliasing={{0}: (6, {})} | custom-call | flops 2415919104 | bytes 1048576 | tf_op jit(solution)/shard_map/pallas_call | solution.py:407
  66.9 4.0 %all-to-all-done.1 = bf16[16,144,128]{2,1,0:T(8,128)(2,1)S(1)} async-done(((bf16[16,144,128]{2,1,0:T(8,128)(2,1)}), bf16[16,144,128]{2,1,0:T(8,128)(2,1)S(1)}, u32[]{:S(2)}, u32[]{:S(2)}) %all-to-all-start.1) | async-done | bytes 589856 | tf_op jit(solution)/shard_map/all_to_all | solution.py:494
  70.8 3.1 %collective-permute-start.7 = (bf16[36,64,128]{2,1,0:T(8,128)(2,1)S(1)}, bf16[36,64,128]{2,1,0:T(8,128)(2,1)S(1)}, u32[]{:S(2)}, u32[]{:S(2)}) collective-permute-start(bf16[36,64,128]{2,1,0:T(8,128)(2,1)S(1)} %shard_map.112.rows_ref), channel_id=1, source_target_pairs={{0,1},{1,0},{2,3},{3,2},{4,5},{5,4},{6,7},{7,6},{8,9},{9,8},{10,11... | collective-permute-start | bytes 1769480 | tf_op jit(solution)/shard_map/ppermute | solution.py:486
  73.9 1.6 %shard_map.113 = (f32[27,128,128]{2,1,0:T(8,128)}, f32[8,128,128]{2,1,0:T(8,128)}, f32[8,128]{1,0:T(8,128)}) custom-call(bf16[36,64,128]{2,1,0:T(8,128)(2,1)S(1)} %shard_map.112.rows_ref), custom_call_target="tpu_custom_call" | custom-call | bytes 1048576 | tf_op jit(solution)/shard_map/pallas_call | solution.py:477
  75.6 0.0 collective-permute-done.7.rows_ref
  75.6 1.6 %shard_map.114 = (f32[27,128,128]{2,1,0:T(8,128)}, f32[8,128,128]{2,1,0:T(8,128)}, f32[8,128]{1,0:T(8,128)}) custom-call(bf16[36,64,128]{2,1,0:T(8,128)(2,1)S(1)} %collective-permute-done.7.rows_ref, f32[27,128,128]{2,1,0:T(8,128)} %get-tuple-element.48.refs_0_, f32[8,128,128]{2,1,0:T(8,128)} %get-tuple-element.49.refs_1_), custom_call_target="tpu_custom_call", output_to_operand_aliasing={{0}: (1, {}), {1}: (2, {})} | custom-call | bytes 1048576 | tf_op jit(solution)/shard_map/pallas_call | solution.py:477
  (1 shorter events, 0.0 us)
Async XLA Ops:
  1.7 4.1 %collective-permute-start = (bf16[8,16,16,128]{3,2,1,0:T(8,128)(2,1)S(1)}, bf16[8,16,16,128]{3,2,1,0:T(8,128)(2,1)S(1)}, u32[]{:S(2)}, u32[]{:S(2)}) collective-permute-start(bf16[8,16,16,128]{3,2,1,0:T(8,128)(2,1)S(1)} %dynamic-slice_bitcast_fusion.after_ref), channel_id=1, source_target_pairs={{0,1},{1,0},{2,3},{3,2},{4,5},{5,4},{6,7},{7,6},{8,9},{9,8},{10,11... | collective-permute-start | bytes 1572872 | tf_op jit(solution)/shard_map/ppermute | solution.py:486
  3.9 7.3 %copy-start = (bf16[1,1,16,16,16,128]{5,4,3,2,1,0:T(8,128)(2,1)S(1)}, bf16[1,1,16,16,16,128]{5,4,3,2,1,0:T(8,128)(2,1)}, u32[]{:S(2)}) copy-start(bf16[1,1,16,16,16,128]{5,4,3,2,1,0:T(8,128)(2,1)} %param.7) | copy-start | bytes 3145732
  3.9 7.3 %copy-start.2 = (bf16[3,3,3,128,128]{4,3,2,1,0:T(8,128)(2,1)S(1)}, bf16[3,3,3,128,128]{4,3,2,1,0:T(8,128)(2,1)}, u32[]{:S(2)}) copy-start(bf16[3,3,3,128,128]{4,3,2,1,0:T(8,128)(2,1)} %conv_hbm.3) | copy-start | bytes 2654212
  7.4 9.2 %collective-permute-start.1 = (bf16[2,8,2,16,128]{4,3,2,1,0:T(8,128)(2,1)S(1)}, bf16[2,8,2,16,128]{4,3,2,1,0:T(8,128)(2,1)S(1)}, u32[]{:S(2)}, u32[]{:S(2)}) collective-permute-start(bf16[2,8,2,16,128]{4,3,2,1,0:T(8,128)(2,1)S(1)} %get-tuple-element.32), channel_id=1, source_target_pairs={{0,1},{1,0},{2,3},{3,2},{4,5},{5,4},{6,7},{7,6},{8,9},{9,8},{10,11... | collective-permute-start | bytes 393224 | tf_op jit(solution)/shard_map/ppermute | solution.py:486
  7.5 9.1 %copy-start.1 = (s32[1,1,3]{2,1,0:T(1,128)S(1)}, s32[1,1,3]{2,1,0:T(1,128)}, u32[]{:S(2)}) copy-start(s32[1,1,3]{2,1,0:T(1,128)} %param.11) | copy-start | bytes 40
  7.5 9.1 %copy-start.3 = (s32[1,1,26]{2,1,0:T(1,128)S(1)}, s32[1,1,26]{2,1,0:T(1,128)}, u32[]{:S(2)}) copy-start(s32[1,1,26]{2,1,0:T(1,128)} %param.12) | copy-start | bytes 316
  7.5 9.1 %collective-permute-start.2 = (bf16[2,8,2,16,128]{4,3,2,1,0:T(8,128)(2,1)S(1)}, bf16[2,8,2,16,128]{4,3,2,1,0:T(8,128)(2,1)S(1)}, u32[]{:S(2)}, u32[]{:S(2)}) collective-permute-start(bf16[2,8,2,16,128]{4,3,2,1,0:T(8,128)(2,1)S(1)} %get-tuple-element.33), channel_id=1, source_target_pairs={{1,2},{3,4},{5,6},{7,8},{9,10},{11,12},{13,14},{15,16},{17,18},{19... | collective-permute-start | bytes 393224 | tf_op jit(solution)/shard_map/ppermute | solution.py:503
  24.9 2.5 %collective-permute-start.3 = (bf16[53,64,128]{2,1,0:T(8,128)(2,1)S(1)}, bf16[53,64,128]{2,1,0:T(8,128)(2,1)S(1)}, u32[]{:S(2)}, u32[]{:S(2)}) collective-permute-start(bf16[53,64,128]{2,1,0:T(8,128)(2,1)S(1)} %get-tuple-element.40), channel_id=1, source_target_pairs={{0,1},{1,0},{2,3},{3,2},{4,5},{5,4},{6,7},{7,6},{8,9},{9,8},{10,11... | collective-permute-start | bytes 2605064 | tf_op jit(solution)/shard_map/ppermute | solution.py:486
  28.3 18.9 %all-to-all-start = ((bf16[16,144,128]{2,1,0:T(8,128)(2,1)}), bf16[16,144,128]{2,1,0:T(8,128)(2,1)S(1)}, u32[]{:S(2)}, u32[]{:S(2)}) async-start(bf16[16,144,128]{2,1,0:T(8,128)(2,1)} %bitcast.7), calls=%async_computation | async-start | bytes 1179648 | tf_op jit(solution)/shard_map/all_to_all | solution.py:494
  47.3 4.2 %collective-permute-start.6 = (f32[144,128]{1,0:T(8,128)S(1)}, f32[144,128]{1,0:T(8,128)S(1)}, u32[]{:S(2)}, u32[]{:S(2)}) collective-permute-start(f32[144,128]{1,0:T(8,128)S(1)} %shard_map.109.own_ref), channel_id=1, source_target_pairs={{0,96},{32,0},{64,32},{96,64},{1,97},{33,1},{65,33},{97,65},{2,98}... | collective-permute-start | bytes 221192 | tf_op jit(solution)/shard_map/ppermute | solution.py:490
  50.1 4.8 %collective-permute-start.5 = (f32[144,128]{1,0:T(8,128)S(1)}, f32[144,128]{1,0:T(8,128)S(1)}, u32[]{:S(2)}, u32[]{:S(2)}) collective-permute-start(f32[144,128]{1,0:T(8,128)S(1)} %shard_map.109.own_ref), channel_id=1, source_target_pairs={{0,64},{32,96},{64,0},{96,32},{1,65},{33,97},{65,1},{97,33},{2,66}... | collective-permute-start | bytes 221192 | tf_op jit(solution)/shard_map/ppermute | solution.py:490
  50.5 5.1 %collective-permute-start.4 = (f32[144,128]{1,0:T(8,128)S(1)}, f32[144,128]{1,0:T(8,128)S(1)}, u32[]{:S(2)}, u32[]{:S(2)}) collective-permute-start(f32[144,128]{1,0:T(8,128)S(1)} %shard_map.109.own_ref), channel_id=1, source_target_pairs={{0,32},{32,64},{64,96},{96,0},{1,33},{33,65},{65,97},{97,1},{2,34}... | collective-permute-start | bytes 221192 | tf_op jit(solution)/shard_map/ppermute | solution.py:490
  56.5 14.3 %all-to-all-start.1 = ((bf16[16,144,128]{2,1,0:T(8,128)(2,1)}), bf16[16,144,128]{2,1,0:T(8,128)(2,1)S(1)}, u32[]{:S(2)}, u32[]{:S(2)}) async-start(bf16[16,144,128]{2,1,0:T(8,128)(2,1)} %shard_map.110.refs_0_), calls=%async_computation.1 | async-start | bytes 1179648 | tf_op jit(solution)/shard_map/all_to_all | solution.py:494
  70.8 4.7 %collective-permute-start.7 = (bf16[36,64,128]{2,1,0:T(8,128)(2,1)S(1)}, bf16[36,64,128]{2,1,0:T(8,128)(2,1)S(1)}, u32[]{:S(2)}, u32[]{:S(2)}) collective-permute-start(bf16[36,64,128]{2,1,0:T(8,128)(2,1)S(1)} %shard_map.112.rows_ref), channel_id=1, source_target_pairs={{0,1},{1,0},{2,3},{3,2},{4,5},{5,4},{6,7},{7,6},{8,9},{9,8},{10,11... | collective-permute-start | bytes 1769480 | tf_op jit(solution)/shard_map/ppermute | solution.py:486

commit v5 on v4

--- a/solution.py
+++ b/solution.py
@@ -25,8 +25,7 @@
 def lay_interior(field_ref, shifts_ref, start=0, stop=16, base=1):
     z = z_index(256)
 
-    @pl.loop(start, stop)
-    def _(x):
+    for x in range(start, stop):
         plain = field_ref[x].reshape(256, 128)
         wide = plain.astype(F32)
         lower = jnp.where(z == 0, 0.0, pltpu.roll(wide, 1, 0)).astype(BF)
@@ -77,37 +76,36 @@
     )
 
 
-def joined_down(down_ref):
-    return jnp.concatenate(
-        [
-            jnp.concatenate([down_ref[p, q, r] for r in range(2)], axis=1)
-            for p in range(2)
-            for q in range(2)
-        ],
-        axis=0,
-    )
-
-
 def prepare_kernel(
-    coords_ref, cotangent_hbm, down_hbm, field_hbm, after_ref,
-    mine_ref, down_ref, partner_ref, other_ref, held_ref, sems,
+    cotangent_hbm, down_hbm, field_hbm, after_ref,
+    mine_ref, down_ref, partner_ref, other_ref, sems,
 ):
-    x, oy = coords_ref[0], coords_ref[1] % 2
-    upper = x % 2
+    upper = lax.axis_index("core")
     copies = [
-        pltpu.make_async_copy(
-            cotangent_hbm.at[pl.ds(8 * upper, 8), pl.ds(8 * oy, 8)], mine_ref, sems.at[0]
-        ),
-        pltpu.make_async_copy(down_hbm, held_ref, sems.at[1]),
-        pltpu.make_async_copy(field_hbm.at[15 - 15 * upper], partner_ref, sems.at[2]),
-        pltpu.make_async_copy(field_hbm.at[15 * upper], other_ref, sems.at[3]),
+        pltpu.make_async_copy(field_hbm.at[15 - 15 * upper], partner_ref, sems.at[0]),
+        pltpu.make_async_copy(field_hbm.at[15 * upper], other_ref, sems.at[1]),
     ]
+    for k in range(4):
+        copies.append(
+            pltpu.make_async_copy(
+                cotangent_hbm.at[pl.ds(8 * upper + 2 * k, 2)], mine_ref.at[2 * k : 2 * k + 2],
+                sems.at[2 + k],
+            )
+        )
+    for p in range(2):
+        for q in range(2):
+            for r in range(2):
+                at = 2 * p + q
+                rows, columns = slice(128 * at, 128 * at + 128), slice(128 * r, 128 * r + 128)
+                copies.append(
+                    pltpu.make_async_copy(
+                        down_hbm.at[p, q, r], down_ref.at[rows, columns], sems.at[6 + 2 * at + r]
+                    )
+                )
     for copy in copies:
         copy.start()
-    copies[1].wait()
-    down_ref[...] = joined_down(held_ref)
-    for k in (0, 2, 3):
-        copies[k].wait()
+    for copy in copies:
+        copy.wait()
 
 
 def grad_kernel(
@@ -121,7 +119,7 @@
     to_other_ref[0] = other_ref[...]
     wide_ref[...] = jnp.zeros_like(wide_ref)
     for i in range(8):
-        mine = mine_ref[i].astype(F32)
+        mine = mine_ref[i, pl.ds(8 * oy, 8)].astype(F32)
         theirs = theirs_ref[i, pl.ds(8 * oy, 8)].astype(F32)
         both = jnp.where(is_own, mine, theirs)
         part = jnp.where(oz == 0, both[:, 0:8], both[:, 8:16]).reshape(64, 128)
@@ -153,9 +151,10 @@
 
 
 def inner_kernel(field_ref, conv_ref, shifts_ref, weights_ref, outputs_ref):
-    lay_interior(field_ref, shifts_ref, 0, 16, 0)
     lay_weights(conv_ref, weights_ref)
-    for first, count in ((1, 7), (8, 7)):
+    lay_interior(field_ref, shifts_ref, 0, 6, 0)
+    for first, count in ((1, 4), (5, 4), (9, 4), (13, 2)):
+        lay_interior(field_ref, shifts_ref, min(first + 5, 16), min(first + 9, 16), 0)
         acc = None
         for a in range(3):
             for c in range(3):
@@ -261,37 +260,29 @@
                 )
 
 
-def input_kernel(near_ref, field_hbm, partner_hbm, other_hbm, conv_hbm, *refs, half, tile=4):
-    (result_ref, token_ref, shifts_ref, weights_ref, held_ref, field_ref, layer_ref, conv_ref,
-     sems) = refs[-9:]
+def input_kernel(near_ref, field_ref, partner_ref, other_ref, conv_hbm, *refs, half, tile=4):
+    result_ref, token_ref, shifts_ref, weights_ref, held_ref, conv_ref, sems = refs[-7:]
     token_ref[...] = jnp.zeros_like(token_ref)
-    first_layer = 7 * half
-    fetches = [
-        pltpu.make_async_copy(
-            field_hbm.at[pl.ds(first_layer + 3 * k, 3)], field_ref.at[pl.ds(3 * k, 3)], sems.at[2 + k]
+    conv_copies = [
+        pltpu.make_async_copy(conv_hbm.at[a], conv_ref.at[a], sems.at[2 + a]) for a in range(3)
+    ]
+    for copy in conv_copies:
+        copy.start()
+    lay = functools.partial(lay_interior, field_ref, shifts_ref, base=1 - 8 * half)
+    if half == 0:
+        lay(0, 5)
+    else:
+        lay(7, 13)
+    layer = jnp.where(
+        lax.axis_index("core") == half, other_ref[1].astype(F32), partner_ref[1].astype(F32)
+    )
+    def lay_edge():
+        lay_slab(
+            layer.reshape(16, 16, 128), near_flag(near_ref, 17 * half), shifts_ref.at[:, 9 * half]
         )
-        for k in range(3)
-    ]
-    layer_copies = [
-        pltpu.make_async_copy(partner_hbm.at[1], layer_ref.at[0], sems.at[5]),
-        pltpu.make_async_copy(other_hbm.at[1], layer_ref.at[1], sems.at[9]),
-    ]
-    conv_copies = [
-        pltpu.make_async_copy(conv_hbm.at[a], conv_ref.at[a], sems.at[6 + a]) for a in range(3)
-    ]
-    for copy in (*fetches, *layer_copies, *conv_copies):
-        copy.start()
-    for k in range(3):
-        fetches[k].wait()
-        lay_interior(field_ref, shifts_ref, 3 * k, 3 * k + 3, 1 - half)
-    for copy in layer_copies:
-        copy.wait()
-    layer = jnp.where(
-        lax.axis_index("core") == half, layer_ref[1].astype(F32), layer_ref[0].astype(F32)
-    )
-    lay_slab(
-        layer.reshape(16, 16, 128), near_flag(near_ref, 17 * half), shifts_ref.at[:, 9 * half]
-    )
+
+    if half == 0:
+        lay_edge()
     zero = jnp.zeros((128, 128), BF)
     for a in (2, 1, 0):
         conv_copies[2 - a].wait()
@@ -304,6 +295,11 @@
     copies = []
     for step in range(8 // tile):
         first = step * tile
+        if step == 1 and half == 0:
+            lay(5, 9)
+        if step == 1 and half == 1:
+            lay(13, 16)
+            lay_edge()
         acc = None
         for a in range(3):
             for c in range(3):
@@ -311,7 +307,7 @@
                 acc = part if acc is None else acc + part
         here = 8 * half + first
         for s in range(2):
-            field = field_ref[first + half : first + half + tile, :, s].astype(F32)
+            field = field_ref[here : here + tile, :, s].astype(F32)
             held_ref[first : first + tile, :, s] = (
                 acc[:, s * 128 : s * 128 + 128].reshape(tile, 8, 16, 128) + field
             ).astype(BF)
@@ -363,13 +359,13 @@
     )
 
 
-def prepare_call(coords, cotangent, down, field, after):
+def prepare_call(cotangent, down, field, after):
     layer = sds((8, 2, 16, 128), BF)
     return call(
-        prepare_kernel, [SMEM] + [HBM] * 3 + [ANY],
-        [sds((8, 8, 16, 128), BF), sds((512, 256), BF), layer, layer],
-        [pltpu.VMEM((2, 2, 2, 128, 128), BF), pltpu.SemaphoreType.DMA((4,))], moved=1 << 20,
-    )(coords, cotangent, down, field, after)
+        prepare_kernel, [HBM] * 3 + [ANY],
+        [sds((8, 16, 16, 128), BF), sds((512, 256), BF), layer, layer],
+        [pltpu.SemaphoreType.DMA((14,))], moved=1 << 20,
+    )(cotangent, down, field, after)
 
 
 def grad_call(coords, parent, mine, theirs, down, partner, other):
@@ -400,16 +396,15 @@
 
 
 def input_call(near, field, partner, other, conv, after, half, base=None):
-    ins, values = [SMEM] + [HBM] * 4 + [ANY], [near, field, partner, other, conv, after]
+    ins, values = [SMEM] + [VMEM] * 3 + [HBM, ANY], [near, field, partner, other, conv, after]
     aliases = {}
     if base is not None:
         ins, values, aliases = ins + [ANY], values + [base], {6: 0}
     return call(
         functools.partial(input_kernel, half=half), ins, [sds((16, 8, 2, 16, 128), BF), TOKEN],
         [pltpu.VMEM((3, 10, 9, 2, 16, 128), BF), pltpu.VMEM((3, 3, 256, 512), BF),
-         pltpu.VMEM((8, 8, 2, 16, 128), BF), pltpu.VMEM((9, 8, 2, 16, 128), BF),
-         pltpu.VMEM((2, 8, 2, 16, 128), BF), pltpu.VMEM((3, 3, 3, 128, 128), BF),
-         pltpu.SemaphoreType.DMA((10,))],
+         pltpu.VMEM((8, 8, 2, 16, 128), BF), pltpu.VMEM((3, 3, 3, 128, 128), BF),
+         pltpu.SemaphoreType.DMA((5,))],
         flops=9 * 2048 * 512 * 256, limit=24, out=ANY, input_output_aliases=aliases,
     )(*values)
 
@@ -511,7 +506,7 @@
     theirs = over_core(half)
     field = features.reshape(16, 8, 2, 16, 128)
     far = functools.partial(pltpu.with_memory_space_constraint, memory_space=pltpu.HBM)
-    mine, down, *layers = prepare_call(far(coords), far(cotangent), far(down_weight), far(field), half)
+    mine, down, *layers = prepare_call(far(cotangent), far(down_weight), far(field), half)
     grads, spread, to_partner, to_other = grad_call(far(coords), parent, mine, theirs, down, *layers)
     partner, other = over_core(to_partner), over_other(to_other)
     inner = inner_call(field, conv_weight)
@@ -523,11 +518,11 @@
     own = stage(add_halves, (kept, got), [sds((36, 64, 128), BF)])[0]
     gots = over_plane(own.reshape(16, 144, 128))
     partial_grad, token = input_call(near, grads, partner, other, far(conv_weight), own, 0)
-    coarse, token = coarse_call(coords, keep, got, token)
     own = stage(add_sixteen, (gots,), [sds((144, 128), F32)], (token,))[0]
     gots = [over_y(own, k) for k in (1, 2, 3)]
+    coarse, token = coarse_call(coords, keep, got, own)
     shares = stage(
-        add_in_order, (own, *gots), [sds((16, 144, 128), BF)],
+        add_in_order, (own, *gots), [sds((16, 144, 128), BF)], (token,),
         scratch=[pltpu.VMEM((4, 144, 128), F32)],
     )[0]
 

time: 77.8 us -> 76.8 us (0.987)
  Pallas kernels: 36.3 us -> 33.4 us
  waiting for transfers between devices: 14.6 us -> 16.5 us
    all_to_all x2, waiting for transfers between devices: 7.71 us -> 11.3 us  [over_plane(): return lax.all_to_all(value, ('z', 'x'), 0, 0, tiled=True)]
    pallas_call x2, Pallas kernels: 12.4 us -> 10.5 us  [input_call(): call(functools.partial(input_kernel, half=half), ins, [sds((16, 8, 2, 16,...]
    ppermute x3, waiting for transfers between devices: 4.46 us -> 2.79 us  [over_y(): return lax.ppermute(value, 'dp', [(i, (i + by) % 4) for i in range(4)])]
  transfers between devices with their start and end apart: 10 -> 10, of which waited for: 6 -> 5; matrix products, arithmetic and copies ran while one was open for 0% -> 0% of each run, Pallas kernels for 30% -> 26%
where the time goes in v5:
time: 76.8 us; the launch traced here: 76.3 us
  Pallas kernels  33.4 us (43%)
  starting transfers between devices  23.8 us (31%)
  waiting for transfers between devices  16.5 us (21%)
  between operations  1.65 us (2%)
  local copies, waits for them, and re-layouts  1.11 us (1%)
    all_to_all x2, starting transfers between devices, over_plane(): return lax.all_to_all(value, ('z', 'x'), 0, 0, tiled=True)  11.5 us
    all_to_all x2, waiting for transfers between devices, over_plane(): return lax.all_to_all(value, ('z', 'x'), 0, 0, tiled=True)  11.3 us
    pallas_call x2, Pallas kernels, input_call(): call(functools.partial(input_kernel, half=half), ins, [sds((16, 8, 2, 16,...  10.5 us
    pallas_call x1, Pallas kernels, main_call(): call(main_kernel, [SMEM] * 3 + [VMEM] * 9, [sds((36, 64, 128), F32), sds(...  8.25 us
    ppermute x4, starting transfers between devices, over_core(): return lax.ppermute(value, 'core', [(0, 1), (1, 0)])  4.78 us
    pallas_call x1, Pallas kernels, inner_call(): call(inner_kernel, [VMEM] * 2, [sds((3, 16, 9, 2, 16, 128), BF), sds((3,...  4.77 us
    ppermute x3, starting transfers between devices, over_y(): return lax.ppermute(value, 'dp', [(i, (i + by) % 4) for i in range(4)])  3.84 us
    ppermute x1, starting transfers between devices, over_other(): return lax.ppermute(value, ('z', 'x', 'core'), pairs)  3.69 us
  transfers between devices with their start and end apart: 10, of which 5 were waited for; matrix products, arithmetic and copies ran while one was open for 0% of the time, Pallas kernels for 26%

profile of v5, /device:TPU:1, one launch (start us, length us, event | category | flops | bytes accessed | tf_op | source)
XLA Modules:
  0.0 76.3 jit_solution(8553999700483911987)
XLA Ops:
  0.6 1.1 %dynamic-slice_bitcast_fusion.after_ref = bf16[8,16,16,128]{3,2,1,0:T(8,128)(2,1)S(1)} fusion(bf16[1,1,16,16,16,128]{5,4,3,2,1,0:T(8,128)(2,1)} %param.10, s32[]{:T(128)S(6)} %select_n.3), kind=kLoop, calls=%fused_computation | loop fusion | bytes 1048580 | tf_op jit(solution)/shard_map/dynamic_slice | solution.py:505
  1.7 1.5 %collective-permute-start = (bf16[8,16,16,128]{3,2,1,0:T(8,128)(2,1)S(1)}, bf16[8,16,16,128]{3,2,1,0:T(8,128)(2,1)S(1)}, u32[]{:S(2)}, u32[]{:S(2)}) collective-permute-start(bf16[8,16,16,128]{3,2,1,0:T(8,128)(2,1)S(1)} %dynamic-slice_bitcast_fusion.after_ref), channel_id=1, source_target_pairs={{0,1},{1,0},{2,3},{3,2},{4,5},{5,4},{6,7},{7,6},{8,9},{9,8},{10,11... | collective-permute-start | bytes 1572872 | tf_op jit(solution)/shard_map/ppermute | solution.py:481
  3.9 0.0 copy-start
  3.9 0.0 copy-start.2
  3.9 1.4 %shard_map.102 = (bf16[8,16,16,128]{3,2,1,0:T(8,128)(2,1)S(1)}, bf16[512,256]{1,0:T(8,128)(2,1)S(1)}, bf16[8,2,16,128]{3,2,1,0:T(8,128)(2,1)S(1)}, bf16[8,2,16,128]{3,2,1,0:T(8,128)(2,1)S(1)}) custom-call(bf16[16,16,16,128]{3,2,1,0:T(8,128)(2,1)} %bitcast.25, bf16[2,2,2,128,128]{4,3,2,1,0:T(8,128)(2,1)} %down_hbm.1, bf16[16,8,2,16,128]{4,3,2,1,0:T(8,128)(2,1)} %bitcast.16, ...), custom_call_target="tpu_custom_call" | custom-call | bytes 1048576 | tf_op jit(solution)/shard_map/pallas_call | solution.py:364
  5.3 0.0 collective-permute-done.theirs_ref
  5.4 1.6 %shard_map.103 = (bf16[16,8,2,16,128]{4,3,2,1,0:T(8,128)(2,1)S(1)}, bf16[8,128,256]{2,1,0:T(8,128)(2,1)S(1)}, bf16[2,8,2,16,128]{4,3,2,1,0:T(8,128)(2,1)S(1)}, bf16[2,8,2,16,128]{4,3,2,1,0:T(8,128)(2,1)S(1)}) custom-call(s32[3]{0:T(128)} %bitcast.19, s32[1]{0:T(128)} %bitcast.13.parent_ref, bf16[8,16,16,128]{3,2,1,0:T(8,128)(2,1)S(1)} %get-tuple-element.28.mine_ref, ...), custom_call_target="tpu_custom_call" | custom-call | flops 268435456 | bytes 4194304 | tf_op jit(solution)/shard_map/pallas_call | solution.py:373
  6.9 0.1 collective-permute-start.1
  7.0 0.0 copy-start.1
  7.0 0.0 copy-start.3
  7.0 3.7 %collective-permute-start.2 = (bf16[2,8,2,16,128]{4,3,2,1,0:T(8,128)(2,1)S(1)}, bf16[2,8,2,16,128]{4,3,2,1,0:T(8,128)(2,1)S(1)}, u32[]{:S(2)}, u32[]{:S(2)}) collective-permute-start(bf16[2,8,2,16,128]{4,3,2,1,0:T(8,128)(2,1)S(1)} %get-tuple-element.33), channel_id=1, source_target_pairs={{1,2},{3,4},{5,6},{7,8},{9,10},{11,12},{13,14},{15,16},{17,18},{19... | collective-permute-start | bytes 393224 | tf_op jit(solution)/shard_map/ppermute | solution.py:498
  10.7 0.0 copy-done
  10.7 0.0 copy-done.2
  10.8 4.8 %shard_map.104 = (bf16[3,16,9,2,16,128]{5,4,3,2,1,0:T(8,128)(2,1)S(1)}, bf16[3,3,512,256]{3,2,1,0:T(8,128)(2,1)S(1)}, bf16[16,8,2,16,128]{4,3,2,1,0:T(8,128)(2,1)S(1)}) custom-call(bf16[16,8,2,16,128]{4,3,2,1,0:T(8,128)(2,1)S(1)} %bitcast.17, bf16[3,3,3,128,128]{4,3,2,1,0:T(8,128)(2,1)S(1)} %copy-done.2), custom_call_target="tpu_custom_call" | custom-call | flops 4831838208 | bytes 2097152 | tf_op jit(solution)/shard_map/pallas_call | solution.py:381
  15.5 0.0 collective-permute-done.1.partner_ref
  15.5 0.0 collective-permute-done.2.other_ref
  15.6 0.0 copy-done.1
  15.6 0.0 copy-done.3
  15.6 8.3 %shard_map.105 = (f32[36,64,128]{2,1,0:T(8,128)S(1)}, bf16[53,64,128]{2,1,0:T(8,128)(2,1)S(1)}, bf16[8,8,16,128]{3,2,1,0:T(8,128)(2,1)S(1)}) custom-call(s32[3]{0:T(128)S(1)} %bitcast.20, s32[1]{0:T(128)} %bitcast.14.parent_ref, s32[26]{0:T(128)S(1)} %bitcast.22, bf16[16,8,2,16,128]{4,3,2,1,0:T(8,128)(2,1)S(1)} %bitcast.18, ...), custom_call_target="tpu_custom_call" | custom-call | flops 4831838208 | bytes 1048576 | tf_op jit(solution)/shard_map/pallas_call | solution.py:390
  23.8 0.1 collective-permute-start.3
  23.9 2.4 %collective-permute-done.3.got_ref = bf16[53,64,128]{2,1,0:T(8,128)(2,1)S(1)} collective-permute-done((bf16[53,64,128]{2,1,0:T(8,128)(2,1)S(1)}, bf16[53,64,128]{2,1,0:T(8,128)(2,1)S(1)}, u32[]{:S(2)}, u32[]{:S(2)}) %collective-permute-start.3) | collective-permute-done | bytes 868384 | tf_op jit(solution)/shard_map/ppermute | solution.py:481
  26.3 0.9 %shard_map.106.refs_0_ = bf16[36,64,128]{2,1,0:T(8,128)(2,1)} custom-call(f32[36,64,128]{2,1,0:T(8,128)S(1)} %get-tuple-element.41.kept_ref, bf16[53,64,128]{2,1,0:T(8,128)(2,1)S(1)} %collective-permute-done.3.got_ref), custom_call_target="tpu_custom_call" | custom-call | bytes 1048576 | tf_op jit(solution)/shard_map/pallas_call | solution.py:493
  27.3 7.3 %all-to-all-start = ((bf16[16,144,128]{2,1,0:T(8,128)(2,1)}), bf16[16,144,128]{2,1,0:T(8,128)(2,1)S(1)}, u32[]{:S(2)}, u32[]{:S(2)}) async-start(bf16[16,144,128]{2,1,0:T(8,128)(2,1)} %bitcast.6), calls=%async_computation | async-start | bytes 1179648 | tf_op jit(solution)/shard_map/all_to_all | solution.py:489
  34.6 5.2 %shard_map.107 = (bf16[16,8,2,16,128]{4,3,2,1,0:T(8,128)(2,1)}, f32[8,128]{1,0:T(8,128)S(1)}) custom-call(s32[26]{0:T(128)S(1)} %bitcast.23, bf16[16,8,2,16,128]{4,3,2,1,0:T(8,128)(2,1)S(1)} %get-tuple-element.37.grads_ref.field_ref, bf16[2,8,2,16,128]{4,3,2,1,0:T(8,128)(2,1)S(1)} %collective-permute-done.1.partner_ref, ...), custom_call_target="tpu_custom_call" | custom-call | flops 2415919104 | bytes 1048576 | tf_op jit(solution)/shard_map/pallas_call | solution.py:403
  39.8 6.4 %all-to-all-done.got_ref = bf16[16,144,128]{2,1,0:T(8,128)(2,1)S(1)} async-done(((bf16[16,144,128]{2,1,0:T(8,128)(2,1)}), bf16[16,144,128]{2,1,0:T(8,128)(2,1)S(1)}, u32[]{:S(2)}, u32[]{:S(2)}) %all-to-all-start) | async-done | bytes 589856 | tf_op jit(solution)/shard_map/all_to_all | solution.py:489
  46.2 0.1 shard_map.108.after_ref.own_ref
  46.3 2.8 %collective-permute-start.6 = (f32[144,128]{1,0:T(8,128)S(1)}, f32[144,128]{1,0:T(8,128)S(1)}, u32[]{:S(2)}, u32[]{:S(2)}) collective-permute-start(f32[144,128]{1,0:T(8,128)S(1)} %shard_map.108.after_ref.own_ref), channel_id=1, source_target_pairs={{0,96},{32,0},{64,32},{96,64},{1,97},{33,1},{65,33},{97,65},{2,98}... | collective-permute-start | bytes 221192 | tf_op jit(solution)/shard_map/ppermute | solution.py:485
  49.1 0.3 collective-permute-start.5
  49.4 0.7 collective-permute-start.4
  50.1 1.7 %shard_map.109 = (bf16[16,16,16,128]{3,2,1,0:T(8,128)(2,1)}, f32[8,128]{1,0:T(8,128)S(1)}) custom-call(s32[3]{0:T(128)S(1)} %bitcast.21, bf16[8,8,16,128]{3,2,1,0:T(8,128)(2,1)S(1)} %get-tuple-element.39.keep_ref, bf16[53,64,128]{2,1,0:T(8,128)(2,1)S(1)} %collective-permute-done.3.got_ref, f32[144,128]{1,0:T(8,128)S(1)} %shard_map.108.after_ref.own_ref), custom_call_target="tpu_custom_call" | custom-call | bytes 1048576 | tf_op jit(solution)/shard_map/pallas_call | solution.py:416
  51.8 0.0 collective-permute-done.6.refs_2_
  51.8 2.1 %collective-permute-done.5.refs_1_ = f32[144,128]{1,0:T(8,128)S(1)} collective-permute-done((f32[144,128]{1,0:T(8,128)S(1)}, f32[144,128]{1,0:T(8,128)S(1)}, u32[]{:S(2)}, u32[]{:S(2)}) %collective-permute-start.5) | collective-permute-done | bytes 73760 | tf_op jit(solution)/shard_map/ppermute | solution.py:485
  53.9 0.7 collective-permute-done.4.refs_0_
  54.6 0.9 %shard_map.110.refs_0_ = bf16[16,144,128]{2,1,0:T(8,128)(2,1)} custom-call(f32[144,128]{1,0:T(8,128)S(1)} %shard_map.108.after_ref.own_ref, f32[144,128]{1,0:T(8,128)S(1)} %collective-permute-done.4.refs_0_, f32[144,128]{1,0:T(8,128)S(1)} %collective-permute-done.5.refs_1_, f32[144,128]{1,0:T(8,128)S(1)} %collective-permute-done.6.refs_2_, ...), custom_call_target="tpu_custom_call" | custom-call | bytes 1048576 | tf_op jit(solution)/shard_map/pallas_call | solution.py:493
  55.5 4.2 %all-to-all-start.1 = ((bf16[16,144,128]{2,1,0:T(8,128)(2,1)}), bf16[16,144,128]{2,1,0:T(8,128)(2,1)S(1)}, u32[]{:S(2)}, u32[]{:S(2)}) async-start(bf16[16,144,128]{2,1,0:T(8,128)(2,1)} %shard_map.110.refs_0_), calls=%async_computation.1 | async-start | bytes 1179648 | tf_op jit(solution)/shard_map/all_to_all | solution.py:489
  59.6 5.2 %shard_map.111 = (bf16[16,8,2,16,128]{4,3,2,1,0:T(8,128)(2,1)}, f32[8,128]{1,0:T(8,128)S(1)}) custom-call(s32[26]{0:T(128)S(1)} %bitcast.24, bf16[16,8,2,16,128]{4,3,2,1,0:T(8,128)(2,1)S(1)} %get-tuple-element.37.grads_ref.field_ref, bf16[2,8,2,16,128]{4,3,2,1,0:T(8,128)(2,1)S(1)} %collective-permute-done.1.partner_ref, ...), custom_call_target="tpu_custom_call", output_to_operand_aliasing={{0}: (6, {})} | custom-call | flops 2415919104 | bytes 1048576 | tf_op jit(solution)/shard_map/pallas_call | solution.py:403
  64.9 4.9 %all-to-all-done.1 = bf16[16,144,128]{2,1,0:T(8,128)(2,1)S(1)} async-done(((bf16[16,144,128]{2,1,0:T(8,128)(2,1)}), bf16[16,144,128]{2,1,0:T(8,128)(2,1)S(1)}, u32[]{:S(2)}, u32[]{:S(2)}) %all-to-all-start.1) | async-done | bytes 589856 | tf_op jit(solution)/shard_map/all_to_all | solution.py:489
  69.8 3.1 %collective-permute-start.7 = (bf16[36,64,128]{2,1,0:T(8,128)(2,1)S(1)}, bf16[36,64,128]{2,1,0:T(8,128)(2,1)S(1)}, u32[]{:S(2)}, u32[]{:S(2)}) collective-permute-start(bf16[36,64,128]{2,1,0:T(8,128)(2,1)S(1)} %shard_map.112.rows_ref), channel_id=1, source_target_pairs={{0,1},{1,0},{2,3},{3,2},{4,5},{5,4},{6,7},{7,6},{8,9},{9,8},{10,11... | collective-permute-start | bytes 1769480 | tf_op jit(solution)/shard_map/ppermute | solution.py:481
  72.9 1.6 %shard_map.113 = (f32[27,128,128]{2,1,0:T(8,128)}, f32[8,128,128]{2,1,0:T(8,128)}, f32[8,128]{1,0:T(8,128)}) custom-call(bf16[36,64,128]{2,1,0:T(8,128)(2,1)S(1)} %shard_map.112.rows_ref), custom_call_target="tpu_custom_call" | custom-call | bytes 1048576 | tf_op jit(solution)/shard_map/pallas_call | solution.py:472
  74.5 0.0 collective-permute-done.7.rows_ref
  74.5 1.6 %shard_map.114 = (f32[27,128,128]{2,1,0:T(8,128)}, f32[8,128,128]{2,1,0:T(8,128)}, f32[8,128]{1,0:T(8,128)}) custom-call(bf16[36,64,128]{2,1,0:T(8,128)(2,1)S(1)} %collective-permute-done.7.rows_ref, f32[27,128,128]{2,1,0:T(8,128)} %get-tuple-element.48.refs_0_, f32[8,128,128]{2,1,0:T(8,128)} %get-tuple-element.49.refs_1_), custom_call_target="tpu_custom_call", output_to_operand_aliasing={{0}: (1, {}), {1}: (2, {})} | custom-call | bytes 1048576 | tf_op jit(solution)/shard_map/pallas_call | solution.py:472
  (1 shorter events, 0.0 us)
Async XLA Ops:
  1.7 3.6 %collective-permute-start = (bf16[8,16,16,128]{3,2,1,0:T(8,128)(2,1)S(1)}, bf16[8,16,16,128]{3,2,1,0:T(8,128)(2,1)S(1)}, u32[]{:S(2)}, u32[]{:S(2)}) collective-permute-start(bf16[8,16,16,128]{3,2,1,0:T(8,128)(2,1)S(1)} %dynamic-slice_bitcast_fusion.after_ref), channel_id=1, source_target_pairs={{0,1},{1,0},{2,3},{3,2},{4,5},{5,4},{6,7},{7,6},{8,9},{9,8},{10,11... | collective-permute-start | bytes 1572872 | tf_op jit(solution)/shard_map/ppermute | solution.py:481
  3.9 6.9 %copy-start = (bf16[1,1,16,16,16,128]{5,4,3,2,1,0:T(8,128)(2,1)S(1)}, bf16[1,1,16,16,16,128]{5,4,3,2,1,0:T(8,128)(2,1)}, u32[]{:S(2)}) copy-start(bf16[1,1,16,16,16,128]{5,4,3,2,1,0:T(8,128)(2,1)} %param.7) | copy-start | bytes 3145732
  3.9 6.9 %copy-start.2 = (bf16[3,3,3,128,128]{4,3,2,1,0:T(8,128)(2,1)S(1)}, bf16[3,3,3,128,128]{4,3,2,1,0:T(8,128)(2,1)}, u32[]{:S(2)}) copy-start(bf16[3,3,3,128,128]{4,3,2,1,0:T(8,128)(2,1)} %conv_hbm.3) | copy-start | bytes 2654212
  6.9 8.6 %collective-permute-start.1 = (bf16[2,8,2,16,128]{4,3,2,1,0:T(8,128)(2,1)S(1)}, bf16[2,8,2,16,128]{4,3,2,1,0:T(8,128)(2,1)S(1)}, u32[]{:S(2)}, u32[]{:S(2)}) collective-permute-start(bf16[2,8,2,16,128]{4,3,2,1,0:T(8,128)(2,1)S(1)} %get-tuple-element.32), channel_id=1, source_target_pairs={{0,1},{1,0},{2,3},{3,2},{4,5},{5,4},{6,7},{7,6},{8,9},{9,8},{10,11... | collective-permute-start | bytes 393224 | tf_op jit(solution)/shard_map/ppermute | solution.py:481
  7.0 8.5 %copy-start.1 = (s32[1,1,3]{2,1,0:T(1,128)S(1)}, s32[1,1,3]{2,1,0:T(1,128)}, u32[]{:S(2)}) copy-start(s32[1,1,3]{2,1,0:T(1,128)} %param.11) | copy-start | bytes 40
  7.0 8.5 %copy-start.3 = (s32[1,1,26]{2,1,0:T(1,128)S(1)}, s32[1,1,26]{2,1,0:T(1,128)}, u32[]{:S(2)}) copy-start(s32[1,1,26]{2,1,0:T(1,128)} %param.12) | copy-start | bytes 316
  7.0 8.5 %collective-permute-start.2 = (bf16[2,8,2,16,128]{4,3,2,1,0:T(8,128)(2,1)S(1)}, bf16[2,8,2,16,128]{4,3,2,1,0:T(8,128)(2,1)S(1)}, u32[]{:S(2)}, u32[]{:S(2)}) collective-permute-start(bf16[2,8,2,16,128]{4,3,2,1,0:T(8,128)(2,1)S(1)} %get-tuple-element.33), channel_id=1, source_target_pairs={{1,2},{3,4},{5,6},{7,8},{9,10},{11,12},{13,14},{15,16},{17,18},{19... | collective-permute-start | bytes 393224 | tf_op jit(solution)/shard_map/ppermute | solution.py:498
  23.8 2.5 %collective-permute-start.3 = (bf16[53,64,128]{2,1,0:T(8,128)(2,1)S(1)}, bf16[53,64,128]{2,1,0:T(8,128)(2,1)S(1)}, u32[]{:S(2)}, u32[]{:S(2)}) collective-permute-start(bf16[53,64,128]{2,1,0:T(8,128)(2,1)S(1)} %get-tuple-element.40), channel_id=1, source_target_pairs={{0,1},{1,0},{2,3},{3,2},{4,5},{5,4},{6,7},{7,6},{8,9},{9,8},{10,11... | collective-permute-start | bytes 2605064 | tf_op jit(solution)/shard_map/ppermute | solution.py:481
  27.3 18.9 %all-to-all-start = ((bf16[16,144,128]{2,1,0:T(8,128)(2,1)}), bf16[16,144,128]{2,1,0:T(8,128)(2,1)S(1)}, u32[]{:S(2)}, u32[]{:S(2)}) async-start(bf16[16,144,128]{2,1,0:T(8,128)(2,1)} %bitcast.6), calls=%async_computation | async-start | bytes 1179648 | tf_op jit(solution)/shard_map/all_to_all | solution.py:489
  46.3 5.5 %collective-permute-start.6 = (f32[144,128]{1,0:T(8,128)S(1)}, f32[144,128]{1,0:T(8,128)S(1)}, u32[]{:S(2)}, u32[]{:S(2)}) collective-permute-start(f32[144,128]{1,0:T(8,128)S(1)} %shard_map.108.after_ref.own_ref), channel_id=1, source_target_pairs={{0,96},{32,0},{64,32},{96,64},{1,97},{33,1},{65,33},{97,65},{2,98}... | collective-permute-start | bytes 221192 | tf_op jit(solution)/shard_map/ppermute | solution.py:485
  49.1 4.8 %collective-permute-start.5 = (f32[144,128]{1,0:T(8,128)S(1)}, f32[144,128]{1,0:T(8,128)S(1)}, u32[]{:S(2)}, u32[]{:S(2)}) collective-permute-start(f32[144,128]{1,0:T(8,128)S(1)} %shard_map.108.after_ref.own_ref), channel_id=1, source_target_pairs={{0,64},{32,96},{64,0},{96,32},{1,65},{33,97},{65,1},{97,33},{2,66}... | collective-permute-start | bytes 221192 | tf_op jit(solution)/shard_map/ppermute | solution.py:485
  49.4 5.1 %collective-permute-start.4 = (f32[144,128]{1,0:T(8,128)S(1)}, f32[144,128]{1,0:T(8,128)S(1)}, u32[]{:S(2)}, u32[]{:S(2)}) collective-permute-start(f32[144,128]{1,0:T(8,128)S(1)} %shard_map.108.after_ref.own_ref), channel_id=1, source_target_pairs={{0,32},{32,64},{64,96},{96,0},{1,33},{33,65},{65,97},{97,1},{2,34}... | collective-permute-start | bytes 221192 | tf_op jit(solution)/shard_map/ppermute | solution.py:485
  55.5 14.3 %all-to-all-start.1 = ((bf16[16,144,128]{2,1,0:T(8,128)(2,1)}), bf16[16,144,128]{2,1,0:T(8,128)(2,1)S(1)}, u32[]{:S(2)}, u32[]{:S(2)}) async-start(bf16[16,144,128]{2,1,0:T(8,128)(2,1)} %shard_map.110.refs_0_), calls=%async_computation.1 | async-start | bytes 1179648 | tf_op jit(solution)/shard_map/all_to_all | solution.py:489
  69.8 4.7 %collective-permute-start.7 = (bf16[36,64,128]{2,1,0:T(8,128)(2,1)S(1)}, bf16[36,64,128]{2,1,0:T(8,128)(2,1)S(1)}, u32[]{:S(2)}, u32[]{:S(2)}) collective-permute-start(bf16[36,64,128]{2,1,0:T(8,128)(2,1)S(1)} %shard_map.112.rows_ref), channel_id=1, source_target_pairs={{0,1},{1,0},{2,3},{3,2},{4,5},{5,4},{6,7},{7,6},{8,9},{9,8},{10,11... | collective-permute-start | bytes 1769480 | tf_op jit(solution)/shard_map/ppermute | solution.py:481

commit v6 on v5

--- a/solution.py
+++ b/solution.py
@@ -152,19 +152,20 @@
 
 def inner_kernel(field_ref, conv_ref, shifts_ref, weights_ref, outputs_ref):
     lay_weights(conv_ref, weights_ref)
-    lay_interior(field_ref, shifts_ref, 0, 6, 0)
-    for first, count in ((1, 4), (5, 4), (9, 4), (13, 2)):
-        lay_interior(field_ref, shifts_ref, min(first + 5, 16), min(first + 9, 16), 0)
+    lay_interior(field_ref, shifts_ref, 0, 11, 0)
+    for first in (1, 5):
         acc = None
         for a in range(3):
             for c in range(3):
-                part = dot(window(shifts_ref, c, first + a - 1, count), weights_ref[a, c], NN)
+                part = dot(window(shifts_ref, c, first + a - 1, 4), weights_ref[a, c], NN)
                 acc = part if acc is None else acc + part
         for s in range(2):
-            field = field_ref[first : first + count, :, s].astype(F32)
-            outputs_ref[first : first + count, :, s] = (
-                acc[:, s * 128 : s * 128 + 128].reshape(count, 8, 16, 128) + field
+            field = field_ref[first : first + 4, :, s].astype(F32)
+            outputs_ref[first - 1 : first + 3, :, s] = (
+                acc[:, s * 128 : s * 128 + 128].reshape(4, 8, 16, 128) + field
             ).astype(BF)
+        if first == 1:
+            lay_interior(field_ref, shifts_ref, 11, 16, 0)
 
 
 def taps(rows):
@@ -198,20 +199,24 @@
     acc = None
     for a in range(3):
         for c in range(3):
-            below = taps(low_shifts_ref[c] if a == 0 else shifts_ref[c, a - 1])
-            above = taps(high_shifts_ref[c] if a == 2 else shifts_ref[c, 14 + a])
-            part = dot(jnp.concatenate([below, above], axis=0), weights_ref[a, c], NN)
+            rows = [
+                taps(low_shifts_ref[c] if a == 0 else shifts_ref[c, a - 1]),
+                window(shifts_ref, c, 8 + a, 6 if a == 2 else 7),
+            ]
+            if a == 2:
+                rows.append(taps(high_shifts_ref[c]))
+            part = dot(jnp.concatenate(rows, axis=0), weights_ref[a, c], NN)
             acc = part if acc is None else acc + part
     for s in range(2):
-        for k in range(2):
-            value = acc[128 * k : 128 * k + 128, s * 128 : s * 128 + 128].reshape(8, 16, 128)
-            edges_ref[k, :, s] = (value + field_ref[15 * k, :, s].astype(F32)).astype(BF)
+        value = acc[:, s * 128 : s * 128 + 128].reshape(8, 8, 16, 128)
+        edges_ref[0, :, s] = (value[0] + field_ref[0, :, s].astype(F32)).astype(BF)
+        edges_ref[1:8, :, s] = (value[1:8] + field_ref[9:16, :, s].astype(F32)).astype(BF)
 
     down = down_ref[...]
 
     def corner(i, p, q):
         at = 2 * i + p
-        rows = edges_ref[at // 15, :, q] if at in (0, 15) else inner_ref[at, :, q]
+        rows = inner_ref[at - 1, :, q] if 1 <= at <= 8 else edges_ref[max(at - 8, 0), :, q]
         return rows.reshape(128, 128)
 
     for i in range(8):
@@ -380,8 +385,8 @@
 def inner_call(field, conv):
     return call(
         inner_kernel, [VMEM] * 2,
-        [sds((3, 16, 9, 2, 16, 128), BF), sds((3, 3, 512, 256), BF), sds((16, 8, 2, 16, 128), BF)],
-        flops=2 * 9 * 2048 * 512 * 256, moved=2 << 20, limit=16,
+        [sds((3, 16, 9, 2, 16, 128), BF), sds((3, 3, 512, 256), BF), sds((8, 8, 2, 16, 128), BF)],
+        flops=9 * 2048 * 512 * 256, moved=2 << 20, limit=16,
     )(field, conv)
 
 
@@ -390,8 +395,8 @@
     return call(
         main_kernel, [SMEM] * 3 + [VMEM] * 9,
         [sds((36, 64, 128), F32), sds((53, 64, 128), BF), sds((8, 8, 16, 128), BF)],
-        [slab, slab, pltpu.VMEM((2, 8, 2, 16, 128), BF), pltpu.VMEM((8, 2, 128, 128), F32)],
-        flops=2 * 9 * 2048 * 512 * 256, limit=24,
+        [slab, slab, pltpu.VMEM((8, 8, 2, 16, 128), BF), pltpu.VMEM((8, 2, 128, 128), F32)],
+        flops=3 * 9 * 2048 * 512 * 256, limit=24,
     )(coords, parent, near, field, partner, other, *inner, down, grads, spread)
 
 
@@ -456,12 +461,13 @@
     core = lax.axis_index("core")
     here = pl.ds(pl.multiple_of(64 * (core if own else 1 - core), 64), 64)
     copies = []
-    for k, (start, stop) in enumerate(((0, 9), (9, 18), (18, 27), (27, 35))):
+    for k, start in enumerate((*range(0, 27, 3), 27, 31)):
+        stop = start + (3 if start < 27 else 4)
         wide_ref[start:stop] = rows_ref[start:stop].astype(F32)
         if start < 27:
             target = conv_ref.at[start:stop, here]
         else:
-            target = down_ref.at[:, here]
+            target = down_ref.at[start - 27 : stop - 27, here]
         copies.append(pltpu.make_async_copy(wide_ref.at[start:stop], target, sems.at[k]))
         copies[-1].start()
     for copy in copies:
@@ -472,7 +478,7 @@
     return call(
         functools.partial(write_half, own=own), [VMEM] + [ANY] * len(bases),
         [sds((27, 128, 128), F32), sds((8, 128, 128), F32), TOKEN],
-        [pltpu.VMEM((36, 64, 128), F32), pltpu.SemaphoreType.DMA((4,))], out=ANY,
+        [pltpu.VMEM((36, 64, 128), F32), pltpu.SemaphoreType.DMA((11,))], out=ANY,
         input_output_aliases={1: 0, 2: 1} if bases else {},
     )(rows, *bases)[:2]
 
@@ -518,11 +524,11 @@
     own = stage(add_halves, (kept, got), [sds((36, 64, 128), BF)])[0]
     gots = over_plane(own.reshape(16, 144, 128))
     partial_grad, token = input_call(near, grads, partner, other, far(conv_weight), own, 0)
+    coarse, token = coarse_call(coords, keep, got, token)
     own = stage(add_sixteen, (gots,), [sds((144, 128), F32)], (token,))[0]
     gots = [over_y(own, k) for k in (1, 2, 3)]
-    coarse, token = coarse_call(coords, keep, got, own)
     shares = stage(
-        add_in_order, (own, *gots), [sds((16, 144, 128), BF)], (token,),
+        add_in_order, (own, *gots), [sds((16, 144, 128), BF)],
         scratch=[pltpu.VMEM((4, 144, 128), F32)],
     )[0]
 

time: 76.8 us -> 81.4 us (1.060)
  Pallas kernels: 33.4 us -> 36.4 us
  starting transfers between devices: 23.8 us -> 25.3 us
    pallas_call x1, Pallas kernels: 8.25 us -> 12.9 us  [main_call(): call(main_kernel, [SMEM] * 3 + [VMEM] * 9, [sds((36, 64, 128), F32), sds(...]
    pallas_call x1, Pallas kernels: 4.77 us -> 3.09 us  [inner_call(): call(inner_kernel, [VMEM] * 2, [sds((3, 16, 9, 2, 16, 128), BF), sds((3,...]
    ppermute x3, waiting for transfers between devices: 2.79 us -> 4.46 us  [over_y(): return lax.ppermute(value, 'dp', [(i, (i + by) % 4) for i in range(4)])]
    all_to_all x2, waiting for transfers between devices: 11.3 us -> 9.6 us  [over_plane(): return lax.all_to_all(value, ('z', 'x'), 0, 0, tiled=True)]
    all_to_all x2, starting transfers between devices: 11.5 us -> 13 us  [over_plane(): return lax.all_to_all(value, ('z', 'x'), 0, 0, tiled=True)]
  transfers between devices with their start and end apart: 10 -> 10, of which waited for: 5 -> 6; matrix products, arithmetic and copies ran while one was open for 0% -> 0% of each run, Pallas kernels for 26% -> 23%
where the time goes in v6:
time: 81.4 us; the launch traced here: 80.9 us
  Pallas kernels  36.4 us (45%)
  starting transfers between devices  25.3 us (31%)
  waiting for transfers between devices  16.5 us (20%)
  between operations  1.64 us (2%)
  local copies, waits for them, and re-layouts  1.11 us (1%)
    all_to_all x2, starting transfers between devices, over_plane(): return lax.all_to_all(value, ('z', 'x'), 0, 0, tiled=True)  13 us
    pallas_call x1, Pallas kernels, main_call(): call(main_kernel, [SMEM] * 3 + [VMEM] * 9, [sds((36, 64, 128), F32), sds(...  12.9 us
    pallas_call x2, Pallas kernels, input_call(): call(functools.partial(input_kernel, half=half), ins, [sds((16, 8, 2, 16,...  10.5 us
    all_to_all x2, waiting for transfers between devices, over_plane(): return lax.all_to_all(value, ('z', 'x'), 0, 0, tiled=True)  9.6 us
    ppermute x4, starting transfers between devices, over_core(): return lax.ppermute(value, 'core', [(0, 1), (1, 0)])  4.77 us
    ppermute x3, waiting for transfers between devices, over_y(): return lax.ppermute(value, 'dp', [(i, (i + by) % 4) for i in range(4)])  4.46 us
    ppermute x3, starting transfers between devices, over_y(): return lax.ppermute(value, 'dp', [(i, (i + by) % 4) for i in range(4)])  3.85 us
    ppermute x1, starting transfers between devices, over_other(): return lax.ppermute(value, ('z', 'x', 'core'), pairs)  3.69 us
  transfers between devices with their start and end apart: 10, of which 6 were waited for; matrix products, arithmetic and copies ran while one was open for 0% of the time, Pallas kernels for 23%

profile of v6, /device:TPU:1, one launch (start us, length us, event | category | flops | bytes accessed | tf_op | source)
XLA Modules:
  0.0 80.9 jit_solution(11336697505264381822)
XLA Ops:
  0.6 1.1 %dynamic-slice_bitcast_fusion.after_ref = bf16[8,16,16,128]{3,2,1,0:T(8,128)(2,1)S(1)} fusion(bf16[1,1,16,16,16,128]{5,4,3,2,1,0:T(8,128)(2,1)} %param.10, s32[]{:T(128)S(6)} %select_n.3), kind=kLoop, calls=%fused_computation | loop fusion | bytes 1048580 | tf_op jit(solution)/shard_map/dynamic_slice | solution.py:511
  1.7 1.5 %collective-permute-start = (bf16[8,16,16,128]{3,2,1,0:T(8,128)(2,1)S(1)}, bf16[8,16,16,128]{3,2,1,0:T(8,128)(2,1)S(1)}, u32[]{:S(2)}, u32[]{:S(2)}) collective-permute-start(bf16[8,16,16,128]{3,2,1,0:T(8,128)(2,1)S(1)} %dynamic-slice_bitcast_fusion.after_ref), channel_id=1, source_target_pairs={{0,1},{1,0},{2,3},{3,2},{4,5},{5,4},{6,7},{7,6},{8,9},{9,8},{10,11... | collective-permute-start | bytes 1572872 | tf_op jit(solution)/shard_map/ppermute | solution.py:487
  3.9 0.0 copy-start
  3.9 0.0 copy-start.2
  3.9 1.4 %shard_map.102 = (bf16[8,16,16,128]{3,2,1,0:T(8,128)(2,1)S(1)}, bf16[512,256]{1,0:T(8,128)(2,1)S(1)}, bf16[8,2,16,128]{3,2,1,0:T(8,128)(2,1)S(1)}, bf16[8,2,16,128]{3,2,1,0:T(8,128)(2,1)S(1)}) custom-call(bf16[16,16,16,128]{3,2,1,0:T(8,128)(2,1)} %bitcast.25, bf16[2,2,2,128,128]{4,3,2,1,0:T(8,128)(2,1)} %down_hbm.1, bf16[16,8,2,16,128]{4,3,2,1,0:T(8,128)(2,1)} %bitcast.16, ...), custom_call_target="tpu_custom_call" | custom-call | bytes 1048576 | tf_op jit(solution)/shard_map/pallas_call | solution.py:369
  5.3 0.0 collective-permute-done.theirs_ref
  5.4 1.6 %shard_map.103 = (bf16[16,8,2,16,128]{4,3,2,1,0:T(8,128)(2,1)S(1)}, bf16[8,128,256]{2,1,0:T(8,128)(2,1)S(1)}, bf16[2,8,2,16,128]{4,3,2,1,0:T(8,128)(2,1)S(1)}, bf16[2,8,2,16,128]{4,3,2,1,0:T(8,128)(2,1)S(1)}) custom-call(s32[3]{0:T(128)} %bitcast.19, s32[1]{0:T(128)} %bitcast.13.parent_ref, bf16[8,16,16,128]{3,2,1,0:T(8,128)(2,1)S(1)} %get-tuple-element.28.mine_ref, ...), custom_call_target="tpu_custom_call" | custom-call | flops 268435456 | bytes 4194304 | tf_op jit(solution)/shard_map/pallas_call | solution.py:378
  6.9 0.1 collective-permute-start.1
  7.0 0.0 copy-start.1
  7.0 0.0 copy-start.3
  7.0 3.7 %collective-permute-start.2 = (bf16[2,8,2,16,128]{4,3,2,1,0:T(8,128)(2,1)S(1)}, bf16[2,8,2,16,128]{4,3,2,1,0:T(8,128)(2,1)S(1)}, u32[]{:S(2)}, u32[]{:S(2)}) collective-permute-start(bf16[2,8,2,16,128]{4,3,2,1,0:T(8,128)(2,1)S(1)} %get-tuple-element.33), channel_id=1, source_target_pairs={{1,2},{3,4},{5,6},{7,8},{9,10},{11,12},{13,14},{15,16},{17,18},{19... | collective-permute-start | bytes 393224 | tf_op jit(solution)/shard_map/ppermute | solution.py:504
  10.7 0.0 copy-done
  10.7 0.0 copy-done.2
  10.8 3.1 %shard_map.104 = (bf16[3,16,9,2,16,128]{5,4,3,2,1,0:T(8,128)(2,1)S(1)}, bf16[3,3,512,256]{3,2,1,0:T(8,128)(2,1)S(1)}, bf16[8,8,2,16,128]{4,3,2,1,0:T(8,128)(2,1)S(1)}) custom-call(bf16[16,8,2,16,128]{4,3,2,1,0:T(8,128)(2,1)S(1)} %bitcast.17, bf16[3,3,3,128,128]{4,3,2,1,0:T(8,128)(2,1)S(1)} %copy-done.2), custom_call_target="tpu_custom_call" | custom-call | flops 2415919104 | bytes 2097152 | tf_op jit(solution)/shard_map/pallas_call | solution.py:386
  13.9 0.0 collective-permute-done.1.partner_ref
  13.9 0.0 collective-permute-done.2.other_ref
  13.9 0.0 copy-done.1
  13.9 0.0 copy-done.3
  13.9 12.9 %shard_map.105 = (f32[36,64,128]{2,1,0:T(8,128)S(1)}, bf16[53,64,128]{2,1,0:T(8,128)(2,1)S(1)}, bf16[8,8,16,128]{3,2,1,0:T(8,128)(2,1)S(1)}) custom-call(s32[3]{0:T(128)S(1)} %bitcast.20, s32[1]{0:T(128)} %bitcast.14.parent_ref, s32[26]{0:T(128)S(1)} %bitcast.22, bf16[16,8,2,16,128]{4,3,2,1,0:T(8,128)(2,1)S(1)} %bitcast.18, ...), custom_call_target="tpu_custom_call" | custom-call | flops 7247757312 | bytes 1048576 | tf_op jit(solution)/shard_map/pallas_call | solution.py:395
  26.8 0.1 collective-permute-start.3
  26.9 2.4 %collective-permute-done.3.got_ref = bf16[53,64,128]{2,1,0:T(8,128)(2,1)S(1)} collective-permute-done((bf16[53,64,128]{2,1,0:T(8,128)(2,1)S(1)}, bf16[53,64,128]{2,1,0:T(8,128)(2,1)S(1)}, u32[]{:S(2)}, u32[]{:S(2)}) %collective-permute-start.3) | collective-permute-done | bytes 868384 | tf_op jit(solution)/shard_map/ppermute | solution.py:487
  29.3 0.9 %shard_map.106.refs_0_ = bf16[36,64,128]{2,1,0:T(8,128)(2,1)} custom-call(f32[36,64,128]{2,1,0:T(8,128)S(1)} %get-tuple-element.41.kept_ref, bf16[53,64,128]{2,1,0:T(8,128)(2,1)S(1)} %collective-permute-done.3.got_ref), custom_call_target="tpu_custom_call" | custom-call | bytes 1048576 | tf_op jit(solution)/shard_map/pallas_call | solution.py:499
  30.2 8.8 %all-to-all-start = ((bf16[16,144,128]{2,1,0:T(8,128)(2,1)}), bf16[16,144,128]{2,1,0:T(8,128)(2,1)S(1)}, u32[]{:S(2)}, u32[]{:S(2)}) async-start(bf16[16,144,128]{2,1,0:T(8,128)(2,1)} %bitcast.7), calls=%async_computation | async-start | bytes 1179648 | tf_op jit(solution)/shard_map/all_to_all | solution.py:495
  39.0 5.2 %shard_map.107 = (bf16[16,8,2,16,128]{4,3,2,1,0:T(8,128)(2,1)}, f32[8,128]{1,0:T(8,128)S(1)}) custom-call(s32[26]{0:T(128)S(1)} %bitcast.23, bf16[16,8,2,16,128]{4,3,2,1,0:T(8,128)(2,1)S(1)} %get-tuple-element.37.grads_ref.field_ref, bf16[2,8,2,16,128]{4,3,2,1,0:T(8,128)(2,1)S(1)} %collective-permute-done.1.partner_ref, ...), custom_call_target="tpu_custom_call" | custom-call | flops 2415919104 | bytes 1048576 | tf_op jit(solution)/shard_map/pallas_call | solution.py:408
  44.3 1.7 %shard_map.108 = (bf16[16,16,16,128]{3,2,1,0:T(8,128)(2,1)}, f32[8,128]{1,0:T(8,128)S(1)}) custom-call(s32[3]{0:T(128)S(1)} %bitcast.21, bf16[8,8,16,128]{3,2,1,0:T(8,128)(2,1)S(1)} %get-tuple-element.39.keep_ref, bf16[53,64,128]{2,1,0:T(8,128)(2,1)S(1)} %collective-permute-done.3.got_ref, f32[8,128]{1,0:T(8,128)S(1)} %get-tuple-element.42.after_ref), custom_call_target="tpu_custom_call" | custom-call | bytes 1048576 | tf_op jit(solution)/shard_map/pallas_call | solution.py:421
  46.0 4.7 %all-to-all-done.got_ref = bf16[16,144,128]{2,1,0:T(8,128)(2,1)S(1)} async-done(((bf16[16,144,128]{2,1,0:T(8,128)(2,1)}), bf16[16,144,128]{2,1,0:T(8,128)(2,1)S(1)}, u32[]{:S(2)}, u32[]{:S(2)}) %all-to-all-start) | async-done | bytes 589856 | tf_op jit(solution)/shard_map/all_to_all | solution.py:495
  50.7 0.1 shard_map.109.own_ref
  50.7 2.8 %collective-permute-start.6 = (f32[144,128]{1,0:T(8,128)S(1)}, f32[144,128]{1,0:T(8,128)S(1)}, u32[]{:S(2)}, u32[]{:S(2)}) collective-permute-start(f32[144,128]{1,0:T(8,128)S(1)} %shard_map.109.own_ref), channel_id=1, source_target_pairs={{0,96},{32,0},{64,32},{96,64},{1,97},{33,1},{65,33},{97,65},{2,98}... | collective-permute-start | bytes 221192 | tf_op jit(solution)/shard_map/ppermute | solution.py:491
  53.6 0.3 collective-permute-start.5
  53.9 0.7 collective-permute-start.4
  54.6 0.4 collective-permute-done.6.refs_2_
  55.0 3.4 %collective-permute-done.5.refs_1_ = f32[144,128]{1,0:T(8,128)S(1)} collective-permute-done((f32[144,128]{1,0:T(8,128)S(1)}, f32[144,128]{1,0:T(8,128)S(1)}, u32[]{:S(2)}, u32[]{:S(2)}) %collective-permute-start.5) | collective-permute-done | bytes 73760 | tf_op jit(solution)/shard_map/ppermute | solution.py:491
  58.3 0.7 collective-permute-done.4.refs_0_
  59.1 0.9 %shard_map.110.refs_0_ = bf16[16,144,128]{2,1,0:T(8,128)(2,1)} custom-call(f32[144,128]{1,0:T(8,128)S(1)} %shard_map.109.own_ref, f32[144,128]{1,0:T(8,128)S(1)} %collective-permute-done.4.refs_0_, f32[144,128]{1,0:T(8,128)S(1)} %collective-permute-done.5.refs_1_, f32[144,128]{1,0:T(8,128)S(1)} %collective-permute-done.6.refs_2_), custom_call_target="tpu_custom_call" | custom-call | bytes 1048576 | tf_op jit(solution)/shard_map/pallas_call | solution.py:499
  60.0 4.2 %all-to-all-start.1 = ((bf16[16,144,128]{2,1,0:T(8,128)(2,1)}), bf16[16,144,128]{2,1,0:T(8,128)(2,1)S(1)}, u32[]{:S(2)}, u32[]{:S(2)}) async-start(bf16[16,144,128]{2,1,0:T(8,128)(2,1)} %shard_map.110.refs_0_), calls=%async_computation.1 | async-start | bytes 1179648 | tf_op jit(solution)/shard_map/all_to_all | solution.py:495
  64.1 5.2 %shard_map.111 = (bf16[16,8,2,16,128]{4,3,2,1,0:T(8,128)(2,1)}, f32[8,128]{1,0:T(8,128)S(1)}) custom-call(s32[26]{0:T(128)S(1)} %bitcast.24, bf16[16,8,2,16,128]{4,3,2,1,0:T(8,128)(2,1)S(1)} %get-tuple-element.37.grads_ref.field_ref, bf16[2,8,2,16,128]{4,3,2,1,0:T(8,128)(2,1)S(1)} %collective-permute-done.1.partner_ref, ...), custom_call_target="tpu_custom_call", output_to_operand_aliasing={{0}: (6, {})} | custom-call | flops 2415919104 | bytes 1048576 | tf_op jit(solution)/shard_map/pallas_call | solution.py:408
  69.4 4.9 %all-to-all-done.1 = bf16[16,144,128]{2,1,0:T(8,128)(2,1)S(1)} async-done(((bf16[16,144,128]{2,1,0:T(8,128)(2,1)}), bf16[16,144,128]{2,1,0:T(8,128)(2,1)S(1)}, u32[]{:S(2)}, u32[]{:S(2)}) %all-to-all-start.1) | async-done | bytes 589856 | tf_op jit(solution)/shard_map/all_to_all | solution.py:495
  74.3 3.1 %collective-permute-start.7 = (bf16[36,64,128]{2,1,0:T(8,128)(2,1)S(1)}, bf16[36,64,128]{2,1,0:T(8,128)(2,1)S(1)}, u32[]{:S(2)}, u32[]{:S(2)}) collective-permute-start(bf16[36,64,128]{2,1,0:T(8,128)(2,1)S(1)} %shard_map.112.rows_ref), channel_id=1, source_target_pairs={{0,1},{1,0},{2,3},{3,2},{4,5},{5,4},{6,7},{7,6},{8,9},{9,8},{10,11... | collective-permute-start | bytes 1769480 | tf_op jit(solution)/shard_map/ppermute | solution.py:487
  77.4 1.7 %shard_map.113 = (f32[27,128,128]{2,1,0:T(8,128)}, f32[8,128,128]{2,1,0:T(8,128)}, f32[8,128]{1,0:T(8,128)}) custom-call(bf16[36,64,128]{2,1,0:T(8,128)(2,1)S(1)} %shard_map.112.rows_ref), custom_call_target="tpu_custom_call" | custom-call | bytes 1048576 | tf_op jit(solution)/shard_map/pallas_call | solution.py:478
  79.0 0.0 collective-permute-done.7.rows_ref
  79.1 1.7 %shard_map.114 = (f32[27,128,128]{2,1,0:T(8,128)}, f32[8,128,128]{2,1,0:T(8,128)}, f32[8,128]{1,0:T(8,128)}) custom-call(bf16[36,64,128]{2,1,0:T(8,128)(2,1)S(1)} %collective-permute-done.7.rows_ref, f32[27,128,128]{2,1,0:T(8,128)} %get-tuple-element.48.refs_0_, f32[8,128,128]{2,1,0:T(8,128)} %get-tuple-element.49.refs_1_), custom_call_target="tpu_custom_call", output_to_operand_aliasing={{0}: (1, {}), {1}: (2, {})} | custom-call | bytes 1048576 | tf_op jit(solution)/shard_map/pallas_call | solution.py:478
  (1 shorter events, 0.0 us)
Async XLA Ops:
  1.7 3.6 %collective-permute-start = (bf16[8,16,16,128]{3,2,1,0:T(8,128)(2,1)S(1)}, bf16[8,16,16,128]{3,2,1,0:T(8,128)(2,1)S(1)}, u32[]{:S(2)}, u32[]{:S(2)}) collective-permute-start(bf16[8,16,16,128]{3,2,1,0:T(8,128)(2,1)S(1)} %dynamic-slice_bitcast_fusion.after_ref), channel_id=1, source_target_pairs={{0,1},{1,0},{2,3},{3,2},{4,5},{5,4},{6,7},{7,6},{8,9},{9,8},{10,11... | collective-permute-start | bytes 1572872 | tf_op jit(solution)/shard_map/ppermute | solution.py:487
  3.9 6.9 %copy-start = (bf16[1,1,16,16,16,128]{5,4,3,2,1,0:T(8,128)(2,1)S(1)}, bf16[1,1,16,16,16,128]{5,4,3,2,1,0:T(8,128)(2,1)}, u32[]{:S(2)}) copy-start(bf16[1,1,16,16,16,128]{5,4,3,2,1,0:T(8,128)(2,1)} %param.7) | copy-start | bytes 3145732
  3.9 6.9 %copy-start.2 = (bf16[3,3,3,128,128]{4,3,2,1,0:T(8,128)(2,1)S(1)}, bf16[3,3,3,128,128]{4,3,2,1,0:T(8,128)(2,1)}, u32[]{:S(2)}) copy-start(bf16[3,3,3,128,128]{4,3,2,1,0:T(8,128)(2,1)} %conv_hbm.3) | copy-start | bytes 2654212
  6.9 6.9 %collective-permute-start.1 = (bf16[2,8,2,16,128]{4,3,2,1,0:T(8,128)(2,1)S(1)}, bf16[2,8,2,16,128]{4,3,2,1,0:T(8,128)(2,1)S(1)}, u32[]{:S(2)}, u32[]{:S(2)}) collective-permute-start(bf16[2,8,2,16,128]{4,3,2,1,0:T(8,128)(2,1)S(1)} %get-tuple-element.32), channel_id=1, source_target_pairs={{0,1},{1,0},{2,3},{3,2},{4,5},{5,4},{6,7},{7,6},{8,9},{9,8},{10,11... | collective-permute-start | bytes 393224 | tf_op jit(solution)/shard_map/ppermute | solution.py:487
  7.0 6.9 %copy-start.1 = (s32[1,1,3]{2,1,0:T(1,128)S(1)}, s32[1,1,3]{2,1,0:T(1,128)}, u32[]{:S(2)}) copy-start(s32[1,1,3]{2,1,0:T(1,128)} %param.11) | copy-start | bytes 40
  7.0 6.9 %copy-start.3 = (s32[1,1,26]{2,1,0:T(1,128)S(1)}, s32[1,1,26]{2,1,0:T(1,128)}, u32[]{:S(2)}) copy-start(s32[1,1,26]{2,1,0:T(1,128)} %param.12) | copy-start | bytes 316
  7.0 6.8 %collective-permute-start.2 = (bf16[2,8,2,16,128]{4,3,2,1,0:T(8,128)(2,1)S(1)}, bf16[2,8,2,16,128]{4,3,2,1,0:T(8,128)(2,1)S(1)}, u32[]{:S(2)}, u32[]{:S(2)}) collective-permute-start(bf16[2,8,2,16,128]{4,3,2,1,0:T(8,128)(2,1)S(1)} %get-tuple-element.33), channel_id=1, source_target_pairs={{1,2},{3,4},{5,6},{7,8},{9,10},{11,12},{13,14},{15,16},{17,18},{19... | collective-permute-start | bytes 393224 | tf_op jit(solution)/shard_map/ppermute | solution.py:504
  26.8 2.5 %collective-permute-start.3 = (bf16[53,64,128]{2,1,0:T(8,128)(2,1)S(1)}, bf16[53,64,128]{2,1,0:T(8,128)(2,1)S(1)}, u32[]{:S(2)}, u32[]{:S(2)}) collective-permute-start(bf16[53,64,128]{2,1,0:T(8,128)(2,1)S(1)} %get-tuple-element.40), channel_id=1, source_target_pairs={{0,1},{1,0},{2,3},{3,2},{4,5},{5,4},{6,7},{7,6},{8,9},{9,8},{10,11... | collective-permute-start | bytes 2605064 | tf_op jit(solution)/shard_map/ppermute | solution.py:487
  30.2 20.4 %all-to-all-start = ((bf16[16,144,128]{2,1,0:T(8,128)(2,1)}), bf16[16,144,128]{2,1,0:T(8,128)(2,1)S(1)}, u32[]{:S(2)}, u32[]{:S(2)}) async-start(bf16[16,144,128]{2,1,0:T(8,128)(2,1)} %bitcast.7), calls=%async_computation | async-start | bytes 1179648 | tf_op jit(solution)/shard_map/all_to_all | solution.py:495
  50.7 4.2 %collective-permute-start.6 = (f32[144,128]{1,0:T(8,128)S(1)}, f32[144,128]{1,0:T(8,128)S(1)}, u32[]{:S(2)}, u32[]{:S(2)}) collective-permute-start(f32[144,128]{1,0:T(8,128)S(1)} %shard_map.109.own_ref), channel_id=1, source_target_pairs={{0,96},{32,0},{64,32},{96,64},{1,97},{33,1},{65,33},{97,65},{2,98}... | collective-permute-start | bytes 221192 | tf_op jit(solution)/shard_map/ppermute | solution.py:491
  53.6 4.8 %collective-permute-start.5 = (f32[144,128]{1,0:T(8,128)S(1)}, f32[144,128]{1,0:T(8,128)S(1)}, u32[]{:S(2)}, u32[]{:S(2)}) collective-permute-start(f32[144,128]{1,0:T(8,128)S(1)} %shard_map.109.own_ref), channel_id=1, source_target_pairs={{0,64},{32,96},{64,0},{96,32},{1,65},{33,97},{65,1},{97,33},{2,66}... | collective-permute-start | bytes 221192 | tf_op jit(solution)/shard_map/ppermute | solution.py:491
  53.9 5.1 %collective-permute-start.4 = (f32[144,128]{1,0:T(8,128)S(1)}, f32[144,128]{1,0:T(8,128)S(1)}, u32[]{:S(2)}, u32[]{:S(2)}) collective-permute-start(f32[144,128]{1,0:T(8,128)S(1)} %shard_map.109.own_ref), channel_id=1, source_target_pairs={{0,32},{32,64},{64,96},{96,0},{1,33},{33,65},{65,97},{97,1},{2,34}... | collective-permute-start | bytes 221192 | tf_op jit(solution)/shard_map/ppermute | solution.py:491
  60.0 14.3 %all-to-all-start.1 = ((bf16[16,144,128]{2,1,0:T(8,128)(2,1)}), bf16[16,144,128]{2,1,0:T(8,128)(2,1)S(1)}, u32[]{:S(2)}, u32[]{:S(2)}) async-start(bf16[16,144,128]{2,1,0:T(8,128)(2,1)} %shard_map.110.refs_0_), calls=%async_computation.1 | async-start | bytes 1179648 | tf_op jit(solution)/shard_map/all_to_all | solution.py:495
  74.3 4.8 %collective-permute-start.7 = (bf16[36,64,128]{2,1,0:T(8,128)(2,1)S(1)}, bf16[36,64,128]{2,1,0:T(8,128)(2,1)S(1)}, u32[]{:S(2)}, u32[]{:S(2)}) collective-permute-start(bf16[36,64,128]{2,1,0:T(8,128)(2,1)S(1)} %shard_map.112.rows_ref), channel_id=1, source_target_pairs={{0,1},{1,0},{2,3},{3,2},{4,5},{5,4},{6,7},{7,6},{8,9},{9,8},{10,11... | collective-permute-start | bytes 1769480 | tf_op jit(solution)/shard_map/ppermute | solution.py:487

commit v7 on v5

--- a/solution.py
+++ b/solution.py
@@ -195,16 +195,18 @@
     lay_slab(low, near_flag(near_ref, 0), low_shifts_ref)
     lay_slab(high, near_flag(near_ref, 17), high_shifts_ref)
 
-    acc = None
+    accs = [None, None]
     for a in range(3):
         for c in range(3):
-            below = taps(low_shifts_ref[c] if a == 0 else shifts_ref[c, a - 1])
-            above = taps(high_shifts_ref[c] if a == 2 else shifts_ref[c, 14 + a])
-            part = dot(jnp.concatenate([below, above], axis=0), weights_ref[a, c], NN)
-            acc = part if acc is None else acc + part
+            for k, rows in enumerate((
+                low_shifts_ref[c] if a == 0 else shifts_ref[c, a - 1],
+                high_shifts_ref[c] if a == 2 else shifts_ref[c, 14 + a],
+            )):
+                part = dot(taps(rows), weights_ref[a, c], NN)
+                accs[k] = part if accs[k] is None else accs[k] + part
     for s in range(2):
         for k in range(2):
-            value = acc[128 * k : 128 * k + 128, s * 128 : s * 128 + 128].reshape(8, 16, 128)
+            value = accs[k][:, s * 128 : s * 128 + 128].reshape(8, 16, 128)
             edges_ref[k, :, s] = (value + field_ref[15 * k, :, s].astype(F32)).astype(BF)
 
     down = down_ref[...]

time: 76.8 us -> 75.5 us (0.983)
  Pallas kernels: 33.4 us -> 32.1 us
    pallas_call x1, Pallas kernels: 8.25 us -> 7 us  [main_call(): call(main_kernel, [SMEM] * 3 + [VMEM] * 9, [sds((36, 64, 128), F32), sds(...]
  transfers between devices with their start and end apart: 10 -> 10, of which waited for: 5 -> 5; matrix products, arithmetic and copies ran while one was open for 0% -> 0% of each run, Pallas kernels for 26% -> 27%
where the time goes in v7:
time: 75.5 us; the launch traced here: 75.1 us
  Pallas kernels  32.1 us (43%)
  starting transfers between devices  23.8 us (32%)
  waiting for transfers between devices  16.4 us (22%)
  between operations  1.65 us (2%)
  local copies, waits for them, and re-layouts  1.11 us (1%)
    all_to_all x2, starting transfers between devices, over_plane(): return lax.all_to_all(value, ('z', 'x'), 0, 0, tiled=True)  11.5 us
    all_to_all x2, waiting for transfers between devices, over_plane(): return lax.all_to_all(value, ('z', 'x'), 0, 0, tiled=True)  11.3 us
    pallas_call x2, Pallas kernels, input_call(): call(functools.partial(input_kernel, half=half), ins, [sds((16, 8, 2, 16,...  10.5 us
    pallas_call x1, Pallas kernels, main_call(): call(main_kernel, [SMEM] * 3 + [VMEM] * 9, [sds((36, 64, 128), F32), sds(...  7 us
    ppermute x4, starting transfers between devices, over_core(): return lax.ppermute(value, 'core', [(0, 1), (1, 0)])  4.78 us
    pallas_call x1, Pallas kernels, inner_call(): call(inner_kernel, [VMEM] * 2, [sds((3, 16, 9, 2, 16, 128), BF), sds((3,...  4.77 us
    ppermute x3, starting transfers between devices, over_y(): return lax.ppermute(value, 'dp', [(i, (i + by) % 4) for i in range(4)])  3.84 us
    ppermute x1, starting transfers between devices, over_other(): return lax.ppermute(value, ('z', 'x', 'core'), pairs)  3.69 us
  transfers between devices with their start and end apart: 10, of which 5 were waited for; matrix products, arithmetic and copies ran while one was open for 0% of the time, Pallas kernels for 27%

profile of v7, /device:TPU:1, one launch (start us, length us, event | category | flops | bytes accessed | tf_op | source)
XLA Modules:
  0.0 75.1 jit_solution(2238934182404168873)
XLA Ops:
  0.6 1.1 %dynamic-slice_bitcast_fusion.after_ref = bf16[8,16,16,128]{3,2,1,0:T(8,128)(2,1)S(1)} fusion(bf16[1,1,16,16,16,128]{5,4,3,2,1,0:T(8,128)(2,1)} %param.10, s32[]{:T(128)S(6)} %select_n.3), kind=kLoop, calls=%fused_computation | loop fusion | bytes 1048580 | tf_op jit(solution)/shard_map/dynamic_slice | solution.py:507
  1.7 1.5 %collective-permute-start = (bf16[8,16,16,128]{3,2,1,0:T(8,128)(2,1)S(1)}, bf16[8,16,16,128]{3,2,1,0:T(8,128)(2,1)S(1)}, u32[]{:S(2)}, u32[]{:S(2)}) collective-permute-start(bf16[8,16,16,128]{3,2,1,0:T(8,128)(2,1)S(1)} %dynamic-slice_bitcast_fusion.after_ref), channel_id=1, source_target_pairs={{0,1},{1,0},{2,3},{3,2},{4,5},{5,4},{6,7},{7,6},{8,9},{9,8},{10,11... | collective-permute-start | bytes 1572872 | tf_op jit(solution)/shard_map/ppermute | solution.py:483
  3.9 0.0 copy-start
  3.9 0.0 copy-start.2
  3.9 1.4 %shard_map.102 = (bf16[8,16,16,128]{3,2,1,0:T(8,128)(2,1)S(1)}, bf16[512,256]{1,0:T(8,128)(2,1)S(1)}, bf16[8,2,16,128]{3,2,1,0:T(8,128)(2,1)S(1)}, bf16[8,2,16,128]{3,2,1,0:T(8,128)(2,1)S(1)}) custom-call(bf16[16,16,16,128]{3,2,1,0:T(8,128)(2,1)} %bitcast.25, bf16[2,2,2,128,128]{4,3,2,1,0:T(8,128)(2,1)} %down_hbm.1, bf16[16,8,2,16,128]{4,3,2,1,0:T(8,128)(2,1)} %bitcast.16, ...), custom_call_target="tpu_custom_call" | custom-call | bytes 1048576 | tf_op jit(solution)/shard_map/pallas_call | solution.py:366
  5.3 0.0 collective-permute-done.theirs_ref
  5.4 1.6 %shard_map.103 = (bf16[16,8,2,16,128]{4,3,2,1,0:T(8,128)(2,1)S(1)}, bf16[8,128,256]{2,1,0:T(8,128)(2,1)S(1)}, bf16[2,8,2,16,128]{4,3,2,1,0:T(8,128)(2,1)S(1)}, bf16[2,8,2,16,128]{4,3,2,1,0:T(8,128)(2,1)S(1)}) custom-call(s32[3]{0:T(128)} %bitcast.19, s32[1]{0:T(128)} %bitcast.13.parent_ref, bf16[8,16,16,128]{3,2,1,0:T(8,128)(2,1)S(1)} %get-tuple-element.28.mine_ref, ...), custom_call_target="tpu_custom_call" | custom-call | flops 268435456 | bytes 4194304 | tf_op jit(solution)/shard_map/pallas_call | solution.py:375
  6.9 0.1 collective-permute-start.1
  7.0 0.0 copy-start.1
  7.0 0.0 copy-start.3
  7.0 3.7 %collective-permute-start.2 = (bf16[2,8,2,16,128]{4,3,2,1,0:T(8,128)(2,1)S(1)}, bf16[2,8,2,16,128]{4,3,2,1,0:T(8,128)(2,1)S(1)}, u32[]{:S(2)}, u32[]{:S(2)}) collective-permute-start(bf16[2,8,2,16,128]{4,3,2,1,0:T(8,128)(2,1)S(1)} %get-tuple-element.33), channel_id=1, source_target_pairs={{1,2},{3,4},{5,6},{7,8},{9,10},{11,12},{13,14},{15,16},{17,18},{19... | collective-permute-start | bytes 393224 | tf_op jit(solution)/shard_map/ppermute | solution.py:500
  10.7 0.0 copy-done
  10.7 0.0 copy-done.2
  10.8 4.8 %shard_map.104 = (bf16[3,16,9,2,16,128]{5,4,3,2,1,0:T(8,128)(2,1)S(1)}, bf16[3,3,512,256]{3,2,1,0:T(8,128)(2,1)S(1)}, bf16[16,8,2,16,128]{4,3,2,1,0:T(8,128)(2,1)S(1)}) custom-call(bf16[16,8,2,16,128]{4,3,2,1,0:T(8,128)(2,1)S(1)} %bitcast.17, bf16[3,3,3,128,128]{4,3,2,1,0:T(8,128)(2,1)S(1)} %copy-done.2), custom_call_target="tpu_custom_call" | custom-call | flops 4831838208 | bytes 2097152 | tf_op jit(solution)/shard_map/pallas_call | solution.py:383
  15.5 0.0 collective-permute-done.1.partner_ref
  15.5 0.0 collective-permute-done.2.other_ref
  15.6 0.0 copy-done.1
  15.6 0.0 copy-done.3
  15.6 7.0 %shard_map.105 = (f32[36,64,128]{2,1,0:T(8,128)S(1)}, bf16[53,64,128]{2,1,0:T(8,128)(2,1)S(1)}, bf16[8,8,16,128]{3,2,1,0:T(8,128)(2,1)S(1)}) custom-call(s32[3]{0:T(128)S(1)} %bitcast.20, s32[1]{0:T(128)} %bitcast.14.parent_ref, s32[26]{0:T(128)S(1)} %bitcast.22, bf16[16,8,2,16,128]{4,3,2,1,0:T(8,128)(2,1)S(1)} %bitcast.18, ...), custom_call_target="tpu_custom_call" | custom-call | flops 4831838208 | bytes 1048576 | tf_op jit(solution)/shard_map/pallas_call | solution.py:392
  22.6 0.1 collective-permute-start.3
  22.7 2.4 %collective-permute-done.3.got_ref = bf16[53,64,128]{2,1,0:T(8,128)(2,1)S(1)} collective-permute-done((bf16[53,64,128]{2,1,0:T(8,128)(2,1)S(1)}, bf16[53,64,128]{2,1,0:T(8,128)(2,1)S(1)}, u32[]{:S(2)}, u32[]{:S(2)}) %collective-permute-start.3) | collective-permute-done | bytes 868384 | tf_op jit(solution)/shard_map/ppermute | solution.py:483
  25.1 0.9 %shard_map.106.refs_0_ = bf16[36,64,128]{2,1,0:T(8,128)(2,1)} custom-call(f32[36,64,128]{2,1,0:T(8,128)S(1)} %get-tuple-element.41.kept_ref, bf16[53,64,128]{2,1,0:T(8,128)(2,1)S(1)} %collective-permute-done.3.got_ref), custom_call_target="tpu_custom_call" | custom-call | bytes 1048576 | tf_op jit(solution)/shard_map/pallas_call | solution.py:495
  26.0 7.3 %all-to-all-start = ((bf16[16,144,128]{2,1,0:T(8,128)(2,1)}), bf16[16,144,128]{2,1,0:T(8,128)(2,1)S(1)}, u32[]{:S(2)}, u32[]{:S(2)}) async-start(bf16[16,144,128]{2,1,0:T(8,128)(2,1)} %bitcast.6), calls=%async_computation | async-start | bytes 1179648 | tf_op jit(solution)/shard_map/all_to_all | solution.py:491
  33.3 5.2 %shard_map.107 = (bf16[16,8,2,16,128]{4,3,2,1,0:T(8,128)(2,1)}, f32[8,128]{1,0:T(8,128)S(1)}) custom-call(s32[26]{0:T(128)S(1)} %bitcast.23, bf16[16,8,2,16,128]{4,3,2,1,0:T(8,128)(2,1)S(1)} %get-tuple-element.37.grads_ref.field_ref, bf16[2,8,2,16,128]{4,3,2,1,0:T(8,128)(2,1)S(1)} %collective-permute-done.1.partner_ref, ...), custom_call_target="tpu_custom_call" | custom-call | flops 2415919104 | bytes 1048576 | tf_op jit(solution)/shard_map/pallas_call | solution.py:405
  38.6 6.4 %all-to-all-done.got_ref = bf16[16,144,128]{2,1,0:T(8,128)(2,1)S(1)} async-done(((bf16[16,144,128]{2,1,0:T(8,128)(2,1)}), bf16[16,144,128]{2,1,0:T(8,128)(2,1)S(1)}, u32[]{:S(2)}, u32[]{:S(2)}) %all-to-all-start) | async-done | bytes 589856 | tf_op jit(solution)/shard_map/all_to_all | solution.py:491
  44.9 0.1 shard_map.108.after_ref.own_ref
  45.0 2.8 %collective-permute-start.6 = (f32[144,128]{1,0:T(8,128)S(1)}, f32[144,128]{1,0:T(8,128)S(1)}, u32[]{:S(2)}, u32[]{:S(2)}) collective-permute-start(f32[144,128]{1,0:T(8,128)S(1)} %shard_map.108.after_ref.own_ref), channel_id=1, source_target_pairs={{0,96},{32,0},{64,32},{96,64},{1,97},{33,1},{65,33},{97,65},{2,98}... | collective-permute-start | bytes 221192 | tf_op jit(solution)/shard_map/ppermute | solution.py:487
  47.8 0.3 collective-permute-start.5
  48.2 0.7 collective-permute-start.4
  48.9 1.7 %shard_map.109 = (bf16[16,16,16,128]{3,2,1,0:T(8,128)(2,1)}, f32[8,128]{1,0:T(8,128)S(1)}) custom-call(s32[3]{0:T(128)S(1)} %bitcast.21, bf16[8,8,16,128]{3,2,1,0:T(8,128)(2,1)S(1)} %get-tuple-element.39.keep_ref, bf16[53,64,128]{2,1,0:T(8,128)(2,1)S(1)} %collective-permute-done.3.got_ref, f32[144,128]{1,0:T(8,128)S(1)} %shard_map.108.after_ref.own_ref), custom_call_target="tpu_custom_call" | custom-call | bytes 1048576 | tf_op jit(solution)/shard_map/pallas_call | solution.py:418
  50.5 0.0 collective-permute-done.6.refs_2_
  50.6 2.1 %collective-permute-done.5.refs_1_ = f32[144,128]{1,0:T(8,128)S(1)} collective-permute-done((f32[144,128]{1,0:T(8,128)S(1)}, f32[144,128]{1,0:T(8,128)S(1)}, u32[]{:S(2)}, u32[]{:S(2)}) %collective-permute-start.5) | collective-permute-done | bytes 73760 | tf_op jit(solution)/shard_map/ppermute | solution.py:487
  52.6 0.7 collective-permute-done.4.refs_0_
  53.3 0.9 %shard_map.110.refs_0_ = bf16[16,144,128]{2,1,0:T(8,128)(2,1)} custom-call(f32[144,128]{1,0:T(8,128)S(1)} %shard_map.108.after_ref.own_ref, f32[144,128]{1,0:T(8,128)S(1)} %collective-permute-done.4.refs_0_, f32[144,128]{1,0:T(8,128)S(1)} %collective-permute-done.5.refs_1_, f32[144,128]{1,0:T(8,128)S(1)} %collective-permute-done.6.refs_2_, ...), custom_call_target="tpu_custom_call" | custom-call | bytes 1048576 | tf_op jit(solution)/shard_map/pallas_call | solution.py:495
  54.2 4.2 %all-to-all-start.1 = ((bf16[16,144,128]{2,1,0:T(8,128)(2,1)}), bf16[16,144,128]{2,1,0:T(8,128)(2,1)S(1)}, u32[]{:S(2)}, u32[]{:S(2)}) async-start(bf16[16,144,128]{2,1,0:T(8,128)(2,1)} %shard_map.110.refs_0_), calls=%async_computation.1 | async-start | bytes 1179648 | tf_op jit(solution)/shard_map/all_to_all | solution.py:491
  58.4 5.2 %shard_map.111 = (bf16[16,8,2,16,128]{4,3,2,1,0:T(8,128)(2,1)}, f32[8,128]{1,0:T(8,128)S(1)}) custom-call(s32[26]{0:T(128)S(1)} %bitcast.24, bf16[16,8,2,16,128]{4,3,2,1,0:T(8,128)(2,1)S(1)} %get-tuple-element.37.grads_ref.field_ref, bf16[2,8,2,16,128]{4,3,2,1,0:T(8,128)(2,1)S(1)} %collective-permute-done.1.partner_ref, ...), custom_call_target="tpu_custom_call", output_to_operand_aliasing={{0}: (6, {})} | custom-call | flops 2415919104 | bytes 1048576 | tf_op jit(solution)/shard_map/pallas_call | solution.py:405
  63.6 4.9 %all-to-all-done.1 = bf16[16,144,128]{2,1,0:T(8,128)(2,1)S(1)} async-done(((bf16[16,144,128]{2,1,0:T(8,128)(2,1)}), bf16[16,144,128]{2,1,0:T(8,128)(2,1)S(1)}, u32[]{:S(2)}, u32[]{:S(2)}) %all-to-all-start.1) | async-done | bytes 589856 | tf_op jit(solution)/shard_map/all_to_all | solution.py:491
  68.5 3.1 %collective-permute-start.7 = (bf16[36,64,128]{2,1,0:T(8,128)(2,1)S(1)}, bf16[36,64,128]{2,1,0:T(8,128)(2,1)S(1)}, u32[]{:S(2)}, u32[]{:S(2)}) collective-permute-start(bf16[36,64,128]{2,1,0:T(8,128)(2,1)S(1)} %shard_map.112.rows_ref), channel_id=1, source_target_pairs={{0,1},{1,0},{2,3},{3,2},{4,5},{5,4},{6,7},{7,6},{8,9},{9,8},{10,11... | collective-permute-start | bytes 1769480 | tf_op jit(solution)/shard_map/ppermute | solution.py:483
  71.6 1.6 %shard_map.113 = (f32[27,128,128]{2,1,0:T(8,128)}, f32[8,128,128]{2,1,0:T(8,128)}, f32[8,128]{1,0:T(8,128)}) custom-call(bf16[36,64,128]{2,1,0:T(8,128)(2,1)S(1)} %shard_map.112.rows_ref), custom_call_target="tpu_custom_call" | custom-call | bytes 1048576 | tf_op jit(solution)/shard_map/pallas_call | solution.py:474
  73.3 0.0 collective-permute-done.7.rows_ref
  73.3 1.6 %shard_map.114 = (f32[27,128,128]{2,1,0:T(8,128)}, f32[8,128,128]{2,1,0:T(8,128)}, f32[8,128]{1,0:T(8,128)}) custom-call(bf16[36,64,128]{2,1,0:T(8,128)(2,1)S(1)} %collective-permute-done.7.rows_ref, f32[27,128,128]{2,1,0:T(8,128)} %get-tuple-element.48.refs_0_, f32[8,128,128]{2,1,0:T(8,128)} %get-tuple-element.49.refs_1_), custom_call_target="tpu_custom_call", output_to_operand_aliasing={{0}: (1, {}), {1}: (2, {})} | custom-call | bytes 1048576 | tf_op jit(solution)/shard_map/pallas_call | solution.py:474
  (1 shorter events, 0.0 us)
Async XLA Ops:
  1.7 3.6 %collective-permute-start = (bf16[8,16,16,128]{3,2,1,0:T(8,128)(2,1)S(1)}, bf16[8,16,16,128]{3,2,1,0:T(8,128)(2,1)S(1)}, u32[]{:S(2)}, u32[]{:S(2)}) collective-permute-start(bf16[8,16,16,128]{3,2,1,0:T(8,128)(2,1)S(1)} %dynamic-slice_bitcast_fusion.after_ref), channel_id=1, source_target_pairs={{0,1},{1,0},{2,3},{3,2},{4,5},{5,4},{6,7},{7,6},{8,9},{9,8},{10,11... | collective-permute-start | bytes 1572872 | tf_op jit(solution)/shard_map/ppermute | solution.py:483
  3.9 6.9 %copy-start = (bf16[1,1,16,16,16,128]{5,4,3,2,1,0:T(8,128)(2,1)S(1)}, bf16[1,1,16,16,16,128]{5,4,3,2,1,0:T(8,128)(2,1)}, u32[]{:S(2)}) copy-start(bf16[1,1,16,16,16,128]{5,4,3,2,1,0:T(8,128)(2,1)} %param.7) | copy-start | bytes 3145732
  3.9 6.9 %copy-start.2 = (bf16[3,3,3,128,128]{4,3,2,1,0:T(8,128)(2,1)S(1)}, bf16[3,3,3,128,128]{4,3,2,1,0:T(8,128)(2,1)}, u32[]{:S(2)}) copy-start(bf16[3,3,3,128,128]{4,3,2,1,0:T(8,128)(2,1)} %conv_hbm.3) | copy-start | bytes 2654212
  6.9 8.6 %collective-permute-start.1 = (bf16[2,8,2,16,128]{4,3,2,1,0:T(8,128)(2,1)S(1)}, bf16[2,8,2,16,128]{4,3,2,1,0:T(8,128)(2,1)S(1)}, u32[]{:S(2)}, u32[]{:S(2)}) collective-permute-start(bf16[2,8,2,16,128]{4,3,2,1,0:T(8,128)(2,1)S(1)} %get-tuple-element.32), channel_id=1, source_target_pairs={{0,1},{1,0},{2,3},{3,2},{4,5},{5,4},{6,7},{7,6},{8,9},{9,8},{10,11... | collective-permute-start | bytes 393224 | tf_op jit(solution)/shard_map/ppermute | solution.py:483
  7.0 8.5 %copy-start.1 = (s32[1,1,3]{2,1,0:T(1,128)S(1)}, s32[1,1,3]{2,1,0:T(1,128)}, u32[]{:S(2)}) copy-start(s32[1,1,3]{2,1,0:T(1,128)} %param.11) | copy-start | bytes 40
  7.0 8.5 %copy-start.3 = (s32[1,1,26]{2,1,0:T(1,128)S(1)}, s32[1,1,26]{2,1,0:T(1,128)}, u32[]{:S(2)}) copy-start(s32[1,1,26]{2,1,0:T(1,128)} %param.12) | copy-start | bytes 316
  7.0 8.5 %collective-permute-start.2 = (bf16[2,8,2,16,128]{4,3,2,1,0:T(8,128)(2,1)S(1)}, bf16[2,8,2,16,128]{4,3,2,1,0:T(8,128)(2,1)S(1)}, u32[]{:S(2)}, u32[]{:S(2)}) collective-permute-start(bf16[2,8,2,16,128]{4,3,2,1,0:T(8,128)(2,1)S(1)} %get-tuple-element.33), channel_id=1, source_target_pairs={{1,2},{3,4},{5,6},{7,8},{9,10},{11,12},{13,14},{15,16},{17,18},{19... | collective-permute-start | bytes 393224 | tf_op jit(solution)/shard_map/ppermute | solution.py:500
  22.6 2.5 %collective-permute-start.3 = (bf16[53,64,128]{2,1,0:T(8,128)(2,1)S(1)}, bf16[53,64,128]{2,1,0:T(8,128)(2,1)S(1)}, u32[]{:S(2)}, u32[]{:S(2)}) collective-permute-start(bf16[53,64,128]{2,1,0:T(8,128)(2,1)S(1)} %get-tuple-element.40), channel_id=1, source_target_pairs={{0,1},{1,0},{2,3},{3,2},{4,5},{5,4},{6,7},{7,6},{8,9},{9,8},{10,11... | collective-permute-start | bytes 2605064 | tf_op jit(solution)/shard_map/ppermute | solution.py:483
  26.0 18.9 %all-to-all-start = ((bf16[16,144,128]{2,1,0:T(8,128)(2,1)}), bf16[16,144,128]{2,1,0:T(8,128)(2,1)S(1)}, u32[]{:S(2)}, u32[]{:S(2)}) async-start(bf16[16,144,128]{2,1,0:T(8,128)(2,1)} %bitcast.6), calls=%async_computation | async-start | bytes 1179648 | tf_op jit(solution)/shard_map/all_to_all | solution.py:491
  45.0 5.5 %collective-permute-start.6 = (f32[144,128]{1,0:T(8,128)S(1)}, f32[144,128]{1,0:T(8,128)S(1)}, u32[]{:S(2)}, u32[]{:S(2)}) collective-permute-start(f32[144,128]{1,0:T(8,128)S(1)} %shard_map.108.after_ref.own_ref), channel_id=1, source_target_pairs={{0,96},{32,0},{64,32},{96,64},{1,97},{33,1},{65,33},{97,65},{2,98}... | collective-permute-start | bytes 221192 | tf_op jit(solution)/shard_map/ppermute | solution.py:487
  47.8 4.8 %collective-permute-start.5 = (f32[144,128]{1,0:T(8,128)S(1)}, f32[144,128]{1,0:T(8,128)S(1)}, u32[]{:S(2)}, u32[]{:S(2)}) collective-permute-start(f32[144,128]{1,0:T(8,128)S(1)} %shard_map.108.after_ref.own_ref), channel_id=1, source_target_pairs={{0,64},{32,96},{64,0},{96,32},{1,65},{33,97},{65,1},{97,33},{2,66}... | collective-permute-start | bytes 221192 | tf_op jit(solution)/shard_map/ppermute | solution.py:487
  48.2 5.1 %collective-permute-start.4 = (f32[144,128]{1,0:T(8,128)S(1)}, f32[144,128]{1,0:T(8,128)S(1)}, u32[]{:S(2)}, u32[]{:S(2)}) collective-permute-start(f32[144,128]{1,0:T(8,128)S(1)} %shard_map.108.after_ref.own_ref), channel_id=1, source_target_pairs={{0,32},{32,64},{64,96},{96,0},{1,33},{33,65},{65,97},{97,1},{2,34}... | collective-permute-start | bytes 221192 | tf_op jit(solution)/shard_map/ppermute | solution.py:487
  54.2 14.3 %all-to-all-start.1 = ((bf16[16,144,128]{2,1,0:T(8,128)(2,1)}), bf16[16,144,128]{2,1,0:T(8,128)(2,1)S(1)}, u32[]{:S(2)}, u32[]{:S(2)}) async-start(bf16[16,144,128]{2,1,0:T(8,128)(2,1)} %shard_map.110.refs_0_), calls=%async_computation.1 | async-start | bytes 1179648 | tf_op jit(solution)/shard_map/all_to_all | solution.py:491
  68.5 4.7 %collective-permute-start.7 = (bf16[36,64,128]{2,1,0:T(8,128)(2,1)S(1)}, bf16[36,64,128]{2,1,0:T(8,128)(2,1)S(1)}, u32[]{:S(2)}, u32[]{:S(2)}) collective-permute-start(bf16[36,64,128]{2,1,0:T(8,128)(2,1)S(1)} %shard_map.112.rows_ref), channel_id=1, source_target_pairs={{0,1},{1,0},{2,3},{3,2},{4,5},{5,4},{6,7},{7,6},{8,9},{9,8},{10,11... | collective-permute-start | bytes 1769480 | tf_op jit(solution)/shard_map/ppermute | solution.py:483

commit v8 on v7

--- a/solution.py
+++ b/solution.py
@@ -361,6 +361,21 @@
     )
 
 
+def halves_call(kept, got):
+    return call(
+        add_halves, [VMEM] * 2, [sds((36, 64, 128), BF)],
+        [pltpu.VMEM((36, 64, 128), BF), pltpu.SemaphoreType.DMA((4,))], out=ANY,
+    )(kept, got)[0]
+
+
+def share_call(own, gots):
+    return call(
+        add_in_order, [VMEM] * 4, [sds((16, 144, 128), BF)],
+        [pltpu.VMEM((4, 144, 128), F32), pltpu.VMEM((144, 128), BF),
+         pltpu.SemaphoreType.DMA((16,))], out=ANY,
+    )(own, *gots)[0]
+
+
 def prepare_call(cotangent, down, field, after):
     layer = sds((8, 2, 16, 128), BF)
     return call(
@@ -421,8 +436,15 @@
     )(coords, keep, got, after)
 
 
-def add_halves(kept_ref, got_ref, total_ref):
-    total_ref[...] = (kept_ref[...] + got_ref[0:36].astype(F32)).astype(BF)
+def add_halves(kept_ref, got_ref, total_ref, held_ref, sems):
+    copies = []
+    for k in range(4):
+        part = slice(9 * k, 9 * k + 9)
+        held_ref[part] = (kept_ref[part] + got_ref[part].astype(F32)).astype(BF)
+        copies.append(pltpu.make_async_copy(held_ref.at[part], total_ref.at[part], sems.at[k]))
+        copies[-1].start()
+    for copy in copies:
+        copy.wait()
 
 
 def add_sixteen(got_ref, *refs):
@@ -434,12 +456,15 @@
 
 def add_in_order(own_ref, *refs):
     y = lax.axis_index("dp")
-    total_ref, slots_ref = refs[-2:]
+    total_ref, slots_ref, held_ref, sems = refs[-4:]
     for k, ref in enumerate((own_ref, *refs[:3])):
         slots_ref[(y - k + 4) % 4] = ref[...]
-    total = ((slots_ref[0] + slots_ref[1]) + (slots_ref[2] + slots_ref[3])).astype(BF)
-    for k in range(16):
-        total_ref[k] = total
+    held_ref[...] = ((slots_ref[0] + slots_ref[1]) + (slots_ref[2] + slots_ref[3])).astype(BF)
+    copies = [pltpu.make_async_copy(held_ref, total_ref.at[k], sems.at[k]) for k in range(16)]
+    for copy in copies:
+        copy.start()
+    for copy in copies:
+        copy.wait()
 
 
 def after_call(value, token):
@@ -517,16 +542,13 @@
     )
 
     got = over_core(sent)
-    own = stage(add_halves, (kept, got), [sds((36, 64, 128), BF)])[0]
+    own = halves_call(kept, got)
     gots = over_plane(own.reshape(16, 144, 128))
     partial_grad, token = input_call(near, grads, partner, other, far(conv_weight), own, 0)
+    coarse, token = coarse_call(coords, keep, got, token)
     own = stage(add_sixteen, (gots,), [sds((144, 128), F32)], (token,))[0]
     gots = [over_y(own, k) for k in (1, 2, 3)]
-    coarse, token = coarse_call(coords, keep, got, own)
-    shares = stage(
-        add_in_order, (own, *gots), [sds((16, 144, 128), BF)], (token,),
-        scratch=[pltpu.VMEM((4, 144, 128), F32)],
-    )[0]
+    shares = share_call(own, gots)
 
     own = over_plane(shares).reshape(36, 64, 128)
     input_grad, token = input_call(near, grads, partner, other, far(conv_weight), shares, 1, partial_grad)

time: 75.5 us -> 75.6 us (level)
    pallas_call x0 -> x2, Pallas kernels: none -> 1.87 us  [the longest x1 0.99 us: share_call(): call(add_in_order, [VMEM] * 4, [sds((16, 144, 128), BF)], [pltpu.VMEM((4,...]
    pallas_call x3 -> x1, Pallas kernels: 1.93 us -> 0.08 us  [stage(): call(kernel, [VMEM] * len(values) + [ANY] * len(after), outs, scratch)]
    all_to_all x2, waiting for transfers between devices: 11.3 us -> 9.58 us  [over_plane(): return lax.all_to_all(value, ('z', 'x'), 0, 0, tiled=True)]
    ppermute x3, waiting for transfers between devices: 2.79 us -> 4.46 us  [over_y(): return lax.ppermute(value, 'dp', [(i, (i + by) % 4) for i in range(4)])]
  transfers between devices with their start and end apart: 10 -> 10, of which waited for: 5 -> 6; matrix products, arithmetic and copies ran while one was open for 0% -> 0% of each run, Pallas kernels for 27% -> 27%
where the time goes in v8:
time: 75.6 us; the launch traced here: 75.2 us
  Pallas kernels  32.2 us (43%)
  starting transfers between devices  23.8 us (31%)
  waiting for transfers between devices  16.4 us (22%)
  between operations  1.66 us (2%)
  local copies, waits for them, and re-layouts  1.11 us (1%)
    all_to_all x2, starting transfers between devices, over_plane(): return lax.all_to_all(value, ('z', 'x'), 0, 0, tiled=True)  11.5 us
    pallas_call x2, Pallas kernels, input_call(): call(functools.partial(input_kernel, half=half), ins, [sds((16, 8, 2, 16,...  10.5 us
    all_to_all x2, waiting for transfers between devices, over_plane(): return lax.all_to_all(value, ('z', 'x'), 0, 0, tiled=True)  9.58 us
    pallas_call x1, Pallas kernels, main_call(): call(main_kernel, [SMEM] * 3 + [VMEM] * 9, [sds((36, 64, 128), F32), sds(...  7 us
    ppermute x4, starting transfers between devices, over_core(): return lax.ppermute(value, 'core', [(0, 1), (1, 0)])  4.78 us
    pallas_call x1, Pallas kernels, inner_call(): call(inner_kernel, [VMEM] * 2, [sds((3, 16, 9, 2, 16, 128), BF), sds((3,...  4.77 us
    ppermute x3, waiting for transfers between devices, over_y(): return lax.ppermute(value, 'dp', [(i, (i + by) % 4) for i in range(4)])  4.46 us
    ppermute x3, starting transfers between devices, over_y(): return lax.ppermute(value, 'dp', [(i, (i + by) % 4) for i in range(4)])  3.84 us
  transfers between devices with their start and end apart: 10, of which 6 were waited for; matrix products, arithmetic and copies ran while one was open for 0% of the time, Pallas kernels for 27%

profile of v8, /device:TPU:1, one launch (start us, length us, event | category | flops | bytes accessed | tf_op | source)
XLA Modules:
  0.0 75.2 jit_solution(15520700849832138562)
XLA Ops:
  0.6 1.1 %dynamic-slice_bitcast_fusion.after_ref = bf16[8,16,16,128]{3,2,1,0:T(8,128)(2,1)S(1)} fusion(bf16[1,1,16,16,16,128]{5,4,3,2,1,0:T(8,128)(2,1)} %param.10, s32[]{:T(128)S(6)} %select_n.3), kind=kLoop, calls=%fused_computation | loop fusion | bytes 1048580 | tf_op jit(solution)/shard_map/dynamic_slice | solution.py:532
  1.7 1.5 %collective-permute-start = (bf16[8,16,16,128]{3,2,1,0:T(8,128)(2,1)S(1)}, bf16[8,16,16,128]{3,2,1,0:T(8,128)(2,1)S(1)}, u32[]{:S(2)}, u32[]{:S(2)}) collective-permute-start(bf16[8,16,16,128]{3,2,1,0:T(8,128)(2,1)S(1)} %dynamic-slice_bitcast_fusion.after_ref), channel_id=1, source_target_pairs={{0,1},{1,0},{2,3},{3,2},{4,5},{5,4},{6,7},{7,6},{8,9},{9,8},{10,11... | collective-permute-start | bytes 1572872 | tf_op jit(solution)/shard_map/ppermute | solution.py:508
  3.9 0.0 copy-start
  3.9 0.0 copy-start.2
  3.9 1.4 %shard_map.102 = (bf16[8,16,16,128]{3,2,1,0:T(8,128)(2,1)S(1)}, bf16[512,256]{1,0:T(8,128)(2,1)S(1)}, bf16[8,2,16,128]{3,2,1,0:T(8,128)(2,1)S(1)}, bf16[8,2,16,128]{3,2,1,0:T(8,128)(2,1)S(1)}) custom-call(bf16[16,16,16,128]{3,2,1,0:T(8,128)(2,1)} %bitcast.25, bf16[2,2,2,128,128]{4,3,2,1,0:T(8,128)(2,1)} %down_hbm.1, bf16[16,8,2,16,128]{4,3,2,1,0:T(8,128)(2,1)} %bitcast.16, ...), custom_call_target="tpu_custom_call" | custom-call | bytes 1048576 | tf_op jit(solution)/shard_map/pallas_call | solution.py:381
  5.3 0.0 collective-permute-done.theirs_ref
  5.4 1.6 %shard_map.103 = (bf16[16,8,2,16,128]{4,3,2,1,0:T(8,128)(2,1)S(1)}, bf16[8,128,256]{2,1,0:T(8,128)(2,1)S(1)}, bf16[2,8,2,16,128]{4,3,2,1,0:T(8,128)(2,1)S(1)}, bf16[2,8,2,16,128]{4,3,2,1,0:T(8,128)(2,1)S(1)}) custom-call(s32[3]{0:T(128)} %bitcast.19, s32[1]{0:T(128)} %bitcast.13.parent_ref, bf16[8,16,16,128]{3,2,1,0:T(8,128)(2,1)S(1)} %get-tuple-element.28.mine_ref, ...), custom_call_target="tpu_custom_call" | custom-call | flops 268435456 | bytes 4194304 | tf_op jit(solution)/shard_map/pallas_call | solution.py:390
  6.9 0.1 collective-permute-start.1
  7.0 0.0 copy-start.1
  7.0 0.0 copy-start.3
  7.0 3.7 %collective-permute-start.2 = (bf16[2,8,2,16,128]{4,3,2,1,0:T(8,128)(2,1)S(1)}, bf16[2,8,2,16,128]{4,3,2,1,0:T(8,128)(2,1)S(1)}, u32[]{:S(2)}, u32[]{:S(2)}) collective-permute-start(bf16[2,8,2,16,128]{4,3,2,1,0:T(8,128)(2,1)S(1)} %get-tuple-element.33), channel_id=1, source_target_pairs={{1,2},{3,4},{5,6},{7,8},{9,10},{11,12},{13,14},{15,16},{17,18},{19... | collective-permute-start | bytes 393224 | tf_op jit(solution)/shard_map/ppermute | solution.py:525
  10.7 0.0 copy-done
  10.7 0.0 copy-done.2
  10.8 4.8 %shard_map.104 = (bf16[3,16,9,2,16,128]{5,4,3,2,1,0:T(8,128)(2,1)S(1)}, bf16[3,3,512,256]{3,2,1,0:T(8,128)(2,1)S(1)}, bf16[16,8,2,16,128]{4,3,2,1,0:T(8,128)(2,1)S(1)}) custom-call(bf16[16,8,2,16,128]{4,3,2,1,0:T(8,128)(2,1)S(1)} %bitcast.17, bf16[3,3,3,128,128]{4,3,2,1,0:T(8,128)(2,1)S(1)} %copy-done.2), custom_call_target="tpu_custom_call" | custom-call | flops 4831838208 | bytes 2097152 | tf_op jit(solution)/shard_map/pallas_call | solution.py:398
  15.5 0.0 collective-permute-done.1.partner_ref
  15.5 0.0 collective-permute-done.2.other_ref
  15.6 0.0 copy-done.1
  15.6 0.0 copy-done.3
  15.6 7.0 %shard_map.105 = (f32[36,64,128]{2,1,0:T(8,128)S(1)}, bf16[53,64,128]{2,1,0:T(8,128)(2,1)S(1)}, bf16[8,8,16,128]{3,2,1,0:T(8,128)(2,1)S(1)}) custom-call(s32[3]{0:T(128)S(1)} %bitcast.20, s32[1]{0:T(128)} %bitcast.14.parent_ref, s32[26]{0:T(128)S(1)} %bitcast.22, bf16[16,8,2,16,128]{4,3,2,1,0:T(8,128)(2,1)S(1)} %bitcast.18, ...), custom_call_target="tpu_custom_call" | custom-call | flops 4831838208 | bytes 1048576 | tf_op jit(solution)/shard_map/pallas_call | solution.py:407
  22.6 0.1 collective-permute-start.3
  22.7 2.4 %collective-permute-done.3.got_ref = bf16[53,64,128]{2,1,0:T(8,128)(2,1)S(1)} collective-permute-done((bf16[53,64,128]{2,1,0:T(8,128)(2,1)S(1)}, bf16[53,64,128]{2,1,0:T(8,128)(2,1)S(1)}, u32[]{:S(2)}, u32[]{:S(2)}) %collective-permute-start.3) | collective-permute-done | bytes 868384 | tf_op jit(solution)/shard_map/ppermute | solution.py:508
  25.1 0.9 %shard_map.106.refs_0_ = bf16[36,64,128]{2,1,0:T(8,128)(2,1)} custom-call(f32[36,64,128]{2,1,0:T(8,128)S(1)} %get-tuple-element.41.kept_ref, bf16[53,64,128]{2,1,0:T(8,128)(2,1)S(1)} %collective-permute-done.3.got_ref), custom_call_target="tpu_custom_call" | custom-call | bytes 1048576 | tf_op jit(solution)/shard_map/pallas_call | solution.py:365
  26.0 7.3 %all-to-all-start = ((bf16[16,144,128]{2,1,0:T(8,128)(2,1)}), bf16[16,144,128]{2,1,0:T(8,128)(2,1)S(1)}, u32[]{:S(2)}, u32[]{:S(2)}) async-start(bf16[16,144,128]{2,1,0:T(8,128)(2,1)} %bitcast.7), calls=%async_computation | async-start | bytes 1179648 | tf_op jit(solution)/shard_map/all_to_all | solution.py:516
  33.3 5.3 %shard_map.107 = (bf16[16,8,2,16,128]{4,3,2,1,0:T(8,128)(2,1)}, f32[8,128]{1,0:T(8,128)S(1)}) custom-call(s32[26]{0:T(128)S(1)} %bitcast.23, bf16[16,8,2,16,128]{4,3,2,1,0:T(8,128)(2,1)S(1)} %get-tuple-element.37.grads_ref.field_ref, bf16[2,8,2,16,128]{4,3,2,1,0:T(8,128)(2,1)S(1)} %collective-permute-done.1.partner_ref, ...), custom_call_target="tpu_custom_call" | custom-call | flops 2415919104 | bytes 1048576 | tf_op jit(solution)/shard_map/pallas_call | solution.py:420
  38.5 1.7 %shard_map.108 = (bf16[16,16,16,128]{3,2,1,0:T(8,128)(2,1)}, f32[8,128]{1,0:T(8,128)S(1)}) custom-call(s32[3]{0:T(128)S(1)} %bitcast.21, bf16[8,8,16,128]{3,2,1,0:T(8,128)(2,1)S(1)} %get-tuple-element.39.keep_ref, bf16[53,64,128]{2,1,0:T(8,128)(2,1)S(1)} %collective-permute-done.3.got_ref, f32[8,128]{1,0:T(8,128)S(1)} %get-tuple-element.42.after_ref), custom_call_target="tpu_custom_call" | custom-call | bytes 1048576 | tf_op jit(solution)/shard_map/pallas_call | solution.py:433
  40.2 4.7 %all-to-all-done.got_ref = bf16[16,144,128]{2,1,0:T(8,128)(2,1)S(1)} async-done(((bf16[16,144,128]{2,1,0:T(8,128)(2,1)}), bf16[16,144,128]{2,1,0:T(8,128)(2,1)S(1)}, u32[]{:S(2)}, u32[]{:S(2)}) %all-to-all-start) | async-done | bytes 589856 | tf_op jit(solution)/shard_map/all_to_all | solution.py:516
  44.9 0.1 shard_map.109.own_ref
  45.0 2.8 %collective-permute-start.6 = (f32[144,128]{1,0:T(8,128)S(1)}, f32[144,128]{1,0:T(8,128)S(1)}, u32[]{:S(2)}, u32[]{:S(2)}) collective-permute-start(f32[144,128]{1,0:T(8,128)S(1)} %shard_map.109.own_ref), channel_id=1, source_target_pairs={{0,96},{32,0},{64,32},{96,64},{1,97},{33,1},{65,33},{97,65},{2,98}... | collective-permute-start | bytes 221192 | tf_op jit(solution)/shard_map/ppermute | solution.py:512
  47.8 0.3 collective-permute-start.5
  48.1 0.7 collective-permute-start.4
  48.8 0.4 collective-permute-done.6.refs_2_
  49.2 3.4 %collective-permute-done.5.refs_1_ = f32[144,128]{1,0:T(8,128)S(1)} collective-permute-done((f32[144,128]{1,0:T(8,128)S(1)}, f32[144,128]{1,0:T(8,128)S(1)}, u32[]{:S(2)}, u32[]{:S(2)}) %collective-permute-start.5) | collective-permute-done | bytes 73760 | tf_op jit(solution)/shard_map/ppermute | solution.py:512
  52.6 0.7 collective-permute-done.4.refs_0_
  53.3 1.0 %shard_map.110.refs_0_ = bf16[16,144,128]{2,1,0:T(8,128)(2,1)} custom-call(f32[144,128]{1,0:T(8,128)S(1)} %shard_map.109.own_ref, f32[144,128]{1,0:T(8,128)S(1)} %collective-permute-done.4.refs_0_, f32[144,128]{1,0:T(8,128)S(1)} %collective-permute-done.5.refs_1_, f32[144,128]{1,0:T(8,128)S(1)} %collective-permute-done.6.refs_2_), custom_call_target="tpu_custom_call" | custom-call | bytes 1048576 | tf_op jit(solution)/shard_map/pallas_call | solution.py:372
  54.3 4.2 %all-to-all-start.1 = ((bf16[16,144,128]{2,1,0:T(8,128)(2,1)}), bf16[16,144,128]{2,1,0:T(8,128)(2,1)S(1)}, u32[]{:S(2)}, u32[]{:S(2)}) async-start(bf16[16,144,128]{2,1,0:T(8,128)(2,1)} %shard_map.110.refs_0_), calls=%async_computation.1 | async-start | bytes 1179648 | tf_op jit(solution)/shard_map/all_to_all | solution.py:516
  58.5 5.2 %shard_map.111 = (bf16[16,8,2,16,128]{4,3,2,1,0:T(8,128)(2,1)}, f32[8,128]{1,0:T(8,128)S(1)}) custom-call(s32[26]{0:T(128)S(1)} %bitcast.24, bf16[16,8,2,16,128]{4,3,2,1,0:T(8,128)(2,1)S(1)} %get-tuple-element.37.grads_ref.field_ref, bf16[2,8,2,16,128]{4,3,2,1,0:T(8,128)(2,1)S(1)} %collective-permute-done.1.partner_ref, ...), custom_call_target="tpu_custom_call", output_to_operand_aliasing={{0}: (6, {})} | custom-call | flops 2415919104 | bytes 1048576 | tf_op jit(solution)/shard_map/pallas_call | solution.py:420
  63.7 4.9 %all-to-all-done.1 = bf16[16,144,128]{2,1,0:T(8,128)(2,1)S(1)} async-done(((bf16[16,144,128]{2,1,0:T(8,128)(2,1)}), bf16[16,144,128]{2,1,0:T(8,128)(2,1)S(1)}, u32[]{:S(2)}, u32[]{:S(2)}) %all-to-all-start.1) | async-done | bytes 589856 | tf_op jit(solution)/shard_map/all_to_all | solution.py:516
  68.6 3.1 %collective-permute-start.7 = (bf16[36,64,128]{2,1,0:T(8,128)(2,1)S(1)}, bf16[36,64,128]{2,1,0:T(8,128)(2,1)S(1)}, u32[]{:S(2)}, u32[]{:S(2)}) collective-permute-start(bf16[36,64,128]{2,1,0:T(8,128)(2,1)S(1)} %shard_map.112.rows_ref), channel_id=1, source_target_pairs={{0,1},{1,0},{2,3},{3,2},{4,5},{5,4},{6,7},{7,6},{8,9},{9,8},{10,11... | collective-permute-start | bytes 1769480 | tf_op jit(solution)/shard_map/ppermute | solution.py:508
  71.7 1.6 %shard_map.113 = (f32[27,128,128]{2,1,0:T(8,128)}, f32[8,128,128]{2,1,0:T(8,128)}, f32[8,128]{1,0:T(8,128)}) custom-call(bf16[36,64,128]{2,1,0:T(8,128)(2,1)S(1)} %shard_map.112.rows_ref), custom_call_target="tpu_custom_call" | custom-call | bytes 1048576 | tf_op jit(solution)/shard_map/pallas_call | solution.py:499
  73.3 0.0 collective-permute-done.7.rows_ref
  73.4 1.6 %shard_map.114 = (f32[27,128,128]{2,1,0:T(8,128)}, f32[8,128,128]{2,1,0:T(8,128)}, f32[8,128]{1,0:T(8,128)}) custom-call(bf16[36,64,128]{2,1,0:T(8,128)(2,1)S(1)} %collective-permute-done.7.rows_ref, f32[27,128,128]{2,1,0:T(8,128)} %get-tuple-element.48.refs_0_, f32[8,128,128]{2,1,0:T(8,128)} %get-tuple-element.49.refs_1_), custom_call_target="tpu_custom_call", output_to_operand_aliasing={{0}: (1, {}), {1}: (2, {})} | custom-call | bytes 1048576 | tf_op jit(solution)/shard_map/pallas_call | solution.py:499
  (1 shorter events, 0.0 us)
Async XLA Ops:
  1.7 3.6 %collective-permute-start = (bf16[8,16,16,128]{3,2,1,0:T(8,128)(2,1)S(1)}, bf16[8,16,16,128]{3,2,1,0:T(8,128)(2,1)S(1)}, u32[]{:S(2)}, u32[]{:S(2)}) collective-permute-start(bf16[8,16,16,128]{3,2,1,0:T(8,128)(2,1)S(1)} %dynamic-slice_bitcast_fusion.after_ref), channel_id=1, source_target_pairs={{0,1},{1,0},{2,3},{3,2},{4,5},{5,4},{6,7},{7,6},{8,9},{9,8},{10,11... | collective-permute-start | bytes 1572872 | tf_op jit(solution)/shard_map/ppermute | solution.py:508
  3.9 6.9 %copy-start = (bf16[1,1,16,16,16,128]{5,4,3,2,1,0:T(8,128)(2,1)S(1)}, bf16[1,1,16,16,16,128]{5,4,3,2,1,0:T(8,128)(2,1)}, u32[]{:S(2)}) copy-start(bf16[1,1,16,16,16,128]{5,4,3,2,1,0:T(8,128)(2,1)} %param.7) | copy-start | bytes 3145732
  3.9 6.9 %copy-start.2 = (bf16[3,3,3,128,128]{4,3,2,1,0:T(8,128)(2,1)S(1)}, bf16[3,3,3,128,128]{4,3,2,1,0:T(8,128)(2,1)}, u32[]{:S(2)}) copy-start(bf16[3,3,3,128,128]{4,3,2,1,0:T(8,128)(2,1)} %conv_hbm.3) | copy-start | bytes 2654212
  6.9 8.6 %collective-permute-start.1 = (bf16[2,8,2,16,128]{4,3,2,1,0:T(8,128)(2,1)S(1)}, bf16[2,8,2,16,128]{4,3,2,1,0:T(8,128)(2,1)S(1)}, u32[]{:S(2)}, u32[]{:S(2)}) collective-permute-start(bf16[2,8,2,16,128]{4,3,2,1,0:T(8,128)(2,1)S(1)} %get-tuple-element.32), channel_id=1, source_target_pairs={{0,1},{1,0},{2,3},{3,2},{4,5},{5,4},{6,7},{7,6},{8,9},{9,8},{10,11... | collective-permute-start | bytes 393224 | tf_op jit(solution)/shard_map/ppermute | solution.py:508
  7.0 8.5 %copy-start.1 = (s32[1,1,3]{2,1,0:T(1,128)S(1)}, s32[1,1,3]{2,1,0:T(1,128)}, u32[]{:S(2)}) copy-start(s32[1,1,3]{2,1,0:T(1,128)} %param.11) | copy-start | bytes 40
  7.0 8.5 %copy-start.3 = (s32[1,1,26]{2,1,0:T(1,128)S(1)}, s32[1,1,26]{2,1,0:T(1,128)}, u32[]{:S(2)}) copy-start(s32[1,1,26]{2,1,0:T(1,128)} %param.12) | copy-start | bytes 316
  7.0 8.5 %collective-permute-start.2 = (bf16[2,8,2,16,128]{4,3,2,1,0:T(8,128)(2,1)S(1)}, bf16[2,8,2,16,128]{4,3,2,1,0:T(8,128)(2,1)S(1)}, u32[]{:S(2)}, u32[]{:S(2)}) collective-permute-start(bf16[2,8,2,16,128]{4,3,2,1,0:T(8,128)(2,1)S(1)} %get-tuple-element.33), channel_id=1, source_target_pairs={{1,2},{3,4},{5,6},{7,8},{9,10},{11,12},{13,14},{15,16},{17,18},{19... | collective-permute-start | bytes 393224 | tf_op jit(solution)/shard_map/ppermute | solution.py:525
  22.6 2.5 %collective-permute-start.3 = (bf16[53,64,128]{2,1,0:T(8,128)(2,1)S(1)}, bf16[53,64,128]{2,1,0:T(8,128)(2,1)S(1)}, u32[]{:S(2)}, u32[]{:S(2)}) collective-permute-start(bf16[53,64,128]{2,1,0:T(8,128)(2,1)S(1)} %get-tuple-element.40), channel_id=1, source_target_pairs={{0,1},{1,0},{2,3},{3,2},{4,5},{5,4},{6,7},{7,6},{8,9},{9,8},{10,11... | collective-permute-start | bytes 2605064 | tf_op jit(solution)/shard_map/ppermute | solution.py:508
  26.0 18.9 %all-to-all-start = ((bf16[16,144,128]{2,1,0:T(8,128)(2,1)}), bf16[16,144,128]{2,1,0:T(8,128)(2,1)S(1)}, u32[]{:S(2)}, u32[]{:S(2)}) async-start(bf16[16,144,128]{2,1,0:T(8,128)(2,1)} %bitcast.7), calls=%async_computation | async-start | bytes 1179648 | tf_op jit(solution)/shard_map/all_to_all | solution.py:516
  45.0 4.2 %collective-permute-start.6 = (f32[144,128]{1,0:T(8,128)S(1)}, f32[144,128]{1,0:T(8,128)S(1)}, u32[]{:S(2)}, u32[]{:S(2)}) collective-permute-start(f32[144,128]{1,0:T(8,128)S(1)} %shard_map.109.own_ref), channel_id=1, source_target_pairs={{0,96},{32,0},{64,32},{96,64},{1,97},{33,1},{65,33},{97,65},{2,98}... | collective-permute-start | bytes 221192 | tf_op jit(solution)/shard_map/ppermute | solution.py:512
  47.8 4.8 %collective-permute-start.5 = (f32[144,128]{1,0:T(8,128)S(1)}, f32[144,128]{1,0:T(8,128)S(1)}, u32[]{:S(2)}, u32[]{:S(2)}) collective-permute-start(f32[144,128]{1,0:T(8,128)S(1)} %shard_map.109.own_ref), channel_id=1, source_target_pairs={{0,64},{32,96},{64,0},{96,32},{1,65},{33,97},{65,1},{97,33},{2,66}... | collective-permute-start | bytes 221192 | tf_op jit(solution)/shard_map/ppermute | solution.py:512
  48.1 5.1 %collective-permute-start.4 = (f32[144,128]{1,0:T(8,128)S(1)}, f32[144,128]{1,0:T(8,128)S(1)}, u32[]{:S(2)}, u32[]{:S(2)}) collective-permute-start(f32[144,128]{1,0:T(8,128)S(1)} %shard_map.109.own_ref), channel_id=1, source_target_pairs={{0,32},{32,64},{64,96},{96,0},{1,33},{33,65},{65,97},{97,1},{2,34}... | collective-permute-start | bytes 221192 | tf_op jit(solution)/shard_map/ppermute | solution.py:512
  54.3 14.3 %all-to-all-start.1 = ((bf16[16,144,128]{2,1,0:T(8,128)(2,1)}), bf16[16,144,128]{2,1,0:T(8,128)(2,1)S(1)}, u32[]{:S(2)}, u32[]{:S(2)}) async-start(bf16[16,144,128]{2,1,0:T(8,128)(2,1)} %shard_map.110.refs_0_), calls=%async_computation.1 | async-start | bytes 1179648 | tf_op jit(solution)/shard_map/all_to_all | solution.py:516
  68.6 4.7 %collective-permute-start.7 = (bf16[36,64,128]{2,1,0:T(8,128)(2,1)S(1)}, bf16[36,64,128]{2,1,0:T(8,128)(2,1)S(1)}, u32[]{:S(2)}, u32[]{:S(2)}) collective-permute-start(bf16[36,64,128]{2,1,0:T(8,128)(2,1)S(1)} %shard_map.112.rows_ref), channel_id=1, source_target_pairs={{0,1},{1,0},{2,3},{3,2},{4,5},{5,4},{6,7},{7,6},{8,9},{9,8},{10,11... | collective-permute-start | bytes 1769480 | tf_op jit(solution)/shard_map/ppermute | solution.py:508

commit v9 on v7

--- a/solution.py
+++ b/solution.py
@@ -77,10 +77,20 @@
 
 
 def prepare_kernel(
-    cotangent_hbm, down_hbm, field_hbm, after_ref,
-    mine_ref, down_ref, partner_ref, other_ref, sems,
+    cotangent_hbm, down_hbm, field_hbm, conv_hbm,
+    mine_ref, down_ref, partner_ref, other_ref, shifts_ref, weights_ref,
+    field_ref, conv_ref, sems,
 ):
     upper = lax.axis_index("core")
+    fetches = [
+        pltpu.make_async_copy(
+            field_hbm.at[pl.ds(4 * k, 4)], field_ref.at[pl.ds(4 * k, 4)], sems.at[14 + k]
+        )
+        for k in range(4)
+    ]
+    conv_copy = pltpu.make_async_copy(conv_hbm, conv_ref, sems.at[18])
+    for copy in (*fetches, conv_copy):
+        copy.start()
     copies = [
         pltpu.make_async_copy(field_hbm.at[15 - 15 * upper], partner_ref, sems.at[0]),
         pltpu.make_async_copy(field_hbm.at[15 * upper], other_ref, sems.at[1]),
@@ -104,6 +114,11 @@
                 )
     for copy in copies:
         copy.start()
+    for k in range(4):
+        fetches[k].wait()
+        lay_interior(field_ref, shifts_ref, 4 * k, 4 * k + 4, 0)
+    conv_copy.wait()
+    lay_weights(conv_ref, weights_ref)
     for copy in copies:
         copy.wait()
 
@@ -120,7 +135,7 @@
     wide_ref[...] = jnp.zeros_like(wide_ref)
     for i in range(8):
         mine = mine_ref[i, pl.ds(8 * oy, 8)].astype(F32)
-        theirs = theirs_ref[i, pl.ds(8 * oy, 8)].astype(F32)
+        theirs = theirs_ref[8 * (x % 2) + i, pl.ds(8 * oy, 8)].astype(F32)
         both = jnp.where(is_own, mine, theirs)
         part = jnp.where(oz == 0, both[:, 0:8], both[:, 8:16]).reshape(64, 128)
         wide_ref[i, pl.ds(0, 64, stride=2), :] = part
@@ -150,23 +165,24 @@
                     )
 
 
-def inner_kernel(field_ref, conv_ref, shifts_ref, weights_ref, outputs_ref):
-    lay_weights(conv_ref, weights_ref)
-    lay_interior(field_ref, shifts_ref, 0, 6, 0)
-    for first, count in ((1, 4), (5, 4), (9, 4), (13, 2)):
-        lay_interior(field_ref, shifts_ref, min(first + 5, 16), min(first + 9, 16), 0)
+def inner_kernel(shifts_ref, weights_ref, outputs_ref):
+    for first, count in ((1, 7), (8, 7)):
         acc = None
         for a in range(3):
             for c in range(3):
                 part = dot(window(shifts_ref, c, first + a - 1, count), weights_ref[a, c], NN)
                 acc = part if acc is None else acc + part
         for s in range(2):
-            field = field_ref[first : first + count, :, s].astype(F32)
+            field = center(shifts_ref, first, count, s)
             outputs_ref[first : first + count, :, s] = (
                 acc[:, s * 128 : s * 128 + 128].reshape(count, 8, 16, 128) + field
             ).astype(BF)
 
 
+def center(shifts_ref, x, count, s):
+    return shifts_ref[1, x : x + count, s : s + 8, 1 - s].astype(F32)
+
+
 def taps(rows):
     return jnp.concatenate(
         [rows[t // 2 : t // 2 + 8, t % 2].reshape(128, 128) for t in range(4)], axis=1
@@ -174,7 +190,7 @@
 
 
 def main_kernel(
-    coords_ref, parent_ref, near_ref, field_ref, partner_ref, other_ref, shifts_ref, weights_ref,
+    coords_ref, parent_ref, near_ref, partner_ref, other_ref, shifts_ref, weights_ref,
     inner_ref, down_ref, grads_ref, spread_ref,
     kept_rows_ref, sent_ref, keep_ref, low_shifts_ref, high_shifts_ref, edges_ref, sums_ref,
 ):
@@ -207,7 +223,7 @@
     for s in range(2):
         for k in range(2):
             value = accs[k][:, s * 128 : s * 128 + 128].reshape(8, 16, 128)
-            edges_ref[k, :, s] = (value + field_ref[15 * k, :, s].astype(F32)).astype(BF)
+            edges_ref[k, :, s] = (value + center(shifts_ref, 15 * k, 1, s)[0]).astype(BF)
 
     down = down_ref[...]
 
@@ -361,13 +377,15 @@
     )
 
 
-def prepare_call(cotangent, down, field, after):
+def prepare_call(cotangent, down, field, conv):
     layer = sds((8, 2, 16, 128), BF)
     return call(
-        prepare_kernel, [HBM] * 3 + [ANY],
-        [sds((8, 16, 16, 128), BF), sds((512, 256), BF), layer, layer],
-        [pltpu.SemaphoreType.DMA((14,))], moved=1 << 20,
-    )(cotangent, down, field, after)
+        prepare_kernel, [HBM] * 4,
+        [sds((8, 16, 16, 128), BF), sds((512, 256), BF), layer, layer,
+         sds((3, 16, 9, 2, 16, 128), BF), sds((3, 3, 512, 256), BF)],
+        [pltpu.VMEM((16, 8, 2, 16, 128), BF), pltpu.VMEM((3, 3, 3, 128, 128), BF),
+         pltpu.SemaphoreType.DMA((19,))], moved=4 << 20,
+    )(cotangent, down, field, conv)
 
 
 def grad_call(coords, parent, mine, theirs, down, partner, other):
@@ -379,22 +397,21 @@
     )(coords, parent, mine, theirs, down, partner, other)
 
 
-def inner_call(field, conv):
-    return call(
-        inner_kernel, [VMEM] * 2,
-        [sds((3, 16, 9, 2, 16, 128), BF), sds((3, 3, 512, 256), BF), sds((16, 8, 2, 16, 128), BF)],
+def inner_call(shifts, weights):
+    return call(
+        inner_kernel, [VMEM] * 2, [sds((16, 8, 2, 16, 128), BF)],
         flops=2 * 9 * 2048 * 512 * 256, moved=2 << 20, limit=16,
-    )(field, conv)
-
-
-def main_call(coords, parent, near, field, partner, other, inner, down, grads, spread):
+    )(shifts, weights)[0]
+
+
+def main_call(coords, parent, near, partner, other, inner, down, grads, spread):
     slab = pltpu.VMEM((3, 9, 2, 16, 128), BF)
     return call(
-        main_kernel, [SMEM] * 3 + [VMEM] * 9,
+        main_kernel, [SMEM] * 3 + [VMEM] * 8,
         [sds((36, 64, 128), F32), sds((53, 64, 128), BF), sds((8, 8, 16, 128), BF)],
         [slab, slab, pltpu.VMEM((2, 8, 2, 16, 128), BF), pltpu.VMEM((8, 2, 128, 128), F32)],
         flops=2 * 9 * 2048 * 512 * 256, limit=24,
-    )(coords, parent, near, field, partner, other, *inner, down, grads, spread)
+    )(coords, parent, near, partner, other, *inner, down, grads, spread)
 
 
 def input_call(near, field, partner, other, conv, after, half, base=None):
@@ -502,18 +519,19 @@
 
 def local(features, conv_weight, down_weight, coarse_cotangent, brick_coords, neighbours, parents):
     coords, near, parent = brick_coords.reshape(3), neighbours.reshape(26), parents.reshape(1)
-    core = lax.axis_index("core")
     cotangent = coarse_cotangent.reshape(16, 16, 16, 128)
-    half = lax.dynamic_slice_in_dim(cotangent, 8 * (1 - core), 8)
-    theirs = over_core(half)
+    theirs = over_core(cotangent)
     field = features.reshape(16, 8, 2, 16, 128)
     far = functools.partial(pltpu.with_memory_space_constraint, memory_space=pltpu.HBM)
-    mine, down, *layers = prepare_call(far(cotangent), far(down_weight), far(field), half)
+    mine, down, partner, other, shifts, weights = prepare_call(
+        far(cotangent), far(down_weight), far(field), far(conv_weight)
+    )
+    layers = (partner, other)
     grads, spread, to_partner, to_other = grad_call(far(coords), parent, mine, theirs, down, *layers)
     partner, other = over_core(to_partner), over_other(to_other)
-    inner = inner_call(field, conv_weight)
+    inner = (shifts, weights, inner_call(shifts, weights))
     kept, sent, keep = main_call(
-        coords, parent, near, field, partner, other, inner, down, grads, spread
+        coords, parent, near, partner, other, inner, down, grads, spread
     )
 
     got = over_core(sent)

time: 75.5 us -> 75 us (level)
  local copies, waits for them, and re-layouts: 1.11 us -> 0.01 us
    dynamic_slice x1 -> x0, local copies, waits for them, and re-layouts: 1.08 us -> none  [local(): half = lax.dynamic_slice_in_dim(cotangent, 8 * (1 - core), 8)]
where the time goes in v9:
time: 75 us; the launch traced here: 74.6 us
  Pallas kernels  32.6 us (43%)
  starting transfers between devices  23.9 us (32%)
  waiting for transfers between devices  16.4 us (22%)
  between operations  1.61 us (2%)
    all_to_all x2, starting transfers between devices, over_plane(): return lax.all_to_all(value, ('z', 'x'), 0, 0, tiled=True)  11.7 us
    all_to_all x2, waiting for transfers between devices, over_plane(): return lax.all_to_all(value, ('z', 'x'), 0, 0, tiled=True)  11.3 us
    pallas_call x2, Pallas kernels, input_call(): call(functools.partial(input_kernel, half=half), ins, [sds((16, 8, 2, 16,...  10.5 us
    pallas_call x1, Pallas kernels, main_call(): call(main_kernel, [SMEM] * 3 + [VMEM] * 8, [sds((36, 64, 128), F32), sds(...  7.06 us
    ppermute x4, starting transfers between devices, over_core(): return lax.ppermute(value, 'core', [(0, 1), (1, 0)])  4.78 us
    pallas_call x1, Pallas kernels, inner_call(): call(inner_kernel, [VMEM] * 2, [sds((16, 8, 2, 16, 128), BF)], flops=2 *...  4.43 us
    ppermute x3, starting transfers between devices, over_y(): return lax.ppermute(value, 'dp', [(i, (i + by) % 4) for i in range(4)])  3.84 us
    ppermute x1, starting transfers between devices, over_other(): return lax.ppermute(value, ('z', 'x', 'core'), pairs)  3.57 us
  transfers between devices with their start and end apart: 10, of which 5 were waited for; matrix products, arithmetic and copies ran while one was open for 0% of the time, Pallas kernels for 27%

profile of v9, /device:TPU:1, one launch (start us, length us, event | category | flops | bytes accessed | tf_op | source)
XLA Modules:
  0.0 74.6 jit_solution(7077002807710611622)
XLA Ops:
  0.6 1.5 %collective-permute-start = (bf16[16,16,16,128]{3,2,1,0:T(8,128)(2,1)}, bf16[16,16,16,128]{3,2,1,0:T(8,128)(2,1)S(1)}, u32[]{:S(2)}, u32[]{:S(2)}) collective-permute-start(bf16[16,16,16,128]{3,2,1,0:T(8,128)(2,1)} %bitcast.22), channel_id=1, source_target_pairs={{0,1},{1,0},{2,3},{3,2},{4,5},{5,4},{6,7},{7,6},{8,9},{9,8},{10,11... | collective-permute-start | bytes 3145736 | tf_op jit(solution)/shard_map/ppermute | solution.py:500
  2.8 2.2 %shard_map.102 = (bf16[8,16,16,128]{3,2,1,0:T(8,128)(2,1)S(1)}, bf16[512,256]{1,0:T(8,128)(2,1)S(1)}, bf16[8,2,16,128]{3,2,1,0:T(8,128)(2,1)S(1)}, bf16[8,2,16,1...) custom-call(bf16[16,16,16,128]{3,2,1,0:T(8,128)(2,1)} %bitcast.23, ...), custom_call_target="tpu_custom_call" | custom-call | bytes 4194304 | tf_op jit(solution)/shard_map/pallas_call | solution.py:382
  5.0 0.0 collective-permute-done.theirs_ref
  5.0 1.6 %shard_map.103 = (bf16[16,8,2,16,128]{4,3,2,1,0:T(8,128)(2,1)S(1)}, bf16[8,128,256]{2,1,0:T(8,128)(2,1)S(1)}, bf16[2,8,2,16,128]{4,3,2,1,0:T(8,128)(2,1)S(1)}, bf16[2,8,2,16,128]{4,3,2,1,0:T(8,128)(2,1)S(1)}) custom-call(s32[3]{0:T(128)} %bitcast.14, s32[1]{0:T(128)} %bitcast.11.parent_ref, bf16[8,16,16,128]{3,2,1,0:T(8,128)(2,1)S(1)} %get-tuple-element.27.mine_ref, ...), custom_call_target="tpu_custom_call" | custom-call | flops 268435456 | bytes 4194304 | tf_op jit(solution)/shard_map/pallas_call | solution.py:393
  6.6 0.1 collective-permute-start.1
  6.7 3.6 %collective-permute-start.2 = (bf16[2,8,2,16,128]{4,3,2,1,0:T(8,128)(2,1)S(1)}, bf16[2,8,2,16,128]{4,3,2,1,0:T(8,128)(2,1)S(1)}, u32[]{:S(2)}, u32[]{:S(2)}) collective-permute-start(bf16[2,8,2,16,128]{4,3,2,1,0:T(8,128)(2,1)S(1)} %get-tuple-element.32), channel_id=1, source_target_pairs={{1,2},{3,4},{5,6},{7,8},{9,10},{11,12},{13,14},{15,16},{17,18},{19... | collective-permute-start | bytes 393224 | tf_op jit(solution)/shard_map/ppermute | solution.py:517
  10.3 0.0 copy-start
  10.3 0.0 copy-start.1
  10.3 4.4 %shard_map.104.inner_ref = bf16[16,8,2,16,128]{4,3,2,1,0:T(8,128)(2,1)S(1)} custom-call(bf16[3,16,9,2,16,128]{5,4,3,2,1,0:T(8,128)(2,1)S(1)} %get-tuple-element.33.shifts_ref, bf16[3,3,512,256]{3,2,1,0:T(8,128)(2,1)S(1)} %get-tuple-element.34.weights_ref), custom_call_target="tpu_custom_call" | custom-call | flops 4831838208 | bytes 2097152 | tf_op jit(solution)/shard_map/pallas_call | solution.py:401
  14.7 0.0 collective-permute-done.1.partner_ref
  14.7 0.0 collective-permute-done.2.other_ref
  14.7 0.0 copy-done
  14.7 0.0 copy-done.1
  14.8 7.1 %shard_map.105 = (f32[36,64,128]{2,1,0:T(8,128)S(1)}, bf16[53,64,128]{2,1,0:T(8,128)(2,1)S(1)}, bf16[8,8,16,128]{3,2,1,0:T(8,128)(2,1)S(1)}) custom-call(s32[3]{0:T(128)S(1)} %bitcast.15, s32[1]{0:T(128)} %bitcast.12.parent_ref, s32[26]{0:T(128)S(1)} %bitcast.17, bf16[2,8,2,16,128]{4,3,2,1,0:T(8,128)(2,1)S(1)} %collective-permute-done.1.partner_ref, ...), custom_call_target="tpu_custom_call" | custom-call | flops 4831838208 | bytes 1048576 | tf_op jit(solution)/shard_map/pallas_call | solution.py:409
  21.8 0.1 collective-permute-start.3
  21.9 2.4 %collective-permute-done.3.got_ref = bf16[53,64,128]{2,1,0:T(8,128)(2,1)S(1)} collective-permute-done((bf16[53,64,128]{2,1,0:T(8,128)(2,1)S(1)}, bf16[53,64,128]{2,1,0:T(8,128)(2,1)S(1)}, u32[]{:S(2)}, u32[]{:S(2)}) %collective-permute-start.3) | collective-permute-done | bytes 868384 | tf_op jit(solution)/shard_map/ppermute | solution.py:500
  24.3 0.9 %shard_map.106.refs_0_ = bf16[36,64,128]{2,1,0:T(8,128)(2,1)} custom-call(f32[36,64,128]{2,1,0:T(8,128)S(1)} %get-tuple-element.39.kept_ref, bf16[53,64,128]{2,1,0:T(8,128)(2,1)S(1)} %collective-permute-done.3.got_ref), custom_call_target="tpu_custom_call" | custom-call | bytes 1048576 | tf_op jit(solution)/shard_map/pallas_call | solution.py:512
  25.2 7.6 %all-to-all-start = ((bf16[16,144,128]{2,1,0:T(8,128)(2,1)}), bf16[16,144,128]{2,1,0:T(8,128)(2,1)S(1)}, u32[]{:S(2)}, u32[]{:S(2)}) async-start(bf16[16,144,128]{2,1,0:T(8,128)(2,1)} %bitcast.5), calls=%async_computation | async-start | bytes 1179648 | tf_op jit(solution)/shard_map/all_to_all | solution.py:508
  32.8 5.2 %shard_map.107 = (bf16[16,8,2,16,128]{4,3,2,1,0:T(8,128)(2,1)}, f32[8,128]{1,0:T(8,128)S(1)}) custom-call(s32[26]{0:T(128)S(1)} %bitcast.18, bf16[16,8,2,16,128]{4,3,2,1,0:T(8,128)(2,1)S(1)} %get-tuple-element.35.grads_ref.field_ref, bf16[2,8,2,16,128]{4,3,2,1,0:T(8,128)(2,1)S(1)} %collective-permute-done.1.partner_ref, ...), custom_call_target="tpu_custom_call" | custom-call | flops 2415919104 | bytes 1048576 | tf_op jit(solution)/shard_map/pallas_call | solution.py:422
  38.1 6.4 %all-to-all-done.got_ref = bf16[16,144,128]{2,1,0:T(8,128)(2,1)S(1)} async-done(((bf16[16,144,128]{2,1,0:T(8,128)(2,1)}), bf16[16,144,128]{2,1,0:T(8,128)(2,1)S(1)}, u32[]{:S(2)}, u32[]{:S(2)}) %all-to-all-start) | async-done | bytes 589856 | tf_op jit(solution)/shard_map/all_to_all | solution.py:508
  44.5 0.1 shard_map.108.after_ref.own_ref
  44.5 2.8 %collective-permute-start.6 = (f32[144,128]{1,0:T(8,128)S(1)}, f32[144,128]{1,0:T(8,128)S(1)}, u32[]{:S(2)}, u32[]{:S(2)}) collective-permute-start(f32[144,128]{1,0:T(8,128)S(1)} %shard_map.108.after_ref.own_ref), channel_id=1, source_target_pairs={{0,96},{32,0},{64,32},{96,64},{1,97},{33,1},{65,33},{97,65},{2,98}... | collective-permute-start | bytes 221192 | tf_op jit(solution)/shard_map/ppermute | solution.py:504
  47.3 0.4 collective-permute-start.5
  47.7 0.7 collective-permute-start.4
  48.4 1.7 %shard_map.109 = (bf16[16,16,16,128]{3,2,1,0:T(8,128)(2,1)}, f32[8,128]{1,0:T(8,128)S(1)}) custom-call(s32[3]{0:T(128)S(1)} %bitcast.16, bf16[8,8,16,128]{3,2,1,0:T(8,128)(2,1)S(1)} %get-tuple-element.37.keep_ref, bf16[53,64,128]{2,1,0:T(8,128)(2,1)S(1)} %collective-permute-done.3.got_ref, f32[144,128]{1,0:T(8,128)S(1)} %shard_map.108.after_ref.own_ref), custom_call_target="tpu_custom_call" | custom-call | bytes 1048576 | tf_op jit(solution)/shard_map/pallas_call | solution.py:435
  50.0 0.0 collective-permute-done.6.refs_2_
  50.1 2.1 %collective-permute-done.5.refs_1_ = f32[144,128]{1,0:T(8,128)S(1)} collective-permute-done((f32[144,128]{1,0:T(8,128)S(1)}, f32[144,128]{1,0:T(8,128)S(1)}, u32[]{:S(2)}, u32[]{:S(2)}) %collective-permute-start.5) | collective-permute-done | bytes 73760 | tf_op jit(solution)/shard_map/ppermute | solution.py:504
  52.1 0.7 collective-permute-done.4.refs_0_
  52.8 0.9 %shard_map.110.refs_0_ = bf16[16,144,128]{2,1,0:T(8,128)(2,1)} custom-call(f32[144,128]{1,0:T(8,128)S(1)} %shard_map.108.after_ref.own_ref, f32[144,128]{1,0:T(8,128)S(1)} %collective-permute-done.4.refs_0_, f32[144,128]{1,0:T(8,128)S(1)} %collective-permute-done.5.refs_1_, f32[144,128]{1,0:T(8,128)S(1)} %collective-permute-done.6.refs_2_, ...), custom_call_target="tpu_custom_call" | custom-call | bytes 1048576 | tf_op jit(solution)/shard_map/pallas_call | solution.py:512
  53.7 4.2 %all-to-all-start.1 = ((bf16[16,144,128]{2,1,0:T(8,128)(2,1)}), bf16[16,144,128]{2,1,0:T(8,128)(2,1)S(1)}, u32[]{:S(2)}, u32[]{:S(2)}) async-start(bf16[16,144,128]{2,1,0:T(8,128)(2,1)} %shard_map.110.refs_0_), calls=%async_computation.1 | async-start | bytes 1179648 | tf_op jit(solution)/shard_map/all_to_all | solution.py:508
  57.9 5.2 %shard_map.111 = (bf16[16,8,2,16,128]{4,3,2,1,0:T(8,128)(2,1)}, f32[8,128]{1,0:T(8,128)S(1)}) custom-call(s32[26]{0:T(128)S(1)} %bitcast.19, bf16[16,8,2,16,128]{4,3,2,1,0:T(8,128)(2,1)S(1)} %get-tuple-element.35.grads_ref.field_ref, bf16[2,8,2,16,128]{4,3,2,1,0:T(8,128)(2,1)S(1)} %collective-permute-done.1.partner_ref, ...), custom_call_target="tpu_custom_call", output_to_operand_aliasing={{0}: (6, {})} | custom-call | flops 2415919104 | bytes 1048576 | tf_op jit(solution)/shard_map/pallas_call | solution.py:422
  63.1 4.9 %all-to-all-done.1 = bf16[16,144,128]{2,1,0:T(8,128)(2,1)S(1)} async-done(((bf16[16,144,128]{2,1,0:T(8,128)(2,1)}), bf16[16,144,128]{2,1,0:T(8,128)(2,1)S(1)}, u32[]{:S(2)}, u32[]{:S(2)}) %all-to-all-start.1) | async-done | bytes 589856 | tf_op jit(solution)/shard_map/all_to_all | solution.py:508
  68.0 3.1 %collective-permute-start.7 = (bf16[36,64,128]{2,1,0:T(8,128)(2,1)S(1)}, bf16[36,64,128]{2,1,0:T(8,128)(2,1)S(1)}, u32[]{:S(2)}, u32[]{:S(2)}) collective-permute-start(bf16[36,64,128]{2,1,0:T(8,128)(2,1)S(1)} %shard_map.112.rows_ref), channel_id=1, source_target_pairs={{0,1},{1,0},{2,3},{3,2},{4,5},{5,4},{6,7},{7,6},{8,9},{9,8},{10,11... | collective-permute-start | bytes 1769480 | tf_op jit(solution)/shard_map/ppermute | solution.py:500
  71.1 1.6 %shard_map.113 = (f32[27,128,128]{2,1,0:T(8,128)}, f32[8,128,128]{2,1,0:T(8,128)}, f32[8,128]{1,0:T(8,128)}) custom-call(bf16[36,64,128]{2,1,0:T(8,128)(2,1)S(1)} %shard_map.112.rows_ref), custom_call_target="tpu_custom_call" | custom-call | bytes 1048576 | tf_op jit(solution)/shard_map/pallas_call | solution.py:491
  72.8 0.0 collective-permute-done.7.rows_ref
  72.8 1.6 %shard_map.114 = (f32[27,128,128]{2,1,0:T(8,128)}, f32[8,128,128]{2,1,0:T(8,128)}, f32[8,128]{1,0:T(8,128)}) custom-call(bf16[36,64,128]{2,1,0:T(8,128)(2,1)S(1)} %collective-permute-done.7.rows_ref, f32[27,128,128]{2,1,0:T(8,128)} %get-tuple-element.46.refs_0_, f32[8,128,128]{2,1,0:T(8,128)} %get-tuple-element.47.refs_1_), custom_call_target="tpu_custom_call", output_to_operand_aliasing={{0}: (1, {}), {1}: (2, {})} | custom-call | bytes 1048576 | tf_op jit(solution)/shard_map/pallas_call | solution.py:491
  (1 shorter events, 0.0 us)
Async XLA Ops:
  0.6 4.4 %collective-permute-start = (bf16[16,16,16,128]{3,2,1,0:T(8,128)(2,1)}, bf16[16,16,16,128]{3,2,1,0:T(8,128)(2,1)S(1)}, u32[]{:S(2)}, u32[]{:S(2)}) collective-permute-start(bf16[16,16,16,128]{3,2,1,0:T(8,128)(2,1)} %bitcast.22), channel_id=1, source_target_pairs={{0,1},{1,0},{2,3},{3,2},{4,5},{5,4},{6,7},{7,6},{8,9},{9,8},{10,11... | collective-permute-start | bytes 3145736 | tf_op jit(solution)/shard_map/ppermute | solution.py:500
  6.6 8.1 %collective-permute-start.1 = (bf16[2,8,2,16,128]{4,3,2,1,0:T(8,128)(2,1)S(1)}, bf16[2,8,2,16,128]{4,3,2,1,0:T(8,128)(2,1)S(1)}, u32[]{:S(2)}, u32[]{:S(2)}) collective-permute-start(bf16[2,8,2,16,128]{4,3,2,1,0:T(8,128)(2,1)S(1)} %get-tuple-element.31), channel_id=1, source_target_pairs={{0,1},{1,0},{2,3},{3,2},{4,5},{5,4},{6,7},{7,6},{8,9},{9,8},{10,11... | collective-permute-start | bytes 393224 | tf_op jit(solution)/shard_map/ppermute | solution.py:500
  6.7 8.1 %collective-permute-start.2 = (bf16[2,8,2,16,128]{4,3,2,1,0:T(8,128)(2,1)S(1)}, bf16[2,8,2,16,128]{4,3,2,1,0:T(8,128)(2,1)S(1)}, u32[]{:S(2)}, u32[]{:S(2)}) collective-permute-start(bf16[2,8,2,16,128]{4,3,2,1,0:T(8,128)(2,1)S(1)} %get-tuple-element.32), channel_id=1, source_target_pairs={{1,2},{3,4},{5,6},{7,8},{9,10},{11,12},{13,14},{15,16},{17,18},{19... | collective-permute-start | bytes 393224 | tf_op jit(solution)/shard_map/ppermute | solution.py:517
  10.3 4.5 %copy-start = (s32[1,1,3]{2,1,0:T(1,128)S(1)}, s32[1,1,3]{2,1,0:T(1,128)}, u32[]{:S(2)}) copy-start(s32[1,1,3]{2,1,0:T(1,128)} %param.11) | copy-start | bytes 40
  10.3 4.5 %copy-start.1 = (s32[1,1,26]{2,1,0:T(1,128)S(1)}, s32[1,1,26]{2,1,0:T(1,128)}, u32[]{:S(2)}) copy-start(s32[1,1,26]{2,1,0:T(1,128)} %param.12) | copy-start | bytes 316
  21.8 2.5 %collective-permute-start.3 = (bf16[53,64,128]{2,1,0:T(8,128)(2,1)S(1)}, bf16[53,64,128]{2,1,0:T(8,128)(2,1)S(1)}, u32[]{:S(2)}, u32[]{:S(2)}) collective-permute-start(bf16[53,64,128]{2,1,0:T(8,128)(2,1)S(1)} %get-tuple-element.38), channel_id=1, source_target_pairs={{0,1},{1,0},{2,3},{3,2},{4,5},{5,4},{6,7},{7,6},{8,9},{9,8},{10,11... | collective-permute-start | bytes 2605064 | tf_op jit(solution)/shard_map/ppermute | solution.py:500
  25.2 19.2 %all-to-all-start = ((bf16[16,144,128]{2,1,0:T(8,128)(2,1)}), bf16[16,144,128]{2,1,0:T(8,128)(2,1)S(1)}, u32[]{:S(2)}, u32[]{:S(2)}) async-start(bf16[16,144,128]{2,1,0:T(8,128)(2,1)} %bitcast.5), calls=%async_computation | async-start | bytes 1179648 | tf_op jit(solution)/shard_map/all_to_all | solution.py:508
  44.5 5.5 %collective-permute-start.6 = (f32[144,128]{1,0:T(8,128)S(1)}, f32[144,128]{1,0:T(8,128)S(1)}, u32[]{:S(2)}, u32[]{:S(2)}) collective-permute-start(f32[144,128]{1,0:T(8,128)S(1)} %shard_map.108.after_ref.own_ref), channel_id=1, source_target_pairs={{0,96},{32,0},{64,32},{96,64},{1,97},{33,1},{65,33},{97,65},{2,98}... | collective-permute-start | bytes 221192 | tf_op jit(solution)/shard_map/ppermute | solution.py:504
  47.3 4.8 %collective-permute-start.5 = (f32[144,128]{1,0:T(8,128)S(1)}, f32[144,128]{1,0:T(8,128)S(1)}, u32[]{:S(2)}, u32[]{:S(2)}) collective-permute-start(f32[144,128]{1,0:T(8,128)S(1)} %shard_map.108.after_ref.own_ref), channel_id=1, source_target_pairs={{0,64},{32,96},{64,0},{96,32},{1,65},{33,97},{65,1},{97,33},{2,66}... | collective-permute-start | bytes 221192 | tf_op jit(solution)/shard_map/ppermute | solution.py:504
  47.7 5.1 %collective-permute-start.4 = (f32[144,128]{1,0:T(8,128)S(1)}, f32[144,128]{1,0:T(8,128)S(1)}, u32[]{:S(2)}, u32[]{:S(2)}) collective-permute-start(f32[144,128]{1,0:T(8,128)S(1)} %shard_map.108.after_ref.own_ref), channel_id=1, source_target_pairs={{0,32},{32,64},{64,96},{96,0},{1,33},{33,65},{65,97},{97,1},{2,34}... | collective-permute-start | bytes 221192 | tf_op jit(solution)/shard_map/ppermute | solution.py:504
  53.7 14.3 %all-to-all-start.1 = ((bf16[16,144,128]{2,1,0:T(8,128)(2,1)}), bf16[16,144,128]{2,1,0:T(8,128)(2,1)S(1)}, u32[]{:S(2)}, u32[]{:S(2)}) async-start(bf16[16,144,128]{2,1,0:T(8,128)(2,1)} %shard_map.110.refs_0_), calls=%async_computation.1 | async-start | bytes 1179648 | tf_op jit(solution)/shard_map/all_to_all | solution.py:508
  68.0 4.7 %collective-permute-start.7 = (bf16[36,64,128]{2,1,0:T(8,128)(2,1)S(1)}, bf16[36,64,128]{2,1,0:T(8,128)(2,1)S(1)}, u32[]{:S(2)}, u32[]{:S(2)}) collective-permute-start(bf16[36,64,128]{2,1,0:T(8,128)(2,1)S(1)} %shard_map.112.rows_ref), channel_id=1, source_target_pairs={{0,1},{1,0},{2,3},{3,2},{4,5},{5,4},{6,7},{7,6},{8,9},{9,8},{10,11... | collective-permute-start | bytes 1769480 | tf_op jit(solution)/shard_map/ppermute | solution.py:500

commit v10 on v9

--- a/solution.py
+++ b/solution.py
@@ -143,12 +143,15 @@
         even = wide_ref[i]
         spread = jnp.concatenate([even, pltpu.roll(even, 1, 0)], axis=1).astype(BF)
         spread_ref[i] = spread
+    for first in (0, 4):
+        spread = spread_ref[first : first + 4].reshape(512, 256)
         grads = dot(spread, down, NT).astype(BF)
         for p in range(2):
             for q in range(2):
                 at = (2 * p + q) * 128
-                part = grads[:, at : at + 128].reshape(8, 16, 128)
-                grads_ref[2 * i + p, :, q] = part
+                part = grads[:, at : at + 128].reshape(4, 8, 16, 128)
+                for i in range(4):
+                    grads_ref[2 * (first + i) + p, :, q] = part[i]
     upper = x % 2
     to_partner_ref[1] = grads_ref[15 - 15 * upper]
     to_other_ref[1] = grads_ref[15 * upper]
@@ -538,11 +541,11 @@
     own = stage(add_halves, (kept, got), [sds((36, 64, 128), BF)])[0]
     gots = over_plane(own.reshape(16, 144, 128))
     partial_grad, token = input_call(near, grads, partner, other, far(conv_weight), own, 0)
+    coarse, token = coarse_call(coords, keep, got, token)
     own = stage(add_sixteen, (gots,), [sds((144, 128), F32)], (token,))[0]
     gots = [over_y(own, k) for k in (1, 2, 3)]
-    coarse, token = coarse_call(coords, keep, got, own)
     shares = stage(
-        add_in_order, (own, *gots), [sds((16, 144, 128), BF)], (token,),
+        add_in_order, (own, *gots), [sds((16, 144, 128), BF)],
         scratch=[pltpu.VMEM((4, 144, 128), F32)],
     )[0]
 

time: 75 us -> 74.7 us (level)
    ppermute x3, waiting for transfers between devices: 2.79 us -> 4.46 us  [over_y(): return lax.ppermute(value, 'dp', [(i, (i + by) % 4) for i in range(4)])]
    all_to_all x2, waiting for transfers between devices: 11.3 us -> 9.61 us  [over_plane(): return lax.all_to_all(value, ('z', 'x'), 0, 0, tiled=True)]
  transfers between devices with their start and end apart: 10 -> 10, of which waited for: 5 -> 6; matrix products, arithmetic and copies ran while one was open for 0% -> 0% of each run, Pallas kernels for 27% -> 27%
where the time goes in v10:
time: 74.7 us; the launch traced here: 74.3 us
  Pallas kernels  32.3 us (43%)
  starting transfers between devices  23.9 us (32%)
  waiting for transfers between devices  16.5 us (22%)
  between operations  1.6 us (2%)
    all_to_all x2, starting transfers between devices, over_plane(): return lax.all_to_all(value, ('z', 'x'), 0, 0, tiled=True)  11.7 us
    pallas_call x2, Pallas kernels, input_call(): call(functools.partial(input_kernel, half=half), ins, [sds((16, 8, 2, 16,...  10.5 us
    all_to_all x2, waiting for transfers between devices, over_plane(): return lax.all_to_all(value, ('z', 'x'), 0, 0, tiled=True)  9.61 us
    pallas_call x1, Pallas kernels, main_call(): call(main_kernel, [SMEM] * 3 + [VMEM] * 8, [sds((36, 64, 128), F32), sds(...  7.06 us
    ppermute x4, starting transfers between devices, over_core(): return lax.ppermute(value, 'core', [(0, 1), (1, 0)])  4.78 us
    ppermute x3, waiting for transfers between devices, over_y(): return lax.ppermute(value, 'dp', [(i, (i + by) % 4) for i in range(4)])  4.46 us
    pallas_call x1, Pallas kernels, inner_call(): call(inner_kernel, [VMEM] * 2, [sds((16, 8, 2, 16, 128), BF)], flops=2 *...  4.43 us
    ppermute x3, starting transfers between devices, over_y(): return lax.ppermute(value, 'dp', [(i, (i + by) % 4) for i in range(4)])  3.85 us
  transfers between devices with their start and end apart: 10, of which 6 were waited for; matrix products, arithmetic and copies ran while one was open for 0% of the time, Pallas kernels for 27%

profile of v10, /device:TPU:1, one launch (start us, length us, event | category | flops | bytes accessed | tf_op | source)
XLA Modules:
  0.0 74.3 jit_solution(7869507542337208227)
XLA Ops:
  0.6 1.5 %collective-permute-start = (bf16[16,16,16,128]{3,2,1,0:T(8,128)(2,1)}, bf16[16,16,16,128]{3,2,1,0:T(8,128)(2,1)S(1)}, u32[]{:S(2)}, u32[]{:S(2)}) collective-permute-start(bf16[16,16,16,128]{3,2,1,0:T(8,128)(2,1)} %bitcast.22), channel_id=1, source_target_pairs={{0,1},{1,0},{2,3},{3,2},{4,5},{5,4},{6,7},{7,6},{8,9},{9,8},{10,11... | collective-permute-start | bytes 3145736 | tf_op jit(solution)/shard_map/ppermute | solution.py:503
  2.8 2.2 %shard_map.102 = (bf16[8,16,16,128]{3,2,1,0:T(8,128)(2,1)S(1)}, bf16[512,256]{1,0:T(8,128)(2,1)S(1)}, bf16[8,2,16,128]{3,2,1,0:T(8,128)(2,1)S(1)}, bf16[8,2,16,1...) custom-call(bf16[16,16,16,128]{3,2,1,0:T(8,128)(2,1)} %bitcast.23, ...), custom_call_target="tpu_custom_call" | custom-call | bytes 4194304 | tf_op jit(solution)/shard_map/pallas_call | solution.py:385
  5.0 0.0 collective-permute-done.theirs_ref
  5.0 1.3 %shard_map.103 = (bf16[16,8,2,16,128]{4,3,2,1,0:T(8,128)(2,1)S(1)}, bf16[8,128,256]{2,1,0:T(8,128)(2,1)S(1)}, bf16[2,8,2,16,128]{4,3,2,1,0:T(8,128)(2,1)S(1)}, bf16[2,8,2,16,128]{4,3,2,1,0:T(8,128)(2,1)S(1)}) custom-call(s32[3]{0:T(128)} %bitcast.14, s32[1]{0:T(128)} %bitcast.11.parent_ref, bf16[8,16,16,128]{3,2,1,0:T(8,128)(2,1)S(1)} %get-tuple-element.27.mine_ref, ...), custom_call_target="tpu_custom_call" | custom-call | flops 268435456 | bytes 4194304 | tf_op jit(solution)/shard_map/pallas_call | solution.py:396
  6.3 0.1 collective-permute-start.1
  6.4 3.6 %collective-permute-start.2 = (bf16[2,8,2,16,128]{4,3,2,1,0:T(8,128)(2,1)S(1)}, bf16[2,8,2,16,128]{4,3,2,1,0:T(8,128)(2,1)S(1)}, u32[]{:S(2)}, u32[]{:S(2)}) collective-permute-start(bf16[2,8,2,16,128]{4,3,2,1,0:T(8,128)(2,1)S(1)} %get-tuple-element.32), channel_id=1, source_target_pairs={{1,2},{3,4},{5,6},{7,8},{9,10},{11,12},{13,14},{15,16},{17,18},{19... | collective-permute-start | bytes 393224 | tf_op jit(solution)/shard_map/ppermute | solution.py:520
  9.9 0.0 copy-start
  9.9 0.0 copy-start.1
  10.0 4.4 %shard_map.104.inner_ref = bf16[16,8,2,16,128]{4,3,2,1,0:T(8,128)(2,1)S(1)} custom-call(bf16[3,16,9,2,16,128]{5,4,3,2,1,0:T(8,128)(2,1)S(1)} %get-tuple-element.33.shifts_ref, bf16[3,3,512,256]{3,2,1,0:T(8,128)(2,1)S(1)} %get-tuple-element.34.weights_ref), custom_call_target="tpu_custom_call" | custom-call | flops 4831838208 | bytes 2097152 | tf_op jit(solution)/shard_map/pallas_call | solution.py:404
  14.4 0.0 collective-permute-done.1.partner_ref
  14.4 0.0 collective-permute-done.2.other_ref
  14.4 0.0 copy-done
  14.4 0.0 copy-done.1
  14.4 7.1 %shard_map.105 = (f32[36,64,128]{2,1,0:T(8,128)S(1)}, bf16[53,64,128]{2,1,0:T(8,128)(2,1)S(1)}, bf16[8,8,16,128]{3,2,1,0:T(8,128)(2,1)S(1)}) custom-call(s32[3]{0:T(128)S(1)} %bitcast.15, s32[1]{0:T(128)} %bitcast.12.parent_ref, s32[26]{0:T(128)S(1)} %bitcast.17, bf16[2,8,2,16,128]{4,3,2,1,0:T(8,128)(2,1)S(1)} %collective-permute-done.1.partner_ref, ...), custom_call_target="tpu_custom_call" | custom-call | flops 4831838208 | bytes 1048576 | tf_op jit(solution)/shard_map/pallas_call | solution.py:412
  21.5 0.1 collective-permute-start.3
  21.6 2.4 %collective-permute-done.3.got_ref = bf16[53,64,128]{2,1,0:T(8,128)(2,1)S(1)} collective-permute-done((bf16[53,64,128]{2,1,0:T(8,128)(2,1)S(1)}, bf16[53,64,128]{2,1,0:T(8,128)(2,1)S(1)}, u32[]{:S(2)}, u32[]{:S(2)}) %collective-permute-start.3) | collective-permute-done | bytes 868384 | tf_op jit(solution)/shard_map/ppermute | solution.py:503
  24.0 0.9 %shard_map.106.refs_0_ = bf16[36,64,128]{2,1,0:T(8,128)(2,1)} custom-call(f32[36,64,128]{2,1,0:T(8,128)S(1)} %get-tuple-element.39.kept_ref, bf16[53,64,128]{2,1,0:T(8,128)(2,1)S(1)} %collective-permute-done.3.got_ref), custom_call_target="tpu_custom_call" | custom-call | bytes 1048576 | tf_op jit(solution)/shard_map/pallas_call | solution.py:515
  24.9 7.6 %all-to-all-start = ((bf16[16,144,128]{2,1,0:T(8,128)(2,1)}), bf16[16,144,128]{2,1,0:T(8,128)(2,1)S(1)}, u32[]{:S(2)}, u32[]{:S(2)}) async-start(bf16[16,144,128]{2,1,0:T(8,128)(2,1)} %bitcast.6), calls=%async_computation | async-start | bytes 1179648 | tf_op jit(solution)/shard_map/all_to_all | solution.py:511
  32.5 5.2 %shard_map.107 = (bf16[16,8,2,16,128]{4,3,2,1,0:T(8,128)(2,1)}, f32[8,128]{1,0:T(8,128)S(1)}) custom-call(s32[26]{0:T(128)S(1)} %bitcast.18, bf16[16,8,2,16,128]{4,3,2,1,0:T(8,128)(2,1)S(1)} %get-tuple-element.35.grads_ref.field_ref, bf16[2,8,2,16,128]{4,3,2,1,0:T(8,128)(2,1)S(1)} %collective-permute-done.1.partner_ref, ...), custom_call_target="tpu_custom_call" | custom-call | flops 2415919104 | bytes 1048576 | tf_op jit(solution)/shard_map/pallas_call | solution.py:425
  37.7 1.7 %shard_map.108 = (bf16[16,16,16,128]{3,2,1,0:T(8,128)(2,1)}, f32[8,128]{1,0:T(8,128)S(1)}) custom-call(s32[3]{0:T(128)S(1)} %bitcast.16, bf16[8,8,16,128]{3,2,1,0:T(8,128)(2,1)S(1)} %get-tuple-element.37.keep_ref, bf16[53,64,128]{2,1,0:T(8,128)(2,1)S(1)} %collective-permute-done.3.got_ref, f32[8,128]{1,0:T(8,128)S(1)} %get-tuple-element.40.after_ref), custom_call_target="tpu_custom_call" | custom-call | bytes 1048576 | tf_op jit(solution)/shard_map/pallas_call | solution.py:438
  39.4 4.7 %all-to-all-done.got_ref = bf16[16,144,128]{2,1,0:T(8,128)(2,1)S(1)} async-done(((bf16[16,144,128]{2,1,0:T(8,128)(2,1)}), bf16[16,144,128]{2,1,0:T(8,128)(2,1)S(1)}, u32[]{:S(2)}, u32[]{:S(2)}) %all-to-all-start) | async-done | bytes 589856 | tf_op jit(solution)/shard_map/all_to_all | solution.py:511
  44.1 0.1 shard_map.109.own_ref
  44.2 2.8 %collective-permute-start.6 = (f32[144,128]{1,0:T(8,128)S(1)}, f32[144,128]{1,0:T(8,128)S(1)}, u32[]{:S(2)}, u32[]{:S(2)}) collective-permute-start(f32[144,128]{1,0:T(8,128)S(1)} %shard_map.109.own_ref), channel_id=1, source_target_pairs={{0,96},{32,0},{64,32},{96,64},{1,97},{33,1},{65,33},{97,65},{2,98}... | collective-permute-start | bytes 221192 | tf_op jit(solution)/shard_map/ppermute | solution.py:507
  47.0 0.4 collective-permute-start.5
  47.4 0.7 collective-permute-start.4
  48.1 0.4 collective-permute-done.6.refs_2_
  48.4 3.4 %collective-permute-done.5.refs_1_ = f32[144,128]{1,0:T(8,128)S(1)} collective-permute-done((f32[144,128]{1,0:T(8,128)S(1)}, f32[144,128]{1,0:T(8,128)S(1)}, u32[]{:S(2)}, u32[]{:S(2)}) %collective-permute-start.5) | collective-permute-done | bytes 73760 | tf_op jit(solution)/shard_map/ppermute | solution.py:507
  51.8 0.7 collective-permute-done.4.refs_0_
  52.5 0.9 %shard_map.110.refs_0_ = bf16[16,144,128]{2,1,0:T(8,128)(2,1)} custom-call(f32[144,128]{1,0:T(8,128)S(1)} %shard_map.109.own_ref, f32[144,128]{1,0:T(8,128)S(1)} %collective-permute-done.4.refs_0_, f32[144,128]{1,0:T(8,128)S(1)} %collective-permute-done.5.refs_1_, f32[144,128]{1,0:T(8,128)S(1)} %collective-permute-done.6.refs_2_), custom_call_target="tpu_custom_call" | custom-call | bytes 1048576 | tf_op jit(solution)/shard_map/pallas_call | solution.py:515
  53.4 4.2 %all-to-all-start.1 = ((bf16[16,144,128]{2,1,0:T(8,128)(2,1)}), bf16[16,144,128]{2,1,0:T(8,128)(2,1)S(1)}, u32[]{:S(2)}, u32[]{:S(2)}) async-start(bf16[16,144,128]{2,1,0:T(8,128)(2,1)} %shard_map.110.refs_0_), calls=%async_computation.1 | async-start | bytes 1179648 | tf_op jit(solution)/shard_map/all_to_all | solution.py:511
  57.6 5.2 %shard_map.111 = (bf16[16,8,2,16,128]{4,3,2,1,0:T(8,128)(2,1)}, f32[8,128]{1,0:T(8,128)S(1)}) custom-call(s32[26]{0:T(128)S(1)} %bitcast.19, bf16[16,8,2,16,128]{4,3,2,1,0:T(8,128)(2,1)S(1)} %get-tuple-element.35.grads_ref.field_ref, bf16[2,8,2,16,128]{4,3,2,1,0:T(8,128)(2,1)S(1)} %collective-permute-done.1.partner_ref, ...), custom_call_target="tpu_custom_call", output_to_operand_aliasing={{0}: (6, {})} | custom-call | flops 2415919104 | bytes 1048576 | tf_op jit(solution)/shard_map/pallas_call | solution.py:425
  62.8 4.9 %all-to-all-done.1 = bf16[16,144,128]{2,1,0:T(8,128)(2,1)S(1)} async-done(((bf16[16,144,128]{2,1,0:T(8,128)(2,1)}), bf16[16,144,128]{2,1,0:T(8,128)(2,1)S(1)}, u32[]{:S(2)}, u32[]{:S(2)}) %all-to-all-start.1) | async-done | bytes 589856 | tf_op jit(solution)/shard_map/all_to_all | solution.py:511
  67.7 3.1 %collective-permute-start.7 = (bf16[36,64,128]{2,1,0:T(8,128)(2,1)S(1)}, bf16[36,64,128]{2,1,0:T(8,128)(2,1)S(1)}, u32[]{:S(2)}, u32[]{:S(2)}) collective-permute-start(bf16[36,64,128]{2,1,0:T(8,128)(2,1)S(1)} %shard_map.112.rows_ref), channel_id=1, source_target_pairs={{0,1},{1,0},{2,3},{3,2},{4,5},{5,4},{6,7},{7,6},{8,9},{9,8},{10,11... | collective-permute-start | bytes 1769480 | tf_op jit(solution)/shard_map/ppermute | solution.py:503
  70.8 1.6 %shard_map.113 = (f32[27,128,128]{2,1,0:T(8,128)}, f32[8,128,128]{2,1,0:T(8,128)}, f32[8,128]{1,0:T(8,128)}) custom-call(bf16[36,64,128]{2,1,0:T(8,128)(2,1)S(1)} %shard_map.112.rows_ref), custom_call_target="tpu_custom_call" | custom-call | bytes 1048576 | tf_op jit(solution)/shard_map/pallas_call | solution.py:494
  72.5 0.0 collective-permute-done.7.rows_ref
  72.5 1.6 %shard_map.114 = (f32[27,128,128]{2,1,0:T(8,128)}, f32[8,128,128]{2,1,0:T(8,128)}, f32[8,128]{1,0:T(8,128)}) custom-call(bf16[36,64,128]{2,1,0:T(8,128)(2,1)S(1)} %collective-permute-done.7.rows_ref, f32[27,128,128]{2,1,0:T(8,128)} %get-tuple-element.46.refs_0_, f32[8,128,128]{2,1,0:T(8,128)} %get-tuple-element.47.refs_1_), custom_call_target="tpu_custom_call", output_to_operand_aliasing={{0}: (1, {}), {1}: (2, {})} | custom-call | bytes 1048576 | tf_op jit(solution)/shard_map/pallas_call | solution.py:494
  (1 shorter events, 0.0 us)
Async XLA Ops:
  0.6 4.4 %collective-permute-start = (bf16[16,16,16,128]{3,2,1,0:T(8,128)(2,1)}, bf16[16,16,16,128]{3,2,1,0:T(8,128)(2,1)S(1)}, u32[]{:S(2)}, u32[]{:S(2)}) collective-permute-start(bf16[16,16,16,128]{3,2,1,0:T(8,128)(2,1)} %bitcast.22), channel_id=1, source_target_pairs={{0,1},{1,0},{2,3},{3,2},{4,5},{5,4},{6,7},{7,6},{8,9},{9,8},{10,11... | collective-permute-start | bytes 3145736 | tf_op jit(solution)/shard_map/ppermute | solution.py:503
  6.3 8.1 %collective-permute-start.1 = (bf16[2,8,2,16,128]{4,3,2,1,0:T(8,128)(2,1)S(1)}, bf16[2,8,2,16,128]{4,3,2,1,0:T(8,128)(2,1)S(1)}, u32[]{:S(2)}, u32[]{:S(2)}) collective-permute-start(bf16[2,8,2,16,128]{4,3,2,1,0:T(8,128)(2,1)S(1)} %get-tuple-element.31), channel_id=1, source_target_pairs={{0,1},{1,0},{2,3},{3,2},{4,5},{5,4},{6,7},{7,6},{8,9},{9,8},{10,11... | collective-permute-start | bytes 393224 | tf_op jit(solution)/shard_map/ppermute | solution.py:503
  6.4 8.0 %collective-permute-start.2 = (bf16[2,8,2,16,128]{4,3,2,1,0:T(8,128)(2,1)S(1)}, bf16[2,8,2,16,128]{4,3,2,1,0:T(8,128)(2,1)S(1)}, u32[]{:S(2)}, u32[]{:S(2)}) collective-permute-start(bf16[2,8,2,16,128]{4,3,2,1,0:T(8,128)(2,1)S(1)} %get-tuple-element.32), channel_id=1, source_target_pairs={{1,2},{3,4},{5,6},{7,8},{9,10},{11,12},{13,14},{15,16},{17,18},{19... | collective-permute-start | bytes 393224 | tf_op jit(solution)/shard_map/ppermute | solution.py:520
  9.9 4.5 %copy-start = (s32[1,1,3]{2,1,0:T(1,128)S(1)}, s32[1,1,3]{2,1,0:T(1,128)}, u32[]{:S(2)}) copy-start(s32[1,1,3]{2,1,0:T(1,128)} %param.11) | copy-start | bytes 40
  9.9 4.5 %copy-start.1 = (s32[1,1,26]{2,1,0:T(1,128)S(1)}, s32[1,1,26]{2,1,0:T(1,128)}, u32[]{:S(2)}) copy-start(s32[1,1,26]{2,1,0:T(1,128)} %param.12) | copy-start | bytes 316
  21.5 2.5 %collective-permute-start.3 = (bf16[53,64,128]{2,1,0:T(8,128)(2,1)S(1)}, bf16[53,64,128]{2,1,0:T(8,128)(2,1)S(1)}, u32[]{:S(2)}, u32[]{:S(2)}) collective-permute-start(bf16[53,64,128]{2,1,0:T(8,128)(2,1)S(1)} %get-tuple-element.38), channel_id=1, source_target_pairs={{0,1},{1,0},{2,3},{3,2},{4,5},{5,4},{6,7},{7,6},{8,9},{9,8},{10,11... | collective-permute-start | bytes 2605064 | tf_op jit(solution)/shard_map/ppermute | solution.py:503
  24.9 19.2 %all-to-all-start = ((bf16[16,144,128]{2,1,0:T(8,128)(2,1)}), bf16[16,144,128]{2,1,0:T(8,128)(2,1)S(1)}, u32[]{:S(2)}, u32[]{:S(2)}) async-start(bf16[16,144,128]{2,1,0:T(8,128)(2,1)} %bitcast.6), calls=%async_computation | async-start | bytes 1179648 | tf_op jit(solution)/shard_map/all_to_all | solution.py:511
  44.2 4.2 %collective-permute-start.6 = (f32[144,128]{1,0:T(8,128)S(1)}, f32[144,128]{1,0:T(8,128)S(1)}, u32[]{:S(2)}, u32[]{:S(2)}) collective-permute-start(f32[144,128]{1,0:T(8,128)S(1)} %shard_map.109.own_ref), channel_id=1, source_target_pairs={{0,96},{32,0},{64,32},{96,64},{1,97},{33,1},{65,33},{97,65},{2,98}... | collective-permute-start | bytes 221192 | tf_op jit(solution)/shard_map/ppermute | solution.py:507
  47.0 4.8 %collective-permute-start.5 = (f32[144,128]{1,0:T(8,128)S(1)}, f32[144,128]{1,0:T(8,128)S(1)}, u32[]{:S(2)}, u32[]{:S(2)}) collective-permute-start(f32[144,128]{1,0:T(8,128)S(1)} %shard_map.109.own_ref), channel_id=1, source_target_pairs={{0,64},{32,96},{64,0},{96,32},{1,65},{33,97},{65,1},{97,33},{2,66}... | collective-permute-start | bytes 221192 | tf_op jit(solution)/shard_map/ppermute | solution.py:507
  47.4 5.1 %collective-permute-start.4 = (f32[144,128]{1,0:T(8,128)S(1)}, f32[144,128]{1,0:T(8,128)S(1)}, u32[]{:S(2)}, u32[]{:S(2)}) collective-permute-start(f32[144,128]{1,0:T(8,128)S(1)} %shard_map.109.own_ref), channel_id=1, source_target_pairs={{0,32},{32,64},{64,96},{96,0},{1,33},{33,65},{65,97},{97,1},{2,34}... | collective-permute-start | bytes 221192 | tf_op jit(solution)/shard_map/ppermute | solution.py:507
  53.4 14.3 %all-to-all-start.1 = ((bf16[16,144,128]{2,1,0:T(8,128)(2,1)}), bf16[16,144,128]{2,1,0:T(8,128)(2,1)S(1)}, u32[]{:S(2)}, u32[]{:S(2)}) async-start(bf16[16,144,128]{2,1,0:T(8,128)(2,1)} %shard_map.110.refs_0_), calls=%async_computation.1 | async-start | bytes 1179648 | tf_op jit(solution)/shard_map/all_to_all | solution.py:511
  67.7 4.7 %collective-permute-start.7 = (bf16[36,64,128]{2,1,0:T(8,128)(2,1)S(1)}, bf16[36,64,128]{2,1,0:T(8,128)(2,1)S(1)}, u32[]{:S(2)}, u32[]{:S(2)}) collective-permute-start(bf16[36,64,128]{2,1,0:T(8,128)(2,1)S(1)} %shard_map.112.rows_ref), channel_id=1, source_target_pairs={{0,1},{1,0},{2,3},{3,2},{4,5},{5,4},{6,7},{7,6},{8,9},{9,8},{10,11... | collective-permute-start | bytes 1769480 | tf_op jit(solution)/shard_map/ppermute | solution.py:503
